TPU v7x, 32 devices: a whole 2x2x4 slice. The times are simulated.
32 devices in a mesh: gx: 4 (over z), gy: 2 (over x), gz: 4 (over y, core).
Axes of the slice: x: 2, y: 2, z: 4, core: 2. Of those that a mesh axis runs over, the one named last changes fastest.
Arguments:
- eigvecs: bfloat16 [8, 8, 16, 2, 3, 256], P('gx', 'gy', 'gz'), may hold values from -6 to 6
- links: float32 [8, 8, 16, 3, 2, 3, 3], P('gx', 'gy', 'gz'), may hold values from -6 to 6
- directions: int32 [4], replicated, may hold values from 0 to 2
- spin_mats: float32 [4, 4, 4], replicated, may hold values from -6 to 6
- forward_peram: bfloat16 [2, 1024, 1024], P(None, 'gx', 'gy'), may hold values from -0.1875 to 0.1875
- backward_peram: bfloat16 [2, 1024, 1024], P(None, 'gx', 'gy'), may hold values from -0.1875 to 0.1875
- chain_order: int32 [16, 2], P('gz'), may hold values from 0 to 3
Outputs:
- operators: bfloat16 [16, 2, 1024, 1024], P('gz', None, 'gx', 'gy')
All inputs are finite; a program needn't handle non-finite values.
Results may differ from a plain program's by a relative error of at most 0.012.
Values may be sent and summed in bfloat16 or wider, within the bound.
No kernel may reach another device: no remote copies, remote signals or barrier semaphores. Data moves between devices by JAX's collectives and lax.ppermute only.
A program may use at most 192 MiB of HBM per device.

v0:
```python
import math

import jax
import jax.numpy as jnp
from jax import lax
from jax.sharding import PartitionSpec as P


def passed_along(value, axis, steps):
    count = lax.axis_size(axis)
    pairs = [(source, (source + steps) % count) for source in range(count)]
    return lax.ppermute(value, axis, pairs)


def transport(link_dir, shifted):
    highest = lax.Precision.HIGHEST
    real_v = shifted[..., 0, :, :].astype(jnp.float32)
    imag_v = shifted[..., 1, :, :].astype(jnp.float32)
    real_u = link_dir[..., 0, :, :]
    imag_u = link_dir[..., 1, :, :]

    def apply_link(matrix, vector):
        return jnp.einsum("...ab,...bn->...an", matrix, vector, precision=highest)

    moved_re = apply_link(real_u, real_v) - apply_link(imag_u, imag_v)
    moved_im = apply_link(real_u, imag_v) + apply_link(imag_u, real_v)
    moved = jnp.stack([moved_re, moved_im], axis=-3).astype(jnp.bfloat16)
    turned = jnp.stack([moved_im, -moved_re], axis=-3).astype(jnp.bfloat16)
    return (moved, turned)


def correlation(vec_part, moved, turned):
    width = vec_part.shape[-1]
    left_side = vec_part.reshape(-1, width)
    right_side = jnp.concatenate([moved.reshape(-1, width), turned.reshape(-1, width)], axis=1)
    product = lax.dot_general(
        left_side, right_side, (((0,), (0,)), ((), ())), preferred_element_type=jnp.float32
    )
    return jnp.stack([product[:, :width], product[:, width:]])


def complex_product(left_mat, right_mat):
    row_count = left_mat.shape[1]
    stacked = left_mat.reshape(2 * row_count, left_mat.shape[2])
    first_half = jnp.dot(stacked, right_mat[0], preferred_element_type=jnp.float32)
    second_half = jnp.dot(stacked, right_mat[1], preferred_element_type=jnp.float32)
    return jnp.stack(
        [
            first_half[:row_count] - second_half[row_count:],
            second_half[:row_count] + first_half[row_count:],
        ]
    )


def product_fold(left_rows, shard_piece):
    return complex_product(left_rows, shard_piece)


def expand_spin(dir_block, chooser, spin_mats):
    highest = lax.Precision.HIGHEST
    chosen = jnp.einsum("ke,ecij->kcij", chooser, dir_block, precision=highest)
    expanded = jnp.einsum("kcij,kst->kcisjt", chosen, spin_mats, precision=highest)
    return expanded.reshape(4, 2, 4 * dir_block.shape[2], 4 * dir_block.shape[3]).astype(
        jnp.bfloat16
    )


def on_device(eigvecs, links, directions, spin_mats, forward_peram, backward_peram, chain_order):
    face_one = passed_along(lax.slice_in_dim(eigvecs, 0, 1, axis=0), "gx", -1)
    face_two = passed_along(lax.slice_in_dim(eigvecs, 0, 1, axis=1), "gy", -1)
    face_three = passed_along(lax.slice_in_dim(eigvecs, 0, 1, axis=2), "gz", -1)
    shifted = [
        jnp.concatenate([eigvecs[1:], face_one], axis=0),
        jnp.concatenate([eigvecs[:, 1:], face_two], axis=1),
        jnp.concatenate([eigvecs[:, :, 1:], face_three], axis=2),
    ]
    terms = []
    for direction in range(3):
        moved, turned = transport(links[:, :, :, direction], shifted[direction])
        terms.append(correlation(eigvecs, moved, turned))
    partial_dirs = jnp.stack(terms)
    num_vecs = eigvecs.shape[-1]
    volume = (
        eigvecs.shape[0]
        * eigvecs.shape[1]
        * eigvecs.shape[2]
        * lax.axis_size("gx")
        * lax.axis_size("gy")
        * lax.axis_size("gz")
    )
    row_tile = num_vecs // lax.axis_size("gx")
    col_tile = num_vecs // lax.axis_size("gy")
    summed = lax.psum(partial_dirs, ("gx", "gy", "gz"))
    row_start = lax.axis_index("gx") * row_tile
    col_start = lax.axis_index("gy") * col_tile
    zero_index = jnp.zeros((), jnp.int32)
    tile_dirs = lax.dynamic_slice(
        summed, (zero_index, zero_index, row_start, col_start), (3, 2, row_tile, col_tile)
    )
    tile_dirs = tile_dirs * (1.0 / math.sqrt(12.0 * volume))
    chooser = (directions[:, None] == jnp.arange(3, dtype=jnp.int32)[None, :]).astype(jnp.float32)
    inverse = 1.0 / math.sqrt(4 * num_vecs)
    peram_block = lax.all_gather(forward_peram, "gy", axis=2, tiled=True)
    results = []
    op_count = chain_order.shape[0]
    spin_tiles = expand_spin(tile_dirs, chooser, spin_mats)
    for op_index in range(op_count):
        left_elem = lax.dynamic_index_in_dim(
            spin_tiles, chain_order[op_index, 0], 0, keepdims=False
        )
        right_elem = lax.dynamic_index_in_dim(
            spin_tiles, chain_order[op_index, 1], 0, keepdims=False
        )
        first = product_fold(peram_block, lax.all_gather(right_elem, "gx", axis=1, tiled=True))
        left_rows = lax.all_gather(left_elem, "gy", axis=2, tiled=True)
        chain_first = first.astype(jnp.bfloat16)
        second = product_fold(left_rows, lax.all_gather(chain_first, "gx", axis=1, tiled=True))
        second = (second * inverse).astype(jnp.bfloat16)
        second_block = lax.all_gather(second, "gy", axis=2, tiled=True)
        final = product_fold(second_block, lax.all_gather(backward_peram, "gx", axis=1, tiled=True))
        results.append(final.astype(jnp.bfloat16))
    return jnp.stack(results)


def solution(mesh):
    in_specs = (
        P("gx", "gy", "gz", None, None, None),
        P("gx", "gy", "gz", None, None, None, None),
        P(),
        P(),
        P(None, "gx", "gy"),
        P(None, "gx", "gy"),
        P("gz", None),
    )
    out_specs = P("gz", None, "gx", "gy")
    return jax.shard_map(
        on_device, mesh=mesh, in_specs=in_specs, out_specs=out_specs, check_vma=False
    )
```

profile of v0, /device:TPU:0, one launch (start us, length us, event | category | flops | bytes accessed | tf_op | source)
XLA Modules:
  0.0 922.4 jit_solution(9469376085601153117)
XLA Ops:
  8.3 5.1 collective-permute-start
  45.6 120.6 %all-reduce.2.cloned.1.call-done = f32[3,2,256,256]{3,2,1,0:T(8,128)} async-done(((f32[3,2,256,256]{3,2,1,0:T(8,128)}), f32[3,2,256,256]{3,2,1,0:T(8,128)}) %all-reduce.2.cloned.1.call-update) | async-done | bytes 1572880 | tf_op jit(solution)/shard_map/psum | solution.py:93
  167.7 21.5 %fusion = bf16[4,2,64,4,128,4]{5,4,3,2,1,0:T(8,128)(2,1)} fusion(f32[4,4,4]{2,1,0:T(4,128)S(1)} %copy-done.1, f32[4,2,64,128]{3,2,1,0:T(8,128)S(1)} %copy.57), kind=kLoop, calls=%fused_computation.1 | loop fusion | flops 2097152 | bytes 2359552 | tf_op jit(solution)/shard_map/convert_element_type | solution.py:63
  189.2 126.6 %convert_element_type.102 = bf16[4,2,256,512]{3,2,1,0:T(8,128)(2,1)S(1)} reshape(bf16[4,2,64,4,128,4]{5,4,3,2,1,0:T(8,128)(2,1)} %fusion) | data formatting | bytes 4194304 | tf_op jit(solution)/shard_map/convert_element_type | solution.py:63
  315.9 2.1 constant_dynamic-slice_fusion.6
  320.9 41.7 %all-gather.49.cloned.1.call-done = bf16[1,2,1024,512]{3,2,1,0:T(8,128)(2,1)} async-done(((bf16[1,2,256,512]{3,2,1,0:T(8,128)(2,1)}), bf16[1,2,1024,512]{3,2,1,0:T(8,128)(2,1)}) %all-gather.49.cloned.1.call-update) | async-done | bytes 2097168 | tf_op jit(solution)/shard_map/all_gather | solution.py:114
  362.5 2.4 convolution_bitcast_fusion.6
  367.6 40.8 %all-gather.53.cloned.1.call-done = bf16[1,2,1024,512]{3,2,1,0:T(8,128)(2,1)} async-done(((bf16[1,2,256,512]{3,2,1,0:T(8,128)(2,1)}), bf16[1,2,1024,512]{3,2,1,0:T(8,128)(2,1)}) %all-gather.53.cloned.1.call-update) | async-done | bytes 2097168 | tf_op jit(solution)/shard_map/all_gather | solution.py:114
  408.4 2.1 convolution_bitcast_fusion.4
  413.1 41.2 %all-gather.57.cloned.1.call-done = bf16[1,2,1024,512]{3,2,1,0:T(8,128)(2,1)} async-done(((bf16[1,2,256,512]{3,2,1,0:T(8,128)(2,1)}), bf16[1,2,1024,512]{3,2,1,0:T(8,128)(2,1)}) %all-gather.57.cloned.1.call-update) | async-done | bytes 2097168 | tf_op jit(solution)/shard_map/all_gather | solution.py:114
  454.3 2.1 convolution_bitcast_fusion.2
  459.1 41.3 %all-gather.61.cloned.1.call-done = bf16[1,2,1024,512]{3,2,1,0:T(8,128)(2,1)} async-done(((bf16[1,2,256,512]{3,2,1,0:T(8,128)(2,1)}), bf16[1,2,1024,512]{3,2,1,0:T(8,128)(2,1)}) %all-gather.61.cloned.1.call-update) | async-done | bytes 2097168 | tf_op jit(solution)/shard_map/all_gather | solution.py:114
  500.3 2.1 convolution_bitcast_fusion
  505.1 16.8 %all-gather.47.cloned.1.call-done = bf16[1,2,256,1024]{3,2,1,0:T(8,128)(2,1)} async-done(((bf16[1,2,256,512]{3,2,1,0:T(8,128)(2,1)}), bf16[1,2,256,1024]{3,2,1,0:T(8,128)(2,1)}) %all-gather.47.cloned.1.call-update) | async-done | bytes 1048592 | tf_op jit(solution)/shard_map/all_gather | solution.py:115
  521.9 47.5 %all-gather.29.cloned.1.call-done = bf16[2,1024,512]{1,2,0:T(8,128)(2,1)} async-done(((bf16[2,256,512]{1,2,0:T(8,128)(2,1)}), bf16[2,1024,512]{1,2,0:T(8,128)(2,1)}) %all-gather.29.cloned.1.call-update) | async-done | bytes 2097168 | tf_op jit(solution)/shard_map/all_gather | solution.py:117
  569.4 2.4 fusion.14
  573.8 16.4 %all-gather.51.cloned.1.call-done = bf16[1,2,256,1024]{3,2,1,0:T(8,128)(2,1)} async-done(((bf16[1,2,256,512]{3,2,1,0:T(8,128)(2,1)}), bf16[1,2,256,1024]{3,2,1,0:T(8,128)(2,1)}) %all-gather.51.cloned.1.call-update) | async-done | bytes 1048592 | tf_op jit(solution)/shard_map/all_gather | solution.py:115
  590.2 47.5 %all-gather.35.cloned.1.call-done = bf16[2,1024,512]{1,2,0:T(8,128)(2,1)} async-done(((bf16[2,256,512]{1,2,0:T(8,128)(2,1)}), bf16[2,1024,512]{1,2,0:T(8,128)(2,1)}) %all-gather.35.cloned.1.call-update) | async-done | bytes 2097168 | tf_op jit(solution)/shard_map/all_gather | solution.py:117
  637.8 2.4 fusion.12
  642.2 16.6 %all-gather.55.cloned.1.call-done = bf16[1,2,256,1024]{3,2,1,0:T(8,128)(2,1)} async-done(((bf16[1,2,256,512]{3,2,1,0:T(8,128)(2,1)}), bf16[1,2,256,1024]{3,2,1,0:T(8,128)(2,1)}) %all-gather.55.cloned.1.call-update) | async-done | bytes 1048592 | tf_op jit(solution)/shard_map/all_gather | solution.py:115
  658.8 47.5 %all-gather.39.cloned.1.call-done = bf16[2,1024,512]{1,2,0:T(8,128)(2,1)} async-done(((bf16[2,256,512]{1,2,0:T(8,128)(2,1)}), bf16[2,1024,512]{1,2,0:T(8,128)(2,1)}) %all-gather.39.cloned.1.call-update) | async-done | bytes 2097168 | tf_op jit(solution)/shard_map/all_gather | solution.py:117
  706.3 2.4 fusion.10
  710.9 16.3 %all-gather.59.cloned.1.call-done = bf16[1,2,256,1024]{3,2,1,0:T(8,128)(2,1)} async-done(((bf16[1,2,256,512]{3,2,1,0:T(8,128)(2,1)}), bf16[1,2,256,1024]{3,2,1,0:T(8,128)(2,1)}) %all-gather.59.cloned.1.call-update) | async-done | bytes 1048592 | tf_op jit(solution)/shard_map/all_gather | solution.py:115
  727.3 47.5 %all-gather.43.cloned.1.call-done = bf16[2,1024,512]{1,2,0:T(8,128)(2,1)} async-done(((bf16[2,256,512]{1,2,0:T(8,128)(2,1)}), bf16[2,1024,512]{1,2,0:T(8,128)(2,1)}) %all-gather.43.cloned.1.call-update) | async-done | bytes 2097168 | tf_op jit(solution)/shard_map/all_gather | solution.py:117
  774.8 2.4 fusion.8
  779.2 41.0 %all-gather.33.cloned.1.call-done = bf16[2,1024,512]{2,1,0:T(8,128)(2,1)} async-done(((bf16[2,256,512]{2,1,0:T(8,128)(2,1)}), bf16[2,1024,512]{2,1,0:T(8,128)(2,1)}) %all-gather.33.cloned.1.call-update) | async-done | bytes 2097168 | tf_op jit(solution)/shard_map/all_gather | solution.py:120
  820.2 21.5 %all-gather.31.cloned.1.call-done = bf16[2,256,1024]{2,1,0:T(8,128)(2,1)} async-done(((bf16[2,256,512]{2,1,0:T(8,128)(2,1)}), bf16[2,256,1024]{2,1,0:T(8,128)(2,1)}) %all-gather.31.cloned.1.call-update) | async-done | bytes 1048592 | tf_op jit(solution)/shard_map/all_gather | solution.py:119
  841.8 2.3 fusion.22
  845.1 19.4 %all-gather.37.cloned.1.call-done = bf16[2,256,1024]{2,1,0:T(8,128)(2,1)} async-done(((bf16[2,256,512]{2,1,0:T(8,128)(2,1)}), bf16[2,256,1024]{2,1,0:T(8,128)(2,1)}) %all-gather.37.cloned.1.call-update) | async-done | bytes 1048592 | tf_op jit(solution)/shard_map/all_gather | solution.py:119
  867.5 19.7 %all-gather.41.cloned.1.call-done = bf16[2,256,1024]{2,1,0:T(8,128)(2,1)} async-done(((bf16[2,256,512]{2,1,0:T(8,128)(2,1)}), bf16[2,256,1024]{2,1,0:T(8,128)(2,1)}) %all-gather.41.cloned.1.call-update) | async-done | bytes 1048592 | tf_op jit(solution)/shard_map/all_gather | solution.py:119
  890.3 19.7 %all-gather.45.cloned.1.call-done = bf16[2,256,1024]{2,1,0:T(8,128)(2,1)} async-done(((bf16[2,256,512]{2,1,0:T(8,128)(2,1)}), bf16[2,256,1024]{2,1,0:T(8,128)(2,1)}) %all-gather.45.cloned.1.call-update) | async-done | bytes 1048592 | tf_op jit(solution)/shard_map/all_gather | solution.py:119
  910.0 2.4 fusion.19
  (183 shorter events, 49.8 us)
Async XLA Ops:
  7.4 158.9 %all-reduce.2.cloned.1.call-start = ((), (), s32[]{:S(2)}) async-start(), calls=%async_computation | async-start | bytes 3145728 | tf_op jit(solution)/shard_map/psum | solution.py:93
  8.3 17.9 %collective-permute-start = (bf16[1,4,4,2,3,256]{5,4,2,1,0,3:T(4,128)(2,1)S(1)}, bf16[1,4,4,2,3,256]{5,4,2,1,0,3:T(4,128)(2,1)S(1)}, u32[]{:S(2)}, u32[]{:S(2)}) collective-permute-start(bf16[1,4,4,2,3,256]{5,4,2,1,0,3:T(4,128)(2,1)S(1)} %copy.63), channel_id=1, source_target_pairs={{0,24},{8,0},{16,8},{24,16},{1,25},{9,1},{17,9},{25,17},{2,26},{10... | collective-permute-start | bytes 147464 | tf_op jit(solution)/shard_map/ppermute | solution.py:12
  14.2 8.4 collective-permute-start.1
  16.5 6.6 collective-permute-start.2
  28.2 139.0 %copy-start.2 = (s32[4]{0:T(128)S(1)}, s32[4]{0:T(128)}, u32[]{:S(2)}) copy-start(s32[4]{0:T(128)} %param.9) | copy-start | bytes 52
  29.4 138.3 %copy-start.1 = (f32[4,4,4]{2,1,0:T(4,128)S(1)}, f32[4,4,4]{2,1,0:T(4,128)}, u32[]{:S(2)}) copy-start(f32[4,4,4]{2,1,0:T(4,128)} %param.10) | copy-start | bytes 772
  29.5 291.4 %all-gather.27.cloned.1.call-start = ((), (), s32[]{:S(2)}) async-start(), calls=%async_computation.1 | async-start | bytes 1572864 | tf_op jit(solution)/shard_map/all_gather | solution.py:103
  30.0 332.5 %all-gather.49.cloned.1.call-start = ((), (), s32[]{:S(2)}) async-start(), calls=%async_computation.12 | async-start | bytes 2621440 | tf_op jit(solution)/shard_map/all_gather | solution.py:114
  318.0 90.4 %all-gather.53.cloned.1.call-start = ((), (), s32[]{:S(2)}) async-start(), calls=%async_computation.14 | async-start | bytes 2621440 | tf_op jit(solution)/shard_map/all_gather | solution.py:114
  318.5 135.8 %all-gather.57.cloned.1.call-start = ((), (), s32[]{:S(2)}) async-start(), calls=%async_computation.16 | async-start | bytes 2621440 | tf_op jit(solution)/shard_map/all_gather | solution.py:114
  319.3 181.0 %all-gather.61.cloned.1.call-start = ((), (), s32[]{:S(2)}) async-start(), calls=%async_computation.18 | async-start | bytes 2621440 | tf_op jit(solution)/shard_map/all_gather | solution.py:114
  320.0 201.8 %all-gather.47.cloned.1.call-start = ((), (), s32[]{:S(2)}) async-start(), calls=%async_computation.11 | async-start | bytes 1572864 | tf_op jit(solution)/shard_map/all_gather | solution.py:115
  320.8 248.6 %all-gather.29.cloned.1.call-start = ((), (), s32[]{:S(2)}) async-start(), calls=%async_computation.2 | async-start | bytes 2621440 | tf_op jit(solution)/shard_map/all_gather | solution.py:117
  320.8 44.1 %copy-start.13 = (bf16[2,256,1024]{2,1,0:T(8,128)(2,1)S(1)}, bf16[2,256,1024]{2,1,0:T(8,128)(2,1)}, u32[]{:S(2)}) copy-start(bf16[2,256,1024]{2,1,0:T(8,128)(2,1)} %all-gather.27.cloned.1.call-done) | copy-start | bytes 3145732
  362.5 2.5 copy-start.12
  366.8 223.5 %all-gather.51.cloned.1.call-start = ((), (), s32[]{:S(2)}) async-start(), calls=%async_computation.13 | async-start | bytes 1572864 | tf_op jit(solution)/shard_map/all_gather | solution.py:115
  367.4 270.4 %all-gather.35.cloned.1.call-start = ((), (), s32[]{:S(2)}) async-start(), calls=%async_computation.5 | async-start | bytes 2621440 | tf_op jit(solution)/shard_map/all_gather | solution.py:117
  412.3 246.5 %all-gather.55.cloned.1.call-start = ((), (), s32[]{:S(2)}) async-start(), calls=%async_computation.15 | async-start | bytes 1572864 | tf_op jit(solution)/shard_map/all_gather | solution.py:115
  413.0 293.2 %all-gather.39.cloned.1.call-start = ((), (), s32[]{:S(2)}) async-start(), calls=%async_computation.7 | async-start | bytes 2621440 | tf_op jit(solution)/shard_map/all_gather | solution.py:117
  458.3 269.0 %all-gather.59.cloned.1.call-start = ((), (), s32[]{:S(2)}) async-start(), calls=%async_computation.17 | async-start | bytes 1572864 | tf_op jit(solution)/shard_map/all_gather | solution.py:115
  459.0 315.8 %all-gather.43.cloned.1.call-start = ((), (), s32[]{:S(2)}) async-start(), calls=%async_computation.9 | async-start | bytes 2621440 | tf_op jit(solution)/shard_map/all_gather | solution.py:117
  504.3 316.0 %all-gather.33.cloned.1.call-start = ((), (), s32[]{:S(2)}) async-start(), calls=%async_computation.4 | async-start | bytes 2621440 | tf_op jit(solution)/shard_map/all_gather | solution.py:120
  505.0 336.8 %all-gather.31.cloned.1.call-start = ((), (), s32[]{:S(2)}) async-start(), calls=%async_computation.3 | async-start | bytes 1572864 | tf_op jit(solution)/shard_map/all_gather | solution.py:119
  521.9 50.0 %copy-start.14 = (bf16[1,2,256,1024]{3,2,1,0:T(8,128)(2,1)S(1)}, bf16[1,2,256,1024]{3,2,1,0:T(8,128)(2,1)}, u32[]{:S(2)}) copy-start(bf16[1,2,256,1024]{3,2,1,0:T(8,128)(2,1)} %all-gather.47.cloned.1.call-done) | copy-start | bytes 3145732
  573.8 290.7 %all-gather.37.cloned.1.call-start = ((), (), s32[]{:S(2)}) async-start(), calls=%async_computation.6 | async-start | bytes 1572864 | tf_op jit(solution)/shard_map/all_gather | solution.py:119
  590.2 50.0 %copy-start.15 = (bf16[1,2,256,1024]{3,2,1,0:T(8,128)(2,1)S(1)}, bf16[1,2,256,1024]{3,2,1,0:T(8,128)(2,1)}, u32[]{:S(2)}) copy-start(bf16[1,2,256,1024]{3,2,1,0:T(8,128)(2,1)} %all-gather.51.cloned.1.call-done) | copy-start | bytes 3145732
  642.1 245.1 %all-gather.41.cloned.1.call-start = ((), (), s32[]{:S(2)}) async-start(), calls=%async_computation.8 | async-start | bytes 1572864 | tf_op jit(solution)/shard_map/all_gather | solution.py:119
  658.8 50.0 %copy-start.16 = (bf16[1,2,256,1024]{3,2,1,0:T(8,128)(2,1)S(1)}, bf16[1,2,256,1024]{3,2,1,0:T(8,128)(2,1)}, u32[]{:S(2)}) copy-start(bf16[1,2,256,1024]{3,2,1,0:T(8,128)(2,1)} %all-gather.55.cloned.1.call-done) | copy-start | bytes 3145732
  710.6 199.4 %all-gather.45.cloned.1.call-start = ((), (), s32[]{:S(2)}) async-start(), calls=%async_computation.10 | async-start | bytes 1572864 | tf_op jit(solution)/shard_map/all_gather | solution.py:119
  727.3 50.0 %copy-start.17 = (bf16[1,2,256,1024]{3,2,1,0:T(8,128)(2,1)S(1)}, bf16[1,2,256,1024]{3,2,1,0:T(8,128)(2,1)}, u32[]{:S(2)}) copy-start(bf16[1,2,256,1024]{3,2,1,0:T(8,128)(2,1)} %all-gather.59.cloned.1.call-done) | copy-start | bytes 3145732
  820.2 23.9 %copy-start.3 = (bf16[2,1024,512]{2,1,0:T(8,128)(2,1)S(1)}, bf16[2,1024,512]{2,1,0:T(8,128)(2,1)}, u32[]{:S(2)}) copy-start(bf16[2,1024,512]{2,1,0:T(8,128)(2,1)} %all-gather.33.cloned.1.call-done) | copy-start | bytes 6291460
  910.0 2.5 copy-start.21
  (12 other events, 26.9 us)
Sparse Core Ops, SparseCore 0:
  29.6 136.6 all-reduce.1
Sparse Core Ops, SparseCore 1:
  31.5 18.7 all-gather.26
  318.0 44.4 all-gather.48
  364.0 44.3 all-gather.52
  409.9 44.3 all-gather.56
  455.9 44.3 all-gather.60
  501.9 19.9 all-gather.46
  523.3 46.1 all-gather.28
  570.8 19.3 all-gather.50
  591.7 46.1 all-gather.34
  639.3 19.3 all-gather.54
  660.2 46.1 all-gather.38
  707.9 19.3 all-gather.58
  728.7 46.1 all-gather.42
  776.4 43.8 all-gather.32
  821.8 19.9 all-gather.30
  843.3 21.1 all-gather.36
  866.1 21.1 all-gather.40
  888.8 21.1 all-gather.44
where the time goes:
time: 923 us; the launch traced here: 922 us
  waiting for transfers between devices  669 us (72%)
  local copies, waits for them, and re-layouts  139 us (15%)
  matrix products  40.4 us (4%)
  other arithmetic  35.3 us (4%)
  between operations  30.7 us (3%)
    all_gather x4, waiting for transfers between devices, on_device(): lax.all_gather(chain_first, 'gx', axis=1, tiled=True)  190 us
    all_gather x4, waiting for transfers between devices, on_device(): lax.all_gather(right_elem, 'gx', axis=1, tiled=True)  165 us
    convert_element_type x1, local copies, waits for them, and re-layouts, expand_spin(): expanded.reshape(4, 2, 4 * dir_block.shape[2], 4 * dir_block.shape[3])  127 us
    psum x1, waiting for transfers between devices, on_device(): summed = lax.psum(partial_dirs, ('gx', 'gy', 'gz'))  121 us
    all_gather x4, waiting for transfers between devices, on_device(): second_block = lax.all_gather(second, 'gy', axis=2, tiled=True)  80.4 us
    all_gather x4, waiting for transfers between devices, on_device(): left_rows = lax.all_gather(left_elem, 'gy', axis=2, tiled=True)  66.1 us
    all_gather x1, waiting for transfers between devices, on_device(): lax.all_gather(backward_peram, 'gx', axis=1, tiled=True)  41 us
    convert_element_type x1, other arithmetic, expand_spin(): expanded.reshape(4, 2, 4 * dir_block.shape[2], 4 * dir_block.shape[3])  21.5 us
  transfers between devices with their start and end apart: 22, of which 18 were waited for; matrix products, arithmetic and copies ran while one was open for 22% of the time, Pallas kernels for 0%

commit v1 on v0

v1 whole, which is shorter than its diff:
```python
import functools
import math

import jax
import jax.numpy as jnp
import numpy as np
from jax import lax
from jax.experimental import pallas as pl
from jax.experimental.pallas import tpu as pltpu
from jax.sharding import PartitionSpec as P

VMEM = pl.BlockSpec(memory_space=pltpu.VMEM)
SMEM = pl.BlockSpec(memory_space=pltpu.SMEM)
BF16 = jnp.bfloat16
F32 = jnp.float32


def passed_along(value, axis, steps):
    count = lax.axis_size(axis)
    pairs = [(source, (source + steps) % count) for source in range(count)]
    return lax.ppermute(value, axis, pairs)


def mm(left, right):
    return jnp.dot(left, right, preferred_element_type=F32)


def site_tables(extent):
    sites = [(a, b, c) for a in range(extent[0]) for b in range(extent[1]) for c in range(extent[2])]
    count = len(sites)
    where = {site: n for n, site in enumerate(sites)}
    rows = [(c, n, a) for c in range(2) for n in range(count) for a in range(3)]
    spread = np.zeros((len(rows), count), np.float32)
    for r, (c, n, a) in enumerate(rows):
        spread[r, n] = 1
    tables = []
    for e in range(3):
        face = [s for s in sites if s[e] == 0]
        inner = sites if e else [s for s in sites if s[0] > 0]
        columns = [(c, s, b) for c in range(2) for s in inner for b in range(3)]
        beyond = [tuple(v + extent[e] * (d == e) for d, v in enumerate(s)) for s in face]
        columns += [(c, s, b) for c in range(2) for s in beyond for b in range(3)]
        mask = np.zeros((len(rows), len(columns)), np.float32)
        keep = np.zeros((len(rows), 108), np.float32)
        place = np.zeros((108, len(columns)), np.float32)
        by_site = {}
        for q, (cc, s, b) in enumerate(columns):
            by_site.setdefault(s, []).append(q)
            place[cc * 9 + b, q] = -1 if cc else 1
            place[54 + (1 - cc) * 9 + b, q] = 1
        full = np.zeros((108, len(columns)), np.float32)
        for c in range(2):
            for cc in range(2):
                for a in range(3):
                    for b in range(3):
                        full[c * 54 + e * 18 + cc * 9 + a * 3 + b] = place[c * 54 + cc * 9 + b]
        for r, (c, n, a) in enumerate(rows):
            s = sites[n]
            mask[r, by_site[tuple(v + (d == e) for d, v in enumerate(s))]] = 1
            for cc in range(2):
                for b in range(3):
                    keep[r, c * 54 + e * 18 + cc * 9 + a * 3 + b] = 1
        tables.append((mask, keep, full))
    return spread, tables


def prepare_kernel(z_ref, link_ref, fwd_ref, bwd_ref, perm_ref, spread_ref, *refs):
    masks, keeps, places = refs[0:3], refs[3:6], refs[6:9]
    fwd_out, bwd_out = refs[9:11]
    link_outs = refs[11:14]
    z = z_ref[0]
    rows = fwd_ref.shape[1]
    piece = fwd_out.shape[1]
    per_spin = rows // 4
    flat = lax.broadcasted_iota(jnp.int32, (piece, rows), 0) + z * piece
    spin = jnp.zeros_like(flat)
    for t in range(1, 4):
        spin += jnp.where(flat >= t * per_spin, 1, 0)
    source = 4 * (flat - spin * per_spin) + spin
    select = jnp.where(lax.broadcasted_iota(jnp.int32, (piece, rows), 1) == source, 1.0, 0.0)
    select = select.astype(BF16)
    for c in range(2):
        picked = mm(select, fwd_ref[c]).astype(BF16)
        fwd_out[c] = mm(picked, perm_ref[...]).astype(BF16)
        bwd_out[c] = mm(select, bwd_ref[c]).astype(BF16)
    link = link_ref[...]
    high = link.astype(BF16)
    rest = link - high.astype(F32)
    mid = rest.astype(BF16)
    low = (rest - mid.astype(F32)).astype(BF16)
    spread = spread_ref[...]
    by_row = [mm(spread, part) for part in (high, mid, low)]
    for e in range(3):
        keep = keeps[e][...].astype(F32)
        picked = jnp.concatenate(
            [jnp.concatenate([part, part], axis=1) * keep for part in by_row], axis=0
        ).astype(BF16)
        placed = mm(picked, places[e][...])
        mask = masks[e][...].astype(F32)
        mask = jnp.concatenate([mask, mask, mask], axis=0)
        link_outs[e][...] = (placed * mask).astype(BF16)


def correlate_kernel(scale, vec_ref, face0, face1, face2, mat0, mat1, mat2, out_ref):
    vec = vec_ref[...]
    rows = vec.shape[0]
    half = rows // 2
    width = vec.shape[1]
    lower = half - face0.shape[0] // 2
    sources = [
        jnp.concatenate([vec[half - lower : half], vec[rows - lower :], face0[...]], axis=0),
        jnp.concatenate([vec, face1[...]], axis=0),
        jnp.concatenate([vec, face2[...]], axis=0),
    ]
    for e, mat in enumerate((mat0, mat1, mat2)):
        terms = mm(mat[...], sources[e])
        moved = terms[:rows] + terms[rows : 2 * rows] + terms[2 * rows :]
        moved = moved.astype(BF16)
        turned = jnp.concatenate([moved[half:], -moved[:half]], axis=0)
        right = jnp.concatenate([moved, turned], axis=1)
        product = lax.dot_general(
            vec, right, (((0,), (0,)), ((), ())), preferred_element_type=F32
        )
        product = (product * scale).astype(BF16)
        out_ref[2 * e] = product[:, :width]
        out_ref[2 * e + 1] = product[:, width:]


def chain_kernel(
    inverse, gx_ref, dirs_ref, spin_ref, chain_ref, elem_ref, fwd_ref, bwd_ref, out_ref, x_ref, p_ref, q_ref, b_ref
):
    num_vecs = elem_ref.shape[2]
    gx_n, gy_n, gz_n, _, _, width = fwd_ref.shape
    op_count = out_ref.shape[0]
    row_count = out_ref.shape[2]
    vec_rows = row_count // 4
    spin_pieces = gz_n // 4
    lane = width // 4
    first_row = pl.multiple_of(gx_ref[0] * vec_rows, vec_rows)

    def own(d, c):
        return elem_ref[d, c, pl.ds(first_row, vec_rows), :]

    real_rows = [jnp.concatenate([own(d, 0), -own(d, 1)], axis=1) for d in range(3)]
    imag_rows = [jnp.concatenate([own(d, 1), own(d, 0)], axis=1) for d in range(3)]
    left = jnp.concatenate([part for d in range(3) for part in (real_rows[d], imag_rows[d])], axis=0)
    for t in range(4):
        planes = slice(t * spin_pieces, (t + 1) * spin_pieces)
        for block in range(gy_n):
            right = jnp.concatenate(
                [fwd_ref[:, block, planes, c].reshape(num_vecs, width) for c in range(2)], axis=0
            )
            result = mm(left, right).astype(BF16)
            for d in range(3):
                for c in range(2):
                    at = (d * 2 + c) * vec_rows
                    x_ref[d, c, t, :, block * width : (block + 1) * width] = result[at : at + vec_rows]
        for c in range(2):
            at = (t * 2 + c) * num_vecs
            b_ref[at : at + num_vecs, :] = bwd_ref[:, planes, c].reshape(num_vecs, width)

    row = lax.broadcasted_iota(jnp.int32, (row_count, row_count), 0)
    column = lax.broadcasted_iota(jnp.int32, (row_count, row_count), 1)
    row_spin = lax.rem(row, 4)
    diagonal = lax.div(row, 4) == lax.rem(column, vec_rows)
    column_spin = lax.div(column, vec_rows)

    def one_operator(op, carry):
        a = chain_ref[op, 0]
        b = chain_ref[op, 1]
        dir_a = dirs_ref[a]
        dir_b = dirs_ref[b]
        mix = jnp.zeros((row_count, row_count), F32)
        for t in range(4):
            in_t = column_spin == t
            for s in range(4):
                mix = jnp.where(in_t & (row_spin == s), spin_ref[a, s, t], mix)
        mix = jnp.where(diagonal, mix, 0.0)
        high = mix.astype(BF16)
        low = (mix - high.astype(F32)).astype(BF16)
        mix = jnp.concatenate([high, low], axis=1)
        for c in range(2):
            source = x_ref[dir_a, c].reshape(row_count, 4 * num_vecs)
            result = mm(mix, jnp.concatenate([source, source], axis=0)).astype(BF16)
            for s in range(4):
                for block in range(gy_n):
                    at = block * width + s * lane
                    to = c * num_vecs + block * lane
                    p_ref[s, :, to : to + lane] = result[:, at : at + lane]
        real_b, imag_b = elem_ref[dir_b, 0], elem_ref[dir_b, 1]
        right = jnp.concatenate(
            [
                jnp.concatenate([real_b, imag_b], axis=1),
                jnp.concatenate([-imag_b, real_b], axis=1),
            ],
            axis=0,
        )
        parts = [mm(p_ref[s], right) for s in range(4)]
        for t in range(4):
            total = parts[0] * (spin_ref[b, 0, t] * inverse)
            for s in range(1, 4):
                total += parts[s] * (spin_ref[b, s, t] * inverse)
            total = total.astype(BF16)
            real, imag = total[:, :num_vecs], total[:, num_vecs:]
            at = 2 * t * num_vecs
            q_ref[:row_count, at : at + num_vecs] = real
            q_ref[:row_count, at + num_vecs : at + 2 * num_vecs] = -imag
            q_ref[row_count:, at : at + num_vecs] = imag
            q_ref[row_count:, at + num_vecs : at + 2 * num_vecs] = real
        final = mm(q_ref[...], b_ref[...]).astype(BF16)
        out_ref[op, 0] = final[:row_count]
        out_ref[op, 1] = final[row_count:]
        return carry

    lax.fori_loop(0, op_count, one_operator, 0)


def summed_over(value, axis):
    total = value.astype(F32)
    for step in range(1, lax.axis_size(axis)):
        total += passed_along(value, axis, step).astype(F32)
    return total


def scattered_over(value, axis):
    count = lax.axis_size(axis)
    me = lax.axis_index(axis)
    total = lax.dynamic_index_in_dim(value, me, 0, keepdims=False).astype(F32)
    for step in range(1, count):
        part = lax.dynamic_index_in_dim(value, lax.rem(me + step, count), 0, keepdims=False)
        total += passed_along(part, axis, step).astype(F32)
    return total


def gathered_over(value, axis):
    count = lax.axis_size(axis)
    me = lax.axis_index(axis)
    result = jnp.zeros((count,) + value.shape, value.dtype)
    for step in range(count):
        part = passed_along(value, axis, step) if step else value
        result = lax.dynamic_update_index_in_dim(result, part, lax.rem(me - step + count, count), 0)
    return result


def on_device(eigvecs, links, directions, spin_mats, forward_peram, backward_peram, chain_order):
    extent = eigvecs.shape[:3]
    num_vecs = eigvecs.shape[-1]
    gx_n, gy_n, gz_n = (lax.axis_size(name) for name in ("gx", "gy", "gz"))
    gx, gz = lax.axis_index("gx"), lax.axis_index("gz")

    ordered = eigvecs.transpose(3, 0, 1, 2, 4, 5)
    faces = []
    for e, axis in enumerate(("gx", "gy", "gz")):
        face = lax.slice_in_dim(ordered, 0, 1, axis=1 + e).reshape(-1, num_vecs)
        faces.append(passed_along(face, axis, -1))
    vec = ordered.reshape(-1, num_vecs)

    rows, cols = forward_peram.shape[1:]
    piece = rows // gz_n
    spread, tables = site_tables(extent)
    lane = cols // 4
    perm = np.zeros((cols, cols), np.float32)
    for s in range(4):
        perm[4 * np.arange(lane) + s, s * lane + np.arange(lane)] = 1
    constants = [perm, spread] + [tables[e][k] for k in range(3) for e in range(3)]
    constants = [jnp.asarray(c, BF16) for c in constants]
    piece_shape = jax.ShapeDtypeStruct((2, piece, cols), BF16)
    fwd_piece, bwd_piece, *link_mats = pl.pallas_call(
        prepare_kernel,
        out_shape=[piece_shape, piece_shape]
        + [jax.ShapeDtypeStruct((3 * t[0].shape[0], t[0].shape[1]), BF16) for t in tables],
        in_specs=[SMEM] + [VMEM] * (3 + len(constants)),
        out_specs=[VMEM] * 5,
        compiler_params=pltpu.CompilerParams(vmem_limit_bytes=24 * 2**20),
        name="prepare",
    )(gz.reshape(1), links.reshape(-1, 54), forward_peram, backward_peram, *constants)

    fwd_all = lax.all_gather(fwd_piece, ("gx", "gy", "gz"), axis=0, tiled=False)
    fwd_all = fwd_all.reshape(gx_n, gy_n, gz_n, 2, piece, cols)
    bwd_all = lax.all_gather(bwd_piece, ("gx", "gz"), axis=0, tiled=False)
    bwd_all = bwd_all.reshape(gx_n, gz_n, 2, piece, cols)

    volume = math.prod(extent) * gx_n * gy_n * gz_n
    partial = pl.pallas_call(
        functools.partial(correlate_kernel, 1.0 / math.sqrt(12.0 * volume)),
        out_shape=jax.ShapeDtypeStruct((6, num_vecs, num_vecs), BF16),
        in_specs=[VMEM] * 7,
        out_specs=VMEM,
        compiler_params=pltpu.CompilerParams(vmem_limit_bytes=24 * 2**20),
        name="correlate",
    )(vec, *faces, *link_mats)

    own_rows = num_vecs // (gz_n * gx_n)
    parts = partial.reshape(6, gz_n, gx_n, own_rows, num_vecs).transpose(1, 2, 0, 3, 4)
    summed = scattered_over(parts, "gz").astype(BF16)
    summed = summed_over(summed, "gy").astype(BF16)
    summed = scattered_over(summed, "gx").astype(BF16)
    elem = gathered_over(gathered_over(summed, "gx"), "gz")
    elem = elem.transpose(2, 0, 1, 3, 4).reshape(3, 2, num_vecs, num_vecs)

    op_count = chain_order.shape[0]
    row_count = rows
    return pl.pallas_call(
        functools.partial(chain_kernel, 1.0 / math.sqrt(4 * num_vecs)),
        out_shape=jax.ShapeDtypeStruct((op_count, 2, row_count, cols), BF16),
        in_specs=[SMEM] * 4 + [VMEM] * 3,
        out_specs=VMEM,
        scratch_shapes=[
            pltpu.VMEM((3, 2, 4, row_count // 4, 4 * num_vecs), BF16),
            pltpu.VMEM((4, row_count, 2 * num_vecs), BF16),
            pltpu.VMEM((2 * row_count, 8 * num_vecs), BF16),
            pltpu.VMEM((8 * num_vecs, cols), BF16),
        ],
        compiler_params=pltpu.CompilerParams(vmem_limit_bytes=48 * 2**20),
        name="chain",
    )(gx.reshape(1), directions, spin_mats, chain_order, elem, fwd_all, bwd_all)


def solution(mesh):
    in_specs = (
        P("gx", "gy", "gz", None, None, None),
        P("gx", "gy", "gz", None, None, None, None),
        P(),
        P(),
        P(None, "gx", "gy"),
        P(None, "gx", "gy"),
        P("gz", None),
    )
    out_specs = P("gz", None, "gx", "gy")
    return jax.shard_map(
        on_device, mesh=mesh, in_specs=in_specs, out_specs=out_specs, check_vma=False
    )
```

time: 923 us -> 158 us (0.17)
  waiting for transfers between devices: 669 us -> 88.6 us
  local copies, waits for them, and re-layouts: 139 us -> 15.1 us
  matrix products: 40.4 us -> 0 us
  other arithmetic: 35.3 us -> 0.2 us
  Pallas kernels: 0 us -> 19.3 us
  between operations: 30.7 us -> 13.7 us
  starting transfers between devices: 8.27 us -> 19.9 us
    all_gather x18 -> x2, waiting for transfers between devices: 543 us -> 48.7 us  [the longest x1 48.7 us: on_device(): fwd_all = lax.all_gather(fwd_piece, ('gx', 'gy', 'gz'), axis=0, tiled=False)]
    convert_element_type x7 -> x0, local copies, waits for them, and re-layouts: 127 us -> none  [the longest x1 127 us: expand_spin(): expanded.reshape(4, 2, 4 * dir_block.shape[2], 4 * dir_block.shape[3])]
    psum x1 -> x0, waiting for transfers between devices: 121 us -> none  [on_device(): summed = lax.psum(partial_dirs, ('gx', 'gy', 'gz'))]
    dot_general x40 -> x0, matrix products: 40.4 us -> none  [the longest x12 21.5 us: complex_product(): jnp.dot(stacked, right_mat[0], preferred_element_type=jnp.float32)]
    ppermute x3 -> x16, waiting for transfers between devices: 0.01 us -> 39.2 us  [passed_along(): return lax.ppermute(value, axis, pairs)]
    convert_element_type x5 -> x2, other arithmetic: 25.2 us -> 0.16 us  [the longest x1 0.11 us: on_device(): summed = scattered_over(parts, 'gz').astype(BF16)]
    pallas_call x0 -> x3, Pallas kernels: none -> 19.3 us  [the longest x1 16.5 us: on_device(): pl.pallas_call(functools.partial(chain_kernel, 1.0 / math.sqrt(4 * num_ve...]
    ppermute x3 -> x16, starting transfers between devices: 7.11 us -> 19.8 us  [passed_along(): return lax.ppermute(value, axis, pairs)]
  transfers between devices with their start and end apart: 22 -> 18, of which waited for: 18 -> 11; matrix products, arithmetic and copies ran while one was open for 22% -> 1% of each run, Pallas kernels for 0% -> 1%
where the time goes in v1:
time: 158 us; the launch traced here: 157 us
  waiting for transfers between devices  88.6 us (56%)
  starting transfers between devices  19.9 us (13%)
  Pallas kernels  19.3 us (12%)
  local copies, waits for them, and re-layouts  15.1 us (10%)
  between operations  13.7 us (9%)
    all_gather x1, waiting for transfers between devices, on_device(): fwd_all = lax.all_gather(fwd_piece, ('gx', 'gy', 'gz'), axis=0, tiled=False)  48.7 us
    ppermute x16, waiting for transfers between devices, passed_along(): return lax.ppermute(value, axis, pairs)  39.2 us
    ppermute x16, starting transfers between devices, passed_along(): return lax.ppermute(value, axis, pairs)  19.8 us
    pallas_call x1, Pallas kernels, on_device(): pl.pallas_call(functools.partial(chain_kernel, 1.0 / math.sqrt(4 * num_ve...  16.5 us
    unnamed x41, local copies, waits for them, and re-layouts  14.2 us
  transfers between devices with their start and end apart: 18, of which 11 were waited for; matrix products, arithmetic and copies ran while one was open for 1% of the time, Pallas kernels for 1%

profile of v1, /device:TPU:0, one launch (start us, length us, event | category | flops | bytes accessed | tf_op | source)
XLA Modules:
  0.0 156.8 jit_solution(9062766015949442825)
XLA Ops:
  6.5 1.0 copy.56
  7.8 1.0 copy-done.1
  8.9 1.0 copy-done.2
  9.9 1.0 copy-done.3
  10.9 0.9 copy-done.4
  11.8 0.9 copy-done.5
  12.7 0.9 copy-done.6
  13.6 0.8 copy-done.7
  15.3 0.8 copy-done.9
  19.3 1.4 prepare.1
  21.6 5.1 %collective-permute-start = (bf16[96,256]{1,0:T(8,128)(2,1)S(1)}, bf16[96,256]{1,0:T(8,128)(2,1)S(1)}, u32[]{:S(2)}, u32[]{:S(2)}) collective-permute-start(bf16[96,256]{1,0:T(8,128)(2,1)S(1)} %reshape.39), channel_id=1, source_target_pairs={{0,24},{8,0},{16,8},{24,16},{1,25},{9,1},{17,9},{25,17},{2,26},{10... | collective-permute-start | bytes 147464 | tf_op jit(solution)/shard_map/ppermute | solution.py:21
  26.8 1.6 collective-permute-start.1
  29.0 1.6 %collective-permute-done.1.face1 = bf16[48,256]{1,0:T(8,128)(2,1)S(1)} collective-permute-done((bf16[48,256]{1,0:T(8,128)(2,1)S(1)}, bf16[48,256]{1,0:T(8,128)(2,1)S(1)}, u32[]{:S(2)}, u32[]{:S(2)}) %collective-permute-start.1) | collective-permute-done | bytes 24608 | tf_op jit(solution)/shard_map/ppermute | solution.py:21
  30.7 1.4 correlate.1
  32.2 1.5 collective-permute-start.5
  33.7 1.2 collective-permute-start.4
  34.9 3.6 %collective-permute-done.5 = bf16[4,6,16,256]{3,2,1,0:T(8,128)(2,1)S(1)} collective-permute-done((bf16[4,6,16,256]{3,2,1,0:T(8,128)(2,1)S(1)}, bf16[4,6,16,256]{3,2,1,0:T(8,128)(2,1)S(1)}, u32[]{:S(2)}, u32[]{:S(2)}) %collective-permute-start.5) | collective-permute-done | bytes 196640 | tf_op jit(solution)/shard_map/ppermute | solution.py:21
  38.5 2.4 %collective-permute-done.3 = bf16[4,6,16,256]{3,2,1,0:T(8,128)(2,1)S(1)} collective-permute-done((bf16[4,6,16,256]{3,2,1,0:T(8,128)(2,1)S(1)}, bf16[4,6,16,256]{3,2,1,0:T(8,128)(2,1)S(1)}, u32[]{:S(2)}, u32[]{:S(2)}) %collective-permute-start.3) | collective-permute-done | bytes 196640 | tf_op jit(solution)/shard_map/ppermute | solution.py:21
  40.9 3.6 %collective-permute-done.4 = bf16[4,6,16,256]{3,2,1,0:T(8,128)(2,1)S(1)} collective-permute-done((bf16[4,6,16,256]{3,2,1,0:T(8,128)(2,1)S(1)}, bf16[4,6,16,256]{3,2,1,0:T(8,128)(2,1)S(1)}, u32[]{:S(2)}, u32[]{:S(2)}) %collective-permute-start.4) | collective-permute-done | bytes 196640 | tf_op jit(solution)/shard_map/ppermute | solution.py:21
  44.6 0.9 collective-permute-start.6
  45.4 6.6 %collective-permute-done.6 = bf16[4,6,16,256]{3,2,1,0:T(8,128)(2,1)S(1)} collective-permute-done((bf16[4,6,16,256]{3,2,1,0:T(8,128)(2,1)S(1)}, bf16[4,6,16,256]{3,2,1,0:T(8,128)(2,1)S(1)}, u32[]{:S(2)}, u32[]{:S(2)}) %collective-permute-start.6) | collective-permute-done | bytes 196640 | tf_op jit(solution)/shard_map/ppermute | solution.py:21
  52.2 3.8 %collective-permute-start.9 = (bf16[6,16,256]{2,1,0:T(8,128)(2,1)S(1)}, bf16[6,16,256]{2,1,0:T(8,128)(2,1)S(1)}, u32[]{:S(2)}, u32[]{:S(2)}) collective-permute-start(bf16[6,16,256]{2,1,0:T(8,128)(2,1)S(1)} %get-tuple-element.22), channel_id=1, source_target_pairs={{0,24},{8,0},{16,8},{24,16},{1,25},{9,1},{17,9},{25,17},{2,26},{10... | collective-permute-start | bytes 147464 | tf_op jit(solution)/shard_map/ppermute | solution.py:21
  56.0 3.5 %collective-permute-done.7 = bf16[6,16,256]{2,1,0:T(8,128)(2,1)S(1)} collective-permute-done((bf16[6,16,256]{2,1,0:T(8,128)(2,1)S(1)}, bf16[6,16,256]{2,1,0:T(8,128)(2,1)S(1)}, u32[]{:S(2)}, u32[]{:S(2)}) %collective-permute-start.7) | collective-permute-done | bytes 49184 | tf_op jit(solution)/shard_map/ppermute | solution.py:21
  59.5 4.7 %collective-permute-done.8 = bf16[6,16,256]{2,1,0:T(8,128)(2,1)S(1)} collective-permute-done((bf16[6,16,256]{2,1,0:T(8,128)(2,1)S(1)}, bf16[6,16,256]{2,1,0:T(8,128)(2,1)S(1)}, u32[]{:S(2)}, u32[]{:S(2)}) %collective-permute-start.8) | collective-permute-done | bytes 49184 | tf_op jit(solution)/shard_map/ppermute | solution.py:21
  64.5 1.8 %collective-permute-start.11 = (bf16[6,16,256]{2,1,0:T(8,128)(2,1)S(1)}, bf16[6,16,256]{2,1,0:T(8,128)(2,1)S(1)}, u32[]{:S(2)}, u32[]{:S(2)}) collective-permute-start(bf16[6,16,256]{2,1,0:T(8,128)(2,1)S(1)} %get-tuple-element.16), channel_id=1, source_target_pairs={{0,16},{8,24},{16,0},{24,8},{1,17},{9,25},{17,1},{25,9},{2,18},{10... | collective-permute-start | bytes 147464 | tf_op jit(solution)/shard_map/ppermute | solution.py:21
  66.3 2.0 %collective-permute-start.12 = (bf16[6,16,256]{2,1,0:T(8,128)(2,1)S(1)}, bf16[6,16,256]{2,1,0:T(8,128)(2,1)S(1)}, u32[]{:S(2)}, u32[]{:S(2)}) collective-permute-start(bf16[6,16,256]{2,1,0:T(8,128)(2,1)S(1)} %get-tuple-element.16), channel_id=1, source_target_pairs={{0,24},{8,0},{16,8},{24,16},{1,25},{9,1},{17,9},{25,17},{2,26},{10... | collective-permute-start | bytes 147464 | tf_op jit(solution)/shard_map/ppermute | solution.py:21
  68.3 2.1 %collective-permute-done.10 = bf16[6,16,256]{2,1,0:T(8,128)(2,1)S(1)} collective-permute-done((bf16[6,16,256]{2,1,0:T(8,128)(2,1)S(1)}, bf16[6,16,256]{2,1,0:T(8,128)(2,1)S(1)}, u32[]{:S(2)}, u32[]{:S(2)}) %collective-permute-start.10) | collective-permute-done | bytes 49184 | tf_op jit(solution)/shard_map/ppermute | solution.py:21
  70.9 1.3 collective-permute-start.14
  72.5 10.6 %collective-permute-done.13 = bf16[4,6,16,256]{3,2,0,1:T(8,128)(2,1)S(1)} collective-permute-done((bf16[4,6,16,256]{3,2,0,1:T(8,128)(2,1)S(1)}, bf16[4,6,16,256]{3,2,0,1:T(8,128)(2,1)S(1)}, u32[]{:S(2)}, u32[]{:S(2)}) %collective-permute-start.13) | collective-permute-done | bytes 196640 | tf_op jit(solution)/shard_map/ppermute | solution.py:21
  83.2 48.7 %all-gather.5.cloned.1.call-done = bf16[64,64,512]{2,1,0:T(8,128)(2,1)} async-done(((bf16[2,64,512]{2,1,0:T(8,128)(2,1)}), bf16[64,64,512]{2,1,0:T(8,128)(2,1)}) %all-gather.5.cloned.1.call-update) | async-done | bytes 4194320 | tf_op jit(solution)/shard_map/all_gather | solution.py:278
  131.9 1.6 %copy-done = bf16[32,64,512]{2,1,0:T(8,128)(2,1)S(1)} copy-done((bf16[32,64,512]{2,1,0:T(8,128)(2,1)S(1)}, bf16[32,64,512]{2,1,0:T(8,128)(2,1)}, u32[]{:S(2)}) %copy-start) | copy-done | bytes 2097176
  133.5 16.5 %chain.1 = bf16[4,2,256,512]{3,2,1,0:T(8,128)(2,1)} custom-call(s32[1]{0:T(128)} %bitcast.gx_ref, s32[4]{0:T(128)S(1)} %copy-done.15, f32[4,4,4]{2,1,0:T(4,128)S(1)} %copy-done.14, s32[4,2]{1,0:T(4,128)S(1)} %copy.68.chain_ref, bf16[3,2,256,256]{3,2,1,0:T(8,128)(2,1)S(1)} %bitcast.81, bf16[4,2,4,2,64,512]{5,4,3,2,1,0:T(8,128)(2,1)} %bitcast.83, ...), custom_call_target="tpu_custom_call" | custom-call | tf_op jit(solution)/shard_map/chain/pallas_call | solution.py:303
  (77 shorter events, 7.3 us)
Async XLA Ops:
  6.5 14.9 %copy-start.16 = (bf16[2,4,4,2,3,256]{5,3,4,2,1,0:T(2,128)(2,1)S(1)}, bf16[2,4,4,2,3,256]{5,3,4,2,1,0:T(2,128)(2,1)}, u32[]{:S(2)}) copy-start(bf16[2,4,4,2,3,256]{5,3,4,2,1,0:T(2,128)(2,1)} %param.18) | copy-start | bytes 294916
  6.5 76.6 %all-gather.7.cloned.1.call-start = ((), (), s32[]{:S(2)}) async-start(), calls=%async_computation.1 | async-start | bytes 2228224 | tf_op jit(solution)/shard_map/all_gather | solution.py:280
  7.8 1.0 copy-start.1
  8.9 1.0 copy-start.2
  9.9 1.0 copy-start.3
  10.9 0.9 copy-start.4
  11.8 0.9 copy-start.5
  12.7 0.9 copy-start.6
  13.6 0.8 copy-start.7
  14.4 0.8 copy-start.8
  15.3 0.8 copy-start.9
  20.7 111.1 %all-gather.5.cloned.1.call-start = ((), (), s32[]{:S(2)}) async-start(), calls=%async_computation | async-start | bytes 4325376 | tf_op jit(solution)/shard_map/all_gather | solution.py:278
  21.6 9.1 %collective-permute-start = (bf16[96,256]{1,0:T(8,128)(2,1)S(1)}, bf16[96,256]{1,0:T(8,128)(2,1)S(1)}, u32[]{:S(2)}, u32[]{:S(2)}) collective-permute-start(bf16[96,256]{1,0:T(8,128)(2,1)S(1)} %reshape.39), channel_id=1, source_target_pairs={{0,24},{8,0},{16,8},{24,16},{1,25},{9,1},{17,9},{25,17},{2,26},{10... | collective-permute-start | bytes 147464 | tf_op jit(solution)/shard_map/ppermute | solution.py:21
  26.8 3.9 %collective-permute-start.1 = (bf16[48,256]{1,0:T(8,128)(2,1)S(1)}, bf16[48,256]{1,0:T(8,128)(2,1)S(1)}, u32[]{:S(2)}, u32[]{:S(2)}) collective-permute-start(bf16[48,256]{1,0:T(8,128)(2,1)S(1)} %reshape.40), channel_id=1, source_target_pairs={{0,4},{4,0},{1,5},{5,1},{2,6},{6,2},{3,7},{7,3},{8,12},{12,8},{9,1... | collective-permute-start | bytes 73736 | tf_op jit(solution)/shard_map/ppermute | solution.py:21
  28.4 2.3 %collective-permute-start.2 = (bf16[48,256]{1,0:T(8,128)(2,1)S(1)}, bf16[48,256]{1,0:T(8,128)(2,1)S(1)}, u32[]{:S(2)}, u32[]{:S(2)}) collective-permute-start(bf16[48,256]{1,0:T(8,128)(2,1)S(1)} %reshape.41), channel_id=1, source_target_pairs={{0,3},{1,0},{2,1},{3,2},{4,7},{5,4},{6,5},{7,6},{8,11},{9,8},{10,9... | collective-permute-start | bytes 73736 | tf_op jit(solution)/shard_map/ppermute | solution.py:21
  32.1 32.3 %copy-start.17 = (s32[4,2]{0,1:T(2,128)S(1)}, s32[4,2]{0,1:T(2,128)}, u32[]{:S(2)}) copy-start(s32[4,2]{0,1:T(2,128)} %param.24) | copy-start | bytes 100
  32.2 6.3 %collective-permute-start.5 = (bf16[4,6,16,256]{3,2,1,0:T(8,128)(2,1)S(1)}, bf16[4,6,16,256]{3,2,1,0:T(8,128)(2,1)S(1)}, u32[]{:S(2)}, u32[]{:S(2)}) collective-permute-start(bf16[4,6,16,256]{3,2,1,0:T(8,128)(2,1)S(1)} %bitcast.90), channel_id=1, source_target_pairs={{0,3},{1,0},{2,1},{3,2},{4,7},{5,4},{6,5},{7,6},{8,11},{9,8},{10,9... | collective-permute-start | bytes 589832 | tf_op jit(solution)/shard_map/ppermute | solution.py:21
  33.7 7.2 %collective-permute-start.3 = (bf16[4,6,16,256]{3,2,1,0:T(8,128)(2,1)S(1)}, bf16[4,6,16,256]{3,2,1,0:T(8,128)(2,1)S(1)}, u32[]{:S(2)}, u32[]{:S(2)}) collective-permute-start(bf16[4,6,16,256]{3,2,1,0:T(8,128)(2,1)S(1)} %bitcast.89), channel_id=1, source_target_pairs={{0,1},{1,2},{2,3},{3,0},{4,5},{5,6},{6,7},{7,4},{8,9},{9,10},{10,1... | collective-permute-start | bytes 589832 | tf_op jit(solution)/shard_map/ppermute | solution.py:21
  33.7 10.8 %collective-permute-start.4 = (bf16[4,6,16,256]{3,2,1,0:T(8,128)(2,1)S(1)}, bf16[4,6,16,256]{3,2,1,0:T(8,128)(2,1)S(1)}, u32[]{:S(2)}, u32[]{:S(2)}) collective-permute-start(bf16[4,6,16,256]{3,2,1,0:T(8,128)(2,1)S(1)} %bitcast.88), channel_id=1, source_target_pairs={{0,2},{1,3},{2,0},{3,1},{4,6},{5,7},{6,4},{7,5},{8,10},{9,11},{10,... | collective-permute-start | bytes 589832 | tf_op jit(solution)/shard_map/ppermute | solution.py:21
  44.6 87.3 %copy-start.14 = (f32[4,4,4]{2,1,0:T(4,128)S(1)}, f32[4,4,4]{2,1,0:T(4,128)}, u32[]{:S(2)}) copy-start(f32[4,4,4]{2,1,0:T(4,128)} %spin_ref.1) | copy-start | bytes 772
  44.6 87.3 %copy-start.15 = (s32[4]{0:T(128)S(1)}, s32[4]{0:T(128)}, u32[]{:S(2)}) copy-start(s32[4]{0:T(128)} %dirs_ref.1) | copy-start | bytes 52
  44.6 7.4 %collective-permute-start.6 = (bf16[4,6,16,256]{3,2,1,0:T(8,128)(2,1)S(1)}, bf16[4,6,16,256]{3,2,1,0:T(8,128)(2,1)S(1)}, u32[]{:S(2)}, u32[]{:S(2)}) collective-permute-start(bf16[4,6,16,256]{3,2,1,0:T(8,128)(2,1)S(1)} %fusion.2), channel_id=1, source_target_pairs={{0,4},{4,0},{1,5},{5,1},{2,6},{6,2},{3,7},{7,3},{8,12},{12,8},{9,1... | collective-permute-start | bytes 589832 | tf_op jit(solution)/shard_map/ppermute | solution.py:21
  52.1 7.4 %collective-permute-start.7 = (bf16[6,16,256]{2,1,0:T(8,128)(2,1)S(1)}, bf16[6,16,256]{2,1,0:T(8,128)(2,1)S(1)}, u32[]{:S(2)}, u32[]{:S(2)}) collective-permute-start(bf16[6,16,256]{2,1,0:T(8,128)(2,1)S(1)} %get-tuple-element.21), channel_id=1, source_target_pairs={{0,8},{8,16},{16,24},{24,0},{1,9},{9,17},{17,25},{25,1},{2,10},{10... | collective-permute-start | bytes 147464 | tf_op jit(solution)/shard_map/ppermute | solution.py:21
  52.2 7.3 %collective-permute-start.9 = (bf16[6,16,256]{2,1,0:T(8,128)(2,1)S(1)}, bf16[6,16,256]{2,1,0:T(8,128)(2,1)S(1)}, u32[]{:S(2)}, u32[]{:S(2)}) collective-permute-start(bf16[6,16,256]{2,1,0:T(8,128)(2,1)S(1)} %get-tuple-element.22), channel_id=1, source_target_pairs={{0,24},{8,0},{16,8},{24,16},{1,25},{9,1},{17,9},{25,17},{2,26},{10... | collective-permute-start | bytes 147464 | tf_op jit(solution)/shard_map/ppermute | solution.py:21
  56.0 8.3 %collective-permute-start.8 = (bf16[6,16,256]{2,1,0:T(8,128)(2,1)S(1)}, bf16[6,16,256]{2,1,0:T(8,128)(2,1)S(1)}, u32[]{:S(2)}, u32[]{:S(2)}) collective-permute-start(bf16[6,16,256]{2,1,0:T(8,128)(2,1)S(1)} %get-tuple-element.23), channel_id=1, source_target_pairs={{0,16},{8,24},{16,0},{24,8},{1,17},{9,25},{17,1},{25,9},{2,18},{10... | collective-permute-start | bytes 147464 | tf_op jit(solution)/shard_map/ppermute | solution.py:21
  64.3 6.1 %collective-permute-start.10 = (bf16[6,16,256]{2,1,0:T(8,128)(2,1)S(1)}, bf16[6,16,256]{2,1,0:T(8,128)(2,1)S(1)}, u32[]{:S(2)}, u32[]{:S(2)}) collective-permute-start(bf16[6,16,256]{2,1,0:T(8,128)(2,1)S(1)} %get-tuple-element.16), channel_id=1, source_target_pairs={{0,8},{8,16},{16,24},{24,0},{1,9},{9,17},{17,25},{25,1},{2,10},{10... | collective-permute-start | bytes 147464 | tf_op jit(solution)/shard_map/ppermute | solution.py:21
  64.5 5.9 %collective-permute-start.11 = (bf16[6,16,256]{2,1,0:T(8,128)(2,1)S(1)}, bf16[6,16,256]{2,1,0:T(8,128)(2,1)S(1)}, u32[]{:S(2)}, u32[]{:S(2)}) collective-permute-start(bf16[6,16,256]{2,1,0:T(8,128)(2,1)S(1)} %get-tuple-element.16), channel_id=1, source_target_pairs={{0,16},{8,24},{16,0},{24,8},{1,17},{9,25},{17,1},{25,9},{2,18},{10... | collective-permute-start | bytes 147464 | tf_op jit(solution)/shard_map/ppermute | solution.py:21
  66.3 4.6 %collective-permute-start.12 = (bf16[6,16,256]{2,1,0:T(8,128)(2,1)S(1)}, bf16[6,16,256]{2,1,0:T(8,128)(2,1)S(1)}, u32[]{:S(2)}, u32[]{:S(2)}) collective-permute-start(bf16[6,16,256]{2,1,0:T(8,128)(2,1)S(1)} %get-tuple-element.16), channel_id=1, source_target_pairs={{0,24},{8,0},{16,8},{24,16},{1,25},{9,1},{17,9},{25,17},{2,26},{10... | collective-permute-start | bytes 147464 | tf_op jit(solution)/shard_map/ppermute | solution.py:21
  70.9 12.2 %collective-permute-start.15 = (bf16[4,6,16,256]{3,2,0,1:T(8,128)(2,1)S(1)}, bf16[4,6,16,256]{3,2,0,1:T(8,128)(2,1)S(1)}, u32[]{:S(2)}, u32[]{:S(2)}) collective-permute-start(bf16[4,6,16,256]{3,2,0,1:T(8,128)(2,1)S(1)} %bitcast_dynamic-update-slice_fusion.7), channel_id=1, source_target_pairs={{0,3},{1,0},{2,1},{3,2},{4,7},{5,4},{6,5},{7,6},{8,11},{9,8},{10,9... | collective-permute-start | bytes 589832 | tf_op jit(solution)/shard_map/ppermute | solution.py:21
  70.9 12.1 %collective-permute-start.14 = (bf16[4,6,16,256]{3,2,0,1:T(8,128)(2,1)S(1)}, bf16[4,6,16,256]{3,2,0,1:T(8,128)(2,1)S(1)}, u32[]{:S(2)}, u32[]{:S(2)}) collective-permute-start(bf16[4,6,16,256]{3,2,0,1:T(8,128)(2,1)S(1)} %bitcast_dynamic-update-slice_fusion.7), channel_id=1, source_target_pairs={{0,2},{1,3},{2,0},{3,1},{4,6},{5,7},{6,4},{7,5},{8,10},{9,11},{10,... | collective-permute-start | bytes 589832 | tf_op jit(solution)/shard_map/ppermute | solution.py:21
  72.2 10.8 %collective-permute-start.13 = (bf16[4,6,16,256]{3,2,0,1:T(8,128)(2,1)S(1)}, bf16[4,6,16,256]{3,2,0,1:T(8,128)(2,1)S(1)}, u32[]{:S(2)}, u32[]{:S(2)}) collective-permute-start(bf16[4,6,16,256]{3,2,0,1:T(8,128)(2,1)S(1)} %bitcast_dynamic-update-slice_fusion.7), channel_id=1, source_target_pairs={{0,1},{1,2},{2,3},{3,0},{4,5},{5,6},{6,7},{7,4},{8,9},{9,10},{10,1... | collective-permute-start | bytes 589832 | tf_op jit(solution)/shard_map/ppermute | solution.py:21
  131.9 1.6 %copy-start = (bf16[32,64,512]{2,1,0:T(8,128)(2,1)S(1)}, bf16[32,64,512]{2,1,0:T(8,128)(2,1)}, u32[]{:S(2)}) copy-start(bf16[32,64,512]{2,1,0:T(8,128)(2,1)} %all-gather.7.cloned.1.call-done) | copy-start | bytes 6291460
  (4 other events, 3.2 us)
Sparse Core Ops, SparseCore 0:
  20.8 46.0 all-gather.6
  69.8 62.0 all-gather.4

commit v2 on v1

v2 whole, which is shorter than its diff:
```python
import functools
import math

import jax
import jax.numpy as jnp
from jax import lax
from jax.experimental import pallas as pl
from jax.experimental.pallas import tpu as pltpu
from jax.sharding import PartitionSpec as P

VMEM = pl.BlockSpec(memory_space=pltpu.VMEM)
SMEM = pl.BlockSpec(memory_space=pltpu.SMEM)
BF16 = jnp.bfloat16
F32 = jnp.float32


def passed_along(value, axis, steps):
    count = lax.axis_size(axis)
    pairs = [(source, (source + steps) % count) for source in range(count)]
    return lax.ppermute(value, axis, pairs)


def mm(left, right):
    return jnp.dot(left, right, preferred_element_type=F32)


def parts_of(value, divisor):
    quotient = jnp.floor((value + 0.5) * (1.0 / divisor))
    return quotient, value - quotient * divisor


def whole_numbers(shape, axis):
    return lax.broadcasted_iota(jnp.int32, shape, axis).astype(F32)


def chosen(condition):
    return jnp.where(condition, 1.0, 0.0)


def coordinates(index, extent):
    rest, third = parts_of(index, extent[2])
    first, second = parts_of(rest, extent[1])
    return [first, second, third]


def source_columns(extent, e):
    count = math.prod(extent)
    face = count // extent[e]
    inner = count - face if e == 0 else count
    total = 6 * (inner + face)
    column = whole_numbers((1, total), 1)
    beyond = chosen(column >= 6 * inner)
    place = column - beyond * (6 * inner)
    block = 3 * inner + beyond * (3 * (face - inner))
    part = chosen(place >= block)
    site, colour = parts_of(place - part * block, 3)
    within = coordinates(site, extent)
    if e == 0:
        within[0] = within[0] + 1
    flat = [n for d, n in enumerate(extent) if d != e]
    outer, last = parts_of(site, flat[1])
    edge = [outer, last]
    edge.insert(e, jnp.full_like(site, extent[e]))
    where = [w + beyond * (o - w) for w, o in zip(within, edge)]
    return total, part, where, colour


def pieces_kernel(z_ref, fwd_ref, bwd_ref, fwd_out, bwd_out):
    rows, cols = fwd_ref.shape[1:]
    piece = fwd_out.shape[1]
    per_spin = rows // 4
    lane = cols // 4
    flat = lax.broadcasted_iota(jnp.int32, (piece, 1), 0) + z_ref[0] * piece
    spin = jnp.zeros_like(flat)
    for t in range(1, 4):
        spin += jnp.where(flat >= t * per_spin, 1, 0)
    source = 4 * (flat - spin * per_spin) + spin
    select = chosen(lax.broadcasted_iota(jnp.int32, (piece, rows), 1) == source).astype(BF16)
    column = lax.broadcasted_iota(jnp.int32, (1, cols), 1)
    spin = jnp.zeros_like(column)
    for t in range(1, 4):
        spin += jnp.where(column >= t * lane, 1, 0)
    source = 4 * (column - spin * lane) + spin
    perm = chosen(lax.broadcasted_iota(jnp.int32, (cols, cols), 0) == source).astype(BF16)
    for c in range(2):
        picked = mm(select, fwd_ref[c]).astype(BF16)
        fwd_out[c] = mm(picked, perm).astype(BF16)
        bwd_out[c] = mm(select, bwd_ref[c]).astype(BF16)


def links_kernel(extent, link_ref, *outs):
    count = math.prod(extent)
    rows = 6 * count
    row = whole_numbers((rows, 1), 0)
    row_part = chosen(row >= 3 * count)
    row_site, row_colour = parts_of(row - row_part * (3 * count), 3)
    row_where = coordinates(row_site, extent)
    link = link_ref[...]
    high = link.astype(BF16)
    rest = link - high.astype(F32)
    mid = rest.astype(BF16)
    low = (rest - mid.astype(F32)).astype(BF16)
    spread = chosen(row_site == whole_numbers((rows, count), 1)).astype(BF16)
    by_row = [mm(spread, part) for part in (high, mid, low)]
    by_row = [jnp.concatenate([part, part], axis=1) for part in by_row]

    def entry_of(entry):
        half = chosen(entry >= 54)
        direction, left = parts_of(entry - 54 * half, 18)
        part, left = parts_of(left, 9)
        into, out_of = parts_of(left, 3)
        return half, direction, part, into, out_of

    half, direction, _, into, _ = entry_of(whole_numbers((1, 108), 1))
    own_part = (half == row_part) & (into == row_colour)
    place_half, _, place_part, _, place_colour = entry_of(whole_numbers((108, 1), 0))
    for e, out in enumerate(outs):
        keep = chosen(own_part & (direction == e))
        picked = jnp.concatenate([part * keep for part in by_row], axis=0).astype(BF16)
        total, part, where, colour = source_columns(extent, e)
        sign = 1.0 - 2.0 * part * (1.0 - place_half)
        match = (place_colour == colour) & (jnp.abs(place_part - part) == place_half)
        placed = mm(picked, jnp.where(match, sign, 0.0).astype(BF16))
        same = None
        for d in range(3):
            hit = row_where[d] + (1.0 if d == e else 0.0) == where[d]
            same = hit if same is None else same & hit
        mask = chosen(same)
        for n in range(3):
            at = slice(n * rows, (n + 1) * rows)
            out[at, :] = (placed[at] * mask).astype(BF16)


def correlate_kernel(scale, vec_ref, face0, face1, face2, mat0, mat1, mat2, out_ref):
    vec = vec_ref[...]
    rows = vec.shape[0]
    half = rows // 2
    width = vec.shape[1]
    lower = half - face0.shape[0] // 2
    sources = [
        jnp.concatenate([vec[half - lower : half], vec[rows - lower :], face0[...]], axis=0),
        jnp.concatenate([vec, face1[...]], axis=0),
        jnp.concatenate([vec, face2[...]], axis=0),
    ]
    for e, mat in enumerate((mat0, mat1, mat2)):
        terms = mm(mat[...], sources[e])
        moved = terms[:rows] + terms[rows : 2 * rows] + terms[2 * rows :]
        moved = moved.astype(BF16)
        turned = jnp.concatenate([moved[half:], -moved[:half]], axis=0)
        right = jnp.concatenate([moved, turned], axis=1)
        product = lax.dot_general(
            vec, right, (((0,), (0,)), ((), ())), preferred_element_type=F32
        )
        product = (product * scale).astype(BF16)
        out_ref[2 * e] = product[:, :width]
        out_ref[2 * e + 1] = product[:, width:]


def chain_kernel(
    inverse, plan, me_ref, dirs_ref, spin_ref, chain_ref, *refs
):
    elem_count, fwd_keys, bwd_keys = plan
    elem_in, refs = refs[:elem_count], refs[elem_count:]
    fwd_in, refs = refs[: len(fwd_keys)], refs[len(fwd_keys) :]
    bwd_in, refs = refs[: len(bwd_keys)], refs[len(bwd_keys) :]
    out_ref, elem_all, fwd_ref, bwd_ref, x_ref, p_ref, q_ref, b_ref, sems = refs
    _, gx_n, gz_n, own_rows, num_vecs = elem_all.shape
    gy_n = fwd_ref.shape[1]
    width = fwd_ref.shape[-1]
    op_count = out_ref.shape[0]
    row_count = out_ref.shape[2]
    vec_rows = row_count // 4
    spin_pieces = gz_n // 4
    lane = width // 4
    gx, gy, gz = me_ref[0], me_ref[1], me_ref[2]

    def back(at, step, count):
        return lax.rem(at - step + count, count)

    def gz_from(dy, dc):
        return back(gz // 2, dy, gz_n // 2) * 2 + back(lax.rem(gz, 2), dc, 2)

    copies = []

    def place(source, target):
        copy = pltpu.make_async_copy(source, target, sems.at[len(copies)])
        copy.start()
        copies.append(copy)

    for n, ref in enumerate(elem_in):
        for step in range(gx_n):
            place(ref.at[step], elem_all.at[:, back(gx, step, gx_n), back(gz, n, gz_n)])
    for (dx, dy, dc), ref in zip(fwd_keys, fwd_in):
        for step in range(gx_n):
            place(ref.at[step], fwd_ref.at[back(gx, step, gx_n), back(gy, dx, gy_n), gz_from(dy, dc)])
    for (dy, dc), ref in zip(bwd_keys, bwd_in):
        for step in range(gx_n):
            place(ref.at[step], bwd_ref.at[back(gx, step, gx_n), gz_from(dy, dc)])
    for copy in copies:
        copy.wait()

    def elem(d, c):
        return elem_all[2 * d + c].reshape(num_vecs, num_vecs)

    def own(d, c):
        return elem_all[2 * d + c, gx].reshape(vec_rows, num_vecs)

    real_rows = [jnp.concatenate([own(d, 0), -own(d, 1)], axis=1) for d in range(3)]
    imag_rows = [jnp.concatenate([own(d, 1), own(d, 0)], axis=1) for d in range(3)]
    left = jnp.concatenate([part for d in range(3) for part in (real_rows[d], imag_rows[d])], axis=0)
    for t in range(4):
        planes = slice(t * spin_pieces, (t + 1) * spin_pieces)
        for block in range(gy_n):
            right = jnp.concatenate(
                [fwd_ref[:, block, planes, c].reshape(num_vecs, width) for c in range(2)], axis=0
            )
            result = mm(left, right).astype(BF16)
            for d in range(3):
                for c in range(2):
                    at = (d * 2 + c) * vec_rows
                    x_ref[d, c, t, :, block * width : (block + 1) * width] = result[at : at + vec_rows]
        for c in range(2):
            at = (t * 2 + c) * num_vecs
            b_ref[at : at + num_vecs, :] = bwd_ref[:, planes, c].reshape(num_vecs, width)

    row = lax.broadcasted_iota(jnp.int32, (row_count, row_count), 0)
    column = lax.broadcasted_iota(jnp.int32, (row_count, row_count), 1)
    row_spin = lax.rem(row, 4)
    diagonal = lax.div(row, 4) == lax.rem(column, vec_rows)
    column_spin = lax.div(column, vec_rows)

    def one_operator(op, carry):
        a = chain_ref[op, 0]
        b = chain_ref[op, 1]
        dir_a = dirs_ref[a]
        dir_b = dirs_ref[b]
        mix = jnp.zeros((row_count, row_count), F32)
        for t in range(4):
            in_t = column_spin == t
            for s in range(4):
                mix = jnp.where(in_t & (row_spin == s), spin_ref[a, s, t], mix)
        mix = jnp.where(diagonal, mix, 0.0)
        high = mix.astype(BF16)
        low = (mix - high.astype(F32)).astype(BF16)
        mix = jnp.concatenate([high, low], axis=1)
        for c in range(2):
            source = x_ref[dir_a, c].reshape(row_count, 4 * num_vecs)
            result = mm(mix, jnp.concatenate([source, source], axis=0)).astype(BF16)
            for s in range(4):
                for block in range(gy_n):
                    at = block * width + s * lane
                    to = c * num_vecs + block * lane
                    p_ref[s, :, to : to + lane] = result[:, at : at + lane]
        real_b, imag_b = elem(dir_b, 0), elem(dir_b, 1)
        right = jnp.concatenate(
            [
                jnp.concatenate([real_b, imag_b], axis=1),
                jnp.concatenate([-imag_b, real_b], axis=1),
            ],
            axis=0,
        )
        parts = [mm(p_ref[s], right) for s in range(4)]
        for t in range(4):
            total = parts[0] * (spin_ref[b, 0, t] * inverse)
            for s in range(1, 4):
                total += parts[s] * (spin_ref[b, s, t] * inverse)
            total = total.astype(BF16)
            real, imag = total[:, :num_vecs], total[:, num_vecs:]
            at = 2 * t * num_vecs
            q_ref[:row_count, at : at + num_vecs] = real
            q_ref[:row_count, at + num_vecs : at + 2 * num_vecs] = -imag
            q_ref[row_count:, at : at + num_vecs] = imag
            q_ref[row_count:, at + num_vecs : at + 2 * num_vecs] = real
        final = mm(q_ref[...], b_ref[...]).astype(BF16)
        out_ref[op, 0] = final[:row_count]
        out_ref[op, 1] = final[row_count:]
        return carry

    lax.fori_loop(0, op_count, one_operator, 0)


def summed_over(value, axis):
    total = value.astype(F32)
    for step in range(1, lax.axis_size(axis)):
        total += passed_along(value, axis, step).astype(F32)
    return total


def scattered_over(value, axis):
    count = lax.axis_size(axis)
    me = lax.axis_index(axis)
    total = lax.dynamic_index_in_dim(value, me, 0, keepdims=False).astype(F32)
    for step in range(1, count):
        part = lax.dynamic_index_in_dim(value, lax.rem(me + step, count), 0, keepdims=False)
        total += passed_along(part, axis, step).astype(F32)
    return total


def gathered_over(value, axis):
    count = lax.axis_size(axis)
    return jnp.stack([value] + [passed_along(value, axis, step) for step in range(1, count)])


def passed_in_gz(value, dy, dc):
    count = lax.axis_size("gz")
    chips = count // 2
    pairs = [(n, ((n // 2 + dy) % chips) * 2 + (n + dc) % 2) for n in range(count)]
    return lax.ppermute(value, "gz", pairs)


def on_device(eigvecs, links, directions, spin_mats, forward_peram, backward_peram, chain_order):
    extent = eigvecs.shape[:3]
    num_vecs = eigvecs.shape[-1]
    gx_n, gy_n, gz_n = (lax.axis_size(name) for name in ("gx", "gy", "gz"))
    chips = gz_n // 2
    me = jnp.stack([lax.axis_index(name) for name in ("gx", "gy", "gz")]).astype(jnp.int32)

    ordered = eigvecs.transpose(3, 0, 1, 2, 4, 5)
    faces = []
    for e, axis in enumerate(("gx", "gy", "gz")):
        face = lax.slice_in_dim(ordered, 0, 1, axis=1 + e).reshape(-1, num_vecs)
        faces.append(passed_along(face, axis, -1))
    vec = ordered.reshape(-1, num_vecs)

    rows, cols = forward_peram.shape[1:]
    piece = rows // gz_n
    piece_shape = jax.ShapeDtypeStruct((2, piece, cols), BF16)
    fwd_piece, bwd_piece = pl.pallas_call(
        pieces_kernel,
        out_shape=[piece_shape, piece_shape],
        in_specs=[SMEM, VMEM, VMEM],
        out_specs=[VMEM, VMEM],
        compiler_params=pltpu.CompilerParams(vmem_limit_bytes=24 * 2**20),
        name="pieces",
    )(me[2:], forward_peram, backward_peram)

    fwd_line = gathered_over(fwd_piece, "gx")
    bwd_line = gathered_over(bwd_piece, "gx")
    fwd_parts, bwd_parts = {}, {}
    for dy in range(chips):
        mine = passed_in_gz(fwd_line, dy, 0) if dy else fwd_line
        for dx in range(gy_n):
            fwd_parts[dx, dy, 0] = passed_along(mine, "gy", dx) if dx else mine
        bwd_parts[dy, 0] = passed_in_gz(bwd_line, dy, 0) if dy else bwd_line
    for dx, dy, _ in list(fwd_parts):
        fwd_parts[dx, dy, 1] = passed_in_gz(fwd_parts[dx, dy, 0], 0, 1)
    for dy, _ in list(bwd_parts):
        bwd_parts[dy, 1] = passed_in_gz(bwd_parts[dy, 0], 0, 1)

    site_rows = 6 * math.prod(extent)
    link_mats = pl.pallas_call(
        functools.partial(links_kernel, extent),
        out_shape=[
            jax.ShapeDtypeStruct((3 * site_rows, site_rows - (0 if e else site_rows // extent[0]) + site_rows // extent[e]), BF16)
            for e in range(3)
        ],
        in_specs=[VMEM],
        out_specs=[VMEM] * 3,
        compiler_params=pltpu.CompilerParams(vmem_limit_bytes=24 * 2**20),
        name="link_matrices",
    )(links.reshape(-1, 54))

    volume = math.prod(extent) * gx_n * gy_n * gz_n
    partial = pl.pallas_call(
        functools.partial(correlate_kernel, 1.0 / math.sqrt(12.0 * volume)),
        out_shape=jax.ShapeDtypeStruct((6, num_vecs, num_vecs), BF16),
        in_specs=[VMEM] * 7,
        out_specs=VMEM,
        compiler_params=pltpu.CompilerParams(vmem_limit_bytes=24 * 2**20),
        name="correlate",
    )(vec, *faces, *link_mats)

    own_rows = num_vecs // (gz_n * gx_n)
    parts = partial.reshape(6, gx_n, gz_n, own_rows, num_vecs).transpose(2, 1, 0, 3, 4)
    summed = scattered_over(parts, "gz").astype(BF16)
    summed = summed_over(summed, "gy").astype(BF16)
    summed = scattered_over(summed, "gx").astype(BF16)
    elem_line = gathered_over(summed, "gx")
    elem_parts = [elem_line] + [passed_along(elem_line, "gz", step) for step in range(1, gz_n)]

    op_count = chain_order.shape[0]
    plan = (len(elem_parts), tuple(fwd_parts), tuple(bwd_parts))
    operands = [*elem_parts, *fwd_parts.values(), *bwd_parts.values()]
    return pl.pallas_call(
        functools.partial(chain_kernel, 1.0 / math.sqrt(4 * num_vecs), plan),
        out_shape=jax.ShapeDtypeStruct((op_count, 2, rows, cols), BF16),
        in_specs=[SMEM] * 4 + [pl.BlockSpec(memory_space=pl.ANY)] * len(operands),
        out_specs=VMEM,
        scratch_shapes=[
            pltpu.VMEM((6, gx_n, gz_n, own_rows, num_vecs), BF16),
            pltpu.VMEM((gx_n, gy_n, gz_n, 2, piece, cols), BF16),
            pltpu.VMEM((gx_n, gz_n, 2, piece, cols), BF16),
            pltpu.VMEM((3, 2, 4, rows // 4, 4 * num_vecs), BF16),
            pltpu.VMEM((4, rows, 2 * num_vecs), BF16),
            pltpu.VMEM((2 * rows, 8 * num_vecs), BF16),
            pltpu.VMEM((8 * num_vecs, cols), BF16),
            pltpu.SemaphoreType.DMA((gx_n * len(operands),)),
        ],
        compiler_params=pltpu.CompilerParams(vmem_limit_bytes=40 * 2**20),
        name="chain",
    )(me, directions, spin_mats, chain_order, *operands)


def solution(mesh):
    in_specs = (
        P("gx", "gy", "gz", None, None, None),
        P("gx", "gy", "gz", None, None, None, None),
        P(),
        P(),
        P(None, "gx", "gy"),
        P(None, "gx", "gy"),
        P("gz", None),
    )
    out_specs = P("gz", None, "gx", "gy")
    return jax.shard_map(
        on_device, mesh=mesh, in_specs=in_specs, out_specs=out_specs, check_vma=False
    )
```

time: 158 us -> 118 us (0.75)
  waiting for transfers between devices: 88.6 us -> 61.2 us
  between operations: 13.7 us -> 0.29 us
  local copies, waits for them, and re-layouts: 15.1 us -> 7.31 us
  Pallas kernels: 19.3 us -> 24.4 us
  starting transfers between devices: 19.9 us -> 23.5 us
    all_gather x2 -> x0, waiting for transfers between devices: 48.7 us -> none  [the longest x1 48.7 us: on_device(): fwd_all = lax.all_gather(fwd_piece, ('gx', 'gy', 'gz'), axis=0, tiled=False)]
    ppermute x16 -> x24, waiting for transfers between devices: 39.2 us -> 54.9 us  [passed_along(): return lax.ppermute(value, axis, pairs)]
    unnamed x41 -> x17, local copies, waits for them, and re-layouts: 14.2 us -> 3.43 us
    ppermute x0 -> x8, waiting for transfers between devices: none -> 6.26 us  [passed_in_gz(): return lax.ppermute(value, 'gz', pairs)]
    pallas_call x1, Pallas kernels: 16.5 us -> 21.8 us  [on_device(): pl.pallas_call(functools.partial(chain_kernel, 1.0 / math.sqrt(4 * num_ve...]
    ppermute x0 -> x8, starting transfers between devices: none -> 2.89 us  [passed_in_gz(): return lax.ppermute(value, 'gz', pairs)]
    slice x6, local copies, waits for them, and re-layouts: 0.13 us -> 2.4 us  [on_device(): face = lax.slice_in_dim(ordered, 0, 1, axis=1 + e).reshape(-1, num_vecs)]
    ppermute x16 -> x24, starting transfers between devices: 19.8 us -> 20.6 us  [passed_along(): return lax.ppermute(value, axis, pairs)]
  transfers between devices with their start and end apart: 18 -> 32, of which waited for: 11 -> 15; matrix products, arithmetic and copies ran while one was open for 1% -> 4% of each run, Pallas kernels for 1% -> 1%
where the time goes in v2:
time: 118 us; the launch traced here: 117 us
  waiting for transfers between devices  61.2 us (52%)
  Pallas kernels  24.4 us (21%)
  starting transfers between devices  23.5 us (20%)
  local copies, waits for them, and re-layouts  7.31 us (6%)
    ppermute x24, waiting for transfers between devices, passed_along(): return lax.ppermute(value, axis, pairs)  54.9 us
    pallas_call x1, Pallas kernels, on_device(): pl.pallas_call(functools.partial(chain_kernel, 1.0 / math.sqrt(4 * num_ve...  21.8 us
    ppermute x24, starting transfers between devices, passed_along(): return lax.ppermute(value, axis, pairs)  20.6 us
    ppermute x8, waiting for transfers between devices, passed_in_gz(): return lax.ppermute(value, 'gz', pairs)  6.26 us
    unnamed x17, local copies, waits for them, and re-layouts  3.43 us
    ppermute x8, starting transfers between devices, passed_in_gz(): return lax.ppermute(value, 'gz', pairs)  2.89 us
    slice x6, local copies, waits for them, and re-layouts, on_device(): face = lax.slice_in_dim(ordered, 0, 1, axis=1 + e).reshape(-1, num_vecs)  2.4 us
  transfers between devices with their start and end apart: 32, of which 15 were waited for; matrix products, arithmetic and copies ran while one was open for 4% of the time, Pallas kernels for 1%

profile of v2, /device:TPU:0, one launch (start us, length us, event | category | flops | bytes accessed | tf_op | source)
XLA Modules:
  0.0 117.1 jit_solution(11823245081371160111)
XLA Ops:
  0.0 0.8 slice.12
  0.9 5.1 %collective-permute-start = (bf16[96,256]{1,0:T(8,128)(2,1)S(1)}, bf16[96,256]{1,0:T(8,128)(2,1)S(1)}, u32[]{:S(2)}, u32[]{:S(2)}) collective-permute-start(bf16[96,256]{1,0:T(8,128)(2,1)S(1)} %reshape.23), channel_id=1, source_target_pairs={{0,24},{8,0},{16,8},{24,16},{1,25},{9,1},{17,9},{25,17},{2,26},{10... | collective-permute-start | bytes 147464 | tf_op jit(solution)/shard_map/ppermute | solution.py:20
  6.0 0.8 slice.13
  6.8 1.6 %collective-permute-start.1 = (bf16[48,256]{1,0:T(8,128)(2,1)S(1)}, bf16[48,256]{1,0:T(8,128)(2,1)S(1)}, u32[]{:S(2)}, u32[]{:S(2)}) collective-permute-start(bf16[48,256]{1,0:T(8,128)(2,1)S(1)} %reshape.24), channel_id=1, source_target_pairs={{0,4},{4,0},{1,5},{5,1},{2,6},{6,2},{3,7},{7,3},{8,12},{12,8},{9,1... | collective-permute-start | bytes 73736 | tf_op jit(solution)/shard_map/ppermute | solution.py:20
  8.4 0.8 slice.14
  9.7 0.9 copy.14
  10.7 1.0 copy.18
  12.6 1.4 %correlate.1 = bf16[6,256,256]{2,1,0:T(8,128)(2,1)S(1)} custom-call(bf16[192,256]{1,0:T(8,128)(2,1)S(1)} %reshape.22.vec_ref, bf16[96,256]{1,0:T(8,128)(2,1)S(1)} %collective-permute-done.face0, bf16[48,256]{1,0:T(8,128)(2,1)S(1)} %collective-permute-done.1.face1, bf16[48,256]{1,0:T(8,128)(2,1)S(1)} %collective-permute-done.2.face2, ...), custom_call_target="tpu_custom_call" | custom-call | tf_op jit(solution)/shard_map/correlate/pallas_call | solution.py:364
  14.1 1.3 %collective-permute-start.5 = (bf16[4,6,16,256]{3,2,1,0:T(8,128)(2,1)S(1)}, bf16[4,6,16,256]{3,2,1,0:T(8,128)(2,1)S(1)}, u32[]{:S(2)}, u32[]{:S(2)}) collective-permute-start(bf16[4,6,16,256]{3,2,1,0:T(8,128)(2,1)S(1)} %bitcast.68), channel_id=1, source_target_pairs={{0,3},{1,0},{2,1},{3,2},{4,7},{5,4},{6,5},{7,6},{8,11},{9,8},{10,9... | collective-permute-start | bytes 589832 | tf_op jit(solution)/shard_map/ppermute | solution.py:20
  17.1 3.6 %collective-permute-done.5 = bf16[4,6,16,256]{3,2,1,0:T(8,128)(2,1)S(1)} collective-permute-done((bf16[4,6,16,256]{3,2,1,0:T(8,128)(2,1)S(1)}, bf16[4,6,16,256]{3,2,1,0:T(8,128)(2,1)S(1)}, u32[]{:S(2)}, u32[]{:S(2)}) %collective-permute-start.5) | collective-permute-done | bytes 196640 | tf_op jit(solution)/shard_map/ppermute | solution.py:20
  20.7 1.9 %collective-permute-done.3 = bf16[4,6,16,256]{3,2,1,0:T(8,128)(2,1)S(1)} collective-permute-done((bf16[4,6,16,256]{3,2,1,0:T(8,128)(2,1)S(1)}, bf16[4,6,16,256]{3,2,1,0:T(8,128)(2,1)S(1)}, u32[]{:S(2)}, u32[]{:S(2)}) %collective-permute-start.3) | collective-permute-done | bytes 196640 | tf_op jit(solution)/shard_map/ppermute | solution.py:20
  22.6 2.3 %collective-permute-done.4 = bf16[4,6,16,256]{3,2,1,0:T(8,128)(2,1)S(1)} collective-permute-done((bf16[4,6,16,256]{3,2,1,0:T(8,128)(2,1)S(1)}, bf16[4,6,16,256]{3,2,1,0:T(8,128)(2,1)S(1)}, u32[]{:S(2)}, u32[]{:S(2)}) %collective-permute-start.4) | collective-permute-done | bytes 196640 | tf_op jit(solution)/shard_map/ppermute | solution.py:20
  26.2 3.9 %collective-permute-done.17 = bf16[2,64,512]{2,1,0:T(8,128)(2,1)S(1)} collective-permute-done((bf16[2,64,512]{2,1,0:T(8,128)(2,1)S(1)}, bf16[2,64,512]{2,1,0:T(8,128)(2,1)S(1)}, u32[]{:S(2)}, u32[]{:S(2)}) %collective-permute-start.17) | collective-permute-done | bytes 131104 | tf_op jit(solution)/shard_map/ppermute | solution.py:20
  30.2 1.6 %collective-permute-start.20 = (bf16[4,2,64,512]{3,2,1,0:T(8,128)(2,1)S(1)}, bf16[4,2,64,512]{3,2,1,0:T(8,128)(2,1)S(1)}, u32[]{:S(2)}, u32[]{:S(2)}) collective-permute-start(bf16[4,2,64,512]{3,2,1,0:T(8,128)(2,1)S(1)} %pad_maximum_fusion.refs_4_), channel_id=1, source_target_pairs={{0,2},{1,3},{2,0},{3,1},{4,6},{5,7},{6,4},{7,5},{8,10},{9,11},{10,... | collective-permute-start | bytes 1572872 | tf_op jit(solution)/shard_map/ppermute | solution.py:308
  31.7 1.1 collective-permute-done.6
  32.9 4.7 %collective-permute-start.7 = (bf16[6,16,256]{2,1,0:T(8,128)(2,1)S(1)}, bf16[6,16,256]{2,1,0:T(8,128)(2,1)S(1)}, u32[]{:S(2)}, u32[]{:S(2)}) collective-permute-start(bf16[6,16,256]{2,1,0:T(8,128)(2,1)S(1)} %get-tuple-element.19), channel_id=1, source_target_pairs={{0,8},{8,16},{16,24},{24,0},{1,9},{9,17},{17,25},{25,1},{2,10},{10... | collective-permute-start | bytes 147464 | tf_op jit(solution)/shard_map/ppermute | solution.py:20
  37.6 4.7 %collective-permute-done.27 = bf16[2,64,512]{2,1,0:T(8,128)(2,1)S(1)} collective-permute-done((bf16[2,64,512]{2,1,0:T(8,128)(2,1)S(1)}, bf16[2,64,512]{2,1,0:T(8,128)(2,1)S(1)}, u32[]{:S(2)}, u32[]{:S(2)}) %collective-permute-start.27) | collective-permute-done | bytes 131104 | tf_op jit(solution)/shard_map/ppermute | solution.py:20
  42.5 0.9 collective-permute-done.9
  43.4 4.0 %collective-permute-done.8 = bf16[6,16,256]{2,1,0:T(8,128)(2,1)S(1)} collective-permute-done((bf16[6,16,256]{2,1,0:T(8,128)(2,1)S(1)}, bf16[6,16,256]{2,1,0:T(8,128)(2,1)S(1)}, u32[]{:S(2)}, u32[]{:S(2)}) %collective-permute-start.8) | collective-permute-done | bytes 49184 | tf_op jit(solution)/shard_map/ppermute | solution.py:20
  47.4 1.8 %collective-permute-start.12 = (bf16[6,16,256]{2,1,0:T(8,128)(2,1)S(1)}, bf16[6,16,256]{2,1,0:T(8,128)(2,1)S(1)}, u32[]{:S(2)}, u32[]{:S(2)}) collective-permute-start(bf16[6,16,256]{2,1,0:T(8,128)(2,1)S(1)} %fusion.5), channel_id=1, source_target_pairs={{0,24},{8,0},{16,8},{24,16},{1,25},{9,1},{17,9},{25,17},{2,26},{10... | collective-permute-start | bytes 147464 | tf_op jit(solution)/shard_map/ppermute | solution.py:20
  49.9 1.7 %collective-permute-done.12 = bf16[6,16,256]{2,1,0:T(8,128)(2,1)S(1)} collective-permute-done((bf16[6,16,256]{2,1,0:T(8,128)(2,1)S(1)}, bf16[6,16,256]{2,1,0:T(8,128)(2,1)S(1)}, u32[]{:S(2)}, u32[]{:S(2)}) %collective-permute-start.12) | collective-permute-done | bytes 49184 | tf_op jit(solution)/shard_map/ppermute | solution.py:20
  51.5 0.7 collective-permute-start.29
  52.3 3.2 %collective-permute-done.11 = bf16[6,16,256]{2,1,0:T(8,128)(2,1)S(1)} collective-permute-done((bf16[6,16,256]{2,1,0:T(8,128)(2,1)S(1)}, bf16[6,16,256]{2,1,0:T(8,128)(2,1)S(1)}, u32[]{:S(2)}, u32[]{:S(2)}) %collective-permute-start.11) | collective-permute-done | bytes 49184 | tf_op jit(solution)/shard_map/ppermute | solution.py:20
  56.0 1.5 %collective-permute-start.21 = (bf16[4,2,64,512]{3,2,1,0:T(8,128)(2,1)S(1)}, bf16[4,2,64,512]{3,2,1,0:T(8,128)(2,1)}, u32[]{:S(2)}, u32[]{:S(2)}) collective-permute-start(bf16[4,2,64,512]{3,2,1,0:T(8,128)(2,1)S(1)} %collective-permute-done.20.refs_6_), channel_id=1, source_target_pairs={{0,4},{4,0},{1,5},{5,1},{2,6},{6,2},{3,7},{7,3},{8,12},{12,8},{9,1... | collective-permute-start | bytes 1572872 | tf_op jit(solution)/shard_map/ppermute | solution.py:20
  57.8 6.2 %collective-permute-done.29.refs_13_ = bf16[4,2,64,512]{3,2,1,0:T(8,128)(2,1)S(1)} collective-permute-done((bf16[4,2,64,512]{3,2,1,0:T(8,128)(2,1)S(1)}, bf16[4,2,64,512]{3,2,1,0:T(8,128)(2,1)S(1)}, u32[]{:S(2)}, u32[]{:S(2)}) %collective-permute-start.29) | collective-permute-done | bytes 524320 | tf_op jit(solution)/shard_map/ppermute | solution.py:308
  64.6 5.7 %collective-permute-done.19.refs_5_ = bf16[4,2,64,512]{3,2,1,0:T(8,128)(2,1)} collective-permute-done((bf16[4,2,64,512]{3,2,1,0:T(8,128)(2,1)S(1)}, bf16[4,2,64,512]{3,2,1,0:T(8,128)(2,1)}, u32[]{:S(2)}, u32[]{:S(2)}) %collective-permute-start.19) | collective-permute-done | bytes 524320 | tf_op jit(solution)/shard_map/ppermute | solution.py:20
  70.3 10.8 %collective-permute-done.21.refs_7_ = bf16[4,2,64,512]{3,2,1,0:T(8,128)(2,1)} collective-permute-done((bf16[4,2,64,512]{3,2,1,0:T(8,128)(2,1)S(1)}, bf16[4,2,64,512]{3,2,1,0:T(8,128)(2,1)}, u32[]{:S(2)}, u32[]{:S(2)}) %collective-permute-start.21) | collective-permute-done | bytes 524320 | tf_op jit(solution)/shard_map/ppermute | solution.py:20
  81.8 6.7 %collective-permute-done.14.refs_2_ = bf16[4,6,16,256]{3,2,1,0:T(8,128)(2,1)S(1)} collective-permute-done((bf16[4,6,16,256]{3,2,1,0:T(8,128)(2,1)S(1)}, bf16[4,6,16,256]{3,2,1,0:T(8,128)(2,1)S(1)}, u32[]{:S(2)}, u32[]{:S(2)}) %collective-permute-start.14) | collective-permute-done | bytes 196640 | tf_op jit(solution)/shard_map/ppermute | solution.py:20
  89.2 0.8 copy.24.chain_ref
  90.0 4.4 %collective-permute-done.13.refs_1_ = bf16[4,6,16,256]{3,2,1,0:T(8,128)(2,1)} collective-permute-done((bf16[4,6,16,256]{3,2,1,0:T(8,128)(2,1)S(1)}, bf16[4,6,16,256]{3,2,1,0:T(8,128)(2,1)}, u32[]{:S(2)}, u32[]{:S(2)}) %collective-permute-start.13) | collective-permute-done | bytes 196640 | tf_op jit(solution)/shard_map/ppermute | solution.py:20
  94.4 0.9 copy-done.3
  95.3 21.8 %chain.1 = bf16[4,2,256,512]{3,2,1,0:T(8,128)(2,1)} custom-call(s32[3]{0:T(128)S(1)} %pad_add_fusion.me_ref, s32[4]{0:T(128)S(1)} %copy-done.5, f32[4,4,4]{2,1,0:T(4,128)S(1)} %copy-done.4, s32[4,2]{1,0:T(4,128)S(1)} %copy.24.chain_ref, bf16[4,6,16,256]{3,2,1,0:T(8,128)(2,1)S(1)} %pad_maximum_fusion.2.refs_0_, ...), custom_call_target="tpu_custom_call" | custom-call | tf_op jit(solution)/shard_map/chain/pallas_call | solution.py:384
  (75 shorter events, 8.3 us)
Async XLA Ops:
  0.9 11.7 %collective-permute-start = (bf16[96,256]{1,0:T(8,128)(2,1)S(1)}, bf16[96,256]{1,0:T(8,128)(2,1)S(1)}, u32[]{:S(2)}, u32[]{:S(2)}) collective-permute-start(bf16[96,256]{1,0:T(8,128)(2,1)S(1)} %reshape.23), channel_id=1, source_target_pairs={{0,24},{8,0},{16,8},{24,16},{1,25},{9,1},{17,9},{25,17},{2,26},{10... | collective-permute-start | bytes 147464 | tf_op jit(solution)/shard_map/ppermute | solution.py:20
  6.8 5.7 %collective-permute-start.1 = (bf16[48,256]{1,0:T(8,128)(2,1)S(1)}, bf16[48,256]{1,0:T(8,128)(2,1)S(1)}, u32[]{:S(2)}, u32[]{:S(2)}) collective-permute-start(bf16[48,256]{1,0:T(8,128)(2,1)S(1)} %reshape.24), channel_id=1, source_target_pairs={{0,4},{4,0},{1,5},{5,1},{2,6},{6,2},{3,7},{7,3},{8,12},{12,8},{9,1... | collective-permute-start | bytes 73736 | tf_op jit(solution)/shard_map/ppermute | solution.py:20
  9.2 3.4 %collective-permute-start.2 = (bf16[48,256]{1,0:T(8,128)(2,1)S(1)}, bf16[48,256]{1,0:T(8,128)(2,1)S(1)}, u32[]{:S(2)}, u32[]{:S(2)}) collective-permute-start(bf16[48,256]{1,0:T(8,128)(2,1)S(1)} %reshape.25), channel_id=1, source_target_pairs={{0,3},{1,0},{2,1},{3,2},{4,7},{5,4},{6,5},{7,6},{8,11},{9,8},{10,9... | collective-permute-start | bytes 73736 | tf_op jit(solution)/shard_map/ppermute | solution.py:20
  14.1 6.6 %collective-permute-start.5 = (bf16[4,6,16,256]{3,2,1,0:T(8,128)(2,1)S(1)}, bf16[4,6,16,256]{3,2,1,0:T(8,128)(2,1)S(1)}, u32[]{:S(2)}, u32[]{:S(2)}) collective-permute-start(bf16[4,6,16,256]{3,2,1,0:T(8,128)(2,1)S(1)} %bitcast.68), channel_id=1, source_target_pairs={{0,3},{1,0},{2,1},{3,2},{4,7},{5,4},{6,5},{7,6},{8,11},{9,8},{10,9... | collective-permute-start | bytes 589832 | tf_op jit(solution)/shard_map/ppermute | solution.py:20
  15.4 7.2 %collective-permute-start.3 = (bf16[4,6,16,256]{3,2,1,0:T(8,128)(2,1)S(1)}, bf16[4,6,16,256]{3,2,1,0:T(8,128)(2,1)S(1)}, u32[]{:S(2)}, u32[]{:S(2)}) collective-permute-start(bf16[4,6,16,256]{3,2,1,0:T(8,128)(2,1)S(1)} %bitcast.67), channel_id=1, source_target_pairs={{0,1},{1,2},{2,3},{3,0},{4,5},{5,6},{6,7},{7,4},{8,9},{9,10},{10,1... | collective-permute-start | bytes 589832 | tf_op jit(solution)/shard_map/ppermute | solution.py:20
  15.4 9.5 %collective-permute-start.4 = (bf16[4,6,16,256]{3,2,1,0:T(8,128)(2,1)S(1)}, bf16[4,6,16,256]{3,2,1,0:T(8,128)(2,1)S(1)}, u32[]{:S(2)}, u32[]{:S(2)}) collective-permute-start(bf16[4,6,16,256]{3,2,1,0:T(8,128)(2,1)S(1)} %bitcast.66), channel_id=1, source_target_pairs={{0,2},{1,3},{2,0},{3,1},{4,6},{5,7},{6,4},{7,5},{8,10},{9,11},{10,... | collective-permute-start | bytes 589832 | tf_op jit(solution)/shard_map/ppermute | solution.py:20
  16.6 9.5 %collective-permute-start.18 = (bf16[2,64,512]{2,1,0:T(8,128)(2,1)S(1)}, bf16[2,64,512]{2,1,0:T(8,128)(2,1)S(1)}, u32[]{:S(2)}, u32[]{:S(2)}) collective-permute-start(bf16[2,64,512]{2,1,0:T(8,128)(2,1)S(1)} %get-tuple-element.13), channel_id=1, source_target_pairs={{0,24},{8,0},{16,8},{24,16},{1,25},{9,1},{17,9},{25,17},{2,26},{10... | collective-permute-start | bytes 393224 | tf_op jit(solution)/shard_map/ppermute | solution.py:20
  17.1 13.0 %collective-permute-start.17 = (bf16[2,64,512]{2,1,0:T(8,128)(2,1)S(1)}, bf16[2,64,512]{2,1,0:T(8,128)(2,1)S(1)}, u32[]{:S(2)}, u32[]{:S(2)}) collective-permute-start(bf16[2,64,512]{2,1,0:T(8,128)(2,1)S(1)} %get-tuple-element.13), channel_id=1, source_target_pairs={{0,16},{8,24},{16,0},{24,8},{1,17},{9,25},{17,1},{25,9},{2,18},{10... | collective-permute-start | bytes 393224 | tf_op jit(solution)/shard_map/ppermute | solution.py:20
  20.7 9.4 %collective-permute-start.16 = (bf16[2,64,512]{2,1,0:T(8,128)(2,1)S(1)}, bf16[2,64,512]{2,1,0:T(8,128)(2,1)S(1)}, u32[]{:S(2)}, u32[]{:S(2)}) collective-permute-start(bf16[2,64,512]{2,1,0:T(8,128)(2,1)S(1)} %get-tuple-element.13), channel_id=1, source_target_pairs={{0,8},{8,16},{16,24},{24,0},{1,9},{9,17},{17,25},{25,1},{2,10},{10... | collective-permute-start | bytes 393224 | tf_op jit(solution)/shard_map/ppermute | solution.py:20
  25.1 7.8 %collective-permute-start.6 = (bf16[4,6,16,256]{3,2,1,0:T(8,128)(2,1)S(1)}, bf16[4,6,16,256]{3,2,1,0:T(8,128)(2,1)S(1)}, u32[]{:S(2)}, u32[]{:S(2)}) collective-permute-start(bf16[4,6,16,256]{3,2,1,0:T(8,128)(2,1)S(1)} %fusion.2), channel_id=1, source_target_pairs={{0,4},{4,0},{1,5},{5,1},{2,6},{6,2},{3,7},{7,3},{8,12},{12,8},{9,1... | collective-permute-start | bytes 589832 | tf_op jit(solution)/shard_map/ppermute | solution.py:20
  25.7 11.9 %collective-permute-start.28 = (bf16[2,64,512]{2,1,0:T(8,128)(2,1)S(1)}, bf16[2,64,512]{2,1,0:T(8,128)(2,1)S(1)}, u32[]{:S(2)}, u32[]{:S(2)}) collective-permute-start(bf16[2,64,512]{2,1,0:T(8,128)(2,1)S(1)} %get-tuple-element.14), channel_id=1, source_target_pairs={{0,24},{8,0},{16,8},{24,16},{1,25},{9,1},{17,9},{25,17},{2,26},{10... | collective-permute-start | bytes 393224 | tf_op jit(solution)/shard_map/ppermute | solution.py:20
  26.2 16.2 %collective-permute-start.27 = (bf16[2,64,512]{2,1,0:T(8,128)(2,1)S(1)}, bf16[2,64,512]{2,1,0:T(8,128)(2,1)S(1)}, u32[]{:S(2)}, u32[]{:S(2)}) collective-permute-start(bf16[2,64,512]{2,1,0:T(8,128)(2,1)S(1)} %get-tuple-element.14), channel_id=1, source_target_pairs={{0,16},{8,24},{16,0},{24,8},{1,17},{9,25},{17,1},{25,9},{2,18},{10... | collective-permute-start | bytes 393224 | tf_op jit(solution)/shard_map/ppermute | solution.py:20
  30.1 12.3 %collective-permute-start.26 = (bf16[2,64,512]{2,1,0:T(8,128)(2,1)S(1)}, bf16[2,64,512]{2,1,0:T(8,128)(2,1)S(1)}, u32[]{:S(2)}, u32[]{:S(2)}) collective-permute-start(bf16[2,64,512]{2,1,0:T(8,128)(2,1)S(1)} %get-tuple-element.14), channel_id=1, source_target_pairs={{0,8},{8,16},{16,24},{24,0},{1,9},{9,17},{17,25},{25,1},{2,10},{10... | collective-permute-start | bytes 393224 | tf_op jit(solution)/shard_map/ppermute | solution.py:20
  30.2 25.9 %collective-permute-start.20 = (bf16[4,2,64,512]{3,2,1,0:T(8,128)(2,1)S(1)}, bf16[4,2,64,512]{3,2,1,0:T(8,128)(2,1)S(1)}, u32[]{:S(2)}, u32[]{:S(2)}) collective-permute-start(bf16[4,2,64,512]{3,2,1,0:T(8,128)(2,1)S(1)} %pad_maximum_fusion.refs_4_), channel_id=1, source_target_pairs={{0,2},{1,3},{2,0},{3,1},{4,6},{5,7},{6,4},{7,5},{8,10},{9,11},{10,... | collective-permute-start | bytes 1572872 | tf_op jit(solution)/shard_map/ppermute | solution.py:308
  32.9 9.6 %collective-permute-start.7 = (bf16[6,16,256]{2,1,0:T(8,128)(2,1)S(1)}, bf16[6,16,256]{2,1,0:T(8,128)(2,1)S(1)}, u32[]{:S(2)}, u32[]{:S(2)}) collective-permute-start(bf16[6,16,256]{2,1,0:T(8,128)(2,1)S(1)} %get-tuple-element.19), channel_id=1, source_target_pairs={{0,8},{8,16},{16,24},{24,0},{1,9},{9,17},{17,25},{25,1},{2,10},{10... | collective-permute-start | bytes 147464 | tf_op jit(solution)/shard_map/ppermute | solution.py:20
  37.6 5.8 %collective-permute-start.9 = (bf16[6,16,256]{2,1,0:T(8,128)(2,1)S(1)}, bf16[6,16,256]{2,1,0:T(8,128)(2,1)S(1)}, u32[]{:S(2)}, u32[]{:S(2)}) collective-permute-start(bf16[6,16,256]{2,1,0:T(8,128)(2,1)S(1)} %get-tuple-element.20), channel_id=1, source_target_pairs={{0,24},{8,0},{16,8},{24,16},{1,25},{9,1},{17,9},{25,17},{2,26},{10... | collective-permute-start | bytes 147464 | tf_op jit(solution)/shard_map/ppermute | solution.py:20
  42.4 5.0 %collective-permute-start.8 = (bf16[6,16,256]{2,1,0:T(8,128)(2,1)S(1)}, bf16[6,16,256]{2,1,0:T(8,128)(2,1)S(1)}, u32[]{:S(2)}, u32[]{:S(2)}) collective-permute-start(bf16[6,16,256]{2,1,0:T(8,128)(2,1)S(1)} %get-tuple-element.21), channel_id=1, source_target_pairs={{0,16},{8,24},{16,0},{24,8},{1,17},{9,25},{17,1},{25,9},{2,18},{10... | collective-permute-start | bytes 147464 | tf_op jit(solution)/shard_map/ppermute | solution.py:20
  42.5 15.1 %collective-permute-start.30 = (bf16[4,2,64,512]{3,2,1,0:T(8,128)(2,1)S(1)}, bf16[4,2,64,512]{3,2,1,0:T(8,128)(2,1)S(1)}, u32[]{:S(2)}, u32[]{:S(2)}) collective-permute-start(bf16[4,2,64,512]{3,2,1,0:T(8,128)(2,1)S(1)} %pad_maximum_fusion.1.refs_12_), channel_id=1, source_target_pairs={{0,1},{1,0},{2,3},{3,2},{4,5},{5,4},{6,7},{7,6},{8,9},{9,8},{10,11... | collective-permute-start | bytes 1572872 | tf_op jit(solution)/shard_map/ppermute | solution.py:308
  47.4 4.1 %collective-permute-start.12 = (bf16[6,16,256]{2,1,0:T(8,128)(2,1)S(1)}, bf16[6,16,256]{2,1,0:T(8,128)(2,1)S(1)}, u32[]{:S(2)}, u32[]{:S(2)}) collective-permute-start(bf16[6,16,256]{2,1,0:T(8,128)(2,1)S(1)} %fusion.5), channel_id=1, source_target_pairs={{0,24},{8,0},{16,8},{24,16},{1,25},{9,1},{17,9},{25,17},{2,26},{10... | collective-permute-start | bytes 147464 | tf_op jit(solution)/shard_map/ppermute | solution.py:20
  49.2 6.3 %collective-permute-start.11 = (bf16[6,16,256]{2,1,0:T(8,128)(2,1)S(1)}, bf16[6,16,256]{2,1,0:T(8,128)(2,1)S(1)}, u32[]{:S(2)}, u32[]{:S(2)}) collective-permute-start(bf16[6,16,256]{2,1,0:T(8,128)(2,1)S(1)} %fusion.5), channel_id=1, source_target_pairs={{0,16},{8,24},{16,0},{24,8},{1,17},{9,25},{17,1},{25,9},{2,18},{10... | collective-permute-start | bytes 147464 | tf_op jit(solution)/shard_map/ppermute | solution.py:20
  49.2 6.3 %collective-permute-start.10 = (bf16[6,16,256]{2,1,0:T(8,128)(2,1)S(1)}, bf16[6,16,256]{2,1,0:T(8,128)(2,1)S(1)}, u32[]{:S(2)}, u32[]{:S(2)}) collective-permute-start(bf16[6,16,256]{2,1,0:T(8,128)(2,1)S(1)} %fusion.5), channel_id=1, source_target_pairs={{0,8},{8,16},{16,24},{24,0},{1,9},{9,17},{17,25},{25,1},{2,10},{10... | collective-permute-start | bytes 147464 | tf_op jit(solution)/shard_map/ppermute | solution.py:20
  51.5 12.5 %collective-permute-start.29 = (bf16[4,2,64,512]{3,2,1,0:T(8,128)(2,1)S(1)}, bf16[4,2,64,512]{3,2,1,0:T(8,128)(2,1)S(1)}, u32[]{:S(2)}, u32[]{:S(2)}) collective-permute-start(bf16[4,2,64,512]{3,2,1,0:T(8,128)(2,1)S(1)} %pad_maximum_fusion.1.refs_12_), channel_id=1, source_target_pairs={{0,2},{1,3},{2,0},{3,1},{4,6},{5,7},{6,4},{7,5},{8,10},{9,11},{10,... | collective-permute-start | bytes 1572872 | tf_op jit(solution)/shard_map/ppermute | solution.py:308
  55.5 8.6 %collective-permute-start.22 = (bf16[4,2,64,512]{3,2,1,0:T(8,128)(2,1)S(1)}, bf16[4,2,64,512]{3,2,1,0:T(8,128)(2,1)S(1)}, u32[]{:S(2)}, u32[]{:S(2)}) collective-permute-start(bf16[4,2,64,512]{3,2,1,0:T(8,128)(2,1)S(1)} %pad_maximum_fusion.refs_4_), channel_id=1, source_target_pairs={{0,1},{1,0},{2,3},{3,2},{4,5},{5,4},{6,7},{7,6},{8,9},{9,8},{10,11... | collective-permute-start | bytes 1572872 | tf_op jit(solution)/shard_map/ppermute | solution.py:308
  55.5 14.8 %collective-permute-start.19 = (bf16[4,2,64,512]{3,2,1,0:T(8,128)(2,1)S(1)}, bf16[4,2,64,512]{3,2,1,0:T(8,128)(2,1)}, u32[]{:S(2)}, u32[]{:S(2)}) collective-permute-start(bf16[4,2,64,512]{3,2,1,0:T(8,128)(2,1)S(1)} %pad_maximum_fusion.refs_4_), channel_id=1, source_target_pairs={{0,4},{4,0},{1,5},{5,1},{2,6},{6,2},{3,7},{7,3},{8,12},{12,8},{9,1... | collective-permute-start | bytes 1572872 | tf_op jit(solution)/shard_map/ppermute | solution.py:20
  56.0 25.1 %collective-permute-start.21 = (bf16[4,2,64,512]{3,2,1,0:T(8,128)(2,1)S(1)}, bf16[4,2,64,512]{3,2,1,0:T(8,128)(2,1)}, u32[]{:S(2)}, u32[]{:S(2)}) collective-permute-start(bf16[4,2,64,512]{3,2,1,0:T(8,128)(2,1)S(1)} %collective-permute-done.20.refs_6_), channel_id=1, source_target_pairs={{0,4},{4,0},{1,5},{5,1},{2,6},{6,2},{3,7},{7,3},{8,12},{12,8},{9,1... | collective-permute-start | bytes 1572872 | tf_op jit(solution)/shard_map/ppermute | solution.py:20
  57.6 23.6 %collective-permute-start.15 = (bf16[4,6,16,256]{3,2,1,0:T(8,128)(2,1)S(1)}, bf16[4,6,16,256]{3,2,1,0:T(8,128)(2,1)S(1)}, u32[]{:S(2)}, u32[]{:S(2)}) collective-permute-start(bf16[4,6,16,256]{3,2,1,0:T(8,128)(2,1)S(1)} %pad_maximum_fusion.2.refs_0_), channel_id=1, source_target_pairs={{0,3},{1,0},{2,1},{3,2},{4,7},{5,4},{6,5},{7,6},{8,11},{9,8},{10,9... | collective-permute-start | bytes 589832 | tf_op jit(solution)/shard_map/ppermute | solution.py:20
  64.1 30.3 %collective-permute-start.24 = (bf16[4,2,64,512]{3,2,1,0:T(8,128)(2,1)S(1)}, bf16[4,2,64,512]{3,2,1,0:T(8,128)(2,1)}, u32[]{:S(2)}, u32[]{:S(2)}) collective-permute-start(bf16[4,2,64,512]{3,2,1,0:T(8,128)(2,1)S(1)} %collective-permute-done.20.refs_6_), channel_id=1, source_target_pairs={{0,1},{1,0},{2,3},{3,2},{4,5},{5,4},{6,7},{7,6},{8,9},{9,8},{10,11... | collective-permute-start | bytes 1572872 | tf_op jit(solution)/shard_map/ppermute | solution.py:308
  64.1 30.3 %collective-permute-start.31 = (bf16[4,2,64,512]{3,2,1,0:T(8,128)(2,1)S(1)}, bf16[4,2,64,512]{3,2,1,0:T(8,128)(2,1)}, u32[]{:S(2)}, u32[]{:S(2)}) collective-permute-start(bf16[4,2,64,512]{3,2,1,0:T(8,128)(2,1)S(1)} %collective-permute-done.29.refs_13_), channel_id=1, source_target_pairs={{0,1},{1,0},{2,3},{3,2},{4,5},{5,4},{6,7},{7,6},{8,9},{9,8},{10,11... | collective-permute-start | bytes 1572872 | tf_op jit(solution)/shard_map/ppermute | solution.py:308
  70.3 24.1 %collective-permute-start.23 = (bf16[4,2,64,512]{3,2,1,0:T(8,128)(2,1)}, bf16[4,2,64,512]{3,2,1,0:T(8,128)(2,1)}, u32[]{:S(2)}, u32[]{:S(2)}) collective-permute-start(bf16[4,2,64,512]{3,2,1,0:T(8,128)(2,1)} %collective-permute-done.19.refs_5_), channel_id=1, source_target_pairs={{0,1},{1,0},{2,3},{3,2},{4,5},{5,4},{6,7},{7,6},{8,9},{9,8},{10,11... | collective-permute-start | bytes 1572872 | tf_op jit(solution)/shard_map/ppermute | solution.py:308
  81.2 13.2 %collective-permute-start.25 = (bf16[4,2,64,512]{3,2,1,0:T(8,128)(2,1)}, bf16[4,2,64,512]{3,2,1,0:T(8,128)(2,1)}, u32[]{:S(2)}, u32[]{:S(2)}) collective-permute-start(bf16[4,2,64,512]{3,2,1,0:T(8,128)(2,1)} %collective-permute-done.21.refs_7_), channel_id=1, source_target_pairs={{0,1},{1,0},{2,3},{3,2},{4,5},{5,4},{6,7},{7,6},{8,9},{9,8},{10,11... | collective-permute-start | bytes 1572872 | tf_op jit(solution)/shard_map/ppermute | solution.py:308
  81.2 7.3 %collective-permute-start.14 = (bf16[4,6,16,256]{3,2,1,0:T(8,128)(2,1)S(1)}, bf16[4,6,16,256]{3,2,1,0:T(8,128)(2,1)S(1)}, u32[]{:S(2)}, u32[]{:S(2)}) collective-permute-start(bf16[4,6,16,256]{3,2,1,0:T(8,128)(2,1)S(1)} %pad_maximum_fusion.2.refs_0_), channel_id=1, source_target_pairs={{0,2},{1,3},{2,0},{3,1},{4,6},{5,7},{6,4},{7,5},{8,10},{9,11},{10,... | collective-permute-start | bytes 589832 | tf_op jit(solution)/shard_map/ppermute | solution.py:20
  89.2 5.2 %collective-permute-start.13 = (bf16[4,6,16,256]{3,2,1,0:T(8,128)(2,1)S(1)}, bf16[4,6,16,256]{3,2,1,0:T(8,128)(2,1)}, u32[]{:S(2)}, u32[]{:S(2)}) collective-permute-start(bf16[4,6,16,256]{3,2,1,0:T(8,128)(2,1)S(1)} %pad_maximum_fusion.2.refs_0_), channel_id=1, source_target_pairs={{0,1},{1,2},{2,3},{3,0},{4,5},{5,6},{6,7},{7,4},{8,9},{9,10},{10,1... | collective-permute-start | bytes 589832 | tf_op jit(solution)/shard_map/ppermute | solution.py:20
  (6 other events, 147.0 us)

commit v3 on v2

--- a/solution.py
+++ b/solution.py
@@ -132,6 +132,7 @@
 
 
 def correlate_kernel(scale, vec_ref, face0, face1, face2, mat0, mat1, mat2, out_ref):
+    gz_n, gx_n, _, own_rows, _ = out_ref.shape
     vec = vec_ref[...]
     rows = vec.shape[0]
     half = rows // 2
@@ -152,82 +153,90 @@
             vec, right, (((0,), (0,)), ((), ())), preferred_element_type=F32
         )
         product = (product * scale).astype(BF16)
-        out_ref[2 * e] = product[:, :width]
-        out_ref[2 * e + 1] = product[:, width:]
-
-
-def chain_kernel(
-    inverse, plan, me_ref, dirs_ref, spin_ref, chain_ref, *refs
-):
-    elem_count, fwd_keys, bwd_keys = plan
-    elem_in, refs = refs[:elem_count], refs[elem_count:]
+        for g in range(gx_n):
+            for z in range(gz_n):
+                at = (g * gz_n + z) * own_rows
+                out_ref[z, g, 2 * e] = product[at : at + own_rows, :width]
+                out_ref[z, g, 2 * e + 1] = product[at : at + own_rows, width:]
+
+
+def chain_kernel(inverse, plan, me_ref, dirs_ref, spin_ref, chain_ref, *refs):
+    line, elem_keys, fwd_keys, bwd_keys = plan
+    elem_in, refs = refs[: len(elem_keys)], refs[len(elem_keys) :]
     fwd_in, refs = refs[: len(fwd_keys)], refs[len(fwd_keys) :]
     bwd_in, refs = refs[: len(bwd_keys)], refs[len(bwd_keys) :]
-    out_ref, elem_all, fwd_ref, bwd_ref, x_ref, p_ref, q_ref, b_ref, sems = refs
+    out_ref, elem_all, elem_ref, x_ref, p_ref, q_ref, b_ref = refs
     _, gx_n, gz_n, own_rows, num_vecs = elem_all.shape
-    gy_n = fwd_ref.shape[1]
-    width = fwd_ref.shape[-1]
+    width = out_ref.shape[3]
     op_count = out_ref.shape[0]
     row_count = out_ref.shape[2]
     vec_rows = row_count // 4
-    spin_pieces = gz_n // 4
+    gy_n = 4 * num_vecs // width
     lane = width // 4
+    halves = gz_n // 4
     gx, gy, gz = me_ref[0], me_ref[1], me_ref[2]
 
     def back(at, step, count):
         return lax.rem(at - step + count, count)
 
     def gz_from(dy, dc):
-        return back(gz // 2, dy, gz_n // 2) * 2 + back(lax.rem(gz, 2), dc, 2)
-
-    copies = []
-
-    def place(source, target):
-        copy = pltpu.make_async_copy(source, target, sems.at[len(copies)])
-        copy.start()
-        copies.append(copy)
-
-    for n, ref in enumerate(elem_in):
+        return back(lax.div(gz, 2), dy, gz_n // 2) * 2 + back(lax.rem(gz, 2), dc, 2)
+
+    for (dy, dc), ref in zip(elem_keys, elem_in):
         for step in range(gx_n):
-            place(ref.at[step], elem_all.at[:, back(gx, step, gx_n), back(gz, n, gz_n)])
-    for (dx, dy, dc), ref in zip(fwd_keys, fwd_in):
-        for step in range(gx_n):
-            place(ref.at[step], fwd_ref.at[back(gx, step, gx_n), back(gy, dx, gy_n), gz_from(dy, dc)])
-    for (dy, dc), ref in zip(bwd_keys, bwd_in):
-        for step in range(gx_n):
-            place(ref.at[step], bwd_ref.at[back(gx, step, gx_n), gz_from(dy, dc)])
-    for copy in copies:
-        copy.wait()
-
-    def elem(d, c):
-        return elem_all[2 * d + c].reshape(num_vecs, num_vecs)
+            elem_all[:, back(gx, step, gx_n), gz_from(dy, dc)] = ref[step]
+    column = lax.broadcasted_iota(jnp.int32, (1, num_vecs), 1)
+    source = jnp.zeros_like(column)
+    half_rows = vec_rows // halves
+    for place, offset in enumerate(line):
+        for half in range(halves):
+            at = place * vec_rows + half * half_rows
+            from_half = lax.bitwise_xor(lax.rem(gz, 2), half) if halves == 2 else half
+            begin = lax.bitwise_xor(gx, offset) * vec_rows + from_half * half_rows
+            inside = (column >= at) & (column < at + half_rows)
+            source = jnp.where(inside, column + (begin - at), source)
+    perm = chosen(lax.broadcasted_iota(jnp.int32, (num_vecs, num_vecs), 0) == source).astype(BF16)
+    for n in range(6):
+        elem_ref[n] = mm(elem_all[n].reshape(num_vecs, num_vecs), perm).astype(BF16)
+
+    if halves == 1:
+        groups = [[key] for key in bwd_keys]
+    else:
+        groups = [[(dy, dc) for dc in range(2)] for dy in range(gz_n // 2)]
+    spins = [lax.div(gz_from(*group[0]), halves) for group in groups]
+
+    def rows_of(parts, c):
+        return jnp.concatenate([part[:, c] for part in parts], axis=1).reshape(num_vecs, width)
+
+    first_row = pl.multiple_of(gx * vec_rows, vec_rows)
 
     def own(d, c):
-        return elem_all[2 * d + c, gx].reshape(vec_rows, num_vecs)
+        return elem_ref[2 * d + c, pl.ds(first_row, vec_rows), :]
 
     real_rows = [jnp.concatenate([own(d, 0), -own(d, 1)], axis=1) for d in range(3)]
     imag_rows = [jnp.concatenate([own(d, 1), own(d, 0)], axis=1) for d in range(3)]
     left = jnp.concatenate([part for d in range(3) for part in (real_rows[d], imag_rows[d])], axis=0)
-    for t in range(4):
-        planes = slice(t * spin_pieces, (t + 1) * spin_pieces)
-        for block in range(gy_n):
-            right = jnp.concatenate(
-                [fwd_ref[:, block, planes, c].reshape(num_vecs, width) for c in range(2)], axis=0
-            )
+    fwd_at = dict(zip(fwd_keys, fwd_in))
+    bwd_at = dict(zip(bwd_keys, bwd_in))
+    for t, group in enumerate(groups):
+        for dx in range(gy_n):
+            parts = [fwd_at[(dx,) + key] for key in group]
+            right = jnp.concatenate([rows_of(parts, c) for c in range(2)], axis=0)
             result = mm(left, right).astype(BF16)
             for d in range(3):
                 for c in range(2):
                     at = (d * 2 + c) * vec_rows
-                    x_ref[d, c, t, :, block * width : (block + 1) * width] = result[at : at + vec_rows]
+                    x_ref[d, c, dx, t] = result[at : at + vec_rows]
         for c in range(2):
             at = (t * 2 + c) * num_vecs
-            b_ref[at : at + num_vecs, :] = bwd_ref[:, planes, c].reshape(num_vecs, width)
+            b_ref[at : at + num_vecs, :] = rows_of([bwd_at[key] for key in group], c)
 
     row = lax.broadcasted_iota(jnp.int32, (row_count, row_count), 0)
     column = lax.broadcasted_iota(jnp.int32, (row_count, row_count), 1)
     row_spin = lax.rem(row, 4)
     diagonal = lax.div(row, 4) == lax.rem(column, vec_rows)
     column_spin = lax.div(column, vec_rows)
+    blocks = [pl.multiple_of(back(gy, dx, gy_n) * lane, lane) for dx in range(gy_n)]
 
     def one_operator(op, carry):
         a = chain_ref[op, 0]
@@ -238,20 +247,23 @@
         for t in range(4):
             in_t = column_spin == t
             for s in range(4):
-                mix = jnp.where(in_t & (row_spin == s), spin_ref[a, s, t], mix)
+                mix = jnp.where(in_t & (row_spin == s), spin_ref[a, s, spins[t]], mix)
         mix = jnp.where(diagonal, mix, 0.0)
         high = mix.astype(BF16)
         low = (mix - high.astype(F32)).astype(BF16)
         mix = jnp.concatenate([high, low], axis=1)
         for c in range(2):
-            source = x_ref[dir_a, c].reshape(row_count, 4 * num_vecs)
-            result = mm(mix, jnp.concatenate([source, source], axis=0)).astype(BF16)
-            for s in range(4):
-                for block in range(gy_n):
-                    at = block * width + s * lane
-                    to = c * num_vecs + block * lane
-                    p_ref[s, :, to : to + lane] = result[:, at : at + lane]
-        real_b, imag_b = elem(dir_b, 0), elem(dir_b, 1)
+            for dx in range(gy_n):
+                source = x_ref[dir_a, c, dx].reshape(row_count, width)
+                result = mm(mix, jnp.concatenate([source, source], axis=0)).astype(BF16)
+                for s in range(4):
+                    to = c * num_vecs + dx * lane
+                    p_ref[s, :, to : to + lane] = result[:, s * lane : (s + 1) * lane]
+
+        def elem(c):
+            return jnp.concatenate([elem_ref[2 * dir_b + c, pl.ds(at, lane), :] for at in blocks], axis=0)
+
+        real_b, imag_b = elem(0), elem(1)
         right = jnp.concatenate(
             [
                 jnp.concatenate([real_b, imag_b], axis=1),
@@ -261,9 +273,9 @@
         )
         parts = [mm(p_ref[s], right) for s in range(4)]
         for t in range(4):
-            total = parts[0] * (spin_ref[b, 0, t] * inverse)
+            total = parts[0] * (spin_ref[b, 0, spins[t]] * inverse)
             for s in range(1, 4):
-                total += parts[s] * (spin_ref[b, s, t] * inverse)
+                total += parts[s] * (spin_ref[b, s, spins[t]] * inverse)
             total = total.astype(BF16)
             real, imag = total[:, :num_vecs], total[:, num_vecs:]
             at = 2 * t * num_vecs
@@ -279,28 +291,6 @@
     lax.fori_loop(0, op_count, one_operator, 0)
 
 
-def summed_over(value, axis):
-    total = value.astype(F32)
-    for step in range(1, lax.axis_size(axis)):
-        total += passed_along(value, axis, step).astype(F32)
-    return total
-
-
-def scattered_over(value, axis):
-    count = lax.axis_size(axis)
-    me = lax.axis_index(axis)
-    total = lax.dynamic_index_in_dim(value, me, 0, keepdims=False).astype(F32)
-    for step in range(1, count):
-        part = lax.dynamic_index_in_dim(value, lax.rem(me + step, count), 0, keepdims=False)
-        total += passed_along(part, axis, step).astype(F32)
-    return total
-
-
-def gathered_over(value, axis):
-    count = lax.axis_size(axis)
-    return jnp.stack([value] + [passed_along(value, axis, step) for step in range(1, count)])
-
-
 def passed_in_gz(value, dy, dc):
     count = lax.axis_size("gz")
     chips = count // 2
@@ -308,12 +298,35 @@
     return lax.ppermute(value, "gz", pairs)
 
 
+def line_exchange(value, axis):
+    count = lax.axis_size(axis)
+    gathered = value[None]
+    offsets = [0]
+    distance = count // 2
+    while distance:
+        pairs = [(n, n ^ distance) for n in range(count)]
+        gathered = jnp.concatenate([gathered, lax.ppermute(gathered, axis, pairs)])
+        offsets += [offset ^ distance for offset in offsets]
+        distance //= 2
+    return gathered, tuple(offsets)
+
+
+def part_at(value, index, axis=0):
+    return lax.dynamic_index_in_dim(value, index, axis, keepdims=False)
+
+
+def added(*values):
+    return sum(value.astype(F32) for value in values).astype(BF16)
+
+
 def on_device(eigvecs, links, directions, spin_mats, forward_peram, backward_peram, chain_order):
     extent = eigvecs.shape[:3]
     num_vecs = eigvecs.shape[-1]
     gx_n, gy_n, gz_n = (lax.axis_size(name) for name in ("gx", "gy", "gz"))
     chips = gz_n // 2
-    me = jnp.stack([lax.axis_index(name) for name in ("gx", "gy", "gz")]).astype(jnp.int32)
+    gx, gy, gz = (lax.axis_index(name).astype(jnp.int32) for name in ("gx", "gy", "gz"))
+    me = jnp.stack([gx, gy, gz])
+    chip, core = lax.div(gz, 2), lax.rem(gz, 2)
 
     ordered = eigvecs.transpose(3, 0, 1, 2, 4, 5)
     faces = []
@@ -334,8 +347,9 @@
         name="pieces",
     )(me[2:], forward_peram, backward_peram)
 
-    fwd_line = gathered_over(fwd_piece, "gx")
-    bwd_line = gathered_over(bwd_piece, "gx")
+    bwd_piece, link_rows = lax.optimization_barrier((bwd_piece, links.reshape(-1, 54)))
+    fwd_line, line = line_exchange(fwd_piece, "gx")
+    bwd_line, _ = line_exchange(bwd_piece, "gx")
     fwd_parts, bwd_parts = {}, {}
     for dy in range(chips):
         mine = passed_in_gz(fwd_line, dy, 0) if dy else fwd_line
@@ -358,45 +372,48 @@
         out_specs=[VMEM] * 3,
         compiler_params=pltpu.CompilerParams(vmem_limit_bytes=24 * 2**20),
         name="link_matrices",
-    )(links.reshape(-1, 54))
+    )(link_rows)
 
     volume = math.prod(extent) * gx_n * gy_n * gz_n
+    own_rows = num_vecs // (gz_n * gx_n)
     partial = pl.pallas_call(
         functools.partial(correlate_kernel, 1.0 / math.sqrt(12.0 * volume)),
-        out_shape=jax.ShapeDtypeStruct((6, num_vecs, num_vecs), BF16),
+        out_shape=jax.ShapeDtypeStruct((gz_n, gx_n, 6, own_rows, num_vecs), BF16),
         in_specs=[VMEM] * 7,
         out_specs=VMEM,
         compiler_params=pltpu.CompilerParams(vmem_limit_bytes=24 * 2**20),
         name="correlate",
     )(vec, *faces, *link_mats)
 
-    own_rows = num_vecs // (gz_n * gx_n)
-    parts = partial.reshape(6, gx_n, gz_n, own_rows, num_vecs).transpose(2, 1, 0, 3, 4)
-    summed = scattered_over(parts, "gz").astype(BF16)
-    summed = summed_over(summed, "gy").astype(BF16)
-    summed = scattered_over(summed, "gx").astype(BF16)
-    elem_line = gathered_over(summed, "gx")
-    elem_parts = [elem_line] + [passed_along(elem_line, "gz", step) for step in range(1, gz_n)]
+    by_core = partial.reshape((chips, 2) + partial.shape[1:])
+    summed = added(part_at(by_core, core, 1), passed_in_gz(part_at(by_core, 1 - core, 1), 0, 1))
+    arrived = [passed_in_gz(part_at(summed, lax.rem(chip + dy, chips)), dy, 0) for dy in range(1, chips)]
+    summed = added(part_at(summed, chip), *arrived)
+    summed = added(summed, *[passed_along(summed, "gy", dx) for dx in range(1, gy_n)])
+    arrived = [passed_along(part_at(summed, lax.rem(gx + dz, gx_n)), "gx", dz) for dz in range(1, gx_n)]
+    summed = added(part_at(summed, gx), *arrived)
+    elem_line = jnp.stack([summed] + [passed_along(summed, "gx", dz) for dz in range(1, gx_n)])
+    elem_parts = {(dy, 0): passed_in_gz(elem_line, dy, 0) if dy else elem_line for dy in range(chips)}
+    for dy in range(chips):
+        elem_parts[dy, 1] = passed_in_gz(elem_parts[dy, 0], 0, 1)
 
     op_count = chain_order.shape[0]
-    plan = (len(elem_parts), tuple(fwd_parts), tuple(bwd_parts))
-    operands = [*elem_parts, *fwd_parts.values(), *bwd_parts.values()]
+    plan = (line, tuple(elem_parts), tuple(fwd_parts), tuple(bwd_parts))
+    operands = [*elem_parts.values(), *fwd_parts.values(), *bwd_parts.values()]
     return pl.pallas_call(
         functools.partial(chain_kernel, 1.0 / math.sqrt(4 * num_vecs), plan),
         out_shape=jax.ShapeDtypeStruct((op_count, 2, rows, cols), BF16),
-        in_specs=[SMEM] * 4 + [pl.BlockSpec(memory_space=pl.ANY)] * len(operands),
+        in_specs=[SMEM] * 4 + [VMEM] * len(operands),
         out_specs=VMEM,
         scratch_shapes=[
             pltpu.VMEM((6, gx_n, gz_n, own_rows, num_vecs), BF16),
-            pltpu.VMEM((gx_n, gy_n, gz_n, 2, piece, cols), BF16),
-            pltpu.VMEM((gx_n, gz_n, 2, piece, cols), BF16),
-            pltpu.VMEM((3, 2, 4, rows // 4, 4 * num_vecs), BF16),
+            pltpu.VMEM((6, num_vecs, num_vecs), BF16),
+            pltpu.VMEM((3, 2, gy_n, 4, rows // 4, cols), BF16),
             pltpu.VMEM((4, rows, 2 * num_vecs), BF16),
             pltpu.VMEM((2 * rows, 8 * num_vecs), BF16),
             pltpu.VMEM((8 * num_vecs, cols), BF16),
-            pltpu.SemaphoreType.DMA((gx_n * len(operands),)),
         ],
-        compiler_params=pltpu.CompilerParams(vmem_limit_bytes=40 * 2**20),
+        compiler_params=pltpu.CompilerParams(vmem_limit_bytes=32 * 2**20),
         name="chain",
     )(me, directions, spin_mats, chain_order, *operands)
 

time: 118 us -> 96.6 us (0.82)
  waiting for transfers between devices: 61.2 us -> 47.3 us
  Pallas kernels: 24.4 us -> 19.3 us
  local copies, waits for them, and re-layouts: 7.31 us -> 5.72 us
    ppermute x24 -> x12, waiting for transfers between devices: 54.9 us -> 24 us  [passed_along(): return lax.ppermute(value, axis, pairs)]
    ppermute x0 -> x4, waiting for transfers between devices: none -> 13.5 us  [line_exchange(): gathered = jnp.concatenate([gathered, lax.ppermute(gathered, axis, pairs)])]
    ppermute x24 -> x12, starting transfers between devices: 20.6 us -> 14.3 us  [passed_along(): return lax.ppermute(value, axis, pairs)]
    pallas_call x1, Pallas kernels: 21.8 us -> 16.7 us  [on_device(): pl.pallas_call(functools.partial(chain_kernel, 1.0 / math.sqrt(4 * num_ve...]
    ppermute x8 -> x13, waiting for transfers between devices: 6.26 us -> 9.79 us  [passed_in_gz(): return lax.ppermute(value, 'gz', pairs)]
    ppermute x8 -> x13, starting transfers between devices: 2.89 us -> 6.05 us  [passed_in_gz(): return lax.ppermute(value, 'gz', pairs)]
    ppermute x0 -> x4, starting transfers between devices: none -> 2.79 us  [line_exchange(): gathered = jnp.concatenate([gathered, lax.ppermute(gathered, axis, pairs)])]
    unnamed x17 -> x10, local copies, waits for them, and re-layouts: 3.43 us -> 1.78 us
  transfers between devices with their start and end apart: 32 -> 29, of which waited for: 15 -> 13; matrix products, arithmetic and copies ran while one was open for 4% -> 5% of each run, Pallas kernels for 1% -> 1%
where the time goes in v3:
time: 96.6 us; the launch traced here: 96.2 us
  waiting for transfers between devices  47.3 us (49%)
  starting transfers between devices  23.1 us (24%)
  Pallas kernels  19.3 us (20%)
  local copies, waits for them, and re-layouts  5.72 us (6%)
    ppermute x12, waiting for transfers between devices, passed_along(): return lax.ppermute(value, axis, pairs)  24 us
    pallas_call x1, Pallas kernels, on_device(): pl.pallas_call(functools.partial(chain_kernel, 1.0 / math.sqrt(4 * num_ve...  16.7 us
    ppermute x12, starting transfers between devices, passed_along(): return lax.ppermute(value, axis, pairs)  14.3 us
    ppermute x4, waiting for transfers between devices, line_exchange(): gathered = jnp.concatenate([gathered, lax.ppermute(gathered, axis, pairs)])  13.5 us
    ppermute x13, waiting for transfers between devices, passed_in_gz(): return lax.ppermute(value, 'gz', pairs)  9.79 us
    ppermute x13, starting transfers between devices, passed_in_gz(): return lax.ppermute(value, 'gz', pairs)  6.05 us
    ppermute x4, starting transfers between devices, line_exchange(): gathered = jnp.concatenate([gathered, lax.ppermute(gathered, axis, pairs)])  2.79 us
    slice x6, local copies, waits for them, and re-layouts, on_device(): face = lax.slice_in_dim(ordered, 0, 1, axis=1 + e).reshape(-1, num_vecs)  2.49 us
  transfers between devices with their start and end apart: 29, of which 13 were waited for; matrix products, arithmetic and copies ran while one was open for 5% of the time, Pallas kernels for 1%

profile of v3, /device:TPU:0, one launch (start us, length us, event | category | flops | bytes accessed | tf_op | source)
XLA Modules:
  0.0 96.2 jit_solution(11822519237828131022)
XLA Ops:
  0.0 0.9 slice.12
  1.0 5.1 %collective-permute-start = (bf16[96,256]{1,0:T(8,128)(2,1)S(1)}, bf16[96,256]{1,0:T(8,128)(2,1)S(1)}, u32[]{:S(2)}, u32[]{:S(2)}) collective-permute-start(bf16[96,256]{1,0:T(8,128)(2,1)S(1)} %reshape.25), channel_id=1, source_target_pairs={{0,24},{8,0},{16,8},{24,16},{1,25},{9,1},{17,9},{25,17},{2,26},{10... | collective-permute-start | bytes 147464 | tf_op jit(solution)/shard_map/ppermute | solution.py:20
  6.1 0.8 slice.13
  6.9 1.6 %collective-permute-start.1 = (bf16[48,256]{1,0:T(8,128)(2,1)S(1)}, bf16[48,256]{1,0:T(8,128)(2,1)S(1)}, u32[]{:S(2)}, u32[]{:S(2)}) collective-permute-start(bf16[48,256]{1,0:T(8,128)(2,1)S(1)} %reshape.26), channel_id=1, source_target_pairs={{0,4},{4,0},{1,5},{5,1},{2,6},{6,2},{3,7},{7,3},{8,12},{12,8},{9,1... | collective-permute-start | bytes 73736 | tf_op jit(solution)/shard_map/ppermute | solution.py:20
  8.5 0.8 slice.14
  9.8 0.9 copy.14
  10.8 1.0 %copy.18 = f32[2,4,4,3,2,3,3]{2,1,0,6,5,4,3:T(4,128)S(1)} copy(f32[2,4,4,3,2,3,3]{2,4,6,5,3,1,0:T(2,128)} %param.8) | data formatting | bytes 13824 | tf_op args[1]
  13.4 1.4 %correlate.1 = bf16[4,4,6,16,256]{4,3,2,1,0:T(8,128)(2,1)S(1)} custom-call(bf16[192,256]{1,0:T(8,128)(2,1)S(1)} %reshape.24.vec_ref, bf16[96,256]{1,0:T(8,128)(2,1)S(1)} %collective-permute-done.face0, bf16[48,256]{1,0:T(8,128)(2,1)S(1)} %collective-permute-done.1.face1, bf16[48,256]{1,0:T(8,128)(2,1)S(1)} %collective-permute-done.2.face2, ...), custom_call_target="tpu_custom_call" | custom-call | tf_op jit(solution)/shard_map/correlate/pallas_call | solution.py:379
  14.9 1.6 %collective-permute-done.3 = bf16[2,4,6,16,256]{4,3,2,1,0:T(8,128)(2,1)S(1)} collective-permute-done((bf16[2,4,6,16,256]{4,3,2,1,0:T(8,128)(2,1)S(1)}, bf16[2,4,6,16,256]{4,3,2,1,0:T(8,128)(2,1)S(1)}, u32[]{:S(2)}, u32[]{:S(2)}) %collective-permute-start.3) | collective-permute-done | bytes 393248 | tf_op jit(solution)/shard_map/ppermute | solution.py:298
  16.7 1.3 %collective-permute-start.4 = (bf16[4,6,16,256]{3,2,1,0:T(8,128)(2,1)S(1)}, bf16[4,6,16,256]{3,2,1,0:T(8,128)(2,1)S(1)}, u32[]{:S(2)}, u32[]{:S(2)}) collective-permute-start(bf16[4,6,16,256]{3,2,1,0:T(8,128)(2,1)S(1)} %dynamic-slice_bitcast_fusion.1), channel_id=1, source_target_pairs={{0,2},{1,3},{2,0},{3,1},{4,6},{5,7},{6,4},{7,5},{8,10},{9,11},{10,... | collective-permute-start | bytes 589832 | tf_op jit(solution)/shard_map/ppermute | solution.py:298
  18.0 4.3 %collective-permute-done.15 = bf16[1,2,64,512]{3,2,1,0:T(8,128)(2,1)S(1)} collective-permute-done((bf16[1,2,64,512]{3,2,1,0:T(8,128)(2,1)S(1)}, bf16[1,2,64,512]{3,2,1,0:T(8,128)(2,1)S(1)}, u32[]{:S(2)}, u32[]{:S(2)}) %collective-permute-start.15) | collective-permute-done | bytes 131104 | tf_op jit(solution)/shard_map/ppermute | solution.py:308
  22.4 1.3 %collective-permute-done.4 = bf16[4,6,16,256]{3,2,1,0:T(8,128)(2,1)S(1)} collective-permute-done((bf16[4,6,16,256]{3,2,1,0:T(8,128)(2,1)S(1)}, bf16[4,6,16,256]{3,2,1,0:T(8,128)(2,1)S(1)}, u32[]{:S(2)}, u32[]{:S(2)}) %collective-permute-start.4) | collective-permute-done | bytes 196640 | tf_op jit(solution)/shard_map/ppermute | solution.py:298
  24.4 1.9 %collective-permute-start.24 = (bf16[1,2,64,512]{3,2,1,0:T(8,128)(2,1)S(1)}, bf16[1,2,64,512]{3,2,1,0:T(8,128)(2,1)S(1)}, u32[]{:S(2)}, u32[]{:S(2)}) collective-permute-start(bf16[1,2,64,512]{3,2,1,0:T(8,128)(2,1)S(1)} %bitcast.42), channel_id=1, source_target_pairs={{0,16},{8,24},{16,0},{24,8},{1,17},{9,25},{17,1},{25,9},{2,18},{10... | collective-permute-start | bytes 393224 | tf_op jit(solution)/shard_map/ppermute | solution.py:308
  26.3 7.2 %collective-permute-done.16 = bf16[2,2,64,512]{3,2,1,0:T(8,128)(2,1)S(1)} collective-permute-done((bf16[2,2,64,512]{3,2,1,0:T(8,128)(2,1)S(1)}, bf16[2,2,64,512]{3,2,1,0:T(8,128)(2,1)S(1)}, u32[]{:S(2)}, u32[]{:S(2)}) %collective-permute-start.16) | collective-permute-done | bytes 262176 | tf_op jit(solution)/shard_map/ppermute | solution.py:308
  33.6 1.1 %collective-permute-start.18 = (bf16[4,2,64,512]{3,2,1,0:T(8,128)(2,1)S(1)}, bf16[4,2,64,512]{3,2,1,0:T(8,128)(2,1)S(1)}, u32[]{:S(2)}, u32[]{:S(2)}) collective-permute-start(bf16[4,2,64,512]{3,2,1,0:T(8,128)(2,1)S(1)} %pad_maximum_fusion.refs_4_), channel_id=1, source_target_pairs={{0,2},{1,3},{2,0},{3,1},{4,6},{5,7},{6,4},{7,5},{8,10},{9,11},{10,... | collective-permute-start | bytes 1572872 | tf_op jit(solution)/shard_map/ppermute | solution.py:298
  34.8 3.8 %collective-permute-start.8 = (bf16[6,16,256]{2,1,0:T(8,128)(2,1)S(1)}, bf16[6,16,256]{2,1,0:T(8,128)(2,1)S(1)}, u32[]{:S(2)}, u32[]{:S(2)}) collective-permute-start(bf16[6,16,256]{2,1,0:T(8,128)(2,1)S(1)} %get-tuple-element.20), channel_id=1, source_target_pairs={{0,24},{8,0},{16,8},{24,16},{1,25},{9,1},{17,9},{25,17},{2,26},{10... | collective-permute-start | bytes 147464 | tf_op jit(solution)/shard_map/ppermute | solution.py:20
  38.6 0.8 collective-permute-start.25
  39.5 1.3 %collective-permute-done.6 = bf16[6,16,256]{2,1,0:T(8,128)(2,1)S(1)} collective-permute-done((bf16[6,16,256]{2,1,0:T(8,128)(2,1)S(1)}, bf16[6,16,256]{2,1,0:T(8,128)(2,1)S(1)}, u32[]{:S(2)}, u32[]{:S(2)}) %collective-permute-start.6) | collective-permute-done | bytes 49184 | tf_op jit(solution)/shard_map/ppermute | solution.py:20
  40.8 3.0 %collective-permute-done.7 = bf16[6,16,256]{2,1,0:T(8,128)(2,1)S(1)} collective-permute-done((bf16[6,16,256]{2,1,0:T(8,128)(2,1)S(1)}, bf16[6,16,256]{2,1,0:T(8,128)(2,1)S(1)}, u32[]{:S(2)}, u32[]{:S(2)}) %collective-permute-start.7) | collective-permute-done | bytes 49184 | tf_op jit(solution)/shard_map/ppermute | solution.py:20
  43.8 1.3 %collective-permute-start.11 = (bf16[6,16,256]{2,1,0:T(8,128)(2,1)S(1)}, bf16[6,16,256]{2,1,0:T(8,128)(2,1)S(1)}, u32[]{:S(2)}, u32[]{:S(2)}) collective-permute-start(bf16[6,16,256]{2,1,0:T(8,128)(2,1)S(1)} %fusion.4), channel_id=1, source_target_pairs={{0,24},{8,0},{16,8},{24,16},{1,25},{9,1},{17,9},{25,17},{2,26},{10... | collective-permute-start | bytes 147464 | tf_op jit(solution)/shard_map/ppermute | solution.py:20
  45.4 1.9 %collective-permute-done.25 = bf16[2,2,64,512]{3,2,1,0:T(8,128)(2,1)S(1)} collective-permute-done((bf16[2,2,64,512]{3,2,1,0:T(8,128)(2,1)S(1)}, bf16[2,2,64,512]{3,2,1,0:T(8,128)(2,1)S(1)}, u32[]{:S(2)}, u32[]{:S(2)}) %collective-permute-start.25) | collective-permute-done | bytes 262176 | tf_op jit(solution)/shard_map/ppermute | solution.py:308
  47.3 1.1 %collective-permute-start.9 = (bf16[6,16,256]{2,1,0:T(8,128)(2,1)S(1)}, bf16[6,16,256]{2,1,0:T(8,128)(2,1)S(1)}, u32[]{:S(2)}, u32[]{:S(2)}) collective-permute-start(bf16[6,16,256]{2,1,0:T(8,128)(2,1)S(1)} %fusion.4), channel_id=1, source_target_pairs={{0,8},{8,16},{16,24},{24,0},{1,9},{9,17},{17,25},{25,1},{2,10},{10... | collective-permute-start | bytes 147464 | tf_op jit(solution)/shard_map/ppermute | solution.py:20
  48.6 2.3 %collective-permute-done.10 = bf16[6,16,256]{2,1,0:T(8,128)(2,1)S(1)} collective-permute-done((bf16[6,16,256]{2,1,0:T(8,128)(2,1)S(1)}, bf16[6,16,256]{2,1,0:T(8,128)(2,1)S(1)}, u32[]{:S(2)}, u32[]{:S(2)}) %collective-permute-start.10) | collective-permute-done | bytes 49184 | tf_op jit(solution)/shard_map/ppermute | solution.py:20
  50.9 1.3 %collective-permute-start.26 = (bf16[4,2,64,512]{3,2,1,0:T(8,128)(2,1)S(1)}, bf16[4,2,64,512]{3,2,1,0:T(8,128)(2,1)}, u32[]{:S(2)}, u32[]{:S(2)}) collective-permute-start(bf16[4,2,64,512]{3,2,1,0:T(8,128)(2,1)S(1)} %pad_maximum_fusion.1.refs_12_), channel_id=1, source_target_pairs={{0,2},{1,3},{2,0},{3,1},{4,6},{5,7},{6,4},{7,5},{8,10},{9,11},{10,... | collective-permute-start | bytes 1572872 | tf_op jit(solution)/shard_map/ppermute | solution.py:298
  52.2 1.0 %collective-permute-done.9 = bf16[6,16,256]{2,1,0:T(8,128)(2,1)S(1)} collective-permute-done((bf16[6,16,256]{2,1,0:T(8,128)(2,1)S(1)}, bf16[6,16,256]{2,1,0:T(8,128)(2,1)S(1)}, u32[]{:S(2)}, u32[]{:S(2)}) %collective-permute-start.9) | collective-permute-done | bytes 49184 | tf_op jit(solution)/shard_map/ppermute | solution.py:20
  53.3 10.0 %collective-permute-done.17.refs_5_ = bf16[4,2,64,512]{3,2,1,0:T(8,128)(2,1)S(1)} collective-permute-done((bf16[4,2,64,512]{3,2,1,0:T(8,128)(2,1)S(1)}, bf16[4,2,64,512]{3,2,1,0:T(8,128)(2,1)S(1)}, u32[]{:S(2)}, u32[]{:S(2)}) %collective-permute-start.17) | collective-permute-done | bytes 524320 | tf_op jit(solution)/shard_map/ppermute | solution.py:20
  64.0 6.3 %collective-permute-done.19.refs_7_ = bf16[4,2,64,512]{3,2,1,0:T(8,128)(2,1)} collective-permute-done((bf16[4,2,64,512]{3,2,1,0:T(8,128)(2,1)S(1)}, bf16[4,2,64,512]{3,2,1,0:T(8,128)(2,1)}, u32[]{:S(2)}, u32[]{:S(2)}) %collective-permute-start.19) | collective-permute-done | bytes 524320 | tf_op jit(solution)/shard_map/ppermute | solution.py:20
  70.3 1.5 %collective-permute-start.12 = (bf16[4,6,16,256]{3,2,1,0:T(8,128)(2,1)S(1)}, bf16[4,6,16,256]{3,2,1,0:T(8,128)(2,1)}, u32[]{:S(2)}, u32[]{:S(2)}) collective-permute-start(bf16[4,6,16,256]{3,2,1,0:T(8,128)(2,1)S(1)} %pad_maximum_fusion.4.refs_0_), channel_id=1, source_target_pairs={{0,2},{1,3},{2,0},{3,1},{4,6},{5,7},{6,4},{7,5},{8,10},{9,11},{10,... | collective-permute-start | bytes 589832 | tf_op jit(solution)/shard_map/ppermute | solution.py:298
  71.7 6.0 %collective-permute-done.12.refs_1_ = bf16[4,6,16,256]{3,2,1,0:T(8,128)(2,1)} collective-permute-done((bf16[4,6,16,256]{3,2,1,0:T(8,128)(2,1)S(1)}, bf16[4,6,16,256]{3,2,1,0:T(8,128)(2,1)}, u32[]{:S(2)}, u32[]{:S(2)}) %collective-permute-start.12) | collective-permute-done | bytes 196640 | tf_op jit(solution)/shard_map/ppermute | solution.py:298
  77.7 0.8 copy.21.chain_ref
  78.6 0.9 collective-permute-done.14.refs_3_
  79.5 16.7 %chain.1 = bf16[4,2,256,512]{3,2,1,0:T(8,128)(2,1)} custom-call(s32[3]{0:T(128)S(1)} %pad_add_fusion.me_ref, s32[4]{0:T(128)S(1)} %copy-done.3, f32[4,4,4]{2,1,0:T(4,128)S(1)} %copy-done.2, s32[4,2]{1,0:T(4,128)S(1)} %copy.21.chain_ref, bf16[4,6,16,256]{3,2,1,0:T(8,128)(2,1)S(1)} %pad_maximum_fusion.4.refs_0_, ...), custom_call_target="tpu_custom_call" | custom-call | tf_op jit(solution)/shard_map/chain/pallas_call | solution.py:403
  (66 shorter events, 4.8 us)
Async XLA Ops:
  0.0 12.0 %copy-start = (bf16[2,256,512]{2,1,0:T(8,128)(2,1)S(1)}, bf16[2,256,512]{2,1,0:T(8,128)(2,1)}, u32[]{:S(2)}) copy-start(bf16[2,256,512]{2,1,0:T(8,128)(2,1)} %fwd_ref.1) | copy-start | bytes 1572868
  1.0 12.3 %collective-permute-start = (bf16[96,256]{1,0:T(8,128)(2,1)S(1)}, bf16[96,256]{1,0:T(8,128)(2,1)S(1)}, u32[]{:S(2)}, u32[]{:S(2)}) collective-permute-start(bf16[96,256]{1,0:T(8,128)(2,1)S(1)} %reshape.25), channel_id=1, source_target_pairs={{0,24},{8,0},{16,8},{24,16},{1,25},{9,1},{17,9},{25,17},{2,26},{10... | collective-permute-start | bytes 147464 | tf_op jit(solution)/shard_map/ppermute | solution.py:20
  6.9 6.4 %collective-permute-start.1 = (bf16[48,256]{1,0:T(8,128)(2,1)S(1)}, bf16[48,256]{1,0:T(8,128)(2,1)S(1)}, u32[]{:S(2)}, u32[]{:S(2)}) collective-permute-start(bf16[48,256]{1,0:T(8,128)(2,1)S(1)} %reshape.26), channel_id=1, source_target_pairs={{0,4},{4,0},{1,5},{5,1},{2,6},{6,2},{3,7},{7,3},{8,12},{12,8},{9,1... | collective-permute-start | bytes 73736 | tf_op jit(solution)/shard_map/ppermute | solution.py:20
  9.3 4.0 %collective-permute-start.2 = (bf16[48,256]{1,0:T(8,128)(2,1)S(1)}, bf16[48,256]{1,0:T(8,128)(2,1)S(1)}, u32[]{:S(2)}, u32[]{:S(2)}) collective-permute-start(bf16[48,256]{1,0:T(8,128)(2,1)S(1)} %reshape.27), channel_id=1, source_target_pairs={{0,3},{1,0},{2,1},{3,2},{4,7},{5,4},{6,5},{7,6},{8,11},{9,8},{10,9... | collective-permute-start | bytes 73736 | tf_op jit(solution)/shard_map/ppermute | solution.py:20
  14.8 1.8 %collective-permute-start.3 = (bf16[2,4,6,16,256]{4,3,2,1,0:T(8,128)(2,1)S(1)}, bf16[2,4,6,16,256]{4,3,2,1,0:T(8,128)(2,1)S(1)}, u32[]{:S(2)}, u32[]{:S(2)}) collective-permute-start(bf16[2,4,6,16,256]{4,3,2,1,0:T(8,128)(2,1)S(1)} %dynamic-slice_bitcast_fusion), channel_id=1, source_target_pairs={{0,1},{1,0},{2,3},{3,2},{4,5},{5,4},{6,7},{7,6},{8,9},{9,8},{10,11... | collective-permute-start | bytes 1179656 | tf_op jit(solution)/shard_map/ppermute | solution.py:298
  14.9 7.4 %collective-permute-start.15 = (bf16[1,2,64,512]{3,2,1,0:T(8,128)(2,1)S(1)}, bf16[1,2,64,512]{3,2,1,0:T(8,128)(2,1)S(1)}, u32[]{:S(2)}, u32[]{:S(2)}) collective-permute-start(bf16[1,2,64,512]{3,2,1,0:T(8,128)(2,1)S(1)} %bitcast.45), channel_id=1, source_target_pairs={{0,16},{8,24},{16,0},{24,8},{1,17},{9,25},{17,1},{25,9},{2,18},{10... | collective-permute-start | bytes 393224 | tf_op jit(solution)/shard_map/ppermute | solution.py:308
  16.7 7.0 %collective-permute-start.4 = (bf16[4,6,16,256]{3,2,1,0:T(8,128)(2,1)S(1)}, bf16[4,6,16,256]{3,2,1,0:T(8,128)(2,1)S(1)}, u32[]{:S(2)}, u32[]{:S(2)}) collective-permute-start(bf16[4,6,16,256]{3,2,1,0:T(8,128)(2,1)S(1)} %dynamic-slice_bitcast_fusion.1), channel_id=1, source_target_pairs={{0,2},{1,3},{2,0},{3,1},{4,6},{5,7},{6,4},{7,5},{8,10},{9,11},{10,... | collective-permute-start | bytes 589832 | tf_op jit(solution)/shard_map/ppermute | solution.py:298
  22.4 11.2 %collective-permute-start.16 = (bf16[2,2,64,512]{3,2,1,0:T(8,128)(2,1)S(1)}, bf16[2,2,64,512]{3,2,1,0:T(8,128)(2,1)S(1)}, u32[]{:S(2)}, u32[]{:S(2)}) collective-permute-start(bf16[2,2,64,512]{3,2,1,0:T(8,128)(2,1)S(1)} %pad_maximum_fusion.2), channel_id=1, source_target_pairs={{0,8},{8,0},{16,24},{24,16},{1,9},{9,1},{17,25},{25,17},{2,10},{10... | collective-permute-start | bytes 786440 | tf_op jit(solution)/shard_map/ppermute | solution.py:308
  23.8 10.9 %collective-permute-start.5 = (bf16[4,6,16,256]{3,2,1,0:T(8,128)(2,1)S(1)}, bf16[4,6,16,256]{3,2,1,0:T(8,128)(2,1)S(1)}, u32[]{:S(2)}, u32[]{:S(2)}) collective-permute-start(bf16[4,6,16,256]{3,2,1,0:T(8,128)(2,1)S(1)} %fusion.1), channel_id=1, source_target_pairs={{0,4},{4,0},{1,5},{5,1},{2,6},{6,2},{3,7},{7,3},{8,12},{12,8},{9,1... | collective-permute-start | bytes 589832 | tf_op jit(solution)/shard_map/ppermute | solution.py:20
  24.4 14.2 %collective-permute-start.24 = (bf16[1,2,64,512]{3,2,1,0:T(8,128)(2,1)S(1)}, bf16[1,2,64,512]{3,2,1,0:T(8,128)(2,1)S(1)}, u32[]{:S(2)}, u32[]{:S(2)}) collective-permute-start(bf16[1,2,64,512]{3,2,1,0:T(8,128)(2,1)S(1)} %bitcast.42), channel_id=1, source_target_pairs={{0,16},{8,24},{16,0},{24,8},{1,17},{9,25},{17,1},{25,9},{2,18},{10... | collective-permute-start | bytes 393224 | tf_op jit(solution)/shard_map/ppermute | solution.py:308
  26.3 53.3 %copy-start.2 = (f32[4,4,4]{2,1,0:T(4,128)S(1)}, f32[4,4,4]{2,1,0:T(4,128)}, u32[]{:S(2)}) copy-start(f32[4,4,4]{2,1,0:T(4,128)} %spin_ref.1) | copy-start | bytes 772
  26.3 53.3 %copy-start.3 = (s32[4]{0:T(128)S(1)}, s32[4]{0:T(128)}, u32[]{:S(2)}) copy-start(s32[4]{0:T(128)} %dirs_ref.1) | copy-start | bytes 52
  33.6 14.9 %collective-permute-start.18 = (bf16[4,2,64,512]{3,2,1,0:T(8,128)(2,1)S(1)}, bf16[4,2,64,512]{3,2,1,0:T(8,128)(2,1)S(1)}, u32[]{:S(2)}, u32[]{:S(2)}) collective-permute-start(bf16[4,2,64,512]{3,2,1,0:T(8,128)(2,1)S(1)} %pad_maximum_fusion.refs_4_), channel_id=1, source_target_pairs={{0,2},{1,3},{2,0},{3,1},{4,6},{5,7},{6,4},{7,5},{8,10},{9,11},{10,... | collective-permute-start | bytes 1572872 | tf_op jit(solution)/shard_map/ppermute | solution.py:298
  34.7 6.1 %collective-permute-start.6 = (bf16[6,16,256]{2,1,0:T(8,128)(2,1)S(1)}, bf16[6,16,256]{2,1,0:T(8,128)(2,1)S(1)}, u32[]{:S(2)}, u32[]{:S(2)}) collective-permute-start(bf16[6,16,256]{2,1,0:T(8,128)(2,1)S(1)} %get-tuple-element.19), channel_id=1, source_target_pairs={{0,8},{8,16},{16,24},{24,0},{1,9},{9,17},{17,25},{25,1},{2,10},{10... | collective-permute-start | bytes 147464 | tf_op jit(solution)/shard_map/ppermute | solution.py:20
  34.8 6.0 %collective-permute-start.8 = (bf16[6,16,256]{2,1,0:T(8,128)(2,1)S(1)}, bf16[6,16,256]{2,1,0:T(8,128)(2,1)S(1)}, u32[]{:S(2)}, u32[]{:S(2)}) collective-permute-start(bf16[6,16,256]{2,1,0:T(8,128)(2,1)S(1)} %get-tuple-element.20), channel_id=1, source_target_pairs={{0,24},{8,0},{16,8},{24,16},{1,25},{9,1},{17,9},{25,17},{2,26},{10... | collective-permute-start | bytes 147464 | tf_op jit(solution)/shard_map/ppermute | solution.py:20
  38.6 5.2 %collective-permute-start.7 = (bf16[6,16,256]{2,1,0:T(8,128)(2,1)S(1)}, bf16[6,16,256]{2,1,0:T(8,128)(2,1)S(1)}, u32[]{:S(2)}, u32[]{:S(2)}) collective-permute-start(bf16[6,16,256]{2,1,0:T(8,128)(2,1)S(1)} %get-tuple-element.21), channel_id=1, source_target_pairs={{0,16},{8,24},{16,0},{24,8},{1,17},{9,25},{17,1},{25,9},{2,18},{10... | collective-permute-start | bytes 147464 | tf_op jit(solution)/shard_map/ppermute | solution.py:20
  38.6 8.7 %collective-permute-start.25 = (bf16[2,2,64,512]{3,2,1,0:T(8,128)(2,1)S(1)}, bf16[2,2,64,512]{3,2,1,0:T(8,128)(2,1)S(1)}, u32[]{:S(2)}, u32[]{:S(2)}) collective-permute-start(bf16[2,2,64,512]{3,2,1,0:T(8,128)(2,1)S(1)} %pad_maximum_fusion.3), channel_id=1, source_target_pairs={{0,8},{8,0},{16,24},{24,16},{1,9},{9,1},{17,25},{25,17},{2,10},{10... | collective-permute-start | bytes 786440 | tf_op jit(solution)/shard_map/ppermute | solution.py:308
  40.8 12.5 %collective-permute-start.20 = (bf16[4,2,64,512]{3,2,1,0:T(8,128)(2,1)S(1)}, bf16[4,2,64,512]{3,2,1,0:T(8,128)(2,1)S(1)}, u32[]{:S(2)}, u32[]{:S(2)}) collective-permute-start(bf16[4,2,64,512]{3,2,1,0:T(8,128)(2,1)S(1)} %pad_maximum_fusion.refs_4_), channel_id=1, source_target_pairs={{0,1},{1,0},{2,3},{3,2},{4,5},{5,4},{6,7},{7,6},{8,9},{9,8},{10,11... | collective-permute-start | bytes 1572872 | tf_op jit(solution)/shard_map/ppermute | solution.py:298
  43.8 4.7 %collective-permute-start.11 = (bf16[6,16,256]{2,1,0:T(8,128)(2,1)S(1)}, bf16[6,16,256]{2,1,0:T(8,128)(2,1)S(1)}, u32[]{:S(2)}, u32[]{:S(2)}) collective-permute-start(bf16[6,16,256]{2,1,0:T(8,128)(2,1)S(1)} %fusion.4), channel_id=1, source_target_pairs={{0,24},{8,0},{16,8},{24,16},{1,25},{9,1},{17,9},{25,17},{2,26},{10... | collective-permute-start | bytes 147464 | tf_op jit(solution)/shard_map/ppermute | solution.py:20
  45.2 5.8 %collective-permute-start.10 = (bf16[6,16,256]{2,1,0:T(8,128)(2,1)S(1)}, bf16[6,16,256]{2,1,0:T(8,128)(2,1)S(1)}, u32[]{:S(2)}, u32[]{:S(2)}) collective-permute-start(bf16[6,16,256]{2,1,0:T(8,128)(2,1)S(1)} %fusion.4), channel_id=1, source_target_pairs={{0,16},{8,24},{16,0},{24,8},{1,17},{9,25},{17,1},{25,9},{2,18},{10... | collective-permute-start | bytes 147464 | tf_op jit(solution)/shard_map/ppermute | solution.py:20
  47.3 5.9 %collective-permute-start.9 = (bf16[6,16,256]{2,1,0:T(8,128)(2,1)S(1)}, bf16[6,16,256]{2,1,0:T(8,128)(2,1)S(1)}, u32[]{:S(2)}, u32[]{:S(2)}) collective-permute-start(bf16[6,16,256]{2,1,0:T(8,128)(2,1)S(1)} %fusion.4), channel_id=1, source_target_pairs={{0,8},{8,16},{16,24},{24,0},{1,9},{9,17},{17,25},{25,1},{2,10},{10... | collective-permute-start | bytes 147464 | tf_op jit(solution)/shard_map/ppermute | solution.py:20
  48.5 14.9 %collective-permute-start.17 = (bf16[4,2,64,512]{3,2,1,0:T(8,128)(2,1)S(1)}, bf16[4,2,64,512]{3,2,1,0:T(8,128)(2,1)S(1)}, u32[]{:S(2)}, u32[]{:S(2)}) collective-permute-start(bf16[4,2,64,512]{3,2,1,0:T(8,128)(2,1)S(1)} %pad_maximum_fusion.refs_4_), channel_id=1, source_target_pairs={{0,4},{4,0},{1,5},{5,1},{2,6},{6,2},{3,7},{7,3},{8,12},{12,8},{9,1... | collective-permute-start | bytes 1572872 | tf_op jit(solution)/shard_map/ppermute | solution.py:20
  48.5 14.8 %collective-permute-start.27 = (bf16[4,2,64,512]{3,2,1,0:T(8,128)(2,1)S(1)}, bf16[4,2,64,512]{3,2,1,0:T(8,128)(2,1)S(1)}, u32[]{:S(2)}, u32[]{:S(2)}) collective-permute-start(bf16[4,2,64,512]{3,2,1,0:T(8,128)(2,1)S(1)} %pad_maximum_fusion.1.refs_12_), channel_id=1, source_target_pairs={{0,1},{1,0},{2,3},{3,2},{4,5},{5,4},{6,7},{7,6},{8,9},{9,8},{10,11... | collective-permute-start | bytes 1572872 | tf_op jit(solution)/shard_map/ppermute | solution.py:298
  50.9 13.0 %collective-permute-start.26 = (bf16[4,2,64,512]{3,2,1,0:T(8,128)(2,1)S(1)}, bf16[4,2,64,512]{3,2,1,0:T(8,128)(2,1)}, u32[]{:S(2)}, u32[]{:S(2)}) collective-permute-start(bf16[4,2,64,512]{3,2,1,0:T(8,128)(2,1)S(1)} %pad_maximum_fusion.1.refs_12_), channel_id=1, source_target_pairs={{0,2},{1,3},{2,0},{3,1},{4,6},{5,7},{6,4},{7,5},{8,10},{9,11},{10,... | collective-permute-start | bytes 1572872 | tf_op jit(solution)/shard_map/ppermute | solution.py:298
  53.2 17.1 %collective-permute-start.19 = (bf16[4,2,64,512]{3,2,1,0:T(8,128)(2,1)S(1)}, bf16[4,2,64,512]{3,2,1,0:T(8,128)(2,1)}, u32[]{:S(2)}, u32[]{:S(2)}) collective-permute-start(bf16[4,2,64,512]{3,2,1,0:T(8,128)(2,1)S(1)} %collective-permute-done.18.refs_6_), channel_id=1, source_target_pairs={{0,4},{4,0},{1,5},{5,1},{2,6},{6,2},{3,7},{7,3},{8,12},{12,8},{9,1... | collective-permute-start | bytes 1572872 | tf_op jit(solution)/shard_map/ppermute | solution.py:20
  53.3 17.0 %collective-permute-start.13 = (bf16[4,6,16,256]{3,2,1,0:T(8,128)(2,1)S(1)}, bf16[4,6,16,256]{3,2,1,0:T(8,128)(2,1)S(1)}, u32[]{:S(2)}, u32[]{:S(2)}) collective-permute-start(bf16[4,6,16,256]{3,2,1,0:T(8,128)(2,1)S(1)} %pad_maximum_fusion.4.refs_0_), channel_id=1, source_target_pairs={{0,1},{1,0},{2,3},{3,2},{4,5},{5,4},{6,7},{7,6},{8,9},{9,8},{10,11... | collective-permute-start | bytes 589832 | tf_op jit(solution)/shard_map/ppermute | solution.py:298
  63.4 16.1 %collective-permute-start.22 = (bf16[4,2,64,512]{3,2,1,0:T(8,128)(2,1)S(1)}, bf16[4,2,64,512]{3,2,1,0:T(8,128)(2,1)}, u32[]{:S(2)}, u32[]{:S(2)}) collective-permute-start(bf16[4,2,64,512]{3,2,1,0:T(8,128)(2,1)S(1)} %collective-permute-done.18.refs_6_), channel_id=1, source_target_pairs={{0,1},{1,0},{2,3},{3,2},{4,5},{5,4},{6,7},{7,6},{8,9},{9,8},{10,11... | collective-permute-start | bytes 1572872 | tf_op jit(solution)/shard_map/ppermute | solution.py:298
  63.4 16.1 %collective-permute-start.21 = (bf16[4,2,64,512]{3,2,1,0:T(8,128)(2,1)S(1)}, bf16[4,2,64,512]{3,2,1,0:T(8,128)(2,1)}, u32[]{:S(2)}, u32[]{:S(2)}) collective-permute-start(bf16[4,2,64,512]{3,2,1,0:T(8,128)(2,1)S(1)} %collective-permute-done.17.refs_5_), channel_id=1, source_target_pairs={{0,1},{1,0},{2,3},{3,2},{4,5},{5,4},{6,7},{7,6},{8,9},{9,8},{10,11... | collective-permute-start | bytes 1572872 | tf_op jit(solution)/shard_map/ppermute | solution.py:298
  63.9 15.6 %collective-permute-start.28 = (bf16[4,2,64,512]{3,2,1,0:T(8,128)(2,1)}, bf16[4,2,64,512]{3,2,1,0:T(8,128)(2,1)}, u32[]{:S(2)}, u32[]{:S(2)}) collective-permute-start(bf16[4,2,64,512]{3,2,1,0:T(8,128)(2,1)} %collective-permute-done.26.refs_13_), channel_id=1, source_target_pairs={{0,1},{1,0},{2,3},{3,2},{4,5},{5,4},{6,7},{7,6},{8,9},{9,8},{10,11... | collective-permute-start | bytes 1572872 | tf_op jit(solution)/shard_map/ppermute | solution.py:298
  70.3 9.2 %collective-permute-start.23 = (bf16[4,2,64,512]{3,2,1,0:T(8,128)(2,1)}, bf16[4,2,64,512]{3,2,1,0:T(8,128)(2,1)}, u32[]{:S(2)}, u32[]{:S(2)}) collective-permute-start(bf16[4,2,64,512]{3,2,1,0:T(8,128)(2,1)} %collective-permute-done.19.refs_7_), channel_id=1, source_target_pairs={{0,1},{1,0},{2,3},{3,2},{4,5},{5,4},{6,7},{7,6},{8,9},{9,8},{10,11... | collective-permute-start | bytes 1572872 | tf_op jit(solution)/shard_map/ppermute | solution.py:298
  70.3 7.4 %collective-permute-start.12 = (bf16[4,6,16,256]{3,2,1,0:T(8,128)(2,1)S(1)}, bf16[4,6,16,256]{3,2,1,0:T(8,128)(2,1)}, u32[]{:S(2)}, u32[]{:S(2)}) collective-permute-start(bf16[4,6,16,256]{3,2,1,0:T(8,128)(2,1)S(1)} %pad_maximum_fusion.4.refs_0_), channel_id=1, source_target_pairs={{0,2},{1,3},{2,0},{3,1},{4,6},{5,7},{6,4},{7,5},{8,10},{9,11},{10,... | collective-permute-start | bytes 589832 | tf_op jit(solution)/shard_map/ppermute | solution.py:298
  77.7 1.8 %collective-permute-start.14 = (bf16[4,6,16,256]{3,2,1,0:T(8,128)(2,1)}, bf16[4,6,16,256]{3,2,1,0:T(8,128)(2,1)}, u32[]{:S(2)}, u32[]{:S(2)}) collective-permute-start(bf16[4,6,16,256]{3,2,1,0:T(8,128)(2,1)} %collective-permute-done.12.refs_1_), channel_id=1, source_target_pairs={{0,1},{1,0},{2,3},{3,2},{4,5},{5,4},{6,7},{7,6},{8,9},{9,8},{10,11... | collective-permute-start | bytes 589832 | tf_op jit(solution)/shard_map/ppermute | solution.py:298
  (1 other events, 12.0 us)

commit v4 on v3

--- a/solution.py
+++ b/solution.py
@@ -50,10 +50,8 @@
     total = 6 * (inner + face)
     column = whole_numbers((1, total), 1)
     beyond = chosen(column >= 6 * inner)
-    place = column - beyond * (6 * inner)
-    block = 3 * inner + beyond * (3 * (face - inner))
-    part = chosen(place >= block)
-    site, colour = parts_of(place - part * block, 3)
+    site, left = parts_of(column - beyond * (6 * inner), 6)
+    colour, part = parts_of(left, 2)
     within = coordinates(site, extent)
     if e == 0:
         within[0] = within[0] + 1
@@ -65,7 +63,16 @@
     return total, part, where, colour
 
 
-def pieces_kernel(z_ref, fwd_ref, bwd_ref, fwd_out, bwd_out):
+def first_kernel(extent, z_ref, fwd_ref, bwd_ref, eig_ref, fwd_out, bwd_out, vec_out, *face_outs):
+    vec = eig_ref[...].astype(F32).reshape(vec_out.shape)
+    vec_out[...] = vec.astype(BF16)
+    strides = (6 * extent[1] * extent[2], 6 * extent[2], 6)
+    for e, out in enumerate(face_outs):
+        begins = [0]
+        for d in range(e):
+            begins = [at + n * strides[d] for at in begins for n in range(extent[d])]
+        runs = [vec[at : at + strides[e]] for at in begins]
+        out[...] = (jnp.concatenate(runs, axis=0) if e else runs[0]).astype(BF16)
     rows, cols = fwd_ref.shape[1:]
     piece = fwd_out.shape[1]
     per_spin = rows // 4
@@ -92,8 +99,8 @@
     count = math.prod(extent)
     rows = 6 * count
     row = whole_numbers((rows, 1), 0)
-    row_part = chosen(row >= 3 * count)
-    row_site, row_colour = parts_of(row - row_part * (3 * count), 3)
+    row_site, left = parts_of(row, 6)
+    row_colour, row_part = parts_of(left, 2)
     row_where = coordinates(row_site, extent)
     link = link_ref[...]
     high = link.astype(BF16)
@@ -132,14 +139,17 @@
 
 
 def correlate_kernel(scale, vec_ref, face0, face1, face2, mat0, mat1, mat2, out_ref):
-    gz_n, gx_n, _, own_rows, _ = out_ref.shape
+    gz_n, gx_n, split, depth, width = out_ref.shape
+    each = 6 // split
+    own_rows = depth // each
     vec = vec_ref[...]
     rows = vec.shape[0]
-    half = rows // 2
-    width = vec.shape[1]
-    lower = half - face0.shape[0] // 2
+    row = lax.broadcasted_iota(jnp.int32, (rows, rows), 0)
+    column = lax.broadcasted_iota(jnp.int32, (rows, rows), 1)
+    odd = lax.rem(row, 2) == 1
+    turn = jnp.where(odd & (column == row - 1), -1.0, chosen((column == row + 1) & ~odd)).astype(BF16)
     sources = [
-        jnp.concatenate([vec[half - lower : half], vec[rows - lower :], face0[...]], axis=0),
+        jnp.concatenate([vec[face0.shape[0] :], face0[...]], axis=0),
         jnp.concatenate([vec, face1[...]], axis=0),
         jnp.concatenate([vec, face2[...]], axis=0),
     ]
@@ -147,26 +157,31 @@
         terms = mm(mat[...], sources[e])
         moved = terms[:rows] + terms[rows : 2 * rows] + terms[2 * rows :]
         moved = moved.astype(BF16)
-        turned = jnp.concatenate([moved[half:], -moved[:half]], axis=0)
+        turned = mm(turn, moved).astype(BF16)
         right = jnp.concatenate([moved, turned], axis=1)
         product = lax.dot_general(
             vec, right, (((0,), (0,)), ((), ())), preferred_element_type=F32
         )
         product = (product * scale).astype(BF16)
-        for g in range(gx_n):
-            for z in range(gz_n):
-                at = (g * gz_n + z) * own_rows
-                out_ref[z, g, 2 * e] = product[at : at + own_rows, :width]
-                out_ref[z, g, 2 * e + 1] = product[at : at + own_rows, width:]
+        for c in range(2):
+            n = 2 * e + c
+            half = product[:, c * width : (c + 1) * width]
+            to = slice(n % each * own_rows, (n % each + 1) * own_rows)
+            for g in range(gx_n):
+                for z in range(gz_n):
+                    at = (g * gz_n + z) * own_rows
+                    out_ref[z, g, n // each, to] = half[at : at + own_rows]
 
 
 def chain_kernel(inverse, plan, me_ref, dirs_ref, spin_ref, chain_ref, *refs):
     line, elem_keys, fwd_keys, bwd_keys = plan
-    elem_in, refs = refs[: len(elem_keys)], refs[len(elem_keys) :]
+    elem_in, refs = refs[:2], refs[2:]
     fwd_in, refs = refs[: len(fwd_keys)], refs[len(fwd_keys) :]
     bwd_in, refs = refs[: len(bwd_keys)], refs[len(bwd_keys) :]
     out_ref, elem_all, elem_ref, x_ref, p_ref, q_ref, b_ref = refs
-    _, gx_n, gz_n, own_rows, num_vecs = elem_all.shape
+    gx_n, gz_n, split, depth, num_vecs = elem_all.shape
+    each = 6 // split
+    own_rows = depth // each
     width = out_ref.shape[3]
     op_count = out_ref.shape[0]
     row_count = out_ref.shape[2]
@@ -182,9 +197,11 @@
     def gz_from(dy, dc):
         return back(lax.div(gz, 2), dy, gz_n // 2) * 2 + back(lax.rem(gz, 2), dc, 2)
 
-    for (dy, dc), ref in zip(elem_keys, elem_in):
-        for step in range(gx_n):
-            elem_all[:, back(gx, step, gx_n), gz_from(dy, dc)] = ref[step]
+    for dc, ref in enumerate(elem_in):
+        for n, (dx, dy) in enumerate(elem_keys):
+            for place, offset in enumerate(line):
+                to = lax.bitwise_xor(gx, offset), gz_from(dy, dc), back(gy, dx, gy_n) if split > 1 else 0
+                elem_all[to] = ref[n, place]
     column = lax.broadcasted_iota(jnp.int32, (1, num_vecs), 1)
     source = jnp.zeros_like(column)
     half_rows = vec_rows // halves
@@ -197,7 +214,9 @@
             source = jnp.where(inside, column + (begin - at), source)
     perm = chosen(lax.broadcasted_iota(jnp.int32, (num_vecs, num_vecs), 0) == source).astype(BF16)
     for n in range(6):
-        elem_ref[n] = mm(elem_all[n].reshape(num_vecs, num_vecs), perm).astype(BF16)
+        rows = slice(n % each * own_rows, (n % each + 1) * own_rows)
+        whole = elem_all[:, :, n // each, rows].reshape(num_vecs, num_vecs)
+        elem_ref[n] = mm(whole, perm).astype(BF16)
 
     if halves == 1:
         groups = [[key] for key in bwd_keys]
@@ -298,12 +317,24 @@
     return lax.ppermute(value, "gz", pairs)
 
 
-def line_exchange(value, axis):
+def passed_in_plane(value, dx, dy):
+    if not dx and not dy:
+        return value
+    gy_n, gz_n = lax.axis_size("gy"), lax.axis_size("gz")
+    chips = gz_n // 2
+    pairs = []
+    for y in range(gy_n):
+        for z in range(gz_n):
+            to = (y + dx) % gy_n * gz_n + ((z // 2 + dy) % chips) * 2 + z % 2
+            pairs.append((y * gz_n + z, to))
+    return lax.ppermute(value, ("gy", "gz"), pairs)
+
+
+def line_exchange(value, axis, distance, steps, offsets=(0,)):
     count = lax.axis_size(axis)
-    gathered = value[None]
-    offsets = [0]
-    distance = count // 2
-    while distance:
+    gathered = value if len(offsets) > 1 else value[None]
+    offsets = list(offsets)
+    for _ in range(steps):
         pairs = [(n, n ^ distance) for n in range(count)]
         gathered = jnp.concatenate([gathered, lax.ppermute(gathered, axis, pairs)])
         offsets += [offset ^ distance for offset in offsets]
@@ -328,44 +359,29 @@
     me = jnp.stack([gx, gy, gz])
     chip, core = lax.div(gz, 2), lax.rem(gz, 2)
 
-    ordered = eigvecs.transpose(3, 0, 1, 2, 4, 5)
-    faces = []
-    for e, axis in enumerate(("gx", "gy", "gz")):
-        face = lax.slice_in_dim(ordered, 0, 1, axis=1 + e).reshape(-1, num_vecs)
-        faces.append(passed_along(face, axis, -1))
-    vec = ordered.reshape(-1, num_vecs)
-
     rows, cols = forward_peram.shape[1:]
     piece = rows // gz_n
+    site_rows = 6 * math.prod(extent)
+    face_rows = [site_rows // n for n in extent]
     piece_shape = jax.ShapeDtypeStruct((2, piece, cols), BF16)
-    fwd_piece, bwd_piece = pl.pallas_call(
-        pieces_kernel,
-        out_shape=[piece_shape, piece_shape],
-        in_specs=[SMEM, VMEM, VMEM],
-        out_specs=[VMEM, VMEM],
+    fwd_piece, bwd_piece, vec, *faces = pl.pallas_call(
+        functools.partial(first_kernel, extent),
+        out_shape=[piece_shape, piece_shape]
+        + [jax.ShapeDtypeStruct((n, num_vecs), BF16) for n in [site_rows] + face_rows],
+        in_specs=[SMEM] + [VMEM] * 3,
+        out_specs=[VMEM] * 6,
         compiler_params=pltpu.CompilerParams(vmem_limit_bytes=24 * 2**20),
-        name="pieces",
-    )(me[2:], forward_peram, backward_peram)
-
-    bwd_piece, link_rows = lax.optimization_barrier((bwd_piece, links.reshape(-1, 54)))
-    fwd_line, line = line_exchange(fwd_piece, "gx")
-    bwd_line, _ = line_exchange(bwd_piece, "gx")
-    fwd_parts, bwd_parts = {}, {}
-    for dy in range(chips):
-        mine = passed_in_gz(fwd_line, dy, 0) if dy else fwd_line
-        for dx in range(gy_n):
-            fwd_parts[dx, dy, 0] = passed_along(mine, "gy", dx) if dx else mine
-        bwd_parts[dy, 0] = passed_in_gz(bwd_line, dy, 0) if dy else bwd_line
-    for dx, dy, _ in list(fwd_parts):
-        fwd_parts[dx, dy, 1] = passed_in_gz(fwd_parts[dx, dy, 0], 0, 1)
-    for dy, _ in list(bwd_parts):
-        bwd_parts[dy, 1] = passed_in_gz(bwd_parts[dy, 0], 0, 1)
-
-    site_rows = 6 * math.prod(extent)
+        name="first",
+    )(me[2:], forward_peram, backward_peram, eigvecs.transpose(0, 1, 2, 4, 3, 5).reshape(-1, 2, num_vecs))
+    faces = [passed_along(face, axis, -1) for face, axis in zip(faces, ("gx", "gy", "gz"))]
+
+    fwd_piece, link_rows = lax.optimization_barrier((fwd_piece, links.reshape(-1, 54)))
+    fwd_line, line = line_exchange(fwd_piece, "gx", gx_n // 2, 1)
+
     link_mats = pl.pallas_call(
         functools.partial(links_kernel, extent),
         out_shape=[
-            jax.ShapeDtypeStruct((3 * site_rows, site_rows - (0 if e else site_rows // extent[0]) + site_rows // extent[e]), BF16)
+            jax.ShapeDtypeStruct((3 * site_rows, site_rows - (0 if e else face_rows[0]) + face_rows[e]), BF16)
             for e in range(3)
         ],
         in_specs=[VMEM],
@@ -376,9 +392,11 @@
 
     volume = math.prod(extent) * gx_n * gy_n * gz_n
     own_rows = num_vecs // (gz_n * gx_n)
+    split = gy_n if 6 % gy_n == 0 and own_rows % 16 == 0 else 1
+    depth = 6 * own_rows // split
     partial = pl.pallas_call(
         functools.partial(correlate_kernel, 1.0 / math.sqrt(12.0 * volume)),
-        out_shape=jax.ShapeDtypeStruct((gz_n, gx_n, 6, own_rows, num_vecs), BF16),
+        out_shape=jax.ShapeDtypeStruct((gz_n, gx_n, split, depth, num_vecs), BF16),
         in_specs=[VMEM] * 7,
         out_specs=VMEM,
         compiler_params=pltpu.CompilerParams(vmem_limit_bytes=24 * 2**20),
@@ -387,26 +405,46 @@
 
     by_core = partial.reshape((chips, 2) + partial.shape[1:])
     summed = added(part_at(by_core, core, 1), passed_in_gz(part_at(by_core, 1 - core, 1), 0, 1))
-    arrived = [passed_in_gz(part_at(summed, lax.rem(chip + dy, chips)), dy, 0) for dy in range(1, chips)]
-    summed = added(part_at(summed, chip), *arrived)
-    summed = added(summed, *[passed_along(summed, "gy", dx) for dx in range(1, gy_n)])
-    arrived = [passed_along(part_at(summed, lax.rem(gx + dz, gx_n)), "gx", dz) for dz in range(1, gx_n)]
-    summed = added(part_at(summed, gx), *arrived)
-    elem_line = jnp.stack([summed] + [passed_along(summed, "gx", dz) for dz in range(1, gx_n)])
-    elem_parts = {(dy, 0): passed_in_gz(elem_line, dy, 0) if dy else elem_line for dy in range(chips)}
+    summed, fwd_line = lax.optimization_barrier((summed, fwd_line))
+    rounds = gx_n.bit_length() - 1
+    fwd_line, line = line_exchange(fwd_line, "gx", gx_n // 4, rounds - 1, line)
+    plane = [(dx, dy) for dy in range(chips) for dx in range(gy_n)]
+
+    def plane_part(dx, dy):
+        part = part_at(summed, lax.rem(chip + dy, chips))
+        return part_at(part, lax.rem(gy + dx, gy_n) if split > 1 else 0, 1)
+
+    summed = added(*[passed_in_plane(plane_part(dx, dy), dx, dy) for dx, dy in plane])
+    summed, fwd_line, bwd_piece = lax.optimization_barrier((summed, fwd_line, bwd_piece))
+    fwd_parts = {(dx, dy, 0): passed_in_plane(fwd_line, dx, dy) for dx, dy in plane}
+    bwd_line, _ = line_exchange(bwd_piece, "gx", gx_n // 2, rounds)
+    bwd_parts = {(dy, 0): passed_in_gz(bwd_line, dy, 0) if dy else bwd_line for dy in range(chips)}
+    for dx, dy in plane:
+        fwd_parts[dx, dy, 1] = passed_in_gz(fwd_parts[dx, dy, 0], 0, 1)
     for dy in range(chips):
-        elem_parts[dy, 1] = passed_in_gz(elem_parts[dy, 0], 0, 1)
+        bwd_parts[dy, 1] = passed_in_gz(bwd_parts[dy, 0], 0, 1)
+    distance = gx_n // 2
+    while distance:
+        halves = summed.reshape((2, distance) + summed.shape[1:])
+        bit = lax.rem(lax.div(gx, distance), 2)
+        pairs = [(n, n ^ distance) for n in range(gx_n)]
+        summed = added(part_at(halves, bit), lax.ppermute(part_at(halves, 1 - bit), "gx", pairs))
+        distance //= 2
+    elem_line, _ = line_exchange(summed[0], "gx", gx_n // 2, rounds)
+    elem_keys = plane if split > 1 else [(0, dy) for dy in range(chips)]
+    elem_own = jnp.stack([passed_in_plane(elem_line, dx, dy) for dx, dy in elem_keys])
+    elem_parts = [elem_own, passed_in_gz(elem_own, 0, 1)]
 
     op_count = chain_order.shape[0]
-    plan = (line, tuple(elem_parts), tuple(fwd_parts), tuple(bwd_parts))
-    operands = [*elem_parts.values(), *fwd_parts.values(), *bwd_parts.values()]
+    plan = (line, tuple(elem_keys), tuple(fwd_parts), tuple(bwd_parts))
+    operands = [*elem_parts, *fwd_parts.values(), *bwd_parts.values()]
     return pl.pallas_call(
         functools.partial(chain_kernel, 1.0 / math.sqrt(4 * num_vecs), plan),
         out_shape=jax.ShapeDtypeStruct((op_count, 2, rows, cols), BF16),
         in_specs=[SMEM] * 4 + [VMEM] * len(operands),
         out_specs=VMEM,
         scratch_shapes=[
-            pltpu.VMEM((6, gx_n, gz_n, own_rows, num_vecs), BF16),
+            pltpu.VMEM((gx_n, gz_n, split, depth, num_vecs), BF16),
             pltpu.VMEM((6, num_vecs, num_vecs), BF16),
             pltpu.VMEM((3, 2, gy_n, 4, rows // 4, cols), BF16),
             pltpu.VMEM((4, rows, 2 * num_vecs), BF16),

time: 96.6 us -> 114 us (1.18)
  waiting for transfers between devices: 47.3 us -> 59.4 us
  starting transfers between devices: 23.1 us -> 27.1 us
  local copies, waits for them, and re-layouts: 5.72 us -> 6.88 us
    ppermute x0 -> x11, waiting for transfers between devices: none -> 35.8 us  [the longest x9 27.5 us: passed_in_plane(): return lax.ppermute(value, ('gy', 'gz'), pairs)]
    ppermute x12 -> x3, waiting for transfers between devices: 24 us -> 0.07 us  [passed_along(): return lax.ppermute(value, axis, pairs)]
    ppermute x0 -> x11, starting transfers between devices: none -> 11.8 us  [the longest x9 10.6 us: passed_in_plane(): return lax.ppermute(value, ('gy', 'gz'), pairs)]
    ppermute x12 -> x3, starting transfers between devices: 14.3 us -> 6.99 us  [passed_along(): return lax.ppermute(value, axis, pairs)]
    unnamed x10 -> x16, local copies, waits for them, and re-layouts: 1.78 us -> 6.49 us
    ppermute x13 -> x9, starting transfers between devices: 6.05 us -> 2.59 us  [passed_in_gz(): return lax.ppermute(value, 'gz', pairs)]
    ppermute x4 -> x6, starting transfers between devices: 2.79 us -> 5.76 us  [line_exchange(): gathered = jnp.concatenate([gathered, lax.ppermute(gathered, axis, pairs)])]
    slice x6 -> x0, local copies, waits for them, and re-layouts: 2.49 us -> none  [on_device(): face = lax.slice_in_dim(ordered, 0, 1, axis=1 + e).reshape(-1, num_vecs)]
  transfers between devices with their start and end apart: 29 -> 29, of which waited for: 13 -> 16; matrix products, arithmetic and copies ran while one was open for 5% -> 2% of each run, Pallas kernels for 1% -> 1%
where the time goes in v4:
time: 114 us; the launch traced here: 113 us
  waiting for transfers between devices  59.4 us (52%)
  starting transfers between devices  27.1 us (24%)
  Pallas kernels  19 us (17%)
  local copies, waits for them, and re-layouts  6.88 us (6%)
    ppermute x9, waiting for transfers between devices, passed_in_plane(): return lax.ppermute(value, ('gy', 'gz'), pairs)  27.5 us
    pallas_call x1, Pallas kernels, on_device(): pl.pallas_call(functools.partial(chain_kernel, 1.0 / math.sqrt(4 * num_ve...  16.5 us
    ppermute x6, waiting for transfers between devices, line_exchange(): gathered = jnp.concatenate([gathered, lax.ppermute(gathered, axis, pairs)])  13.5 us
    ppermute x9, starting transfers between devices, passed_in_plane(): return lax.ppermute(value, ('gy', 'gz'), pairs)  10.6 us
    ppermute x9, waiting for transfers between devices, passed_in_gz(): return lax.ppermute(value, 'gz', pairs)  10.1 us
    ppermute x2, waiting for transfers between devices, on_device(): lax.ppermute(part_at(halves, 1 - bit), 'gx', pairs)  8.26 us
    ppermute x3, starting transfers between devices, passed_along(): return lax.ppermute(value, axis, pairs)  6.99 us
    unnamed x16, local copies, waits for them, and re-layouts  6.49 us
  transfers between devices with their start and end apart: 29, of which 16 were waited for; matrix products, arithmetic and copies ran while one was open for 2% of the time, Pallas kernels for 1%

profile of v4, /device:TPU:0, one launch (start us, length us, event | category | flops | bytes accessed | tf_op | source)
XLA Modules:
  0.0 113.2 jit_solution(16283713858951097465)
XLA Ops:
  0.0 1.0 copy-done
  1.0 1.0 copy-done.1
  2.1 0.9 copy-done.4
  3.7 5.1 %collective-permute-start = (bf16[96,256]{1,0:T(8,128)(2,1)S(1)}, bf16[96,256]{1,0:T(8,128)(2,1)S(1)}, u32[]{:S(2)}, u32[]{:S(2)}) collective-permute-start(bf16[96,256]{1,0:T(8,128)(2,1)S(1)} %get-tuple-element.22), channel_id=1, source_target_pairs={{0,24},{8,0},{16,8},{24,16},{1,25},{9,1},{17,9},{25,17},{2,26},{10... | collective-permute-start | bytes 147464 | tf_op jit(solution)/shard_map/ppermute | solution.py:20
  8.8 1.5 %collective-permute-start.1 = (bf16[48,256]{1,0:T(8,128)(2,1)S(1)}, bf16[48,256]{1,0:T(8,128)(2,1)S(1)}, u32[]{:S(2)}, u32[]{:S(2)}) collective-permute-start(bf16[48,256]{1,0:T(8,128)(2,1)S(1)} %get-tuple-element.23), channel_id=1, source_target_pairs={{0,4},{4,0},{1,5},{5,1},{2,6},{6,2},{3,7},{7,3},{8,12},{12,8},{9,1... | collective-permute-start | bytes 73736 | tf_op jit(solution)/shard_map/ppermute | solution.py:20
  10.7 1.0 copy.12
  12.6 1.3 %correlate.1 = bf16[4,4,2,48,256]{4,3,2,1,0:T(8,128)(2,1)S(1)} custom-call(bf16[192,256]{1,0:T(8,128)(2,1)S(1)} %get-tuple-element.21.vec_ref, bf16[96,256]{1,0:T(8,128)(2,1)S(1)} %collective-permute-done.face0, bf16[48,256]{1,0:T(8,128)(2,1)S(1)} %collective-permute-done.1.face1, bf16[48,256]{1,0:T(8,128)(2,1)S(1)} %collective-permute-done.2.face2, ...), custom_call_target="tpu_custom_call" | custom-call | tf_op jit(solution)/shard_map/correlate/pallas_call | solution.py:397
  14.0 0.9 collective-permute-start.3
  14.9 8.2 %collective-permute-done.4 = bf16[1,2,64,512]{3,2,1,0:T(8,128)(2,1)S(1)} collective-permute-done((bf16[1,2,64,512]{3,2,1,0:T(8,128)(2,1)S(1)}, bf16[1,2,64,512]{3,2,1,0:T(8,128)(2,1)S(1)}, u32[]{:S(2)}, u32[]{:S(2)}) %collective-permute-start.4) | collective-permute-done | bytes 131104 | tf_op jit(solution)/shard_map/ppermute | solution.py:339
  23.3 1.6 %collective-permute-start.5 = (bf16[4,48,256]{2,1,0:T(8,128)(2,1)S(1)}, bf16[4,48,256]{2,1,0:T(8,128)(2,1)S(1)}, u32[]{:S(2)}, u32[]{:S(2)}) collective-permute-start(bf16[4,48,256]{2,1,0:T(8,128)(2,1)S(1)} %get-tuple-element.39), channel_id=1, source_target_pairs={{0,4},{1,5},{2,6},{3,7},{4,0},{5,1},{6,2},{7,3},{8,12},{9,13},{10,... | collective-permute-start | bytes 294920 | tf_op jit(solution)/shard_map/ppermute | solution.py:330
  24.8 1.5 %collective-permute-start.7 = (bf16[4,48,256]{2,1,0:T(8,128)(2,1)S(1)}, bf16[4,48,256]{2,1,0:T(8,128)(2,1)S(1)}, u32[]{:S(2)}, u32[]{:S(2)}) collective-permute-start(bf16[4,48,256]{2,1,0:T(8,128)(2,1)S(1)} %get-tuple-element.40), channel_id=1, source_target_pairs={{0,6},{1,7},{2,4},{3,5},{4,2},{5,3},{6,0},{7,1},{8,14},{9,15},{10,... | collective-permute-start | bytes 294920 | tf_op jit(solution)/shard_map/ppermute | solution.py:330
  26.8 1.2 %collective-permute-done.5 = bf16[4,48,256]{2,1,0:T(8,128)(2,1)S(1)} collective-permute-done((bf16[4,48,256]{2,1,0:T(8,128)(2,1)S(1)}, bf16[4,48,256]{2,1,0:T(8,128)(2,1)S(1)}, u32[]{:S(2)}, u32[]{:S(2)}) %collective-permute-start.5) | collective-permute-done | bytes 98336 | tf_op jit(solution)/shard_map/ppermute | solution.py:330
  28.1 3.2 %collective-permute-done.7 = bf16[4,48,256]{2,1,0:T(8,128)(2,1)S(1)} collective-permute-done((bf16[4,48,256]{2,1,0:T(8,128)(2,1)S(1)}, bf16[4,48,256]{2,1,0:T(8,128)(2,1)S(1)}, u32[]{:S(2)}, u32[]{:S(2)}) %collective-permute-start.7) | collective-permute-done | bytes 98336 | tf_op jit(solution)/shard_map/ppermute | solution.py:330
  31.3 1.2 %collective-permute-done.6 = bf16[4,48,256]{2,1,0:T(8,128)(2,1)S(1)} collective-permute-done((bf16[4,48,256]{2,1,0:T(8,128)(2,1)S(1)}, bf16[4,48,256]{2,1,0:T(8,128)(2,1)S(1)}, u32[]{:S(2)}, u32[]{:S(2)}) %collective-permute-start.6) | collective-permute-done | bytes 98336 | tf_op jit(solution)/shard_map/ppermute | solution.py:330
  32.6 1.6 %collective-permute-done.8 = bf16[2,2,64,512]{3,2,1,0:T(8,128)(2,1)S(1)} collective-permute-done((bf16[2,2,64,512]{3,2,1,0:T(8,128)(2,1)S(1)}, bf16[2,2,64,512]{3,2,1,0:T(8,128)(2,1)S(1)}, u32[]{:S(2)}, u32[]{:S(2)}) %collective-permute-start.8) | collective-permute-done | bytes 262176 | tf_op jit(solution)/shard_map/ppermute | solution.py:339
  34.3 1.1 collective-permute-start.9
  35.4 4.2 %collective-permute-done.9 = bf16[2,48,256]{2,1,0:T(8,128)(2,1)S(1)} collective-permute-done((bf16[2,48,256]{2,1,0:T(8,128)(2,1)S(1)}, bf16[2,48,256]{2,1,0:T(8,128)(2,1)S(1)}, u32[]{:S(2)}, u32[]{:S(2)}) %collective-permute-start.9) | collective-permute-done | bytes 49184 | tf_op jit(solution)/shard_map/ppermute | solution.py:431
  39.8 4.0 %collective-permute-done.10 = bf16[1,48,256]{2,1,0:T(8,128)(2,1)S(1)} collective-permute-done((bf16[1,48,256]{2,1,0:T(8,128)(2,1)S(1)}, bf16[1,48,256]{2,1,0:T(8,128)(2,1)S(1)}, u32[]{:S(2)}, u32[]{:S(2)}) %collective-permute-start.10) | collective-permute-done | bytes 24608 | tf_op jit(solution)/shard_map/ppermute | solution.py:431
  44.4 2.4 %collective-permute-start.24 = (bf16[1,2,64,512]{3,2,1,0:T(8,128)(2,1)S(1)}, bf16[1,2,64,512]{3,2,1,0:T(8,128)(2,1)S(1)}, u32[]{:S(2)}, u32[]{:S(2)}) collective-permute-start(bf16[1,2,64,512]{3,2,1,0:T(8,128)(2,1)S(1)} %bitcast.40), channel_id=1, source_target_pairs={{0,16},{8,24},{16,0},{24,8},{1,17},{9,25},{17,1},{25,9},{2,18},{10... | collective-permute-start | bytes 393224 | tf_op jit(solution)/shard_map/ppermute | solution.py:339
  46.8 1.8 %collective-permute-done.11 = bf16[1,48,256]{2,1,0:T(8,128)(2,1)S(1)} collective-permute-done((bf16[1,48,256]{2,1,0:T(8,128)(2,1)S(1)}, bf16[1,48,256]{2,1,0:T(8,128)(2,1)S(1)}, u32[]{:S(2)}, u32[]{:S(2)}) %collective-permute-start.11) | collective-permute-done | bytes 24608 | tf_op jit(solution)/shard_map/ppermute | solution.py:339
  48.6 1.7 %collective-permute-done.24 = bf16[1,2,64,512]{3,2,1,0:T(8,128)(2,1)S(1)} collective-permute-done((bf16[1,2,64,512]{3,2,1,0:T(8,128)(2,1)S(1)}, bf16[1,2,64,512]{3,2,1,0:T(8,128)(2,1)S(1)}, u32[]{:S(2)}, u32[]{:S(2)}) %collective-permute-start.24) | collective-permute-done | bytes 131104 | tf_op jit(solution)/shard_map/ppermute | solution.py:339
  50.3 2.8 %collective-permute-start.25 = (bf16[2,2,64,512]{3,2,1,0:T(8,128)(2,1)S(1)}, bf16[2,2,64,512]{3,2,1,0:T(8,128)(2,1)S(1)}, u32[]{:S(2)}, u32[]{:S(2)}) collective-permute-start(bf16[2,2,64,512]{3,2,1,0:T(8,128)(2,1)S(1)} %pad_maximum_fusion.4), channel_id=1, source_target_pairs={{0,8},{8,0},{16,24},{24,16},{1,9},{9,1},{17,25},{25,17},{2,10},{10... | collective-permute-start | bytes 786440 | tf_op jit(solution)/shard_map/ppermute | solution.py:339
  53.3 1.5 %collective-permute-start.14 = (bf16[4,48,256]{2,1,0:T(8,128)(2,1)S(1)}, bf16[4,48,256]{2,1,0:T(8,128)(2,1)S(1)}, u32[]{:S(2)}, u32[]{:S(2)}) collective-permute-start(bf16[4,48,256]{2,1,0:T(8,128)(2,1)S(1)} %get-tuple-element.43), channel_id=1, source_target_pairs={{0,2},{1,3},{2,0},{3,1},{4,6},{5,7},{6,4},{7,5},{8,10},{9,11},{10,... | collective-permute-start | bytes 294920 | tf_op jit(solution)/shard_map/ppermute | solution.py:330
  54.8 1.5 %collective-permute-start.13 = (bf16[4,48,256]{2,1,0:T(8,128)(2,1)S(1)}, bf16[4,48,256]{2,1,0:T(8,128)(2,1)S(1)}, u32[]{:S(2)}, u32[]{:S(2)}) collective-permute-start(bf16[4,48,256]{2,1,0:T(8,128)(2,1)S(1)} %get-tuple-element.43), channel_id=1, source_target_pairs={{0,4},{1,5},{2,6},{3,7},{4,0},{5,1},{6,2},{7,3},{8,12},{9,13},{10,... | collective-permute-start | bytes 294920 | tf_op jit(solution)/shard_map/ppermute | solution.py:330
  56.9 10.8 %collective-permute-done.14 = bf16[4,48,256]{2,1,0:T(8,128)(2,1)S(1)} collective-permute-done((bf16[4,48,256]{2,1,0:T(8,128)(2,1)S(1)}, bf16[4,48,256]{2,1,0:T(8,128)(2,1)S(1)}, u32[]{:S(2)}, u32[]{:S(2)}) %collective-permute-start.14) | collective-permute-done | bytes 98336 | tf_op jit(solution)/shard_map/ppermute | solution.py:330
  67.7 1.1 collective-permute-start.17
  68.8 2.4 %collective-permute-start.15 = (bf16[4,48,256]{2,1,0:T(8,128)(2,1)S(1)}, bf16[4,48,256]{2,1,0:T(8,128)(2,1)S(1)}, u32[]{:S(2)}, u32[]{:S(2)}) collective-permute-start(bf16[4,48,256]{2,1,0:T(8,128)(2,1)S(1)} %get-tuple-element.43), channel_id=1, source_target_pairs={{0,6},{1,7},{2,4},{3,5},{4,2},{5,3},{6,0},{7,1},{8,14},{9,15},{10,... | collective-permute-start | bytes 294920 | tf_op jit(solution)/shard_map/ppermute | solution.py:330
  71.2 11.0 %collective-permute-done.15 = bf16[4,48,256]{2,1,0:T(8,128)(2,1)S(1)} collective-permute-done((bf16[4,48,256]{2,1,0:T(8,128)(2,1)S(1)}, bf16[4,48,256]{2,1,0:T(8,128)(2,1)S(1)}, u32[]{:S(2)}, u32[]{:S(2)}) %collective-permute-start.15) | collective-permute-done | bytes 98336 | tf_op jit(solution)/shard_map/ppermute | solution.py:330
  85.5 8.0 %collective-permute-done.26.refs_11_ = bf16[4,2,64,512]{3,2,1,0:T(8,128)(2,1)} collective-permute-done((bf16[4,2,64,512]{3,2,1,0:T(8,128)(2,1)S(1)}, bf16[4,2,64,512]{3,2,1,0:T(8,128)(2,1)}, u32[]{:S(2)}, u32[]{:S(2)}) %collective-permute-start.26) | collective-permute-done | bytes 524320 | tf_op jit(solution)/shard_map/ppermute | solution.py:317
  94.3 1.4 %collective-permute-done.28.refs_13_ = bf16[4,2,64,512]{3,2,1,0:T(8,128)(2,1)} collective-permute-done((bf16[4,2,64,512]{3,2,1,0:T(8,128)(2,1)}, bf16[4,2,64,512]{3,2,1,0:T(8,128)(2,1)}, u32[]{:S(2)}, u32[]{:S(2)}) %collective-permute-start.28) | collective-permute-done | bytes 524320 | tf_op jit(solution)/shard_map/ppermute | solution.py:317
  95.7 1.0 copy-done.3
  96.7 16.5 %chain.1 = bf16[4,2,256,512]{3,2,1,0:T(8,128)(2,1)} custom-call(s32[3]{0:T(128)S(1)} %pad_add_fusion.me_ref, s32[4]{0:T(128)S(1)} %copy-done.6, f32[4,4,4]{2,1,0:T(4,128)S(1)} %copy-done.5, s32[4,2]{1,0:T(4,128)S(1)} %copy.16.chain_ref, bf16[4,4,48,256]{3,2,1,0:T(8,128)(2,1)S(1)} %pad_maximum_fusion.2.refs_0_, bf16[4,4,48,256]{3,2,1,0:T(8,128)(2,1)S(1)} %copy-done.3, ...), custom_call_target="tpu_custom_call" | custom-call | tf_op jit(solution)/shard_map/chain/pallas_call | solution.py:441
  (65 shorter events, 8.7 us)
Async XLA Ops:
  1.0 1.0 copy-start.1
  3.7 8.9 %collective-permute-start = (bf16[96,256]{1,0:T(8,128)(2,1)S(1)}, bf16[96,256]{1,0:T(8,128)(2,1)S(1)}, u32[]{:S(2)}, u32[]{:S(2)}) collective-permute-start(bf16[96,256]{1,0:T(8,128)(2,1)S(1)} %get-tuple-element.22), channel_id=1, source_target_pairs={{0,24},{8,0},{16,8},{24,16},{1,25},{9,1},{17,9},{25,17},{2,26},{10... | collective-permute-start | bytes 147464 | tf_op jit(solution)/shard_map/ppermute | solution.py:20
  8.8 3.8 %collective-permute-start.1 = (bf16[48,256]{1,0:T(8,128)(2,1)S(1)}, bf16[48,256]{1,0:T(8,128)(2,1)S(1)}, u32[]{:S(2)}, u32[]{:S(2)}) collective-permute-start(bf16[48,256]{1,0:T(8,128)(2,1)S(1)} %get-tuple-element.23), channel_id=1, source_target_pairs={{0,4},{4,0},{1,5},{5,1},{2,6},{6,2},{3,7},{7,3},{8,12},{12,8},{9,1... | collective-permute-start | bytes 73736 | tf_op jit(solution)/shard_map/ppermute | solution.py:20
  10.3 2.3 %collective-permute-start.2 = (bf16[48,256]{1,0:T(8,128)(2,1)S(1)}, bf16[48,256]{1,0:T(8,128)(2,1)S(1)}, u32[]{:S(2)}, u32[]{:S(2)}) collective-permute-start(bf16[48,256]{1,0:T(8,128)(2,1)S(1)} %get-tuple-element.24), channel_id=1, source_target_pairs={{0,3},{1,0},{2,1},{3,2},{4,7},{5,4},{6,5},{7,6},{8,11},{9,8},{10,9... | collective-permute-start | bytes 73736 | tf_op jit(solution)/shard_map/ppermute | solution.py:20
  14.0 9.1 %collective-permute-start.3 = (bf16[2,4,2,48,256]{4,3,1,2,0:T(8,128)(2,1)S(1)}, bf16[2,4,2,48,256]{4,3,1,2,0:T(8,128)(2,1)S(1)}, u32[]{:S(2)}, u32[]{:S(2)}) collective-permute-start(bf16[2,4,2,48,256]{4,3,1,2,0:T(8,128)(2,1)S(1)} %bitcast.46), channel_id=1, source_target_pairs={{0,1},{1,0},{2,3},{3,2},{4,5},{5,4},{6,7},{7,6},{8,9},{9,8},{10,11... | collective-permute-start | bytes 1179656 | tf_op jit(solution)/shard_map/ppermute | solution.py:317
  14.9 8.2 %collective-permute-start.4 = (bf16[1,2,64,512]{3,2,1,0:T(8,128)(2,1)S(1)}, bf16[1,2,64,512]{3,2,1,0:T(8,128)(2,1)S(1)}, u32[]{:S(2)}, u32[]{:S(2)}) collective-permute-start(bf16[1,2,64,512]{3,2,1,0:T(8,128)(2,1)S(1)} %bitcast.43), channel_id=1, source_target_pairs={{0,16},{8,24},{16,0},{24,8},{1,17},{9,25},{17,1},{25,9},{2,18},{10... | collective-permute-start | bytes 393224 | tf_op jit(solution)/shard_map/ppermute | solution.py:339
  23.3 4.8 %collective-permute-start.5 = (bf16[4,48,256]{2,1,0:T(8,128)(2,1)S(1)}, bf16[4,48,256]{2,1,0:T(8,128)(2,1)S(1)}, u32[]{:S(2)}, u32[]{:S(2)}) collective-permute-start(bf16[4,48,256]{2,1,0:T(8,128)(2,1)S(1)} %get-tuple-element.39), channel_id=1, source_target_pairs={{0,4},{1,5},{2,6},{3,7},{4,0},{5,1},{6,2},{7,3},{8,12},{9,13},{10,... | collective-permute-start | bytes 294920 | tf_op jit(solution)/shard_map/ppermute | solution.py:330
  24.8 6.4 %collective-permute-start.7 = (bf16[4,48,256]{2,1,0:T(8,128)(2,1)S(1)}, bf16[4,48,256]{2,1,0:T(8,128)(2,1)S(1)}, u32[]{:S(2)}, u32[]{:S(2)}) collective-permute-start(bf16[4,48,256]{2,1,0:T(8,128)(2,1)S(1)} %get-tuple-element.40), channel_id=1, source_target_pairs={{0,6},{1,7},{2,4},{3,5},{4,2},{5,3},{6,0},{7,1},{8,14},{9,15},{10,... | collective-permute-start | bytes 294920 | tf_op jit(solution)/shard_map/ppermute | solution.py:330
  26.3 6.2 %collective-permute-start.6 = (bf16[4,48,256]{2,1,0:T(8,128)(2,1)S(1)}, bf16[4,48,256]{2,1,0:T(8,128)(2,1)S(1)}, u32[]{:S(2)}, u32[]{:S(2)}) collective-permute-start(bf16[4,48,256]{2,1,0:T(8,128)(2,1)S(1)} %get-tuple-element.41), channel_id=1, source_target_pairs={{0,2},{1,3},{2,0},{3,1},{4,6},{5,7},{6,4},{7,5},{8,10},{9,11},{10,... | collective-permute-start | bytes 294920 | tf_op jit(solution)/shard_map/ppermute | solution.py:330
  26.8 7.4 %collective-permute-start.8 = (bf16[2,2,64,512]{3,2,1,0:T(8,128)(2,1)S(1)}, bf16[2,2,64,512]{3,2,1,0:T(8,128)(2,1)S(1)}, u32[]{:S(2)}, u32[]{:S(2)}) collective-permute-start(bf16[2,2,64,512]{3,2,1,0:T(8,128)(2,1)S(1)} %pad_maximum_fusion.3), channel_id=1, source_target_pairs={{0,8},{8,0},{16,24},{24,16},{1,9},{9,1},{17,25},{25,17},{2,10},{10... | collective-permute-start | bytes 786440 | tf_op jit(solution)/shard_map/ppermute | solution.py:339
  32.6 63.1 %copy-start.5 = (f32[4,4,4]{2,1,0:T(4,128)S(1)}, f32[4,4,4]{2,1,0:T(4,128)}, u32[]{:S(2)}) copy-start(f32[4,4,4]{2,1,0:T(4,128)} %spin_ref.1) | copy-start | bytes 772
  32.6 63.1 %copy-start.6 = (s32[4]{0:T(128)S(1)}, s32[4]{0:T(128)}, u32[]{:S(2)}) copy-start(s32[4]{0:T(128)} %dirs_ref.1) | copy-start | bytes 52
  34.3 5.3 %collective-permute-start.9 = (bf16[2,48,256]{2,1,0:T(8,128)(2,1)S(1)}, bf16[2,48,256]{2,1,0:T(8,128)(2,1)S(1)}, u32[]{:S(2)}, u32[]{:S(2)}) collective-permute-start(bf16[2,48,256]{2,1,0:T(8,128)(2,1)S(1)} %dynamic-slice_bitcast_fusion.3), channel_id=1, source_target_pairs={{0,16},{8,24},{16,0},{24,8},{1,17},{9,25},{17,1},{25,9},{2,18},{10... | collective-permute-start | bytes 147464 | tf_op jit(solution)/shard_map/ppermute | solution.py:431
  39.6 4.2 %collective-permute-start.10 = (bf16[1,48,256]{2,1,0:T(8,128)(2,1)S(1)}, bf16[1,48,256]{2,1,0:T(8,128)(2,1)S(1)}, u32[]{:S(2)}, u32[]{:S(2)}) collective-permute-start(bf16[1,48,256]{2,1,0:T(8,128)(2,1)S(1)} %constant_dynamic-slice_fusion), channel_id=1, source_target_pairs={{0,8},{8,0},{16,24},{24,16},{1,9},{9,1},{17,25},{25,17},{2,10},{10... | collective-permute-start | bytes 73736 | tf_op jit(solution)/shard_map/ppermute | solution.py:431
  43.8 4.8 %collective-permute-start.11 = (bf16[1,48,256]{2,1,0:T(8,128)(2,1)S(1)}, bf16[1,48,256]{2,1,0:T(8,128)(2,1)S(1)}, u32[]{:S(2)}, u32[]{:S(2)}) collective-permute-start(bf16[1,48,256]{2,1,0:T(8,128)(2,1)S(1)} %add_convert_fusion), channel_id=1, source_target_pairs={{0,16},{8,24},{16,0},{24,8},{1,17},{9,25},{17,1},{25,9},{2,18},{10... | collective-permute-start | bytes 73736 | tf_op jit(solution)/shard_map/ppermute | solution.py:339
  44.4 5.9 %collective-permute-start.24 = (bf16[1,2,64,512]{3,2,1,0:T(8,128)(2,1)S(1)}, bf16[1,2,64,512]{3,2,1,0:T(8,128)(2,1)S(1)}, u32[]{:S(2)}, u32[]{:S(2)}) collective-permute-start(bf16[1,2,64,512]{3,2,1,0:T(8,128)(2,1)S(1)} %bitcast.40), channel_id=1, source_target_pairs={{0,16},{8,24},{16,0},{24,8},{1,17},{9,25},{17,1},{25,9},{2,18},{10... | collective-permute-start | bytes 393224 | tf_op jit(solution)/shard_map/ppermute | solution.py:339
  46.8 36.0 %collective-permute-start.20 = (bf16[4,2,64,512]{3,2,1,0:T(8,128)(2,1)S(1)}, bf16[4,2,64,512]{3,2,1,0:T(8,128)(2,1)S(1)}, u32[]{:S(2)}, u32[]{:S(2)}) collective-permute-start(bf16[4,2,64,512]{3,2,1,0:T(8,128)(2,1)S(1)} %pad_maximum_fusion.refs_2_), channel_id=1, source_target_pairs={{0,1},{1,0},{2,3},{3,2},{4,5},{5,4},{6,7},{7,6},{8,9},{9,8},{10,11... | collective-permute-start | bytes 1572872 | tf_op jit(solution)/shard_map/ppermute | solution.py:317
  48.6 4.7 %collective-permute-start.12 = (bf16[2,48,256]{2,1,0:T(8,128)(2,1)S(1)}, bf16[2,48,256]{2,1,0:T(8,128)(2,1)S(1)}, u32[]{:S(2)}, u32[]{:S(2)}) collective-permute-start(bf16[2,48,256]{2,1,0:T(8,128)(2,1)S(1)} %pad_maximum_fusion.6), channel_id=1, source_target_pairs={{0,8},{8,0},{16,24},{24,16},{1,9},{9,1},{17,25},{25,17},{2,10},{10... | collective-permute-start | bytes 147464 | tf_op jit(solution)/shard_map/ppermute | solution.py:339
  50.3 18.5 %collective-permute-start.25 = (bf16[2,2,64,512]{3,2,1,0:T(8,128)(2,1)S(1)}, bf16[2,2,64,512]{3,2,1,0:T(8,128)(2,1)S(1)}, u32[]{:S(2)}, u32[]{:S(2)}) collective-permute-start(bf16[2,2,64,512]{3,2,1,0:T(8,128)(2,1)S(1)} %pad_maximum_fusion.4), channel_id=1, source_target_pairs={{0,8},{8,0},{16,24},{24,16},{1,9},{9,1},{17,25},{25,17},{2,10},{10... | collective-permute-start | bytes 786440 | tf_op jit(solution)/shard_map/ppermute | solution.py:339
  53.3 14.3 %collective-permute-start.14 = (bf16[4,48,256]{2,1,0:T(8,128)(2,1)S(1)}, bf16[4,48,256]{2,1,0:T(8,128)(2,1)S(1)}, u32[]{:S(2)}, u32[]{:S(2)}) collective-permute-start(bf16[4,48,256]{2,1,0:T(8,128)(2,1)S(1)} %get-tuple-element.43), channel_id=1, source_target_pairs={{0,2},{1,3},{2,0},{3,1},{4,6},{5,7},{6,4},{7,5},{8,10},{9,11},{10,... | collective-permute-start | bytes 294920 | tf_op jit(solution)/shard_map/ppermute | solution.py:330
  54.8 12.9 %collective-permute-start.13 = (bf16[4,48,256]{2,1,0:T(8,128)(2,1)S(1)}, bf16[4,48,256]{2,1,0:T(8,128)(2,1)S(1)}, u32[]{:S(2)}, u32[]{:S(2)}) collective-permute-start(bf16[4,48,256]{2,1,0:T(8,128)(2,1)S(1)} %get-tuple-element.43), channel_id=1, source_target_pairs={{0,4},{1,5},{2,6},{3,7},{4,0},{5,1},{6,2},{7,3},{8,12},{9,13},{10,... | collective-permute-start | bytes 294920 | tf_op jit(solution)/shard_map/ppermute | solution.py:330
  56.3 26.6 %collective-permute-start.19 = (bf16[4,2,64,512]{3,2,1,0:T(8,128)(2,1)S(1)}, bf16[4,2,64,512]{3,2,1,0:T(8,128)(2,1)S(1)}, u32[]{:S(2)}, u32[]{:S(2)}) collective-permute-start(bf16[4,2,64,512]{3,2,1,0:T(8,128)(2,1)S(1)} %pad_maximum_fusion.refs_2_), channel_id=1, source_target_pairs={{0,6},{1,7},{2,4},{3,5},{4,2},{5,3},{6,0},{7,1},{8,14},{9,15},{10,... | collective-permute-start | bytes 1572872 | tf_op jit(solution)/shard_map/ppermute | solution.py:330
  67.7 15.7 %collective-permute-start.18 = (bf16[4,2,64,512]{3,2,1,0:T(8,128)(2,1)S(1)}, bf16[4,2,64,512]{3,2,1,0:T(8,128)(2,1)S(1)}, u32[]{:S(2)}, u32[]{:S(2)}) collective-permute-start(bf16[4,2,64,512]{3,2,1,0:T(8,128)(2,1)S(1)} %pad_maximum_fusion.refs_2_), channel_id=1, source_target_pairs={{0,2},{1,3},{2,0},{3,1},{4,6},{5,7},{6,4},{7,5},{8,10},{9,11},{10,... | collective-permute-start | bytes 1572872 | tf_op jit(solution)/shard_map/ppermute | solution.py:330
  67.7 15.8 %collective-permute-start.17 = (bf16[4,2,64,512]{3,2,1,0:T(8,128)(2,1)S(1)}, bf16[4,2,64,512]{3,2,1,0:T(8,128)(2,1)S(1)}, u32[]{:S(2)}, u32[]{:S(2)}) collective-permute-start(bf16[4,2,64,512]{3,2,1,0:T(8,128)(2,1)S(1)} %pad_maximum_fusion.refs_2_), channel_id=1, source_target_pairs={{0,4},{1,5},{2,6},{3,7},{4,0},{5,1},{6,2},{7,3},{8,12},{9,13},{10,... | collective-permute-start | bytes 1572872 | tf_op jit(solution)/shard_map/ppermute | solution.py:330
  68.8 13.5 %collective-permute-start.15 = (bf16[4,48,256]{2,1,0:T(8,128)(2,1)S(1)}, bf16[4,48,256]{2,1,0:T(8,128)(2,1)S(1)}, u32[]{:S(2)}, u32[]{:S(2)}) collective-permute-start(bf16[4,48,256]{2,1,0:T(8,128)(2,1)S(1)} %get-tuple-element.43), channel_id=1, source_target_pairs={{0,6},{1,7},{2,4},{3,5},{4,2},{5,3},{6,0},{7,1},{8,14},{9,15},{10,... | collective-permute-start | bytes 294920 | tf_op jit(solution)/shard_map/ppermute | solution.py:330
  82.2 11.2 %collective-permute-start.26 = (bf16[4,2,64,512]{3,2,1,0:T(8,128)(2,1)S(1)}, bf16[4,2,64,512]{3,2,1,0:T(8,128)(2,1)}, u32[]{:S(2)}, u32[]{:S(2)}) collective-permute-start(bf16[4,2,64,512]{3,2,1,0:T(8,128)(2,1)S(1)} %pad_maximum_fusion.1.refs_10_), channel_id=1, source_target_pairs={{0,2},{1,3},{2,0},{3,1},{4,6},{5,7},{6,4},{7,5},{8,10},{9,11},{10,... | collective-permute-start | bytes 1572872 | tf_op jit(solution)/shard_map/ppermute | solution.py:317
  82.8 1.8 %collective-permute-start.16 = (bf16[4,4,48,256]{3,2,1,0:T(8,128)(2,1)S(1)}, bf16[4,4,48,256]{3,2,1,0:T(8,128)(2,1)S(1)}, u32[]{:S(2)}, u32[]{:S(2)}) collective-permute-start(bf16[4,4,48,256]{3,2,1,0:T(8,128)(2,1)S(1)} %pad_maximum_fusion.2.refs_0_), channel_id=1, source_target_pairs={{0,1},{1,0},{2,3},{3,2},{4,5},{5,4},{6,7},{7,6},{8,9},{9,8},{10,11... | collective-permute-start | bytes 1179656 | tf_op jit(solution)/shard_map/ppermute | solution.py:317
  82.9 11.4 %collective-permute-start.27 = (bf16[4,2,64,512]{3,2,1,0:T(8,128)(2,1)S(1)}, bf16[4,2,64,512]{3,2,1,0:T(8,128)(2,1)}, u32[]{:S(2)}, u32[]{:S(2)}) collective-permute-start(bf16[4,2,64,512]{3,2,1,0:T(8,128)(2,1)S(1)} %pad_maximum_fusion.1.refs_10_), channel_id=1, source_target_pairs={{0,1},{1,0},{2,3},{3,2},{4,5},{5,4},{6,7},{7,6},{8,9},{9,8},{10,11... | collective-permute-start | bytes 1572872 | tf_op jit(solution)/shard_map/ppermute | solution.py:317
  83.4 10.9 %collective-permute-start.23 = (bf16[4,2,64,512]{3,2,1,0:T(8,128)(2,1)S(1)}, bf16[4,2,64,512]{3,2,1,0:T(8,128)(2,1)}, u32[]{:S(2)}, u32[]{:S(2)}) collective-permute-start(bf16[4,2,64,512]{3,2,1,0:T(8,128)(2,1)S(1)} %collective-permute-done.19.refs_5_), channel_id=1, source_target_pairs={{0,1},{1,0},{2,3},{3,2},{4,5},{5,4},{6,7},{7,6},{8,9},{9,8},{10,11... | collective-permute-start | bytes 1572872 | tf_op jit(solution)/shard_map/ppermute | solution.py:317
  83.5 10.8 %collective-permute-start.22 = (bf16[4,2,64,512]{3,2,1,0:T(8,128)(2,1)S(1)}, bf16[4,2,64,512]{3,2,1,0:T(8,128)(2,1)}, u32[]{:S(2)}, u32[]{:S(2)}) collective-permute-start(bf16[4,2,64,512]{3,2,1,0:T(8,128)(2,1)S(1)} %collective-permute-done.18.refs_4_), channel_id=1, source_target_pairs={{0,1},{1,0},{2,3},{3,2},{4,5},{5,4},{6,7},{7,6},{8,9},{9,8},{10,11... | collective-permute-start | bytes 1572872 | tf_op jit(solution)/shard_map/ppermute | solution.py:317
  85.4 9.0 %collective-permute-start.21 = (bf16[4,2,64,512]{3,2,1,0:T(8,128)(2,1)S(1)}, bf16[4,2,64,512]{3,2,1,0:T(8,128)(2,1)}, u32[]{:S(2)}, u32[]{:S(2)}) collective-permute-start(bf16[4,2,64,512]{3,2,1,0:T(8,128)(2,1)S(1)} %collective-permute-done.17.refs_3_), channel_id=1, source_target_pairs={{0,1},{1,0},{2,3},{3,2},{4,5},{5,4},{6,7},{7,6},{8,9},{9,8},{10,11... | collective-permute-start | bytes 1572872 | tf_op jit(solution)/shard_map/ppermute | solution.py:317
  93.5 2.3 %collective-permute-start.28 = (bf16[4,2,64,512]{3,2,1,0:T(8,128)(2,1)}, bf16[4,2,64,512]{3,2,1,0:T(8,128)(2,1)}, u32[]{:S(2)}, u32[]{:S(2)}) collective-permute-start(bf16[4,2,64,512]{3,2,1,0:T(8,128)(2,1)} %collective-permute-done.26.refs_11_), channel_id=1, source_target_pairs={{0,1},{1,0},{2,3},{3,2},{4,5},{5,4},{6,7},{7,6},{8,9},{9,8},{10,11... | collective-permute-start | bytes 1572872 | tf_op jit(solution)/shard_map/ppermute | solution.py:317
  (4 other events, 3.7 us)

commit v5 on v4

--- a/solution.py
+++ b/solution.py
@@ -63,7 +63,13 @@
     return total, part, where, colour
 
 
-def first_kernel(extent, z_ref, fwd_ref, bwd_ref, eig_ref, fwd_out, bwd_out, vec_out, *face_outs):
+def first_kernel(extent, z_ref, fwd_in, bwd_in, eig_in, fwd_out, bwd_out, vec_out, *refs):
+    face_outs, (fwd_ref, bwd_ref, eig_ref, sems) = refs[:3], refs[3:]
+    pairs = ((eig_in, eig_ref), (fwd_in, fwd_ref), (bwd_in, bwd_ref))
+    copies = [pltpu.make_async_copy(source, target, sems.at[n]) for n, (source, target) in enumerate(pairs)]
+    for copy in copies:
+        copy.start()
+    copies[0].wait()
     vec = eig_ref[...].astype(F32).reshape(vec_out.shape)
     vec_out[...] = vec.astype(BF16)
     strides = (6 * extent[1] * extent[2], 6 * extent[2], 6)
@@ -89,9 +95,12 @@
         spin += jnp.where(column >= t * lane, 1, 0)
     source = 4 * (column - spin * lane) + spin
     perm = chosen(lax.broadcasted_iota(jnp.int32, (cols, cols), 0) == source).astype(BF16)
+    copies[1].wait()
     for c in range(2):
         picked = mm(select, fwd_ref[c]).astype(BF16)
         fwd_out[c] = mm(picked, perm).astype(BF16)
+    copies[2].wait()
+    for c in range(2):
         bwd_out[c] = mm(select, bwd_ref[c]).astype(BF16)
 
 
@@ -173,18 +182,49 @@
                     out_ref[z, g, n // each, to] = half[at : at + own_rows]
 
 
-def chain_kernel(inverse, plan, me_ref, dirs_ref, spin_ref, chain_ref, *refs):
-    line, elem_keys, fwd_keys, bwd_keys = plan
+def spin_groups(gz_n):
+    keys = [(dy, dc) for dc in range(2) for dy in range(gz_n // 2)]
+    if gz_n == 4:
+        return [[key] for key in keys]
+    return [[(dy, dc) for dc in range(2)] for dy in range(gz_n // 2)]
+
+
+def rows_of(parts, c, count):
+    rows = jnp.concatenate([part[:, c] for part in parts], axis=1)
+    return rows.reshape(count, rows.shape[-1])
+
+
+def right_kernel(gz_n, keys, left_ref, *refs):
+    bwd_at = dict(zip(keys, refs))
+    out_ref, b_ref = refs[len(keys) :]
+    num_vecs = b_ref.shape[0] // 8
+    op_count, _, row_count, width = out_ref.shape
+    for t, group in enumerate(spin_groups(gz_n)):
+        real, imag = [rows_of([bwd_at[key] for key in group], c, num_vecs) for c in range(2)]
+        at = 2 * t * num_vecs
+        b_ref[at : at + num_vecs, :width] = real
+        b_ref[at : at + num_vecs, width:] = imag
+        b_ref[at + num_vecs : at + 2 * num_vecs, :width] = -imag
+        b_ref[at + num_vecs : at + 2 * num_vecs, width:] = real
+    left = left_ref[...].reshape(op_count * row_count, 8 * num_vecs)
+    block = min(width, 256)
+    for c in range(2):
+        for begin in range(0, width, block):
+            at = c * width + begin
+            result = mm(left, b_ref[:, at : at + block]).astype(BF16)
+            out_ref[:, c, :, begin : begin + block] = result.reshape(op_count, row_count, block)
+
+
+def left_kernel(inverse, plan, me_ref, dirs_ref, spin_ref, chain_ref, *refs):
+    line, elem_keys, fwd_keys = plan
     elem_in, refs = refs[:2], refs[2:]
     fwd_in, refs = refs[: len(fwd_keys)], refs[len(fwd_keys) :]
-    bwd_in, refs = refs[: len(bwd_keys)], refs[len(bwd_keys) :]
-    out_ref, elem_all, elem_ref, x_ref, p_ref, q_ref, b_ref = refs
+    out_ref, elem_all, elem_ref, x_ref, p_ref = refs
     gx_n, gz_n, split, depth, num_vecs = elem_all.shape
     each = 6 // split
     own_rows = depth // each
-    width = out_ref.shape[3]
-    op_count = out_ref.shape[0]
-    row_count = out_ref.shape[2]
+    width = fwd_in[0].shape[3]
+    op_count, row_count, _ = out_ref.shape
     vec_rows = row_count // 4
     gy_n = 4 * num_vecs // width
     lane = width // 4
@@ -218,14 +258,8 @@
         whole = elem_all[:, :, n // each, rows].reshape(num_vecs, num_vecs)
         elem_ref[n] = mm(whole, perm).astype(BF16)
 
-    if halves == 1:
-        groups = [[key] for key in bwd_keys]
-    else:
-        groups = [[(dy, dc) for dc in range(2)] for dy in range(gz_n // 2)]
+    groups = spin_groups(gz_n)
     spins = [lax.div(gz_from(*group[0]), halves) for group in groups]
-
-    def rows_of(parts, c):
-        return jnp.concatenate([part[:, c] for part in parts], axis=1).reshape(num_vecs, width)
 
     first_row = pl.multiple_of(gx * vec_rows, vec_rows)
 
@@ -236,19 +270,15 @@
     imag_rows = [jnp.concatenate([own(d, 1), own(d, 0)], axis=1) for d in range(3)]
     left = jnp.concatenate([part for d in range(3) for part in (real_rows[d], imag_rows[d])], axis=0)
     fwd_at = dict(zip(fwd_keys, fwd_in))
-    bwd_at = dict(zip(bwd_keys, bwd_in))
     for t, group in enumerate(groups):
         for dx in range(gy_n):
             parts = [fwd_at[(dx,) + key] for key in group]
-            right = jnp.concatenate([rows_of(parts, c) for c in range(2)], axis=0)
+            right = jnp.concatenate([rows_of(parts, c, num_vecs) for c in range(2)], axis=0)
             result = mm(left, right).astype(BF16)
             for d in range(3):
                 for c in range(2):
                     at = (d * 2 + c) * vec_rows
                     x_ref[d, c, dx, t] = result[at : at + vec_rows]
-        for c in range(2):
-            at = (t * 2 + c) * num_vecs
-            b_ref[at : at + num_vecs, :] = rows_of([bwd_at[key] for key in group], c)
 
     row = lax.broadcasted_iota(jnp.int32, (row_count, row_count), 0)
     column = lax.broadcasted_iota(jnp.int32, (row_count, row_count), 1)
@@ -296,15 +326,7 @@
             for s in range(1, 4):
                 total += parts[s] * (spin_ref[b, s, spins[t]] * inverse)
             total = total.astype(BF16)
-            real, imag = total[:, :num_vecs], total[:, num_vecs:]
-            at = 2 * t * num_vecs
-            q_ref[:row_count, at : at + num_vecs] = real
-            q_ref[:row_count, at + num_vecs : at + 2 * num_vecs] = -imag
-            q_ref[row_count:, at : at + num_vecs] = imag
-            q_ref[row_count:, at + num_vecs : at + 2 * num_vecs] = real
-        final = mm(q_ref[...], b_ref[...]).astype(BF16)
-        out_ref[op, 0] = final[:row_count]
-        out_ref[op, 1] = final[row_count:]
+            out_ref[op, :, 2 * t * num_vecs : 2 * (t + 1) * num_vecs] = total
         return carry
 
     lax.fori_loop(0, op_count, one_operator, 0)
@@ -368,9 +390,15 @@
         functools.partial(first_kernel, extent),
         out_shape=[piece_shape, piece_shape]
         + [jax.ShapeDtypeStruct((n, num_vecs), BF16) for n in [site_rows] + face_rows],
-        in_specs=[SMEM] + [VMEM] * 3,
+        in_specs=[SMEM] + [pl.BlockSpec(memory_space=pl.ANY)] * 3,
         out_specs=[VMEM] * 6,
-        compiler_params=pltpu.CompilerParams(vmem_limit_bytes=24 * 2**20),
+        scratch_shapes=[
+            pltpu.VMEM(forward_peram.shape, BF16),
+            pltpu.VMEM(backward_peram.shape, BF16),
+            pltpu.VMEM((site_rows // 2, 2, num_vecs), BF16),
+            pltpu.SemaphoreType.DMA((3,)),
+        ],
+        compiler_params=pltpu.CompilerParams(vmem_limit_bytes=60 * 2**20),
         name="first",
     )(me[2:], forward_peram, backward_peram, eigvecs.transpose(0, 1, 2, 4, 3, 5).reshape(-1, 2, num_vecs))
     faces = [passed_along(face, axis, -1) for face, axis in zip(faces, ("gx", "gy", "gz"))]
@@ -403,9 +431,9 @@
         name="correlate",
     )(vec, *faces, *link_mats)
 
+    partial, fwd_line = lax.optimization_barrier((partial, fwd_line))
     by_core = partial.reshape((chips, 2) + partial.shape[1:])
     summed = added(part_at(by_core, core, 1), passed_in_gz(part_at(by_core, 1 - core, 1), 0, 1))
-    summed, fwd_line = lax.optimization_barrier((summed, fwd_line))
     rounds = gx_n.bit_length() - 1
     fwd_line, line = line_exchange(fwd_line, "gx", gx_n // 4, rounds - 1, line)
     plane = [(dx, dy) for dy in range(chips) for dx in range(gy_n)]
@@ -416,13 +444,12 @@
 
     summed = added(*[passed_in_plane(plane_part(dx, dy), dx, dy) for dx, dy in plane])
     summed, fwd_line, bwd_piece = lax.optimization_barrier((summed, fwd_line, bwd_piece))
-    fwd_parts = {(dx, dy, 0): passed_in_plane(fwd_line, dx, dy) for dx, dy in plane}
+
+    four = gy_n == 2 and chips == 2
+    fwd_parts = {(dx, dy, 0): passed_in_plane(fwd_line, dx, dy) for dx, dy in plane if not (four and dx and dy)}
     bwd_line, _ = line_exchange(bwd_piece, "gx", gx_n // 2, rounds)
     bwd_parts = {(dy, 0): passed_in_gz(bwd_line, dy, 0) if dy else bwd_line for dy in range(chips)}
-    for dx, dy in plane:
-        fwd_parts[dx, dy, 1] = passed_in_gz(fwd_parts[dx, dy, 0], 0, 1)
-    for dy in range(chips):
-        bwd_parts[dy, 1] = passed_in_gz(bwd_parts[dy, 0], 0, 1)
+
     distance = gx_n // 2
     while distance:
         halves = summed.reshape((2, distance) + summed.shape[1:])
@@ -430,30 +457,49 @@
         pairs = [(n, n ^ distance) for n in range(gx_n)]
         summed = added(part_at(halves, bit), lax.ppermute(part_at(halves, 1 - bit), "gx", pairs))
         distance //= 2
-    elem_line, _ = line_exchange(summed[0], "gx", gx_n // 2, rounds)
+    elem_line, offsets = line_exchange(summed[0], "gx", gx_n // 2, rounds - 1)
+    if four:
+        over_x, over_y = fwd_parts[1, 0, 0], fwd_parts[0, 1, 0]
+        elem_line, over_x, over_y = lax.optimization_barrier((elem_line, over_x, over_y))
+        fwd_parts[1, 0, 0], fwd_parts[0, 1, 0] = over_x, over_y
+        corner = [passed_in_plane(over_y[:, :1], 1, 0), passed_in_plane(over_x[:, 1:], 0, 1)]
+        fwd_parts[1, 1, 0] = jnp.concatenate(corner, axis=1)
+    elem_line, _ = line_exchange(elem_line, "gx", 1, 1, offsets)
+    for dx, dy in plane:
+        fwd_parts[dx, dy, 1] = passed_in_gz(fwd_parts[dx, dy, 0], 0, 1)
+    for dy in range(chips):
+        bwd_parts[dy, 1] = passed_in_gz(bwd_parts[dy, 0], 0, 1)
     elem_keys = plane if split > 1 else [(0, dy) for dy in range(chips)]
     elem_own = jnp.stack([passed_in_plane(elem_line, dx, dy) for dx, dy in elem_keys])
     elem_parts = [elem_own, passed_in_gz(elem_own, 0, 1)]
 
     op_count = chain_order.shape[0]
-    plan = (line, tuple(elem_keys), tuple(fwd_parts), tuple(bwd_parts))
-    operands = [*elem_parts, *fwd_parts.values(), *bwd_parts.values()]
-    return pl.pallas_call(
-        functools.partial(chain_kernel, 1.0 / math.sqrt(4 * num_vecs), plan),
-        out_shape=jax.ShapeDtypeStruct((op_count, 2, rows, cols), BF16),
-        in_specs=[SMEM] * 4 + [VMEM] * len(operands),
+    plan = (line, tuple(elem_keys), tuple(fwd_parts))
+    left_shape = (op_count, rows, 8 * num_vecs)
+    left = pl.pallas_call(
+        functools.partial(left_kernel, 1.0 / math.sqrt(4 * num_vecs), plan),
+        out_shape=jax.ShapeDtypeStruct(left_shape, BF16),
+        in_specs=[SMEM] * 4 + [VMEM] * (len(elem_parts) + len(fwd_parts)),
         out_specs=VMEM,
         scratch_shapes=[
             pltpu.VMEM((gx_n, gz_n, split, depth, num_vecs), BF16),
             pltpu.VMEM((6, num_vecs, num_vecs), BF16),
             pltpu.VMEM((3, 2, gy_n, 4, rows // 4, cols), BF16),
             pltpu.VMEM((4, rows, 2 * num_vecs), BF16),
-            pltpu.VMEM((2 * rows, 8 * num_vecs), BF16),
-            pltpu.VMEM((8 * num_vecs, cols), BF16),
         ],
-        compiler_params=pltpu.CompilerParams(vmem_limit_bytes=32 * 2**20),
-        name="chain",
-    )(me, directions, spin_mats, chain_order, *operands)
+        compiler_params=pltpu.CompilerParams(vmem_limit_bytes=24 * 2**20),
+        cost_estimate=pl.CostEstimate(flops=8 * 10**9, bytes_accessed=10**7, transcendentals=0),
+        name="left",
+    )(me, directions, spin_mats, chain_order, *elem_parts, *fwd_parts.values())
+    return pl.pallas_call(
+        functools.partial(right_kernel, gz_n, tuple(bwd_parts)),
+        out_shape=jax.ShapeDtypeStruct((op_count, 2, rows, cols), BF16),
+        in_specs=[VMEM] * (1 + len(bwd_parts)),
+        out_specs=VMEM,
+        scratch_shapes=[pltpu.VMEM((8 * num_vecs, 2 * cols), BF16)],
+        compiler_params=pltpu.CompilerParams(vmem_limit_bytes=24 * 2**20),
+        name="right",
+    )(left, *bwd_parts.values())
 
 
 def solution(mesh):

time: 114 us -> 94.5 us (0.83)
  waiting for transfers between devices: 59.4 us -> 30.1 us
  starting transfers between devices: 27.1 us -> 36 us
  local copies, waits for them, and re-layouts: 6.88 us -> 4.96 us
  Pallas kernels: 19 us -> 20.7 us
    ppermute x9 -> x10, waiting for transfers between devices: 27.5 us -> 16.5 us  [passed_in_plane(): return lax.ppermute(value, ('gy', 'gz'), pairs)]
    ppermute x9, waiting for transfers between devices: 10.1 us -> 0.13 us  [passed_in_gz(): return lax.ppermute(value, 'gz', pairs)]
    ppermute x2, waiting for transfers between devices: 8.26 us -> 0.16 us  [on_device(): lax.ppermute(part_at(halves, 1 - bit), 'gx', pairs)]
    ppermute x6, starting transfers between devices: 5.76 us -> 12.5 us  [line_exchange(): gathered = jnp.concatenate([gathered, lax.ppermute(gathered, axis, pairs)])]
    ppermute x3, starting transfers between devices: 6.99 us -> 2.97 us  [passed_along(): return lax.ppermute(value, axis, pairs)]
    ppermute x9 -> x10, starting transfers between devices: 10.6 us -> 13.6 us  [passed_in_plane(): return lax.ppermute(value, ('gy', 'gz'), pairs)]
    unnamed x16, local copies, waits for them, and re-layouts: 6.49 us -> 4.51 us
    ppermute x6, waiting for transfers between devices: 13.5 us -> 11.6 us  [line_exchange(): gathered = jnp.concatenate([gathered, lax.ppermute(gathered, axis, pairs)])]
  transfers between devices with their start and end apart: 29 -> 30, of which waited for: 16 -> 11; matrix products, arithmetic and copies ran while one was open for 2% -> 1% of each run, Pallas kernels for 1% -> 13%
where the time goes in v5:
time: 94.5 us; the launch traced here: 93.4 us
  starting transfers between devices  36 us (38%)
  waiting for transfers between devices  30.1 us (32%)
  Pallas kernels  20.7 us (22%)
  local copies, waits for them, and re-layouts  4.96 us (5%)
  other arithmetic  1.38 us (1%)
    ppermute x10, waiting for transfers between devices, passed_in_plane(): return lax.ppermute(value, ('gy', 'gz'), pairs)  16.5 us
    ppermute x10, starting transfers between devices, passed_in_plane(): return lax.ppermute(value, ('gy', 'gz'), pairs)  13.6 us
    ppermute x6, starting transfers between devices, line_exchange(): gathered = jnp.concatenate([gathered, lax.ppermute(gathered, axis, pairs)])  12.5 us
    ppermute x6, waiting for transfers between devices, line_exchange(): gathered = jnp.concatenate([gathered, lax.ppermute(gathered, axis, pairs)])  11.6 us
    pallas_call x1, Pallas kernels, on_device(): pl.pallas_call(functools.partial(left_kernel, 1.0 / math.sqrt(4 * num_vec...  10.4 us
    pallas_call x1, Pallas kernels, on_device(): pl.pallas_call(functools.partial(right_kernel, gz_n, tuple(bwd_parts)), o...  5.81 us
    unnamed x16, local copies, waits for them, and re-layouts  4.51 us
    ppermute x9, starting transfers between devices, passed_in_gz(): return lax.ppermute(value, 'gz', pairs)  4.02 us
  transfers between devices with their start and end apart: 30, of which 11 were waited for; matrix products, arithmetic and copies ran while one was open for 1% of the time, Pallas kernels for 13%

profile of v5, /device:TPU:0, one launch (start us, length us, event | category | flops | bytes accessed | tf_op | source)
XLA Modules:
  0.0 93.4 jit_solution(10029368969971412123)
XLA Ops:
  0.0 1.0 %copy.12 = f32[2,4,4,3,2,3,3]{2,1,0,6,5,4,3:T(4,128)S(1)} copy(f32[2,4,4,3,2,3,3]{2,4,6,5,3,1,0:T(2,128)} %param.8) | data formatting | bytes 13824 | tf_op args[1]
  1.2 2.6 %first.1 = (bf16[2,64,512]{2,1,0:T(8,128)(2,1)}, bf16[2,64,512]{2,1,0:T(8,128)(2,1)}, bf16[192,256]{1,0:T(8,128)(2,1)}, bf16[96,256]{1,0:T(8,128)(2,1)}, bf16[48...) custom-call(s32[1]{0:T(128)} %bitcast.2.z_ref, bf16[2,256,512]{2,1,0:T(8,128)(2,1)} %fwd_in.1, bf16[2,256,512]{2,1,0:T(8,128)(2,1)} %bwd_in.1, ...), custom_call_target="tpu_custom_call" | custom-call | tf_op jit(solution)/shard_map/first/pallas_call | solution.py:389
  3.7 4.1 %collective-permute-start.3 = (bf16[1,2,64,512]{3,2,1,0:T(8,128)(2,1)}, bf16[1,2,64,512]{3,2,1,0:T(8,128)(2,1)S(1)}, u32[]{:S(2)}, u32[]{:S(2)}) collective-permute-start(bf16[1,2,64,512]{3,2,1,0:T(8,128)(2,1)} %bitcast.46), channel_id=1, source_target_pairs={{0,16},{8,24},{16,0},{24,8},{1,17},{9,25},{17,1},{25,9},{2,18},{10... | collective-permute-start | bytes 393224 | tf_op jit(solution)/shard_map/ppermute | solution.py:361
  7.8 1.3 %collective-permute-start = (bf16[96,256]{1,0:T(8,128)(2,1)}, bf16[96,256]{1,0:T(8,128)(2,1)S(1)}, u32[]{:S(2)}, u32[]{:S(2)}) collective-permute-start(bf16[96,256]{1,0:T(8,128)(2,1)} %get-tuple-element.25), channel_id=1, source_target_pairs={{0,24},{8,0},{16,8},{24,16},{1,25},{9,1},{17,9},{25,17},{2,26},{10... | collective-permute-start | bytes 147464 | tf_op jit(solution)/shard_map/ppermute | solution.py:20
  9.2 1.5 %collective-permute-start.1 = (bf16[48,256]{1,0:T(8,128)(2,1)}, bf16[48,256]{1,0:T(8,128)(2,1)S(1)}, u32[]{:S(2)}, u32[]{:S(2)}) collective-permute-start(bf16[48,256]{1,0:T(8,128)(2,1)} %get-tuple-element.26), channel_id=1, source_target_pairs={{0,4},{4,0},{1,5},{5,1},{2,6},{6,2},{3,7},{7,3},{8,12},{12,8},{9,1... | collective-permute-start | bytes 73736 | tf_op jit(solution)/shard_map/ppermute | solution.py:20
  11.5 1.7 %collective-permute-done.1.face1 = bf16[48,256]{1,0:T(8,128)(2,1)S(1)} collective-permute-done((bf16[48,256]{1,0:T(8,128)(2,1)}, bf16[48,256]{1,0:T(8,128)(2,1)S(1)}, u32[]{:S(2)}, u32[]{:S(2)}) %collective-permute-start.1) | collective-permute-done | bytes 24608 | tf_op jit(solution)/shard_map/ppermute | solution.py:20
  14.1 1.3 %correlate.1 = bf16[4,4,2,48,256]{4,3,2,1,0:T(8,128)(2,1)S(1)} custom-call(bf16[192,256]{1,0:T(8,128)(2,1)S(1)} %copy-done, bf16[96,256]{1,0:T(8,128)(2,1)S(1)} %collective-permute-done.face0, bf16[48,256]{1,0:T(8,128)(2,1)S(1)} %collective-permute-done.1.face1, bf16[48,256]{1,0:T(8,128)(2,1)S(1)} %collective-permute-done.2.face2, ...), custom_call_target="tpu_custom_call" | custom-call | tf_op jit(solution)/shard_map/correlate/pallas_call | solution.py:425
  15.4 0.9 pad_maximum_fusion.3
  16.5 1.2 %collective-permute-start.4 = (bf16[2,4,2,48,256]{4,3,1,2,0:T(8,128)(2,1)S(1)}, bf16[2,4,2,48,256]{4,3,1,2,0:T(8,128)(2,1)S(1)}, u32[]{:S(2)}, u32[]{:S(2)}) collective-permute-start(bf16[2,4,2,48,256]{4,3,1,2,0:T(8,128)(2,1)S(1)} %bitcast.42), channel_id=1, source_target_pairs={{0,1},{1,0},{2,3},{3,2},{4,5},{5,4},{6,7},{7,6},{8,9},{9,8},{10,11... | collective-permute-start | bytes 1179656 | tf_op jit(solution)/shard_map/ppermute | solution.py:339
  17.6 1.8 %collective-permute-start.8 = (bf16[2,2,64,512]{3,2,1,0:T(8,128)(2,1)S(1)}, bf16[2,2,64,512]{3,2,1,0:T(8,128)(2,1)S(1)}, u32[]{:S(2)}, u32[]{:S(2)}) collective-permute-start(bf16[2,2,64,512]{3,2,1,0:T(8,128)(2,1)S(1)} %pad_maximum_fusion.3), channel_id=1, source_target_pairs={{0,8},{8,0},{16,24},{24,16},{1,9},{9,1},{17,25},{25,17},{2,10},{10... | collective-permute-start | bytes 786440 | tf_op jit(solution)/shard_map/ppermute | solution.py:361
  19.6 2.6 %collective-permute-start.7 = (bf16[4,48,256]{2,1,0:T(8,128)(2,1)S(1)}, bf16[4,48,256]{2,1,0:T(8,128)(2,1)S(1)}, u32[]{:S(2)}, u32[]{:S(2)}) collective-permute-start(bf16[4,48,256]{2,1,0:T(8,128)(2,1)S(1)} %get-tuple-element.46), channel_id=1, source_target_pairs={{0,6},{1,7},{2,4},{3,5},{4,2},{5,3},{6,0},{7,1},{8,14},{9,15},{10,... | collective-permute-start | bytes 294920 | tf_op jit(solution)/shard_map/ppermute | solution.py:352
  23.1 3.1 %collective-permute-done.8 = bf16[2,2,64,512]{3,2,1,0:T(8,128)(2,1)S(1)} collective-permute-done((bf16[2,2,64,512]{3,2,1,0:T(8,128)(2,1)S(1)}, bf16[2,2,64,512]{3,2,1,0:T(8,128)(2,1)S(1)}, u32[]{:S(2)}, u32[]{:S(2)}) %collective-permute-start.8) | collective-permute-done | bytes 262176 | tf_op jit(solution)/shard_map/ppermute | solution.py:361
  26.3 1.1 %collective-permute-done.6 = bf16[4,48,256]{2,1,0:T(8,128)(2,1)S(1)} collective-permute-done((bf16[4,48,256]{2,1,0:T(8,128)(2,1)S(1)}, bf16[4,48,256]{2,1,0:T(8,128)(2,1)S(1)}, u32[]{:S(2)}, u32[]{:S(2)}) %collective-permute-start.6) | collective-permute-done | bytes 98336 | tf_op jit(solution)/shard_map/ppermute | solution.py:352
  27.6 1.4 %collective-permute-start.9 = (bf16[2,48,256]{2,1,0:T(8,128)(2,1)S(1)}, bf16[2,48,256]{2,1,0:T(8,128)(2,1)S(1)}, u32[]{:S(2)}, u32[]{:S(2)}) collective-permute-start(bf16[2,48,256]{2,1,0:T(8,128)(2,1)S(1)} %dynamic-slice_bitcast_fusion.3), channel_id=1, source_target_pairs={{0,16},{8,24},{16,0},{24,8},{1,17},{9,25},{17,1},{25,9},{2,18},{10... | collective-permute-start | bytes 147464 | tf_op jit(solution)/shard_map/ppermute | solution.py:458
  29.0 1.5 %collective-permute-start.12 = (bf16[4,2,64,512]{3,2,1,0:T(8,128)(2,1)S(1)}, bf16[4,2,64,512]{3,2,1,0:T(8,128)(2,1)S(1)}, u32[]{:S(2)}, u32[]{:S(2)}) collective-permute-start(bf16[4,2,64,512]{3,2,1,0:T(8,128)(2,1)S(1)} %pad_maximum_fusion.refs_2_), channel_id=1, source_target_pairs={{0,4},{1,5},{2,6},{3,7},{4,0},{5,1},{6,2},{7,3},{8,12},{9,13},{10,... | collective-permute-start | bytes 1572872 | tf_op jit(solution)/shard_map/ppermute | solution.py:352
  31.2 1.6 %collective-permute-start.25 = (bf16[1,2,64,512]{3,2,1,0:T(8,128)(2,1)S(1)}, bf16[1,2,64,512]{3,2,1,0:T(8,128)(2,1)S(1)}, u32[]{:S(2)}, u32[]{:S(2)}) collective-permute-start(bf16[1,2,64,512]{3,2,1,0:T(8,128)(2,1)S(1)} %bitcast.39), channel_id=1, source_target_pairs={{0,16},{8,24},{16,0},{24,8},{1,17},{9,25},{17,1},{25,9},{2,18},{10... | collective-permute-start | bytes 393224 | tf_op jit(solution)/shard_map/ppermute | solution.py:361
  33.0 1.5 %collective-permute-start.10 = (bf16[1,48,256]{2,1,0:T(8,128)(2,1)S(1)}, bf16[1,48,256]{2,1,0:T(8,128)(2,1)S(1)}, u32[]{:S(2)}, u32[]{:S(2)}) collective-permute-start(bf16[1,48,256]{2,1,0:T(8,128)(2,1)S(1)} %constant_dynamic-slice_fusion), channel_id=1, source_target_pairs={{0,8},{8,0},{16,24},{24,16},{1,9},{9,1},{17,25},{25,17},{2,10},{10... | collective-permute-start | bytes 73736 | tf_op jit(solution)/shard_map/ppermute | solution.py:458
  34.5 4.8 %collective-permute-done.25 = bf16[1,2,64,512]{3,2,1,0:T(8,128)(2,1)S(1)} collective-permute-done((bf16[1,2,64,512]{3,2,1,0:T(8,128)(2,1)S(1)}, bf16[1,2,64,512]{3,2,1,0:T(8,128)(2,1)S(1)}, u32[]{:S(2)}, u32[]{:S(2)}) %collective-permute-start.25) | collective-permute-done | bytes 131104 | tf_op jit(solution)/shard_map/ppermute | solution.py:361
  39.5 2.8 %collective-permute-start.11 = (bf16[1,48,256]{2,1,0:T(8,128)(2,1)S(1)}, bf16[1,48,256]{2,1,0:T(8,128)(2,1)S(1)}, u32[]{:S(2)}, u32[]{:S(2)}) collective-permute-start(bf16[1,48,256]{2,1,0:T(8,128)(2,1)S(1)} %add_convert_fusion), channel_id=1, source_target_pairs={{0,16},{8,24},{16,0},{24,8},{1,17},{9,25},{17,1},{25,9},{2,18},{10... | collective-permute-start | bytes 73736 | tf_op jit(solution)/shard_map/ppermute | solution.py:361
  42.3 2.9 %collective-permute-done.11 = bf16[1,48,256]{2,1,0:T(8,128)(2,1)S(1)} collective-permute-done((bf16[1,48,256]{2,1,0:T(8,128)(2,1)S(1)}, bf16[1,48,256]{2,1,0:T(8,128)(2,1)S(1)}, u32[]{:S(2)}, u32[]{:S(2)}) %collective-permute-start.11) | collective-permute-done | bytes 24608 | tf_op jit(solution)/shard_map/ppermute | solution.py:361
  45.2 1.4 %collective-permute-start.19 = (bf16[4,1,64,512]{3,2,1,0:T(8,128)(2,1)S(1)}, bf16[4,1,64,512]{3,2,1,0:T(8,128)(2,1)S(1)}, u32[]{:S(2)}, u32[]{:S(2)}) collective-permute-start(bf16[4,1,64,512]{3,2,1,0:T(8,128)(2,1)S(1)} %slice.6), channel_id=1, source_target_pairs={{0,4},{1,5},{2,6},{3,7},{4,0},{5,1},{6,2},{7,3},{8,12},{9,13},{10,... | collective-permute-start | bytes 786440 | tf_op jit(solution)/shard_map/ppermute | solution.py:352
  47.4 1.3 %collective-permute-start.27 = (bf16[4,2,64,512]{3,2,1,0:T(8,128)(2,1)S(1)}, bf16[4,2,64,512]{3,2,1,0:T(8,128)(2,1)S(1)}, u32[]{:S(2)}, u32[]{:S(2)}) collective-permute-start(bf16[4,2,64,512]{3,2,1,0:T(8,128)(2,1)S(1)} %pad_maximum_fusion.1.refs_0_), channel_id=1, source_target_pairs={{0,2},{1,3},{2,0},{3,1},{4,6},{5,7},{6,4},{7,5},{8,10},{9,11},{10,... | collective-permute-start | bytes 1572872 | tf_op jit(solution)/shard_map/ppermute | solution.py:339
  48.7 2.2 %collective-permute-start.14 = (bf16[2,48,256]{2,1,0:T(8,128)(2,1)S(1)}, bf16[2,48,256]{2,1,0:T(8,128)(2,1)S(1)}, u32[]{:S(2)}, u32[]{:S(2)}) collective-permute-start(bf16[2,48,256]{2,1,0:T(8,128)(2,1)S(1)} %pad_maximum_fusion.5), channel_id=1, source_target_pairs={{0,8},{8,0},{16,24},{24,16},{1,9},{9,1},{17,25},{25,17},{2,10},{10... | collective-permute-start | bytes 147464 | tf_op jit(solution)/shard_map/ppermute | solution.py:361
  50.9 2.0 %collective-permute-start.20 = (bf16[4,1,64,512]{3,2,1,0:T(8,128)(2,1)S(1)}, bf16[4,1,64,512]{3,2,1,0:T(8,128)(2,1)S(1)}, u32[]{:S(2)}, u32[]{:S(2)}) collective-permute-start(bf16[4,1,64,512]{3,2,1,0:T(8,128)(2,1)S(1)} %slice.7), channel_id=1, source_target_pairs={{0,2},{1,3},{2,0},{3,1},{4,6},{5,7},{6,4},{7,5},{8,10},{9,11},{10,... | collective-permute-start | bytes 786440 | tf_op jit(solution)/shard_map/ppermute | solution.py:352
  53.0 1.4 %collective-permute-start.17 = (bf16[4,48,256]{2,1,0:T(8,128)(2,1)S(1)}, bf16[4,48,256]{2,1,0:T(8,128)(2,1)S(1)}, u32[]{:S(2)}, u32[]{:S(2)}) collective-permute-start(bf16[4,48,256]{2,1,0:T(8,128)(2,1)S(1)} %constant_dynamic-update-slice_fusion), channel_id=1, source_target_pairs={{0,6},{1,7},{2,4},{3,5},{4,2},{5,3},{6,0},{7,1},{8,14},{9,15},{10,... | collective-permute-start | bytes 294920 | tf_op jit(solution)/shard_map/ppermute | solution.py:352
  54.4 1.9 %collective-permute-start.16 = (bf16[4,48,256]{2,1,0:T(8,128)(2,1)S(1)}, bf16[4,48,256]{2,1,0:T(8,128)(2,1)S(1)}, u32[]{:S(2)}, u32[]{:S(2)}) collective-permute-start(bf16[4,48,256]{2,1,0:T(8,128)(2,1)S(1)} %constant_dynamic-update-slice_fusion), channel_id=1, source_target_pairs={{0,2},{1,3},{2,0},{3,1},{4,6},{5,7},{6,4},{7,5},{8,10},{9,11},{10,... | collective-permute-start | bytes 294920 | tf_op jit(solution)/shard_map/ppermute | solution.py:352
  56.3 12.4 %collective-permute-done.20 = bf16[4,1,64,512]{3,2,1,0:T(8,128)(2,1)S(1)} collective-permute-done((bf16[4,1,64,512]{3,2,1,0:T(8,128)(2,1)S(1)}, bf16[4,1,64,512]{3,2,1,0:T(8,128)(2,1)S(1)}, u32[]{:S(2)}, u32[]{:S(2)}) %collective-permute-start.20) | collective-permute-done | bytes 262176 | tf_op jit(solution)/shard_map/ppermute | solution.py:352
  68.7 1.1 %collective-permute-start.15 = (bf16[4,48,256]{2,1,0:T(8,128)(2,1)S(1)}, bf16[4,48,256]{2,1,0:T(8,128)(2,1)S(1)}, u32[]{:S(2)}, u32[]{:S(2)}) collective-permute-start(bf16[4,48,256]{2,1,0:T(8,128)(2,1)S(1)} %constant_dynamic-update-slice_fusion), channel_id=1, source_target_pairs={{0,4},{1,5},{2,6},{3,7},{4,0},{5,1},{6,2},{7,3},{8,12},{9,13},{10,... | collective-permute-start | bytes 294920 | tf_op jit(solution)/shard_map/ppermute | solution.py:352
  70.3 2.9 %collective-permute-done.15 = bf16[4,48,256]{2,1,0:T(8,128)(2,1)S(1)} collective-permute-done((bf16[4,48,256]{2,1,0:T(8,128)(2,1)S(1)}, bf16[4,48,256]{2,1,0:T(8,128)(2,1)S(1)}, u32[]{:S(2)}, u32[]{:S(2)}) %collective-permute-start.15) | collective-permute-done | bytes 98336 | tf_op jit(solution)/shard_map/ppermute | solution.py:352
  76.1 1.0 %copy-done.2 = bf16[4,2,64,512]{3,2,1,0:T(8,128)(2,1)S(1)} copy-done((bf16[4,2,64,512]{3,2,1,0:T(8,128)(2,1)S(1)}, bf16[4,2,64,512]{3,2,1,0:T(8,128)(2,1)}, u32[]{:S(2)}) %copy-start.2) | copy-done | bytes 524312
  77.2 10.4 %left.1.left_ref = bf16[4,256,2048]{2,1,0:T(8,128)(2,1)S(1)} custom-call(s32[3]{0:T(128)S(1)} %pad_add_fusion.me_ref, s32[4]{0:T(128)S(1)} %copy-done.4, f32[4,4,4]{2,1,0:T(4,128)S(1)} %copy-done.3, s32[4,2]{1,0:T(4,128)S(1)} %copy.16.chain_ref, bf16[4,4,48,256]{3,2,1,0:T(8,128)(2,1)S(1)} %pad_maximum_fusion.2.refs_0_, ...), custom_call_target="tpu_custom_call" | custom-call | flops 8000000000 | bytes 10000000 | tf_op jit(solution)/shard_map/left/pallas_call | solution.py:479
  87.6 5.8 %right.1 = bf16[4,2,256,512]{3,2,1,0:T(8,128)(2,1)} custom-call(bf16[4,256,2048]{2,1,0:T(8,128)(2,1)S(1)} %left.1.left_ref, bf16[4,2,64,512]{3,2,1,0:T(8,128)(2,1)S(1)} %pad_maximum_fusion.1.refs_0_, bf16[4,2,64,512]{3,2,1,0:T(8,128)(2,1)S(1)} %collective-permute-done.27.refs_1_, bf16[4,2,64,512]{3,2,1,0:T(8,128)(2,1)S(1)} %collective-permute-done.28.refs_2_, ...), custom_call_target="tpu_custom_call" | custom-call | tf_op jit(solution)/shard_map/right/pallas_call | solution.py:494
  (71 shorter events, 8.7 us)
Async XLA Ops:
  3.7 11.7 %collective-permute-start.3 = (bf16[1,2,64,512]{3,2,1,0:T(8,128)(2,1)}, bf16[1,2,64,512]{3,2,1,0:T(8,128)(2,1)S(1)}, u32[]{:S(2)}, u32[]{:S(2)}) collective-permute-start(bf16[1,2,64,512]{3,2,1,0:T(8,128)(2,1)} %bitcast.46), channel_id=1, source_target_pairs={{0,16},{8,24},{16,0},{24,8},{1,17},{9,25},{17,1},{25,9},{2,18},{10... | collective-permute-start | bytes 393224 | tf_op jit(solution)/shard_map/ppermute | solution.py:361
  7.8 5.4 %collective-permute-start = (bf16[96,256]{1,0:T(8,128)(2,1)}, bf16[96,256]{1,0:T(8,128)(2,1)S(1)}, u32[]{:S(2)}, u32[]{:S(2)}) collective-permute-start(bf16[96,256]{1,0:T(8,128)(2,1)} %get-tuple-element.25), channel_id=1, source_target_pairs={{0,24},{8,0},{16,8},{24,16},{1,25},{9,1},{17,9},{25,17},{2,26},{10... | collective-permute-start | bytes 147464 | tf_op jit(solution)/shard_map/ppermute | solution.py:20
  9.2 4.0 %collective-permute-start.1 = (bf16[48,256]{1,0:T(8,128)(2,1)}, bf16[48,256]{1,0:T(8,128)(2,1)S(1)}, u32[]{:S(2)}, u32[]{:S(2)}) collective-permute-start(bf16[48,256]{1,0:T(8,128)(2,1)} %get-tuple-element.26), channel_id=1, source_target_pairs={{0,4},{4,0},{1,5},{5,1},{2,6},{6,2},{3,7},{7,3},{8,12},{12,8},{9,1... | collective-permute-start | bytes 73736 | tf_op jit(solution)/shard_map/ppermute | solution.py:20
  10.7 2.5 %collective-permute-start.2 = (bf16[48,256]{1,0:T(8,128)(2,1)}, bf16[48,256]{1,0:T(8,128)(2,1)S(1)}, u32[]{:S(2)}, u32[]{:S(2)}) collective-permute-start(bf16[48,256]{1,0:T(8,128)(2,1)} %get-tuple-element.27), channel_id=1, source_target_pairs={{0,3},{1,0},{2,1},{3,2},{4,7},{5,4},{6,5},{7,6},{8,11},{9,8},{10,9... | collective-permute-start | bytes 73736 | tf_op jit(solution)/shard_map/ppermute | solution.py:20
  16.5 3.0 %collective-permute-start.4 = (bf16[2,4,2,48,256]{4,3,1,2,0:T(8,128)(2,1)S(1)}, bf16[2,4,2,48,256]{4,3,1,2,0:T(8,128)(2,1)S(1)}, u32[]{:S(2)}, u32[]{:S(2)}) collective-permute-start(bf16[2,4,2,48,256]{4,3,1,2,0:T(8,128)(2,1)S(1)} %bitcast.42), channel_id=1, source_target_pairs={{0,1},{1,0},{2,3},{3,2},{4,5},{5,4},{6,7},{7,6},{8,9},{9,8},{10,11... | collective-permute-start | bytes 1179656 | tf_op jit(solution)/shard_map/ppermute | solution.py:339
  17.6 8.6 %collective-permute-start.8 = (bf16[2,2,64,512]{3,2,1,0:T(8,128)(2,1)S(1)}, bf16[2,2,64,512]{3,2,1,0:T(8,128)(2,1)S(1)}, u32[]{:S(2)}, u32[]{:S(2)}) collective-permute-start(bf16[2,2,64,512]{3,2,1,0:T(8,128)(2,1)S(1)} %pad_maximum_fusion.3), channel_id=1, source_target_pairs={{0,8},{8,0},{16,24},{24,16},{1,9},{9,1},{17,25},{25,17},{2,10},{10... | collective-permute-start | bytes 786440 | tf_op jit(solution)/shard_map/ppermute | solution.py:361
  19.4 56.7 %copy-start.3 = (f32[4,4,4]{2,1,0:T(4,128)S(1)}, f32[4,4,4]{2,1,0:T(4,128)}, u32[]{:S(2)}) copy-start(f32[4,4,4]{2,1,0:T(4,128)} %spin_ref.1) | copy-start | bytes 772
  19.4 56.7 %copy-start.4 = (s32[4]{0:T(128)S(1)}, s32[4]{0:T(128)}, u32[]{:S(2)}) copy-start(s32[4]{0:T(128)} %dirs_ref.1) | copy-start | bytes 52
  19.6 6.7 %collective-permute-start.7 = (bf16[4,48,256]{2,1,0:T(8,128)(2,1)S(1)}, bf16[4,48,256]{2,1,0:T(8,128)(2,1)S(1)}, u32[]{:S(2)}, u32[]{:S(2)}) collective-permute-start(bf16[4,48,256]{2,1,0:T(8,128)(2,1)S(1)} %get-tuple-element.46), channel_id=1, source_target_pairs={{0,6},{1,7},{2,4},{3,5},{4,2},{5,3},{6,0},{7,1},{8,14},{9,15},{10,... | collective-permute-start | bytes 294920 | tf_op jit(solution)/shard_map/ppermute | solution.py:352
  22.1 5.3 %collective-permute-start.6 = (bf16[4,48,256]{2,1,0:T(8,128)(2,1)S(1)}, bf16[4,48,256]{2,1,0:T(8,128)(2,1)S(1)}, u32[]{:S(2)}, u32[]{:S(2)}) collective-permute-start(bf16[4,48,256]{2,1,0:T(8,128)(2,1)S(1)} %get-tuple-element.47), channel_id=1, source_target_pairs={{0,2},{1,3},{2,0},{3,1},{4,6},{5,7},{6,4},{7,5},{8,10},{9,11},{10,... | collective-permute-start | bytes 294920 | tf_op jit(solution)/shard_map/ppermute | solution.py:352
  22.6 4.9 %collective-permute-start.5 = (bf16[4,48,256]{2,1,0:T(8,128)(2,1)S(1)}, bf16[4,48,256]{2,1,0:T(8,128)(2,1)S(1)}, u32[]{:S(2)}, u32[]{:S(2)}) collective-permute-start(bf16[4,48,256]{2,1,0:T(8,128)(2,1)S(1)} %get-tuple-element.45), channel_id=1, source_target_pairs={{0,4},{1,5},{2,6},{3,7},{4,0},{5,1},{6,2},{7,3},{8,12},{9,13},{10,... | collective-permute-start | bytes 294920 | tf_op jit(solution)/shard_map/ppermute | solution.py:352
  27.6 5.4 %collective-permute-start.9 = (bf16[2,48,256]{2,1,0:T(8,128)(2,1)S(1)}, bf16[2,48,256]{2,1,0:T(8,128)(2,1)S(1)}, u32[]{:S(2)}, u32[]{:S(2)}) collective-permute-start(bf16[2,48,256]{2,1,0:T(8,128)(2,1)S(1)} %dynamic-slice_bitcast_fusion.3), channel_id=1, source_target_pairs={{0,16},{8,24},{16,0},{24,8},{1,17},{9,25},{17,1},{25,9},{2,18},{10... | collective-permute-start | bytes 147464 | tf_op jit(solution)/shard_map/ppermute | solution.py:458
  29.0 16.2 %collective-permute-start.12 = (bf16[4,2,64,512]{3,2,1,0:T(8,128)(2,1)S(1)}, bf16[4,2,64,512]{3,2,1,0:T(8,128)(2,1)S(1)}, u32[]{:S(2)}, u32[]{:S(2)}) collective-permute-start(bf16[4,2,64,512]{3,2,1,0:T(8,128)(2,1)S(1)} %pad_maximum_fusion.refs_2_), channel_id=1, source_target_pairs={{0,4},{1,5},{2,6},{3,7},{4,0},{5,1},{6,2},{7,3},{8,12},{9,13},{10,... | collective-permute-start | bytes 1572872 | tf_op jit(solution)/shard_map/ppermute | solution.py:352
  30.5 14.7 %collective-permute-start.13 = (bf16[4,2,64,512]{3,2,1,0:T(8,128)(2,1)S(1)}, bf16[4,2,64,512]{3,2,1,0:T(8,128)(2,1)S(1)}, u32[]{:S(2)}, u32[]{:S(2)}) collective-permute-start(bf16[4,2,64,512]{3,2,1,0:T(8,128)(2,1)S(1)} %pad_maximum_fusion.refs_2_), channel_id=1, source_target_pairs={{0,2},{1,3},{2,0},{3,1},{4,6},{5,7},{6,4},{7,5},{8,10},{9,11},{10,... | collective-permute-start | bytes 1572872 | tf_op jit(solution)/shard_map/ppermute | solution.py:352
  31.2 8.1 %collective-permute-start.25 = (bf16[1,2,64,512]{3,2,1,0:T(8,128)(2,1)S(1)}, bf16[1,2,64,512]{3,2,1,0:T(8,128)(2,1)S(1)}, u32[]{:S(2)}, u32[]{:S(2)}) collective-permute-start(bf16[1,2,64,512]{3,2,1,0:T(8,128)(2,1)S(1)} %bitcast.39), channel_id=1, source_target_pairs={{0,16},{8,24},{16,0},{24,8},{1,17},{9,25},{17,1},{25,9},{2,18},{10... | collective-permute-start | bytes 393224 | tf_op jit(solution)/shard_map/ppermute | solution.py:361
  33.0 6.5 %collective-permute-start.10 = (bf16[1,48,256]{2,1,0:T(8,128)(2,1)S(1)}, bf16[1,48,256]{2,1,0:T(8,128)(2,1)S(1)}, u32[]{:S(2)}, u32[]{:S(2)}) collective-permute-start(bf16[1,48,256]{2,1,0:T(8,128)(2,1)S(1)} %constant_dynamic-slice_fusion), channel_id=1, source_target_pairs={{0,8},{8,0},{16,24},{24,16},{1,9},{9,1},{17,25},{25,17},{2,10},{10... | collective-permute-start | bytes 73736 | tf_op jit(solution)/shard_map/ppermute | solution.py:458
  39.4 8.0 %collective-permute-start.26 = (bf16[2,2,64,512]{3,2,1,0:T(8,128)(2,1)S(1)}, bf16[2,2,64,512]{3,2,1,0:T(8,128)(2,1)S(1)}, u32[]{:S(2)}, u32[]{:S(2)}) collective-permute-start(bf16[2,2,64,512]{3,2,1,0:T(8,128)(2,1)S(1)} %pad_maximum_fusion.4), channel_id=1, source_target_pairs={{0,8},{8,0},{16,24},{24,16},{1,9},{9,1},{17,25},{25,17},{2,10},{10... | collective-permute-start | bytes 786440 | tf_op jit(solution)/shard_map/ppermute | solution.py:361
  39.5 5.7 %collective-permute-start.11 = (bf16[1,48,256]{2,1,0:T(8,128)(2,1)S(1)}, bf16[1,48,256]{2,1,0:T(8,128)(2,1)S(1)}, u32[]{:S(2)}, u32[]{:S(2)}) collective-permute-start(bf16[1,48,256]{2,1,0:T(8,128)(2,1)S(1)} %add_convert_fusion), channel_id=1, source_target_pairs={{0,16},{8,24},{16,0},{24,8},{1,17},{9,25},{17,1},{25,9},{2,18},{10... | collective-permute-start | bytes 73736 | tf_op jit(solution)/shard_map/ppermute | solution.py:361
  42.3 31.1 %collective-permute-start.21 = (bf16[4,2,64,512]{3,2,1,0:T(8,128)(2,1)S(1)}, bf16[4,2,64,512]{3,2,1,0:T(8,128)(2,1)S(1)}, u32[]{:S(2)}, u32[]{:S(2)}) collective-permute-start(bf16[4,2,64,512]{3,2,1,0:T(8,128)(2,1)S(1)} %pad_maximum_fusion.refs_2_), channel_id=1, source_target_pairs={{0,1},{1,0},{2,3},{3,2},{4,5},{5,4},{6,7},{7,6},{8,9},{9,8},{10,11... | collective-permute-start | bytes 1572872 | tf_op jit(solution)/shard_map/ppermute | solution.py:339
  45.2 9.2 %collective-permute-start.19 = (bf16[4,1,64,512]{3,2,1,0:T(8,128)(2,1)S(1)}, bf16[4,1,64,512]{3,2,1,0:T(8,128)(2,1)S(1)}, u32[]{:S(2)}, u32[]{:S(2)}) collective-permute-start(bf16[4,1,64,512]{3,2,1,0:T(8,128)(2,1)S(1)} %slice.6), channel_id=1, source_target_pairs={{0,4},{1,5},{2,6},{3,7},{4,0},{5,1},{6,2},{7,3},{8,12},{9,13},{10,... | collective-permute-start | bytes 786440 | tf_op jit(solution)/shard_map/ppermute | solution.py:352
  47.4 28.1 %collective-permute-start.27 = (bf16[4,2,64,512]{3,2,1,0:T(8,128)(2,1)S(1)}, bf16[4,2,64,512]{3,2,1,0:T(8,128)(2,1)S(1)}, u32[]{:S(2)}, u32[]{:S(2)}) collective-permute-start(bf16[4,2,64,512]{3,2,1,0:T(8,128)(2,1)S(1)} %pad_maximum_fusion.1.refs_0_), channel_id=1, source_target_pairs={{0,2},{1,3},{2,0},{3,1},{4,6},{5,7},{6,4},{7,5},{8,10},{9,11},{10,... | collective-permute-start | bytes 1572872 | tf_op jit(solution)/shard_map/ppermute | solution.py:339
  48.7 4.3 %collective-permute-start.14 = (bf16[2,48,256]{2,1,0:T(8,128)(2,1)S(1)}, bf16[2,48,256]{2,1,0:T(8,128)(2,1)S(1)}, u32[]{:S(2)}, u32[]{:S(2)}) collective-permute-start(bf16[2,48,256]{2,1,0:T(8,128)(2,1)S(1)} %pad_maximum_fusion.5), channel_id=1, source_target_pairs={{0,8},{8,0},{16,24},{24,16},{1,9},{9,1},{17,25},{25,17},{2,10},{10... | collective-permute-start | bytes 147464 | tf_op jit(solution)/shard_map/ppermute | solution.py:361
  50.9 17.7 %collective-permute-start.20 = (bf16[4,1,64,512]{3,2,1,0:T(8,128)(2,1)S(1)}, bf16[4,1,64,512]{3,2,1,0:T(8,128)(2,1)S(1)}, u32[]{:S(2)}, u32[]{:S(2)}) collective-permute-start(bf16[4,1,64,512]{3,2,1,0:T(8,128)(2,1)S(1)} %slice.7), channel_id=1, source_target_pairs={{0,2},{1,3},{2,0},{3,1},{4,6},{5,7},{6,4},{7,5},{8,10},{9,11},{10,... | collective-permute-start | bytes 786440 | tf_op jit(solution)/shard_map/ppermute | solution.py:352
  53.0 16.7 %collective-permute-start.17 = (bf16[4,48,256]{2,1,0:T(8,128)(2,1)S(1)}, bf16[4,48,256]{2,1,0:T(8,128)(2,1)S(1)}, u32[]{:S(2)}, u32[]{:S(2)}) collective-permute-start(bf16[4,48,256]{2,1,0:T(8,128)(2,1)S(1)} %constant_dynamic-update-slice_fusion), channel_id=1, source_target_pairs={{0,6},{1,7},{2,4},{3,5},{4,2},{5,3},{6,0},{7,1},{8,14},{9,15},{10,... | collective-permute-start | bytes 294920 | tf_op jit(solution)/shard_map/ppermute | solution.py:352
  54.4 15.4 %collective-permute-start.16 = (bf16[4,48,256]{2,1,0:T(8,128)(2,1)S(1)}, bf16[4,48,256]{2,1,0:T(8,128)(2,1)S(1)}, u32[]{:S(2)}, u32[]{:S(2)}) collective-permute-start(bf16[4,48,256]{2,1,0:T(8,128)(2,1)S(1)} %constant_dynamic-update-slice_fusion), channel_id=1, source_target_pairs={{0,2},{1,3},{2,0},{3,1},{4,6},{5,7},{6,4},{7,5},{8,10},{9,11},{10,... | collective-permute-start | bytes 294920 | tf_op jit(solution)/shard_map/ppermute | solution.py:352
  68.7 4.6 %collective-permute-start.15 = (bf16[4,48,256]{2,1,0:T(8,128)(2,1)S(1)}, bf16[4,48,256]{2,1,0:T(8,128)(2,1)S(1)}, u32[]{:S(2)}, u32[]{:S(2)}) collective-permute-start(bf16[4,48,256]{2,1,0:T(8,128)(2,1)S(1)} %constant_dynamic-update-slice_fusion), channel_id=1, source_target_pairs={{0,4},{1,5},{2,6},{3,7},{4,0},{5,1},{6,2},{7,3},{8,12},{9,13},{10,... | collective-permute-start | bytes 294920 | tf_op jit(solution)/shard_map/ppermute | solution.py:352
  69.7 5.8 %collective-permute-start.22 = (bf16[4,2,64,512]{3,2,1,0:T(8,128)(2,1)S(1)}, bf16[4,2,64,512]{3,2,1,0:T(8,128)(2,1)}, u32[]{:S(2)}, u32[]{:S(2)}) collective-permute-start(bf16[4,2,64,512]{3,2,1,0:T(8,128)(2,1)S(1)} %collective-permute-done.12.refs_3_), channel_id=1, source_target_pairs={{0,1},{1,0},{2,3},{3,2},{4,5},{5,4},{6,7},{7,6},{8,9},{9,8},{10,11... | collective-permute-start | bytes 1572872 | tf_op jit(solution)/shard_map/ppermute | solution.py:339
  69.8 6.2 %collective-permute-start.23 = (bf16[4,2,64,512]{3,2,1,0:T(8,128)(2,1)S(1)}, bf16[4,2,64,512]{3,2,1,0:T(8,128)(2,1)}, u32[]{:S(2)}, u32[]{:S(2)}) collective-permute-start(bf16[4,2,64,512]{3,2,1,0:T(8,128)(2,1)S(1)} %collective-permute-done.13.refs_4_), channel_id=1, source_target_pairs={{0,1},{1,0},{2,3},{3,2},{4,5},{5,4},{6,7},{7,6},{8,9},{9,8},{10,11... | collective-permute-start | bytes 1572872 | tf_op jit(solution)/shard_map/ppermute | solution.py:339
  73.3 2.9 %collective-permute-start.24 = (bf16[4,2,64,512]{3,2,1,0:T(8,128)(2,1)S(1)}, bf16[4,2,64,512]{3,2,1,0:T(8,128)(2,1)}, u32[]{:S(2)}, u32[]{:S(2)}) collective-permute-start(bf16[4,2,64,512]{3,2,1,0:T(8,128)(2,1)S(1)} %constant_dynamic-update-slice_fusion.2.refs_5_), channel_id=1, source_target_pairs={{0,1},{1,0},{2,3},{3,2},{4,5},{5,4},{6,7},{7,6},{8,9},{9,8},{10,11... | collective-permute-start | bytes 1572872 | tf_op jit(solution)/shard_map/ppermute | solution.py:339
  74.1 2.0 %collective-permute-start.18 = (bf16[4,4,48,256]{3,2,1,0:T(8,128)(2,1)S(1)}, bf16[4,4,48,256]{3,2,1,0:T(8,128)(2,1)}, u32[]{:S(2)}, u32[]{:S(2)}) collective-permute-start(bf16[4,4,48,256]{3,2,1,0:T(8,128)(2,1)S(1)} %pad_maximum_fusion.2.refs_0_), channel_id=1, source_target_pairs={{0,1},{1,0},{2,3},{3,2},{4,5},{5,4},{6,7},{7,6},{8,9},{9,8},{10,11... | collective-permute-start | bytes 1179656 | tf_op jit(solution)/shard_map/ppermute | solution.py:339
  75.5 12.1 %collective-permute-start.28 = (bf16[4,2,64,512]{3,2,1,0:T(8,128)(2,1)S(1)}, bf16[4,2,64,512]{3,2,1,0:T(8,128)(2,1)S(1)}, u32[]{:S(2)}, u32[]{:S(2)}) collective-permute-start(bf16[4,2,64,512]{3,2,1,0:T(8,128)(2,1)S(1)} %pad_maximum_fusion.1.refs_0_), channel_id=1, source_target_pairs={{0,1},{1,0},{2,3},{3,2},{4,5},{5,4},{6,7},{7,6},{8,9},{9,8},{10,11... | collective-permute-start | bytes 1572872 | tf_op jit(solution)/shard_map/ppermute | solution.py:339
  75.5 12.1 %collective-permute-start.29 = (bf16[4,2,64,512]{3,2,1,0:T(8,128)(2,1)S(1)}, bf16[4,2,64,512]{3,2,1,0:T(8,128)(2,1)S(1)}, u32[]{:S(2)}, u32[]{:S(2)}) collective-permute-start(bf16[4,2,64,512]{3,2,1,0:T(8,128)(2,1)S(1)} %collective-permute-done.27.refs_1_), channel_id=1, source_target_pairs={{0,1},{1,0},{2,3},{3,2},{4,5},{5,4},{6,7},{7,6},{8,9},{9,8},{10,11... | collective-permute-start | bytes 1572872 | tf_op jit(solution)/shard_map/ppermute | solution.py:339
  (4 other events, 19.8 us)

commit v6 on v5

--- a/solution.py
+++ b/solution.py
@@ -63,13 +63,7 @@
     return total, part, where, colour
 
 
-def first_kernel(extent, z_ref, fwd_in, bwd_in, eig_in, fwd_out, bwd_out, vec_out, *refs):
-    face_outs, (fwd_ref, bwd_ref, eig_ref, sems) = refs[:3], refs[3:]
-    pairs = ((eig_in, eig_ref), (fwd_in, fwd_ref), (bwd_in, bwd_ref))
-    copies = [pltpu.make_async_copy(source, target, sems.at[n]) for n, (source, target) in enumerate(pairs)]
-    for copy in copies:
-        copy.start()
-    copies[0].wait()
+def rows_kernel(extent, eig_ref, vec_out, *face_outs):
     vec = eig_ref[...].astype(F32).reshape(vec_out.shape)
     vec_out[...] = vec.astype(BF16)
     strides = (6 * extent[1] * extent[2], 6 * extent[2], 6)
@@ -79,8 +73,15 @@
             begins = [at + n * strides[d] for at in begins for n in range(extent[d])]
         runs = [vec[at : at + strides[e]] for at in begins]
         out[...] = (jnp.concatenate(runs, axis=0) if e else runs[0]).astype(BF16)
+
+
+def pieces_kernel(z_ref, fwd_in, bwd_in, both_out, fwd_ref, bwd_ref, sems):
+    pairs = ((fwd_in, fwd_ref), (bwd_in, bwd_ref))
+    copies = [pltpu.make_async_copy(source, target, sems.at[n]) for n, (source, target) in enumerate(pairs)]
+    for copy in copies:
+        copy.start()
     rows, cols = fwd_ref.shape[1:]
-    piece = fwd_out.shape[1]
+    piece = both_out.shape[2]
     per_spin = rows // 4
     lane = cols // 4
     flat = lax.broadcasted_iota(jnp.int32, (piece, 1), 0) + z_ref[0] * piece
@@ -95,13 +96,13 @@
         spin += jnp.where(column >= t * lane, 1, 0)
     source = 4 * (column - spin * lane) + spin
     perm = chosen(lax.broadcasted_iota(jnp.int32, (cols, cols), 0) == source).astype(BF16)
+    copies[0].wait()
+    for c in range(2):
+        picked = mm(select, fwd_ref[c]).astype(BF16)
+        both_out[0, c] = mm(picked, perm).astype(BF16)
     copies[1].wait()
     for c in range(2):
-        picked = mm(select, fwd_ref[c]).astype(BF16)
-        fwd_out[c] = mm(picked, perm).astype(BF16)
-    copies[2].wait()
-    for c in range(2):
-        bwd_out[c] = mm(select, bwd_ref[c]).astype(BF16)
+        both_out[1, c] = mm(select, bwd_ref[c]).astype(BF16)
 
 
 def links_kernel(extent, link_ref, *outs):
@@ -280,23 +281,24 @@
                     at = (d * 2 + c) * vec_rows
                     x_ref[d, c, dx, t] = result[at : at + vec_rows]
 
-    row = lax.broadcasted_iota(jnp.int32, (row_count, row_count), 0)
-    column = lax.broadcasted_iota(jnp.int32, (row_count, row_count), 1)
+    row = lax.broadcasted_iota(jnp.int32, (row_count, 1), 0)
+    column = lax.broadcasted_iota(jnp.int32, (1, row_count), 1)
     row_spin = lax.rem(row, 4)
     diagonal = lax.div(row, 4) == lax.rem(column, vec_rows)
     column_spin = lax.div(column, vec_rows)
     blocks = [pl.multiple_of(back(gy, dx, gy_n) * lane, lane) for dx in range(gy_n)]
 
-    def one_operator(op, carry):
+    def one_operator(op):
         a = chain_ref[op, 0]
         b = chain_ref[op, 1]
         dir_a = dirs_ref[a]
         dir_b = dirs_ref[b]
-        mix = jnp.zeros((row_count, row_count), F32)
+        mix = None
         for t in range(4):
-            in_t = column_spin == t
-            for s in range(4):
-                mix = jnp.where(in_t & (row_spin == s), spin_ref[a, s, spins[t]], mix)
+            weight = jnp.full((row_count, 1), spin_ref[a, 0, spins[t]])
+            for s in range(1, 4):
+                weight = jnp.where(row_spin == s, spin_ref[a, s, spins[t]], weight)
+            mix = weight if mix is None else jnp.where(column_spin == t, weight, mix)
         mix = jnp.where(diagonal, mix, 0.0)
         high = mix.astype(BF16)
         low = (mix - high.astype(F32)).astype(BF16)
@@ -327,9 +329,9 @@
                 total += parts[s] * (spin_ref[b, s, spins[t]] * inverse)
             total = total.astype(BF16)
             out_ref[op, :, 2 * t * num_vecs : 2 * (t + 1) * num_vecs] = total
-        return carry
-
-    lax.fori_loop(0, op_count, one_operator, 0)
+
+    for op in range(op_count):
+        one_operator(op)
 
 
 def passed_in_gz(value, dy, dc):
@@ -385,26 +387,31 @@
     piece = rows // gz_n
     site_rows = 6 * math.prod(extent)
     face_rows = [site_rows // n for n in extent]
-    piece_shape = jax.ShapeDtypeStruct((2, piece, cols), BF16)
-    fwd_piece, bwd_piece, vec, *faces = pl.pallas_call(
-        functools.partial(first_kernel, extent),
-        out_shape=[piece_shape, piece_shape]
-        + [jax.ShapeDtypeStruct((n, num_vecs), BF16) for n in [site_rows] + face_rows],
-        in_specs=[SMEM] + [pl.BlockSpec(memory_space=pl.ANY)] * 3,
-        out_specs=[VMEM] * 6,
+    vec, *faces = pl.pallas_call(
+        functools.partial(rows_kernel, extent),
+        out_shape=[jax.ShapeDtypeStruct((n, num_vecs), BF16) for n in [site_rows] + face_rows],
+        in_specs=[VMEM],
+        out_specs=[VMEM] * 4,
+        compiler_params=pltpu.CompilerParams(vmem_limit_bytes=24 * 2**20),
+        name="rows",
+    )(eigvecs.transpose(0, 1, 2, 4, 3, 5).reshape(-1, 2, num_vecs))
+    faces = [passed_along(face, axis, -1) for face, axis in zip(faces, ("gx", "gy", "gz"))]
+
+    both_pieces = pl.pallas_call(
+        pieces_kernel,
+        out_shape=jax.ShapeDtypeStruct((2, 2, piece, cols), BF16),
+        in_specs=[SMEM] + [pl.BlockSpec(memory_space=pl.ANY)] * 2,
+        out_specs=VMEM,
         scratch_shapes=[
             pltpu.VMEM(forward_peram.shape, BF16),
             pltpu.VMEM(backward_peram.shape, BF16),
-            pltpu.VMEM((site_rows // 2, 2, num_vecs), BF16),
-            pltpu.SemaphoreType.DMA((3,)),
+            pltpu.SemaphoreType.DMA((2,)),
         ],
         compiler_params=pltpu.CompilerParams(vmem_limit_bytes=60 * 2**20),
-        name="first",
-    )(me[2:], forward_peram, backward_peram, eigvecs.transpose(0, 1, 2, 4, 3, 5).reshape(-1, 2, num_vecs))
-    faces = [passed_along(face, axis, -1) for face, axis in zip(faces, ("gx", "gy", "gz"))]
-
-    fwd_piece, link_rows = lax.optimization_barrier((fwd_piece, links.reshape(-1, 54)))
-    fwd_line, line = line_exchange(fwd_piece, "gx", gx_n // 2, 1)
+        name="pieces",
+    )(me[2:], forward_peram, backward_peram)
+    both_pieces, links = lax.optimization_barrier((both_pieces, links))
+    both_line, line = line_exchange(both_pieces, "gx", gx_n // 2, 1)
 
     link_mats = pl.pallas_call(
         functools.partial(links_kernel, extent),
@@ -416,7 +423,7 @@
         out_specs=[VMEM] * 3,
         compiler_params=pltpu.CompilerParams(vmem_limit_bytes=24 * 2**20),
         name="link_matrices",
-    )(link_rows)
+    )(links.reshape(-1, 54))
 
     volume = math.prod(extent) * gx_n * gy_n * gz_n
     own_rows = num_vecs // (gz_n * gx_n)
@@ -431,11 +438,13 @@
         name="correlate",
     )(vec, *faces, *link_mats)
 
-    partial, fwd_line = lax.optimization_barrier((partial, fwd_line))
+    partial, both_line = lax.optimization_barrier((partial, both_line))
     by_core = partial.reshape((chips, 2) + partial.shape[1:])
     summed = added(part_at(by_core, core, 1), passed_in_gz(part_at(by_core, 1 - core, 1), 0, 1))
     rounds = gx_n.bit_length() - 1
-    fwd_line, line = line_exchange(fwd_line, "gx", gx_n // 4, rounds - 1, line)
+    first_line = line
+    fwd_line, line = line_exchange(both_line[:, 0], "gx", gx_n // 4, rounds - 1, first_line)
+    bwd_line, _ = line_exchange(both_line[:, 1], "gx", gx_n // 4, rounds - 1, first_line)
     plane = [(dx, dy) for dy in range(chips) for dx in range(gy_n)]
 
     def plane_part(dx, dy):
@@ -443,12 +452,10 @@
         return part_at(part, lax.rem(gy + dx, gy_n) if split > 1 else 0, 1)
 
     summed = added(*[passed_in_plane(plane_part(dx, dy), dx, dy) for dx, dy in plane])
-    summed, fwd_line, bwd_piece = lax.optimization_barrier((summed, fwd_line, bwd_piece))
+    summed, fwd_line, bwd_line = lax.optimization_barrier((summed, fwd_line, bwd_line))
 
     four = gy_n == 2 and chips == 2
     fwd_parts = {(dx, dy, 0): passed_in_plane(fwd_line, dx, dy) for dx, dy in plane if not (four and dx and dy)}
-    bwd_line, _ = line_exchange(bwd_piece, "gx", gx_n // 2, rounds)
-    bwd_parts = {(dy, 0): passed_in_gz(bwd_line, dy, 0) if dy else bwd_line for dy in range(chips)}
 
     distance = gx_n // 2
     while distance:
@@ -467,11 +474,13 @@
     elem_line, _ = line_exchange(elem_line, "gx", 1, 1, offsets)
     for dx, dy in plane:
         fwd_parts[dx, dy, 1] = passed_in_gz(fwd_parts[dx, dy, 0], 0, 1)
+    elem_keys = plane if split > 1 else [(0, dy) for dy in range(chips)]
+    elem_own = jnp.stack([passed_in_plane(elem_line, dx, dy) for dx, dy in elem_keys])
+    elem_own, bwd_line = lax.optimization_barrier((elem_own, bwd_line))
+    elem_parts = [elem_own, passed_in_gz(elem_own, 0, 1)]
+    bwd_parts = {(dy, 0): passed_in_gz(bwd_line, dy, 0) if dy else bwd_line for dy in range(chips)}
     for dy in range(chips):
         bwd_parts[dy, 1] = passed_in_gz(bwd_parts[dy, 0], 0, 1)
-    elem_keys = plane if split > 1 else [(0, dy) for dy in range(chips)]
-    elem_own = jnp.stack([passed_in_plane(elem_line, dx, dy) for dx, dy in elem_keys])
-    elem_parts = [elem_own, passed_in_gz(elem_own, 0, 1)]
 
     op_count = chain_order.shape[0]
     plan = (line, tuple(elem_keys), tuple(fwd_parts))

time: 94.5 us -> 99.2 us (1.050)
  waiting for transfers between devices: 30.1 us -> 42.5 us
  starting transfers between devices: 36 us -> 29.5 us
    ppermute x9, waiting for transfers between devices: 0.13 us -> 6.6 us  [passed_in_gz(): return lax.ppermute(value, 'gz', pairs)]
    ppermute x6 -> x5, waiting for transfers between devices: 11.6 us -> 17.8 us  [line_exchange(): gathered = jnp.concatenate([gathered, lax.ppermute(gathered, axis, pairs)])]
    ppermute x10, starting transfers between devices: 13.6 us -> 9.96 us  [passed_in_plane(): return lax.ppermute(value, ('gy', 'gz'), pairs)]
    ppermute x2, waiting for transfers between devices: 0.16 us -> 3.43 us  [on_device(): lax.ppermute(part_at(halves, 1 - bit), 'gx', pairs)]
    ppermute x10, waiting for transfers between devices: 16.5 us -> 13.6 us  [passed_in_plane(): return lax.ppermute(value, ('gy', 'gz'), pairs)]
    ppermute x6 -> x5, starting transfers between devices: 12.5 us -> 9.86 us  [line_exchange(): gathered = jnp.concatenate([gathered, lax.ppermute(gathered, axis, pairs)])]
    ppermute x9, starting transfers between devices: 4.02 us -> 2.39 us  [passed_in_gz(): return lax.ppermute(value, 'gz', pairs)]
    ppermute x2, starting transfers between devices: 2.92 us -> 4.25 us  [on_device(): lax.ppermute(part_at(halves, 1 - bit), 'gx', pairs)]
  transfers between devices with their start and end apart: 30 -> 29, of which waited for: 11 -> 16; matrix products, arithmetic and copies ran while one was open for 1% -> 3% of each run, Pallas kernels for 13% -> 12%
where the time goes in v6:
time: 99.2 us; the launch traced here: 98.8 us
  waiting for transfers between devices  42.5 us (43%)
  starting transfers between devices  29.5 us (30%)
  Pallas kernels  20.1 us (20%)
  local copies, waits for them, and re-layouts  5.01 us (5%)
  other arithmetic  1.42 us (1%)
    ppermute x5, waiting for transfers between devices, line_exchange(): gathered = jnp.concatenate([gathered, lax.ppermute(gathered, axis, pairs)])  17.8 us
    ppermute x10, waiting for transfers between devices, passed_in_plane(): return lax.ppermute(value, ('gy', 'gz'), pairs)  13.6 us
    ppermute x10, starting transfers between devices, passed_in_plane(): return lax.ppermute(value, ('gy', 'gz'), pairs)  9.96 us
    pallas_call x1, Pallas kernels, on_device(): pl.pallas_call(functools.partial(left_kernel, 1.0 / math.sqrt(4 * num_vec...  9.89 us
    ppermute x5, starting transfers between devices, line_exchange(): gathered = jnp.concatenate([gathered, lax.ppermute(gathered, axis, pairs)])  9.86 us
    ppermute x9, waiting for transfers between devices, passed_in_gz(): return lax.ppermute(value, 'gz', pairs)  6.6 us
    pallas_call x1, Pallas kernels, on_device(): pl.pallas_call(functools.partial(right_kernel, gz_n, tuple(bwd_parts)), o...  5.81 us
    ppermute x2, starting transfers between devices, on_device(): lax.ppermute(part_at(halves, 1 - bit), 'gx', pairs)  4.25 us
  transfers between devices with their start and end apart: 29, of which 16 were waited for; matrix products, arithmetic and copies ran while one was open for 3% of the time, Pallas kernels for 12%

profile of v6, /device:TPU:0, one launch (start us, length us, event | category | flops | bytes accessed | tf_op | source)
XLA Modules:
  0.0 98.8 jit_solution(5839233509369464678)
XLA Ops:
  0.0 2.5 %pieces.1 = bf16[2,2,64,512]{3,2,1,0:T(8,128)(2,1)} custom-call(s32[1]{0:T(128)} %bitcast.2.z_ref, bf16[2,256,512]{2,1,0:T(8,128)(2,1)} %fwd_in.1, bf16[2,256,512]{2,1,0:T(8,128)(2,1)} %bwd_in.1), custom_call_target="tpu_custom_call" | custom-call | tf_op jit(solution)/shard_map/pieces/pallas_call | solution.py:400
  2.5 4.1 %collective-permute-start.3 = (bf16[1,2,2,64,512]{4,3,2,0,1:T(8,128)(2,1)}, bf16[1,2,2,64,512]{4,3,2,0,1:T(8,128)(2,1)S(1)}, u32[]{:S(2)}, u32[]{:S(2)}) collective-permute-start(bf16[1,2,2,64,512]{4,3,2,0,1:T(8,128)(2,1)} %bitcast.43), channel_id=1, source_target_pairs={{0,16},{8,24},{16,0},{24,8},{1,17},{9,25},{17,1},{25,9},{2,18},{10... | collective-permute-start | bytes 786440 | tf_op jit(solution)/shard_map/ppermute | solution.py:363
  7.6 1.4 %collective-permute-start = (bf16[96,256]{1,0:T(8,128)(2,1)S(1)}, bf16[96,256]{1,0:T(8,128)(2,1)S(1)}, u32[]{:S(2)}, u32[]{:S(2)}) collective-permute-start(bf16[96,256]{1,0:T(8,128)(2,1)S(1)} %get-tuple-element.25), channel_id=1, source_target_pairs={{0,24},{8,0},{16,8},{24,16},{1,25},{9,1},{17,9},{25,17},{2,26},{10... | collective-permute-start | bytes 147464 | tf_op jit(solution)/shard_map/ppermute | solution.py:20
  9.0 1.5 %collective-permute-start.1 = (bf16[48,256]{1,0:T(8,128)(2,1)S(1)}, bf16[48,256]{1,0:T(8,128)(2,1)S(1)}, u32[]{:S(2)}, u32[]{:S(2)}) collective-permute-start(bf16[48,256]{1,0:T(8,128)(2,1)S(1)} %get-tuple-element.26), channel_id=1, source_target_pairs={{0,4},{4,0},{1,5},{5,1},{2,6},{6,2},{3,7},{7,3},{8,12},{12,8},{9,1... | collective-permute-start | bytes 73736 | tf_op jit(solution)/shard_map/ppermute | solution.py:20
  13.5 1.3 %correlate.1 = bf16[4,4,2,48,256]{4,3,2,1,0:T(8,128)(2,1)S(1)} custom-call(bf16[192,256]{1,0:T(8,128)(2,1)S(1)} %get-tuple-element.24.vec_ref, bf16[96,256]{1,0:T(8,128)(2,1)S(1)} %collective-permute-done.face0, bf16[48,256]{1,0:T(8,128)(2,1)S(1)} %collective-permute-done.1.face1, bf16[48,256]{1,0:T(8,128)(2,1)S(1)} %collective-permute-done.2.face2, ...), custom_call_target="tpu_custom_call" | custom-call | tf_op jit(solution)/shard_map/correlate/pallas_call | solution.py:432
  14.8 4.5 %collective-permute-done.3 = bf16[1,2,2,64,512]{4,3,2,0,1:T(8,128)(2,1)S(1)} collective-permute-done((bf16[1,2,2,64,512]{4,3,2,0,1:T(8,128)(2,1)}, bf16[1,2,2,64,512]{4,3,2,0,1:T(8,128)(2,1)S(1)}, u32[]{:S(2)}, u32[]{:S(2)}) %collective-permute-start.3) | collective-permute-done | bytes 262176 | tf_op jit(solution)/shard_map/ppermute | solution.py:363
  19.3 1.0 %pad_maximum_fusion = bf16[2,2,2,64,512]{4,3,2,0,1:T(8,128)(2,1)S(1)} fusion(bf16[1,2,2,64,512]{4,3,2,0,1:T(8,128)(2,1)S(1)} %collective-permute-done.3, bf16[1,2,2,64,512]{4,3,2,0,1:T(8,128)(2,1)} %bitcast.44), kind=kLoop, calls=%fused_computation.2 | loop fusion | flops 262144 | bytes 1048576 | tf_op jit(solution)/shard_map/concatenate | solution.py:363
  20.5 2.4 %collective-permute-start.9 = (bf16[2,2,64,512]{3,2,1,0:T(8,128)(2,1)S(1)}, bf16[2,2,64,512]{3,2,1,0:T(8,128)(2,1)S(1)}, u32[]{:S(2)}, u32[]{:S(2)}) collective-permute-start(bf16[2,2,64,512]{3,2,1,0:T(8,128)(2,1)S(1)} %get-tuple-element.45), channel_id=1, source_target_pairs={{0,8},{8,0},{16,24},{24,16},{1,9},{9,1},{17,25},{25,17},{2,10},{10... | collective-permute-start | bytes 786440 | tf_op jit(solution)/shard_map/ppermute | solution.py:363
  23.1 7.0 %collective-permute-done.9 = bf16[2,2,64,512]{3,2,1,0:T(8,128)(2,1)S(1)} collective-permute-done((bf16[2,2,64,512]{3,2,1,0:T(8,128)(2,1)S(1)}, bf16[2,2,64,512]{3,2,1,0:T(8,128)(2,1)S(1)}, u32[]{:S(2)}, u32[]{:S(2)}) %collective-permute-start.9) | collective-permute-done | bytes 262176 | tf_op jit(solution)/shard_map/ppermute | solution.py:363
  30.3 1.6 %collective-permute-start.5 = (bf16[4,48,256]{2,1,0:T(8,128)(2,1)S(1)}, bf16[4,48,256]{2,1,0:T(8,128)(2,1)S(1)}, u32[]{:S(2)}, u32[]{:S(2)}) collective-permute-start(bf16[4,48,256]{2,1,0:T(8,128)(2,1)S(1)} %get-tuple-element.47), channel_id=1, source_target_pairs={{0,4},{1,5},{2,6},{3,7},{4,0},{5,1},{6,2},{7,3},{8,12},{9,13},{10,... | collective-permute-start | bytes 294920 | tf_op jit(solution)/shard_map/ppermute | solution.py:354
  32.0 1.5 %collective-permute-start.6 = (bf16[4,48,256]{2,1,0:T(8,128)(2,1)S(1)}, bf16[4,48,256]{2,1,0:T(8,128)(2,1)S(1)}, u32[]{:S(2)}, u32[]{:S(2)}) collective-permute-start(bf16[4,48,256]{2,1,0:T(8,128)(2,1)S(1)} %get-tuple-element.49), channel_id=1, source_target_pairs={{0,2},{1,3},{2,0},{3,1},{4,6},{5,7},{6,4},{7,5},{8,10},{9,11},{10,... | collective-permute-start | bytes 294920 | tf_op jit(solution)/shard_map/ppermute | solution.py:354
  33.9 1.7 %collective-permute-done.8 = bf16[2,2,64,512]{3,2,1,0:T(8,128)(2,1)S(1)} collective-permute-done((bf16[2,2,64,512]{3,2,1,0:T(8,128)(2,1)S(1)}, bf16[2,2,64,512]{3,2,1,0:T(8,128)(2,1)S(1)}, u32[]{:S(2)}, u32[]{:S(2)}) %collective-permute-start.8) | collective-permute-done | bytes 262176 | tf_op jit(solution)/shard_map/ppermute | solution.py:363
  35.6 2.0 %collective-permute-done.6 = bf16[4,48,256]{2,1,0:T(8,128)(2,1)S(1)} collective-permute-done((bf16[4,48,256]{2,1,0:T(8,128)(2,1)S(1)}, bf16[4,48,256]{2,1,0:T(8,128)(2,1)S(1)}, u32[]{:S(2)}, u32[]{:S(2)}) %collective-permute-start.6) | collective-permute-done | bytes 98336 | tf_op jit(solution)/shard_map/ppermute | solution.py:354
  37.6 1.4 %collective-permute-done.7 = bf16[4,48,256]{2,1,0:T(8,128)(2,1)S(1)} collective-permute-done((bf16[4,48,256]{2,1,0:T(8,128)(2,1)S(1)}, bf16[4,48,256]{2,1,0:T(8,128)(2,1)S(1)}, u32[]{:S(2)}, u32[]{:S(2)}) %collective-permute-start.7) | collective-permute-done | bytes 98336 | tf_op jit(solution)/shard_map/ppermute | solution.py:354
  39.1 2.3 %collective-permute-start.10 = (bf16[2,48,256]{2,1,0:T(8,128)(2,1)S(1)}, bf16[2,48,256]{2,1,0:T(8,128)(2,1)S(1)}, u32[]{:S(2)}, u32[]{:S(2)}) collective-permute-start(bf16[2,48,256]{2,1,0:T(8,128)(2,1)S(1)} %dynamic-slice_bitcast_fusion.3), channel_id=1, source_target_pairs={{0,16},{8,24},{16,0},{24,8},{1,17},{9,25},{17,1},{25,9},{2,18},{10... | collective-permute-start | bytes 147464 | tf_op jit(solution)/shard_map/ppermute | solution.py:465
  42.9 1.3 %collective-permute-done.10 = bf16[2,48,256]{2,1,0:T(8,128)(2,1)S(1)} collective-permute-done((bf16[2,48,256]{2,1,0:T(8,128)(2,1)S(1)}, bf16[2,48,256]{2,1,0:T(8,128)(2,1)S(1)}, u32[]{:S(2)}, u32[]{:S(2)}) %collective-permute-start.10) | collective-permute-done | bytes 49184 | tf_op jit(solution)/shard_map/ppermute | solution.py:465
  44.2 2.0 %collective-permute-start.11 = (bf16[1,48,256]{2,1,0:T(8,128)(2,1)S(1)}, bf16[1,48,256]{2,1,0:T(8,128)(2,1)S(1)}, u32[]{:S(2)}, u32[]{:S(2)}) collective-permute-start(bf16[1,48,256]{2,1,0:T(8,128)(2,1)S(1)} %constant_dynamic-slice_fusion), channel_id=1, source_target_pairs={{0,8},{8,0},{16,24},{24,16},{1,9},{9,1},{17,25},{25,17},{2,10},{10... | collective-permute-start | bytes 73736 | tf_op jit(solution)/shard_map/ppermute | solution.py:465
  46.2 2.2 %collective-permute-done.11 = bf16[1,48,256]{2,1,0:T(8,128)(2,1)S(1)} collective-permute-done((bf16[1,48,256]{2,1,0:T(8,128)(2,1)S(1)}, bf16[1,48,256]{2,1,0:T(8,128)(2,1)S(1)}, u32[]{:S(2)}, u32[]{:S(2)}) %collective-permute-start.11) | collective-permute-done | bytes 24608 | tf_op jit(solution)/shard_map/ppermute | solution.py:465
  48.4 2.0 %collective-permute-start.12 = (bf16[1,48,256]{2,1,0:T(8,128)(2,1)S(1)}, bf16[1,48,256]{2,1,0:T(8,128)(2,1)S(1)}, u32[]{:S(2)}, u32[]{:S(2)}) collective-permute-start(bf16[1,48,256]{2,1,0:T(8,128)(2,1)S(1)} %add_convert_fusion), channel_id=1, source_target_pairs={{0,16},{8,24},{16,0},{24,8},{1,17},{9,25},{17,1},{25,9},{2,18},{10... | collective-permute-start | bytes 73736 | tf_op jit(solution)/shard_map/ppermute | solution.py:363
  50.4 2.8 %collective-permute-done.12 = bf16[1,48,256]{2,1,0:T(8,128)(2,1)S(1)} collective-permute-done((bf16[1,48,256]{2,1,0:T(8,128)(2,1)S(1)}, bf16[1,48,256]{2,1,0:T(8,128)(2,1)S(1)}, u32[]{:S(2)}, u32[]{:S(2)}) %collective-permute-start.12) | collective-permute-done | bytes 24608 | tf_op jit(solution)/shard_map/ppermute | solution.py:363
  53.2 1.2 %collective-permute-done.14.refs_4_ = bf16[4,2,64,512]{3,2,1,0:T(8,128)(2,1)S(1)} collective-permute-done((bf16[4,2,64,512]{3,2,1,0:T(8,128)(2,1)S(1)}, bf16[4,2,64,512]{3,2,1,0:T(8,128)(2,1)S(1)}, u32[]{:S(2)}, u32[]{:S(2)}) %collective-permute-start.14) | collective-permute-done | bytes 524320 | tf_op jit(solution)/shard_map/ppermute | solution.py:354
  54.4 1.2 %collective-permute-start.15 = (bf16[2,48,256]{2,1,0:T(8,128)(2,1)S(1)}, bf16[2,48,256]{2,1,0:T(8,128)(2,1)S(1)}, u32[]{:S(2)}, u32[]{:S(2)}) collective-permute-start(bf16[2,48,256]{2,1,0:T(8,128)(2,1)S(1)} %pad_maximum_fusion.4), channel_id=1, source_target_pairs={{0,8},{8,0},{16,24},{24,16},{1,9},{9,1},{17,25},{25,17},{2,10},{10... | collective-permute-start | bytes 147464 | tf_op jit(solution)/shard_map/ppermute | solution.py:363
  55.6 1.1 %collective-permute-start.20 = (bf16[4,1,64,512]{3,2,1,0:T(8,128)(2,1)S(1)}, bf16[4,1,64,512]{3,2,1,0:T(8,128)(2,1)S(1)}, u32[]{:S(2)}, u32[]{:S(2)}) collective-permute-start(bf16[4,1,64,512]{3,2,1,0:T(8,128)(2,1)S(1)} %slice.14), channel_id=1, source_target_pairs={{0,4},{1,5},{2,6},{3,7},{4,0},{5,1},{6,2},{7,3},{8,12},{9,13},{10,... | collective-permute-start | bytes 786440 | tf_op jit(solution)/shard_map/ppermute | solution.py:354
  56.7 1.8 %collective-permute-done.15 = bf16[2,48,256]{2,1,0:T(8,128)(2,1)S(1)} collective-permute-done((bf16[2,48,256]{2,1,0:T(8,128)(2,1)S(1)}, bf16[2,48,256]{2,1,0:T(8,128)(2,1)S(1)}, u32[]{:S(2)}, u32[]{:S(2)}) %collective-permute-start.15) | collective-permute-done | bytes 49184 | tf_op jit(solution)/shard_map/ppermute | solution.py:363
  59.3 2.6 %collective-permute-start.18 = (bf16[4,48,256]{2,1,0:T(8,128)(2,1)S(1)}, bf16[4,48,256]{2,1,0:T(8,128)(2,1)S(1)}, u32[]{:S(2)}, u32[]{:S(2)}) collective-permute-start(bf16[4,48,256]{2,1,0:T(8,128)(2,1)S(1)} %constant_dynamic-update-slice_fusion), channel_id=1, source_target_pairs={{0,6},{1,7},{2,4},{3,5},{4,2},{5,3},{6,0},{7,1},{8,14},{9,15},{10,... | collective-permute-start | bytes 294920 | tf_op jit(solution)/shard_map/ppermute | solution.py:354
  62.0 1.9 %collective-permute-done.16 = bf16[4,48,256]{2,1,0:T(8,128)(2,1)S(1)} collective-permute-done((bf16[4,48,256]{2,1,0:T(8,128)(2,1)S(1)}, bf16[4,48,256]{2,1,0:T(8,128)(2,1)S(1)}, u32[]{:S(2)}, u32[]{:S(2)}) %collective-permute-start.16) | collective-permute-done | bytes 98336 | tf_op jit(solution)/shard_map/ppermute | solution.py:354
  64.9 1.7 %collective-permute-start.26 = (bf16[4,2,64,512]{3,2,1,0:T(8,128)(2,1)S(1)}, bf16[4,2,64,512]{3,2,1,0:T(8,128)(2,1)S(1)}, u32[]{:S(2)}, u32[]{:S(2)}) collective-permute-start(bf16[4,2,64,512]{3,2,1,0:T(8,128)(2,1)S(1)} %pad_maximum_fusion.2.refs_0_), channel_id=1, source_target_pairs={{0,2},{1,3},{2,0},{3,1},{4,6},{5,7},{6,4},{7,5},{8,10},{9,11},{10,... | collective-permute-start | bytes 1572872 | tf_op jit(solution)/shard_map/ppermute | solution.py:341
  66.7 6.5 %collective-permute-done.21 = bf16[4,1,64,512]{3,2,1,0:T(8,128)(2,1)S(1)} collective-permute-done((bf16[4,1,64,512]{3,2,1,0:T(8,128)(2,1)S(1)}, bf16[4,1,64,512]{3,2,1,0:T(8,128)(2,1)S(1)}, u32[]{:S(2)}, u32[]{:S(2)}) %collective-permute-start.21) | collective-permute-done | bytes 262176 | tf_op jit(solution)/shard_map/ppermute | solution.py:354
  75.4 6.6 %collective-permute-done.26.refs_1_ = bf16[4,2,64,512]{3,2,1,0:T(8,128)(2,1)S(1)} collective-permute-done((bf16[4,2,64,512]{3,2,1,0:T(8,128)(2,1)S(1)}, bf16[4,2,64,512]{3,2,1,0:T(8,128)(2,1)S(1)}, u32[]{:S(2)}, u32[]{:S(2)}) %collective-permute-start.26) | collective-permute-done | bytes 524320 | tf_op jit(solution)/shard_map/ppermute | solution.py:341
  82.1 1.0 %copy-done.2 = bf16[4,2,64,512]{3,2,1,0:T(8,128)(2,1)S(1)} copy-done((bf16[4,2,64,512]{3,2,1,0:T(8,128)(2,1)S(1)}, bf16[4,2,64,512]{3,2,1,0:T(8,128)(2,1)}, u32[]{:S(2)}) %copy-start.2) | copy-done | bytes 524312
  83.1 9.9 %left.1.left_ref = bf16[4,256,2048]{2,1,0:T(8,128)(2,1)S(1)} custom-call(s32[3]{0:T(128)S(1)} %pad_add_fusion.me_ref, s32[4]{0:T(128)S(1)} %copy-done.4, f32[4,4,4]{2,1,0:T(4,128)S(1)} %copy-done.3, s32[4,2]{1,0:T(4,128)S(1)} %copy.16.chain_ref, bf16[4,4,48,256]{3,2,1,0:T(8,128)(2,1)S(1)} %pad_maximum_fusion.3.refs_0_, ...), custom_call_target="tpu_custom_call" | custom-call | flops 8000000000 | bytes 10000000 | tf_op jit(solution)/shard_map/left/pallas_call | solution.py:488
  93.0 5.8 %right.1 = bf16[4,2,256,512]{3,2,1,0:T(8,128)(2,1)} custom-call(bf16[4,256,2048]{2,1,0:T(8,128)(2,1)S(1)} %left.1.left_ref, bf16[4,2,64,512]{3,2,1,0:T(8,128)(2,1)S(1)} %pad_maximum_fusion.2.refs_0_, bf16[4,2,64,512]{3,2,1,0:T(8,128)(2,1)S(1)} %collective-permute-done.26.refs_1_, bf16[4,2,64,512]{3,2,1,0:T(8,128)(2,1)S(1)} %collective-permute-done.27.refs_2_, ...), custom_call_target="tpu_custom_call" | custom-call | tf_op jit(solution)/shard_map/right/pallas_call | solution.py:503
  (68 shorter events, 10.9 us)
Async XLA Ops:
  2.5 16.8 %collective-permute-start.3 = (bf16[1,2,2,64,512]{4,3,2,0,1:T(8,128)(2,1)}, bf16[1,2,2,64,512]{4,3,2,0,1:T(8,128)(2,1)S(1)}, u32[]{:S(2)}, u32[]{:S(2)}) collective-permute-start(bf16[1,2,2,64,512]{4,3,2,0,1:T(8,128)(2,1)} %bitcast.43), channel_id=1, source_target_pairs={{0,16},{8,24},{16,0},{24,8},{1,17},{9,25},{17,1},{25,9},{2,18},{10... | collective-permute-start | bytes 786440 | tf_op jit(solution)/shard_map/ppermute | solution.py:363
  7.6 5.9 %collective-permute-start = (bf16[96,256]{1,0:T(8,128)(2,1)S(1)}, bf16[96,256]{1,0:T(8,128)(2,1)S(1)}, u32[]{:S(2)}, u32[]{:S(2)}) collective-permute-start(bf16[96,256]{1,0:T(8,128)(2,1)S(1)} %get-tuple-element.25), channel_id=1, source_target_pairs={{0,24},{8,0},{16,8},{24,16},{1,25},{9,1},{17,9},{25,17},{2,26},{10... | collective-permute-start | bytes 147464 | tf_op jit(solution)/shard_map/ppermute | solution.py:20
  9.0 3.8 %collective-permute-start.1 = (bf16[48,256]{1,0:T(8,128)(2,1)S(1)}, bf16[48,256]{1,0:T(8,128)(2,1)S(1)}, u32[]{:S(2)}, u32[]{:S(2)}) collective-permute-start(bf16[48,256]{1,0:T(8,128)(2,1)S(1)} %get-tuple-element.26), channel_id=1, source_target_pairs={{0,4},{4,0},{1,5},{5,1},{2,6},{6,2},{3,7},{7,3},{8,12},{12,8},{9,1... | collective-permute-start | bytes 73736 | tf_op jit(solution)/shard_map/ppermute | solution.py:20
  10.4 2.3 %collective-permute-start.2 = (bf16[48,256]{1,0:T(8,128)(2,1)S(1)}, bf16[48,256]{1,0:T(8,128)(2,1)S(1)}, u32[]{:S(2)}, u32[]{:S(2)}) collective-permute-start(bf16[48,256]{1,0:T(8,128)(2,1)S(1)} %get-tuple-element.27), channel_id=1, source_target_pairs={{0,3},{1,0},{2,1},{3,2},{4,7},{5,4},{6,5},{7,6},{8,11},{9,8},{10,9... | collective-permute-start | bytes 73736 | tf_op jit(solution)/shard_map/ppermute | solution.py:20
  20.4 9.8 %collective-permute-start.4 = (bf16[2,4,2,48,256]{4,3,1,2,0:T(8,128)(2,1)S(1)}, bf16[2,4,2,48,256]{4,3,1,2,0:T(8,128)(2,1)S(1)}, u32[]{:S(2)}, u32[]{:S(2)}) collective-permute-start(bf16[2,4,2,48,256]{4,3,1,2,0:T(8,128)(2,1)S(1)} %bitcast.45), channel_id=1, source_target_pairs={{0,1},{1,0},{2,3},{3,2},{4,5},{5,4},{6,7},{7,6},{8,9},{9,8},{10,11... | collective-permute-start | bytes 1179656 | tf_op jit(solution)/shard_map/ppermute | solution.py:341
  20.5 61.5 %copy-start.3 = (f32[4,4,4]{2,1,0:T(4,128)S(1)}, f32[4,4,4]{2,1,0:T(4,128)}, u32[]{:S(2)}) copy-start(f32[4,4,4]{2,1,0:T(4,128)} %spin_ref.1) | copy-start | bytes 772
  20.5 61.5 %copy-start.4 = (s32[4]{0:T(128)S(1)}, s32[4]{0:T(128)}, u32[]{:S(2)}) copy-start(s32[4]{0:T(128)} %dirs_ref.1) | copy-start | bytes 52
  20.5 9.6 %collective-permute-start.9 = (bf16[2,2,64,512]{3,2,1,0:T(8,128)(2,1)S(1)}, bf16[2,2,64,512]{3,2,1,0:T(8,128)(2,1)S(1)}, u32[]{:S(2)}, u32[]{:S(2)}) collective-permute-start(bf16[2,2,64,512]{3,2,1,0:T(8,128)(2,1)S(1)} %get-tuple-element.45), channel_id=1, source_target_pairs={{0,8},{8,0},{16,24},{24,16},{1,9},{9,1},{17,25},{25,17},{2,10},{10... | collective-permute-start | bytes 786440 | tf_op jit(solution)/shard_map/ppermute | solution.py:363
  23.0 12.6 %collective-permute-start.8 = (bf16[2,2,64,512]{3,2,1,0:T(8,128)(2,1)S(1)}, bf16[2,2,64,512]{3,2,1,0:T(8,128)(2,1)S(1)}, u32[]{:S(2)}, u32[]{:S(2)}) collective-permute-start(bf16[2,2,64,512]{3,2,1,0:T(8,128)(2,1)S(1)} %get-tuple-element.46), channel_id=1, source_target_pairs={{0,8},{8,0},{16,24},{24,16},{1,9},{9,1},{17,25},{25,17},{2,10},{10... | collective-permute-start | bytes 786440 | tf_op jit(solution)/shard_map/ppermute | solution.py:363
  30.3 5.3 %collective-permute-start.5 = (bf16[4,48,256]{2,1,0:T(8,128)(2,1)S(1)}, bf16[4,48,256]{2,1,0:T(8,128)(2,1)S(1)}, u32[]{:S(2)}, u32[]{:S(2)}) collective-permute-start(bf16[4,48,256]{2,1,0:T(8,128)(2,1)S(1)} %get-tuple-element.47), channel_id=1, source_target_pairs={{0,4},{1,5},{2,6},{3,7},{4,0},{5,1},{6,2},{7,3},{8,12},{9,13},{10,... | collective-permute-start | bytes 294920 | tf_op jit(solution)/shard_map/ppermute | solution.py:354
  32.0 5.7 %collective-permute-start.6 = (bf16[4,48,256]{2,1,0:T(8,128)(2,1)S(1)}, bf16[4,48,256]{2,1,0:T(8,128)(2,1)S(1)}, u32[]{:S(2)}, u32[]{:S(2)}) collective-permute-start(bf16[4,48,256]{2,1,0:T(8,128)(2,1)S(1)} %get-tuple-element.49), channel_id=1, source_target_pairs={{0,2},{1,3},{2,0},{3,1},{4,6},{5,7},{6,4},{7,5},{8,10},{9,11},{10,... | collective-permute-start | bytes 294920 | tf_op jit(solution)/shard_map/ppermute | solution.py:354
  33.5 5.5 %collective-permute-start.7 = (bf16[4,48,256]{2,1,0:T(8,128)(2,1)S(1)}, bf16[4,48,256]{2,1,0:T(8,128)(2,1)S(1)}, u32[]{:S(2)}, u32[]{:S(2)}) collective-permute-start(bf16[4,48,256]{2,1,0:T(8,128)(2,1)S(1)} %get-tuple-element.48), channel_id=1, source_target_pairs={{0,6},{1,7},{2,4},{3,5},{4,2},{5,3},{6,0},{7,1},{8,14},{9,15},{10,... | collective-permute-start | bytes 294920 | tf_op jit(solution)/shard_map/ppermute | solution.py:354
  39.1 5.1 %collective-permute-start.10 = (bf16[2,48,256]{2,1,0:T(8,128)(2,1)S(1)}, bf16[2,48,256]{2,1,0:T(8,128)(2,1)S(1)}, u32[]{:S(2)}, u32[]{:S(2)}) collective-permute-start(bf16[2,48,256]{2,1,0:T(8,128)(2,1)S(1)} %dynamic-slice_bitcast_fusion.3), channel_id=1, source_target_pairs={{0,16},{8,24},{16,0},{24,8},{1,17},{9,25},{17,1},{25,9},{2,18},{10... | collective-permute-start | bytes 147464 | tf_op jit(solution)/shard_map/ppermute | solution.py:465
  41.4 11.8 %collective-permute-start.13 = (bf16[4,2,64,512]{3,2,1,0:T(8,128)(2,1)S(1)}, bf16[4,2,64,512]{3,2,1,0:T(8,128)(2,1)S(1)}, u32[]{:S(2)}, u32[]{:S(2)}) collective-permute-start(bf16[4,2,64,512]{3,2,1,0:T(8,128)(2,1)S(1)} %pad_maximum_fusion.1.refs_2_), channel_id=1, source_target_pairs={{0,4},{1,5},{2,6},{3,7},{4,0},{5,1},{6,2},{7,3},{8,12},{9,13},{10,... | collective-permute-start | bytes 1572872 | tf_op jit(solution)/shard_map/ppermute | solution.py:354
  42.0 12.4 %collective-permute-start.14 = (bf16[4,2,64,512]{3,2,1,0:T(8,128)(2,1)S(1)}, bf16[4,2,64,512]{3,2,1,0:T(8,128)(2,1)S(1)}, u32[]{:S(2)}, u32[]{:S(2)}) collective-permute-start(bf16[4,2,64,512]{3,2,1,0:T(8,128)(2,1)S(1)} %pad_maximum_fusion.1.refs_2_), channel_id=1, source_target_pairs={{0,2},{1,3},{2,0},{3,1},{4,6},{5,7},{6,4},{7,5},{8,10},{9,11},{10,... | collective-permute-start | bytes 1572872 | tf_op jit(solution)/shard_map/ppermute | solution.py:354
  44.2 4.1 %collective-permute-start.11 = (bf16[1,48,256]{2,1,0:T(8,128)(2,1)S(1)}, bf16[1,48,256]{2,1,0:T(8,128)(2,1)S(1)}, u32[]{:S(2)}, u32[]{:S(2)}) collective-permute-start(bf16[1,48,256]{2,1,0:T(8,128)(2,1)S(1)} %constant_dynamic-slice_fusion), channel_id=1, source_target_pairs={{0,8},{8,0},{16,24},{24,16},{1,9},{9,1},{17,25},{25,17},{2,10},{10... | collective-permute-start | bytes 73736 | tf_op jit(solution)/shard_map/ppermute | solution.py:465
  48.4 4.8 %collective-permute-start.12 = (bf16[1,48,256]{2,1,0:T(8,128)(2,1)S(1)}, bf16[1,48,256]{2,1,0:T(8,128)(2,1)S(1)}, u32[]{:S(2)}, u32[]{:S(2)}) collective-permute-start(bf16[1,48,256]{2,1,0:T(8,128)(2,1)S(1)} %add_convert_fusion), channel_id=1, source_target_pairs={{0,16},{8,24},{16,0},{24,8},{1,17},{9,25},{17,1},{25,9},{2,18},{10... | collective-permute-start | bytes 73736 | tf_op jit(solution)/shard_map/ppermute | solution.py:363
  54.4 4.1 %collective-permute-start.15 = (bf16[2,48,256]{2,1,0:T(8,128)(2,1)S(1)}, bf16[2,48,256]{2,1,0:T(8,128)(2,1)S(1)}, u32[]{:S(2)}, u32[]{:S(2)}) collective-permute-start(bf16[2,48,256]{2,1,0:T(8,128)(2,1)S(1)} %pad_maximum_fusion.4), channel_id=1, source_target_pairs={{0,8},{8,0},{16,24},{24,16},{1,9},{9,1},{17,25},{25,17},{2,10},{10... | collective-permute-start | bytes 147464 | tf_op jit(solution)/shard_map/ppermute | solution.py:363
  55.6 9.3 %collective-permute-start.20 = (bf16[4,1,64,512]{3,2,1,0:T(8,128)(2,1)S(1)}, bf16[4,1,64,512]{3,2,1,0:T(8,128)(2,1)S(1)}, u32[]{:S(2)}, u32[]{:S(2)}) collective-permute-start(bf16[4,1,64,512]{3,2,1,0:T(8,128)(2,1)S(1)} %slice.14), channel_id=1, source_target_pairs={{0,4},{1,5},{2,6},{3,7},{4,0},{5,1},{6,2},{7,3},{8,12},{9,13},{10,... | collective-permute-start | bytes 786440 | tf_op jit(solution)/shard_map/ppermute | solution.py:354
  58.5 5.4 %collective-permute-start.16 = (bf16[4,48,256]{2,1,0:T(8,128)(2,1)S(1)}, bf16[4,48,256]{2,1,0:T(8,128)(2,1)S(1)}, u32[]{:S(2)}, u32[]{:S(2)}) collective-permute-start(bf16[4,48,256]{2,1,0:T(8,128)(2,1)S(1)} %constant_dynamic-update-slice_fusion), channel_id=1, source_target_pairs={{0,4},{1,5},{2,6},{3,7},{4,0},{5,1},{6,2},{7,3},{8,12},{9,13},{10,... | collective-permute-start | bytes 294920 | tf_op jit(solution)/shard_map/ppermute | solution.py:354
  58.9 5.3 %collective-permute-start.17 = (bf16[4,48,256]{2,1,0:T(8,128)(2,1)S(1)}, bf16[4,48,256]{2,1,0:T(8,128)(2,1)S(1)}, u32[]{:S(2)}, u32[]{:S(2)}) collective-permute-start(bf16[4,48,256]{2,1,0:T(8,128)(2,1)S(1)} %constant_dynamic-update-slice_fusion), channel_id=1, source_target_pairs={{0,2},{1,3},{2,0},{3,1},{4,6},{5,7},{6,4},{7,5},{8,10},{9,11},{10,... | collective-permute-start | bytes 294920 | tf_op jit(solution)/shard_map/ppermute | solution.py:354
  59.3 5.5 %collective-permute-start.18 = (bf16[4,48,256]{2,1,0:T(8,128)(2,1)S(1)}, bf16[4,48,256]{2,1,0:T(8,128)(2,1)S(1)}, u32[]{:S(2)}, u32[]{:S(2)}) collective-permute-start(bf16[4,48,256]{2,1,0:T(8,128)(2,1)S(1)} %constant_dynamic-update-slice_fusion), channel_id=1, source_target_pairs={{0,6},{1,7},{2,4},{3,5},{4,2},{5,3},{6,0},{7,1},{8,14},{9,15},{10,... | collective-permute-start | bytes 294920 | tf_op jit(solution)/shard_map/ppermute | solution.py:354
  62.0 11.3 %collective-permute-start.22 = (bf16[4,2,64,512]{3,2,1,0:T(8,128)(2,1)S(1)}, bf16[4,2,64,512]{3,2,1,0:T(8,128)(2,1)S(1)}, u32[]{:S(2)}, u32[]{:S(2)}) collective-permute-start(bf16[4,2,64,512]{3,2,1,0:T(8,128)(2,1)S(1)} %pad_maximum_fusion.1.refs_2_), channel_id=1, source_target_pairs={{0,1},{1,0},{2,3},{3,2},{4,5},{5,4},{6,7},{7,6},{8,9},{9,8},{10,11... | collective-permute-start | bytes 1572872 | tf_op jit(solution)/shard_map/ppermute | solution.py:341
  63.9 9.2 %collective-permute-start.21 = (bf16[4,1,64,512]{3,2,1,0:T(8,128)(2,1)S(1)}, bf16[4,1,64,512]{3,2,1,0:T(8,128)(2,1)S(1)}, u32[]{:S(2)}, u32[]{:S(2)}) collective-permute-start(bf16[4,1,64,512]{3,2,1,0:T(8,128)(2,1)S(1)} %slice.15), channel_id=1, source_target_pairs={{0,2},{1,3},{2,0},{3,1},{4,6},{5,7},{6,4},{7,5},{8,10},{9,11},{10,... | collective-permute-start | bytes 786440 | tf_op jit(solution)/shard_map/ppermute | solution.py:354
  64.2 11.2 %collective-permute-start.23 = (bf16[4,2,64,512]{3,2,1,0:T(8,128)(2,1)S(1)}, bf16[4,2,64,512]{3,2,1,0:T(8,128)(2,1)}, u32[]{:S(2)}, u32[]{:S(2)}) collective-permute-start(bf16[4,2,64,512]{3,2,1,0:T(8,128)(2,1)S(1)} %collective-permute-done.13.refs_3_), channel_id=1, source_target_pairs={{0,1},{1,0},{2,3},{3,2},{4,5},{5,4},{6,7},{7,6},{8,9},{9,8},{10,11... | collective-permute-start | bytes 1572872 | tf_op jit(solution)/shard_map/ppermute | solution.py:341
  64.9 17.2 %collective-permute-start.24 = (bf16[4,2,64,512]{3,2,1,0:T(8,128)(2,1)S(1)}, bf16[4,2,64,512]{3,2,1,0:T(8,128)(2,1)}, u32[]{:S(2)}, u32[]{:S(2)}) collective-permute-start(bf16[4,2,64,512]{3,2,1,0:T(8,128)(2,1)S(1)} %collective-permute-done.14.refs_4_), channel_id=1, source_target_pairs={{0,1},{1,0},{2,3},{3,2},{4,5},{5,4},{6,7},{7,6},{8,9},{9,8},{10,11... | collective-permute-start | bytes 1572872 | tf_op jit(solution)/shard_map/ppermute | solution.py:341
  64.9 17.1 %collective-permute-start.26 = (bf16[4,2,64,512]{3,2,1,0:T(8,128)(2,1)S(1)}, bf16[4,2,64,512]{3,2,1,0:T(8,128)(2,1)S(1)}, u32[]{:S(2)}, u32[]{:S(2)}) collective-permute-start(bf16[4,2,64,512]{3,2,1,0:T(8,128)(2,1)S(1)} %pad_maximum_fusion.2.refs_0_), channel_id=1, source_target_pairs={{0,2},{1,3},{2,0},{3,1},{4,6},{5,7},{6,4},{7,5},{8,10},{9,11},{10,... | collective-permute-start | bytes 1572872 | tf_op jit(solution)/shard_map/ppermute | solution.py:341
  73.2 8.8 %collective-permute-start.25 = (bf16[4,2,64,512]{3,2,1,0:T(8,128)(2,1)S(1)}, bf16[4,2,64,512]{3,2,1,0:T(8,128)(2,1)}, u32[]{:S(2)}, u32[]{:S(2)}) collective-permute-start(bf16[4,2,64,512]{3,2,1,0:T(8,128)(2,1)S(1)} %constant_dynamic-update-slice_fusion.2.refs_5_), channel_id=1, source_target_pairs={{0,1},{1,0},{2,3},{3,2},{4,5},{5,4},{6,7},{7,6},{8,9},{9,8},{10,11... | collective-permute-start | bytes 1572872 | tf_op jit(solution)/shard_map/ppermute | solution.py:341
  74.1 8.0 %collective-permute-start.19 = (bf16[4,4,48,256]{3,2,1,0:T(8,128)(2,1)S(1)}, bf16[4,4,48,256]{3,2,1,0:T(8,128)(2,1)}, u32[]{:S(2)}, u32[]{:S(2)}) collective-permute-start(bf16[4,4,48,256]{3,2,1,0:T(8,128)(2,1)S(1)} %pad_maximum_fusion.3.refs_0_), channel_id=1, source_target_pairs={{0,1},{1,0},{2,3},{3,2},{4,5},{5,4},{6,7},{7,6},{8,9},{9,8},{10,11... | collective-permute-start | bytes 1179656 | tf_op jit(solution)/shard_map/ppermute | solution.py:341
  75.4 17.6 %collective-permute-start.27 = (bf16[4,2,64,512]{3,2,1,0:T(8,128)(2,1)S(1)}, bf16[4,2,64,512]{3,2,1,0:T(8,128)(2,1)S(1)}, u32[]{:S(2)}, u32[]{:S(2)}) collective-permute-start(bf16[4,2,64,512]{3,2,1,0:T(8,128)(2,1)S(1)} %pad_maximum_fusion.2.refs_0_), channel_id=1, source_target_pairs={{0,1},{1,0},{2,3},{3,2},{4,5},{5,4},{6,7},{7,6},{8,9},{9,8},{10,11... | collective-permute-start | bytes 1572872 | tf_op jit(solution)/shard_map/ppermute | solution.py:341
  82.0 11.0 %collective-permute-start.28 = (bf16[4,2,64,512]{3,2,1,0:T(8,128)(2,1)S(1)}, bf16[4,2,64,512]{3,2,1,0:T(8,128)(2,1)S(1)}, u32[]{:S(2)}, u32[]{:S(2)}) collective-permute-start(bf16[4,2,64,512]{3,2,1,0:T(8,128)(2,1)S(1)} %collective-permute-done.26.refs_1_), channel_id=1, source_target_pairs={{0,1},{1,0},{2,3},{3,2},{4,5},{5,4},{6,7},{7,6},{8,9},{9,8},{10,11... | collective-permute-start | bytes 1572872 | tf_op jit(solution)/shard_map/ppermute | solution.py:341
  82.0 1.0 %copy-start.2 = (bf16[4,2,64,512]{3,2,1,0:T(8,128)(2,1)S(1)}, bf16[4,2,64,512]{3,2,1,0:T(8,128)(2,1)}, u32[]{:S(2)}) copy-start(bf16[4,2,64,512]{3,2,1,0:T(8,128)(2,1)} %copy-done.1) | copy-start | bytes 1572868
  (2 other events, 1.7 us)

commit v7 on v6

--- a/solution.py
+++ b/solution.py
@@ -75,13 +75,13 @@
         out[...] = (jnp.concatenate(runs, axis=0) if e else runs[0]).astype(BF16)
 
 
-def pieces_kernel(z_ref, fwd_in, bwd_in, both_out, fwd_ref, bwd_ref, sems):
+def pieces_kernel(z_ref, fwd_in, bwd_in, fwd_out, bwd_out, fwd_ref, bwd_ref, sems):
     pairs = ((fwd_in, fwd_ref), (bwd_in, bwd_ref))
     copies = [pltpu.make_async_copy(source, target, sems.at[n]) for n, (source, target) in enumerate(pairs)]
     for copy in copies:
         copy.start()
     rows, cols = fwd_ref.shape[1:]
-    piece = both_out.shape[2]
+    piece = fwd_out.shape[1]
     per_spin = rows // 4
     lane = cols // 4
     flat = lax.broadcasted_iota(jnp.int32, (piece, 1), 0) + z_ref[0] * piece
@@ -99,10 +99,10 @@
     copies[0].wait()
     for c in range(2):
         picked = mm(select, fwd_ref[c]).astype(BF16)
-        both_out[0, c] = mm(picked, perm).astype(BF16)
+        fwd_out[c] = mm(picked, perm).astype(BF16)
     copies[1].wait()
     for c in range(2):
-        both_out[1, c] = mm(select, bwd_ref[c]).astype(BF16)
+        bwd_out[c] = mm(select, bwd_ref[c]).astype(BF16)
 
 
 def links_kernel(extent, link_ref, *outs):
@@ -397,21 +397,23 @@
     )(eigvecs.transpose(0, 1, 2, 4, 3, 5).reshape(-1, 2, num_vecs))
     faces = [passed_along(face, axis, -1) for face, axis in zip(faces, ("gx", "gy", "gz"))]
 
-    both_pieces = pl.pallas_call(
+    piece_shape = jax.ShapeDtypeStruct((2, piece, cols), BF16)
+    fwd_piece, bwd_piece = pl.pallas_call(
         pieces_kernel,
-        out_shape=jax.ShapeDtypeStruct((2, 2, piece, cols), BF16),
+        out_shape=[piece_shape] * 2,
         in_specs=[SMEM] + [pl.BlockSpec(memory_space=pl.ANY)] * 2,
-        out_specs=VMEM,
+        out_specs=[VMEM] * 2,
         scratch_shapes=[
             pltpu.VMEM(forward_peram.shape, BF16),
             pltpu.VMEM(backward_peram.shape, BF16),
             pltpu.SemaphoreType.DMA((2,)),
         ],
         compiler_params=pltpu.CompilerParams(vmem_limit_bytes=60 * 2**20),
+        cost_estimate=pl.CostEstimate(flops=10**8, bytes_accessed=10**7, transcendentals=0),
         name="pieces",
     )(me[2:], forward_peram, backward_peram)
-    both_pieces, links = lax.optimization_barrier((both_pieces, links))
-    both_line, line = line_exchange(both_pieces, "gx", gx_n // 2, 1)
+    fwd_piece, links = lax.optimization_barrier((fwd_piece, links))
+    fwd_line, line = line_exchange(fwd_piece, "gx", gx_n // 2, 1)
 
     link_mats = pl.pallas_call(
         functools.partial(links_kernel, extent),
@@ -438,13 +440,11 @@
         name="correlate",
     )(vec, *faces, *link_mats)
 
-    partial, both_line = lax.optimization_barrier((partial, both_line))
+    partial, fwd_line = lax.optimization_barrier((partial, fwd_line))
     by_core = partial.reshape((chips, 2) + partial.shape[1:])
     summed = added(part_at(by_core, core, 1), passed_in_gz(part_at(by_core, 1 - core, 1), 0, 1))
     rounds = gx_n.bit_length() - 1
-    first_line = line
-    fwd_line, line = line_exchange(both_line[:, 0], "gx", gx_n // 4, rounds - 1, first_line)
-    bwd_line, _ = line_exchange(both_line[:, 1], "gx", gx_n // 4, rounds - 1, first_line)
+    fwd_line, line = line_exchange(fwd_line, "gx", gx_n // 4, rounds - 1, line)
     plane = [(dx, dy) for dy in range(chips) for dx in range(gy_n)]
 
     def plane_part(dx, dy):
@@ -452,7 +452,8 @@
         return part_at(part, lax.rem(gy + dx, gy_n) if split > 1 else 0, 1)
 
     summed = added(*[passed_in_plane(plane_part(dx, dy), dx, dy) for dx, dy in plane])
-    summed, fwd_line, bwd_line = lax.optimization_barrier((summed, fwd_line, bwd_line))
+    summed, fwd_line, bwd_piece = lax.optimization_barrier((summed, fwd_line, bwd_piece))
+    bwd_line, _ = line_exchange(bwd_piece, "gx", gx_n // 2, rounds)
 
     four = gy_n == 2 and chips == 2
     fwd_parts = {(dx, dy, 0): passed_in_plane(fwd_line, dx, dy) for dx, dy in plane if not (four and dx and dy)}
@@ -465,20 +466,23 @@
         summed = added(part_at(halves, bit), lax.ppermute(part_at(halves, 1 - bit), "gx", pairs))
         distance //= 2
     elem_line, offsets = line_exchange(summed[0], "gx", gx_n // 2, rounds - 1)
+    fwd_parts[0, 0, 1] = passed_in_gz(fwd_line, 0, 1)
     if four:
-        over_x, over_y = fwd_parts[1, 0, 0], fwd_parts[0, 1, 0]
-        elem_line, over_x, over_y = lax.optimization_barrier((elem_line, over_x, over_y))
-        fwd_parts[1, 0, 0], fwd_parts[0, 1, 0] = over_x, over_y
-        corner = [passed_in_plane(over_y[:, :1], 1, 0), passed_in_plane(over_x[:, 1:], 0, 1)]
-        fwd_parts[1, 1, 0] = jnp.concatenate(corner, axis=1)
+        keys = [(1, 0, 0), (0, 1, 0), (0, 0, 1)]
+        elem_line, bwd_line, *parts = lax.optimization_barrier((elem_line, bwd_line, *[fwd_parts[key] for key in keys]))
+        fwd_parts.update(zip(keys, parts))
+        fwd_parts[1, 1, 0] = passed_in_plane(fwd_parts[0, 1, 0], 1, 0)
+    bwd_parts = {(dy, 0): passed_in_gz(bwd_line, dy, 0) if dy else bwd_line for dy in range(chips)}
     elem_line, _ = line_exchange(elem_line, "gx", 1, 1, offsets)
-    for dx, dy in plane:
-        fwd_parts[dx, dy, 1] = passed_in_gz(fwd_parts[dx, dy, 0], 0, 1)
     elem_keys = plane if split > 1 else [(0, dy) for dy in range(chips)]
     elem_own = jnp.stack([passed_in_plane(elem_line, dx, dy) for dx, dy in elem_keys])
-    elem_own, bwd_line = lax.optimization_barrier((elem_own, bwd_line))
+    late = [(1, 1, 0)] if four else []
+    elem_own, *parts = lax.optimization_barrier((elem_own, *[fwd_parts[key] for key in late], *bwd_parts.values()))
+    fwd_parts.update(zip(late, parts))
+    bwd_parts.update(zip(list(bwd_parts), parts[len(late) :]))
     elem_parts = [elem_own, passed_in_gz(elem_own, 0, 1)]
-    bwd_parts = {(dy, 0): passed_in_gz(bwd_line, dy, 0) if dy else bwd_line for dy in range(chips)}
+    for dx, dy in plane[1:]:
+        fwd_parts[dx, dy, 1] = passed_in_gz(fwd_parts[dx, dy, 0], 0, 1)
     for dy in range(chips):
         bwd_parts[dy, 1] = passed_in_gz(bwd_parts[dy, 0], 0, 1)
 

time: 99.2 us -> 85.5 us (0.86)
  waiting for transfers between devices: 42.5 us -> 29.8 us
  local copies, waits for them, and re-layouts: 5.01 us -> 3.07 us
  starting transfers between devices: 29.5 us -> 30.5 us
    ppermute x9, waiting for transfers between devices: 6.6 us -> 1.72 us  [passed_in_gz(): return lax.ppermute(value, 'gz', pairs)]
    ppermute x10 -> x9, waiting for transfers between devices: 13.6 us -> 9.73 us  [passed_in_plane(): return lax.ppermute(value, ('gy', 'gz'), pairs)]
    ppermute x2, waiting for transfers between devices: 3.43 us -> 0.08 us  [on_device(): lax.ppermute(part_at(halves, 1 - bit), 'gx', pairs)]
    unnamed x13 -> x10, local copies, waits for them, and re-layouts: 3.52 us -> 1.68 us
    ppermute x9, starting transfers between devices: 2.39 us -> 4.12 us  [passed_in_gz(): return lax.ppermute(value, 'gz', pairs)]
    ppermute x10 -> x9, starting transfers between devices: 9.96 us -> 9.59 us  [passed_in_plane(): return lax.ppermute(value, ('gy', 'gz'), pairs)]
    ppermute x5 -> x6, waiting for transfers between devices: 17.8 us -> 17.9 us  [line_exchange(): gathered = jnp.concatenate([gathered, lax.ppermute(gathered, axis, pairs)])]
    ppermute x5 -> x6, starting transfers between devices: 9.86 us -> 9.78 us  [line_exchange(): gathered = jnp.concatenate([gathered, lax.ppermute(gathered, axis, pairs)])]
  transfers between devices with their start and end apart: 29 -> 29, of which waited for: 16 -> 15; matrix products, arithmetic and copies ran while one was open for 3% -> 3% of each run, Pallas kernels for 12% -> 14%
where the time goes in v7:
time: 85.5 us; the launch traced here: 85.2 us
  starting transfers between devices  30.5 us (36%)
  waiting for transfers between devices  29.8 us (35%)
  Pallas kernels  20.2 us (24%)
  local copies, waits for them, and re-layouts  3.07 us (4%)
  other arithmetic  1.38 us (2%)
    ppermute x6, waiting for transfers between devices, line_exchange(): gathered = jnp.concatenate([gathered, lax.ppermute(gathered, axis, pairs)])  17.9 us
    pallas_call x1, Pallas kernels, on_device(): pl.pallas_call(functools.partial(left_kernel, 1.0 / math.sqrt(4 * num_vec...  10.1 us
    ppermute x6, starting transfers between devices, line_exchange(): gathered = jnp.concatenate([gathered, lax.ppermute(gathered, axis, pairs)])  9.78 us
    ppermute x9, waiting for transfers between devices, passed_in_plane(): return lax.ppermute(value, ('gy', 'gz'), pairs)  9.73 us
    ppermute x9, starting transfers between devices, passed_in_plane(): return lax.ppermute(value, ('gy', 'gz'), pairs)  9.59 us
    pallas_call x1, Pallas kernels, on_device(): pl.pallas_call(functools.partial(right_kernel, gz_n, tuple(bwd_parts)), o...  5.81 us
    ppermute x9, starting transfers between devices, passed_in_gz(): return lax.ppermute(value, 'gz', pairs)  4.12 us
    ppermute x2, starting transfers between devices, on_device(): lax.ppermute(part_at(halves, 1 - bit), 'gx', pairs)  3.98 us
  transfers between devices with their start and end apart: 29, of which 15 were waited for; matrix products, arithmetic and copies ran while one was open for 3% of the time, Pallas kernels for 14%

profile of v7, /device:TPU:0, one launch (start us, length us, event | category | flops | bytes accessed | tf_op | source)
XLA Modules:
  0.0 85.2 jit_solution(13492500352057370202)
XLA Ops:
  0.0 2.4 %pieces.1 = (bf16[2,64,512]{2,1,0:T(8,128)(2,1)}, bf16[2,64,512]{2,1,0:T(8,128)(2,1)}) custom-call(s32[1]{0:T(128)} %bitcast.2.z_ref, bf16[2,256,512]{2,1,0:T(8,128)(2,1)} %fwd_in.1, bf16[2,256,512]{2,1,0:T(8,128)(2,1)} %bwd_in.1), custom_call_target="tpu_custom_call" | custom-call | flops 100000000 | bytes 10000000 | tf_op jit(solution)/shard_map/pieces/pallas_call | solution.py:401
  2.5 4.1 %collective-permute-start.3 = (bf16[1,2,64,512]{3,2,1,0:T(8,128)(2,1)}, bf16[1,2,64,512]{3,2,1,0:T(8,128)(2,1)S(1)}, u32[]{:S(2)}, u32[]{:S(2)}) collective-permute-start(bf16[1,2,64,512]{3,2,1,0:T(8,128)(2,1)} %bitcast.47), channel_id=1, source_target_pairs={{0,16},{8,24},{16,0},{24,8},{1,17},{9,25},{17,1},{25,9},{2,18},{10... | collective-permute-start | bytes 393224 | tf_op jit(solution)/shard_map/ppermute | solution.py:363
  6.6 0.9 %copy-done = bf16[2,4,4,2,3,256]{5,3,4,2,1,0:T(2,128)(2,1)S(1)} copy-done((bf16[2,4,4,2,3,256]{5,3,4,2,1,0:T(2,128)(2,1)S(1)}, bf16[2,4,4,2,3,256]{5,3,4,2,1,0:T(2,128)(2,1)}, u32[]{:S(2)}) %copy-start) | copy-done | bytes 98328
  7.5 1.4 %collective-permute-start = (bf16[96,256]{1,0:T(8,128)(2,1)S(1)}, bf16[96,256]{1,0:T(8,128)(2,1)S(1)}, u32[]{:S(2)}, u32[]{:S(2)}) collective-permute-start(bf16[96,256]{1,0:T(8,128)(2,1)S(1)} %get-tuple-element.31), channel_id=1, source_target_pairs={{0,24},{8,0},{16,8},{24,16},{1,25},{9,1},{17,9},{25,17},{2,26},{10... | collective-permute-start | bytes 147464 | tf_op jit(solution)/shard_map/ppermute | solution.py:20
  8.9 1.5 %collective-permute-start.1 = (bf16[48,256]{1,0:T(8,128)(2,1)S(1)}, bf16[48,256]{1,0:T(8,128)(2,1)S(1)}, u32[]{:S(2)}, u32[]{:S(2)}) collective-permute-start(bf16[48,256]{1,0:T(8,128)(2,1)S(1)} %get-tuple-element.32), channel_id=1, source_target_pairs={{0,4},{4,0},{1,5},{5,1},{2,6},{6,2},{3,7},{7,3},{8,12},{12,8},{9,1... | collective-permute-start | bytes 73736 | tf_op jit(solution)/shard_map/ppermute | solution.py:20
  10.5 1.0 %copy.12 = f32[2,4,4,3,2,3,3]{2,1,0,6,5,4,3:T(4,128)S(1)} copy(f32[2,4,4,3,2,3,3]{2,4,6,5,3,1,0:T(2,128)} %param.8) | data formatting | bytes 13824 | tf_op jit(solution)/shard_map/optimization_barrier | solution.py:415
  12.7 1.3 %correlate.1 = bf16[4,4,2,48,256]{4,3,2,1,0:T(8,128)(2,1)S(1)} custom-call(bf16[192,256]{1,0:T(8,128)(2,1)S(1)} %get-tuple-element.30.vec_ref, bf16[96,256]{1,0:T(8,128)(2,1)S(1)} %collective-permute-done.face0, bf16[48,256]{1,0:T(8,128)(2,1)S(1)} %collective-permute-done.1.face1, bf16[48,256]{1,0:T(8,128)(2,1)S(1)} %collective-permute-done.2.face2, ...), custom_call_target="tpu_custom_call" | custom-call | tf_op jit(solution)/shard_map/correlate/pallas_call | solution.py:434
  14.0 0.9 %pad_maximum_fusion.3 = bf16[2,2,64,512]{3,2,1,0:T(8,128)(2,1)S(1)} fusion(bf16[1,2,64,512]{3,2,1,0:T(8,128)(2,1)S(1)} %collective-permute-done.3, bf16[1,2,64,512]{3,2,1,0:T(8,128)(2,1)} %bitcast.48), kind=kLoop, calls=%fused_computation.7 | loop fusion | flops 131072 | bytes 524288 | tf_op jit(solution)/shard_map/concatenate | solution.py:363
  15.1 1.0 %collective-permute-start.4 = (bf16[2,4,2,48,256]{4,3,1,2,0:T(8,128)(2,1)S(1)}, bf16[2,4,2,48,256]{4,3,1,2,0:T(8,128)(2,1)S(1)}, u32[]{:S(2)}, u32[]{:S(2)}) collective-permute-start(bf16[2,4,2,48,256]{4,3,1,2,0:T(8,128)(2,1)S(1)} %bitcast.43), channel_id=1, source_target_pairs={{0,1},{1,0},{2,3},{3,2},{4,5},{5,4},{6,7},{7,6},{8,9},{9,8},{10,11... | collective-permute-start | bytes 1179656 | tf_op jit(solution)/shard_map/ppermute | solution.py:341
  16.1 1.1 %collective-permute-start.8 = (bf16[2,2,64,512]{3,2,1,0:T(8,128)(2,1)S(1)}, bf16[2,2,64,512]{3,2,1,0:T(8,128)(2,1)S(1)}, u32[]{:S(2)}, u32[]{:S(2)}) collective-permute-start(bf16[2,2,64,512]{3,2,1,0:T(8,128)(2,1)S(1)} %pad_maximum_fusion.3), channel_id=1, source_target_pairs={{0,8},{8,0},{16,24},{24,16},{1,9},{9,1},{17,25},{25,17},{2,10},{10... | collective-permute-start | bytes 786440 | tf_op jit(solution)/shard_map/ppermute | solution.py:363
  17.6 1.4 %collective-permute-start.5 = (bf16[4,48,256]{2,1,0:T(8,128)(2,1)S(1)}, bf16[4,48,256]{2,1,0:T(8,128)(2,1)S(1)}, u32[]{:S(2)}, u32[]{:S(2)}) collective-permute-start(bf16[4,48,256]{2,1,0:T(8,128)(2,1)S(1)} %get-tuple-element.57), channel_id=1, source_target_pairs={{0,4},{1,5},{2,6},{3,7},{4,0},{5,1},{6,2},{7,3},{8,12},{9,13},{10,... | collective-permute-start | bytes 294920 | tf_op jit(solution)/shard_map/ppermute | solution.py:354
  19.0 1.5 %collective-permute-start.7 = (bf16[4,48,256]{2,1,0:T(8,128)(2,1)S(1)}, bf16[4,48,256]{2,1,0:T(8,128)(2,1)S(1)}, u32[]{:S(2)}, u32[]{:S(2)}) collective-permute-start(bf16[4,48,256]{2,1,0:T(8,128)(2,1)S(1)} %get-tuple-element.58), channel_id=1, source_target_pairs={{0,6},{1,7},{2,4},{3,5},{4,2},{5,3},{6,0},{7,1},{8,14},{9,15},{10,... | collective-permute-start | bytes 294920 | tf_op jit(solution)/shard_map/ppermute | solution.py:354
  21.2 3.3 %collective-permute-done.8 = bf16[2,2,64,512]{3,2,1,0:T(8,128)(2,1)S(1)} collective-permute-done((bf16[2,2,64,512]{3,2,1,0:T(8,128)(2,1)S(1)}, bf16[2,2,64,512]{3,2,1,0:T(8,128)(2,1)S(1)}, u32[]{:S(2)}, u32[]{:S(2)}) %collective-permute-start.8) | collective-permute-done | bytes 262176 | tf_op jit(solution)/shard_map/ppermute | solution.py:363
  24.5 0.9 %collective-permute-done.7 = bf16[4,48,256]{2,1,0:T(8,128)(2,1)S(1)} collective-permute-done((bf16[4,48,256]{2,1,0:T(8,128)(2,1)S(1)}, bf16[4,48,256]{2,1,0:T(8,128)(2,1)S(1)}, u32[]{:S(2)}, u32[]{:S(2)}) %collective-permute-start.7) | collective-permute-done | bytes 98336 | tf_op jit(solution)/shard_map/ppermute | solution.py:354
  25.5 1.2 %collective-permute-done.6 = bf16[4,48,256]{2,1,0:T(8,128)(2,1)S(1)} collective-permute-done((bf16[4,48,256]{2,1,0:T(8,128)(2,1)S(1)}, bf16[4,48,256]{2,1,0:T(8,128)(2,1)S(1)}, u32[]{:S(2)}, u32[]{:S(2)}) %collective-permute-start.6) | collective-permute-done | bytes 98336 | tf_op jit(solution)/shard_map/ppermute | solution.py:354
  26.8 2.3 %collective-permute-start.9 = (bf16[2,48,256]{2,1,0:T(8,128)(2,1)S(1)}, bf16[2,48,256]{2,1,0:T(8,128)(2,1)S(1)}, u32[]{:S(2)}, u32[]{:S(2)}) collective-permute-start(bf16[2,48,256]{2,1,0:T(8,128)(2,1)S(1)} %dynamic-slice_bitcast_fusion.3), channel_id=1, source_target_pairs={{0,16},{8,24},{16,0},{24,8},{1,17},{9,25},{17,1},{25,9},{2,18},{10... | collective-permute-start | bytes 147464 | tf_op jit(solution)/shard_map/ppermute | solution.py:466
  29.7 1.4 %collective-permute-start.14 = (bf16[4,2,64,512]{3,2,1,0:T(8,128)(2,1)S(1)}, bf16[4,2,64,512]{3,2,1,0:T(8,128)(2,1)S(1)}, u32[]{:S(2)}, u32[]{:S(2)}) collective-permute-start(bf16[4,2,64,512]{3,2,1,0:T(8,128)(2,1)S(1)} %pad_maximum_fusion.refs_2_), channel_id=1, source_target_pairs={{0,4},{1,5},{2,6},{3,7},{4,0},{5,1},{6,2},{7,3},{8,12},{9,13},{10,... | collective-permute-start | bytes 1572872 | tf_op jit(solution)/shard_map/ppermute | solution.py:354
  31.9 1.7 %collective-permute-start.10 = (bf16[1,48,256]{2,1,0:T(8,128)(2,1)S(1)}, bf16[1,48,256]{2,1,0:T(8,128)(2,1)S(1)}, u32[]{:S(2)}, u32[]{:S(2)}) collective-permute-start(bf16[1,48,256]{2,1,0:T(8,128)(2,1)S(1)} %constant_dynamic-slice_fusion), channel_id=1, source_target_pairs={{0,8},{8,0},{16,24},{24,16},{1,9},{9,1},{17,25},{25,17},{2,10},{10... | collective-permute-start | bytes 73736 | tf_op jit(solution)/shard_map/ppermute | solution.py:466
  33.6 6.5 %collective-permute-done.12 = bf16[1,2,64,512]{3,2,1,0:T(8,128)(2,1)S(1)} collective-permute-done((bf16[1,2,64,512]{3,2,1,0:T(8,128)(2,1)S(1)}, bf16[1,2,64,512]{3,2,1,0:T(8,128)(2,1)S(1)}, u32[]{:S(2)}, u32[]{:S(2)}) %collective-permute-start.12) | collective-permute-done | bytes 131104 | tf_op jit(solution)/shard_map/ppermute | solution.py:363
  40.3 2.3 %collective-permute-start.11 = (bf16[1,48,256]{2,1,0:T(8,128)(2,1)S(1)}, bf16[1,48,256]{2,1,0:T(8,128)(2,1)S(1)}, u32[]{:S(2)}, u32[]{:S(2)}) collective-permute-start(bf16[1,48,256]{2,1,0:T(8,128)(2,1)S(1)} %add_convert_fusion), channel_id=1, source_target_pairs={{0,16},{8,24},{16,0},{24,8},{1,17},{9,25},{17,1},{25,9},{2,18},{10... | collective-permute-start | bytes 73736 | tf_op jit(solution)/shard_map/ppermute | solution.py:363
  42.6 3.3 %collective-permute-done.11 = bf16[1,48,256]{2,1,0:T(8,128)(2,1)S(1)} collective-permute-done((bf16[1,48,256]{2,1,0:T(8,128)(2,1)S(1)}, bf16[1,48,256]{2,1,0:T(8,128)(2,1)S(1)}, u32[]{:S(2)}, u32[]{:S(2)}) %collective-permute-start.11) | collective-permute-done | bytes 24608 | tf_op jit(solution)/shard_map/ppermute | solution.py:363
  45.9 2.2 %collective-permute-done.13 = bf16[2,2,64,512]{3,2,1,0:T(8,128)(2,1)S(1)} collective-permute-done((bf16[2,2,64,512]{3,2,1,0:T(8,128)(2,1)S(1)}, bf16[2,2,64,512]{3,2,1,0:T(8,128)(2,1)S(1)}, u32[]{:S(2)}, u32[]{:S(2)}) %collective-permute-start.13) | collective-permute-done | bytes 262176 | tf_op jit(solution)/shard_map/ppermute | solution.py:363
  48.1 1.6 %collective-permute-start.22 = (bf16[4,2,64,512]{3,2,1,0:T(8,128)(2,1)S(1)}, bf16[4,2,64,512]{3,2,1,0:T(8,128)(2,1)S(1)}, u32[]{:S(2)}, u32[]{:S(2)}) collective-permute-start(bf16[4,2,64,512]{3,2,1,0:T(8,128)(2,1)S(1)} %pad_maximum_fusion.1.refs_0_), channel_id=1, source_target_pairs={{0,2},{1,3},{2,0},{3,1},{4,6},{5,7},{6,4},{7,5},{8,10},{9,11},{10,... | collective-permute-start | bytes 1572872 | tf_op jit(solution)/shard_map/ppermute | solution.py:341
  50.3 1.4 %collective-permute-start.17 = (bf16[2,48,256]{2,1,0:T(8,128)(2,1)S(1)}, bf16[2,48,256]{2,1,0:T(8,128)(2,1)S(1)}, u32[]{:S(2)}, u32[]{:S(2)}) collective-permute-start(bf16[2,48,256]{2,1,0:T(8,128)(2,1)S(1)} %pad_maximum_fusion.5), channel_id=1, source_target_pairs={{0,8},{8,0},{16,24},{24,16},{1,9},{9,1},{17,25},{25,17},{2,10},{10... | collective-permute-start | bytes 147464 | tf_op jit(solution)/shard_map/ppermute | solution.py:363
  51.7 2.7 %collective-permute-done.17 = bf16[2,48,256]{2,1,0:T(8,128)(2,1)S(1)} collective-permute-done((bf16[2,48,256]{2,1,0:T(8,128)(2,1)S(1)}, bf16[2,48,256]{2,1,0:T(8,128)(2,1)S(1)}, u32[]{:S(2)}, u32[]{:S(2)}) %collective-permute-start.17) | collective-permute-done | bytes 49184 | tf_op jit(solution)/shard_map/ppermute | solution.py:363
  54.4 1.4 %collective-permute-start.20 = (bf16[4,48,256]{2,1,0:T(8,128)(2,1)S(1)}, bf16[4,48,256]{2,1,0:T(8,128)(2,1)S(1)}, u32[]{:S(2)}, u32[]{:S(2)}) collective-permute-start(bf16[4,48,256]{2,1,0:T(8,128)(2,1)S(1)} %constant_dynamic-update-slice_fusion), channel_id=1, source_target_pairs={{0,6},{1,7},{2,4},{3,5},{4,2},{5,3},{6,0},{7,1},{8,14},{9,15},{10,... | collective-permute-start | bytes 294920 | tf_op jit(solution)/shard_map/ppermute | solution.py:354
  55.8 1.5 %collective-permute-start.19 = (bf16[4,48,256]{2,1,0:T(8,128)(2,1)S(1)}, bf16[4,48,256]{2,1,0:T(8,128)(2,1)S(1)}, u32[]{:S(2)}, u32[]{:S(2)}) collective-permute-start(bf16[4,48,256]{2,1,0:T(8,128)(2,1)S(1)} %constant_dynamic-update-slice_fusion), channel_id=1, source_target_pairs={{0,2},{1,3},{2,0},{3,1},{4,6},{5,7},{6,4},{7,5},{8,10},{9,11},{10,... | collective-permute-start | bytes 294920 | tf_op jit(solution)/shard_map/ppermute | solution.py:354
  57.8 7.0 %collective-permute-done.20 = bf16[4,48,256]{2,1,0:T(8,128)(2,1)S(1)} collective-permute-done((bf16[4,48,256]{2,1,0:T(8,128)(2,1)S(1)}, bf16[4,48,256]{2,1,0:T(8,128)(2,1)S(1)}, u32[]{:S(2)}, u32[]{:S(2)}) %collective-permute-start.20) | collective-permute-done | bytes 98336 | tf_op jit(solution)/shard_map/ppermute | solution.py:354
  66.6 0.8 copy.16.chain_ref
  67.9 0.8 collective-permute-done.23.refs_1_
  69.3 10.1 %left.1.left_ref = bf16[4,256,2048]{2,1,0:T(8,128)(2,1)S(1)} custom-call(s32[3]{0:T(128)S(1)} %pad_add_fusion.me_ref, s32[4]{0:T(128)S(1)} %copy-done.2, f32[4,4,4]{2,1,0:T(4,128)S(1)} %copy-done.1, s32[4,2]{1,0:T(4,128)S(1)} %copy.16.chain_ref, bf16[4,4,48,256]{3,2,1,0:T(8,128)(2,1)S(1)} %pad_maximum_fusion.2.refs_0_, ...), custom_call_target="tpu_custom_call" | custom-call | flops 8000000000 | bytes 10000000 | tf_op jit(solution)/shard_map/left/pallas_call | solution.py:492
  79.4 5.8 %right.1 = bf16[4,2,256,512]{3,2,1,0:T(8,128)(2,1)} custom-call(bf16[4,256,2048]{2,1,0:T(8,128)(2,1)S(1)} %left.1.left_ref, bf16[4,2,64,512]{3,2,1,0:T(8,128)(2,1)S(1)} %pad_maximum_fusion.1.refs_0_, bf16[4,2,64,512]{3,2,1,0:T(8,128)(2,1)S(1)} %collective-permute-done.22.refs_1_, bf16[4,2,64,512]{3,2,1,0:T(8,128)(2,1)S(1)} %collective-permute-done.27.refs_2_, ...), custom_call_target="tpu_custom_call" | custom-call | tf_op jit(solution)/shard_map/right/pallas_call | solution.py:507
  (62 shorter events, 8.3 us)
Async XLA Ops:
  2.5 11.6 %collective-permute-start.3 = (bf16[1,2,64,512]{3,2,1,0:T(8,128)(2,1)}, bf16[1,2,64,512]{3,2,1,0:T(8,128)(2,1)S(1)}, u32[]{:S(2)}, u32[]{:S(2)}) collective-permute-start(bf16[1,2,64,512]{3,2,1,0:T(8,128)(2,1)} %bitcast.47), channel_id=1, source_target_pairs={{0,16},{8,24},{16,0},{24,8},{1,17},{9,25},{17,1},{25,9},{2,18},{10... | collective-permute-start | bytes 393224 | tf_op jit(solution)/shard_map/ppermute | solution.py:363
  7.5 5.2 %collective-permute-start = (bf16[96,256]{1,0:T(8,128)(2,1)S(1)}, bf16[96,256]{1,0:T(8,128)(2,1)S(1)}, u32[]{:S(2)}, u32[]{:S(2)}) collective-permute-start(bf16[96,256]{1,0:T(8,128)(2,1)S(1)} %get-tuple-element.31), channel_id=1, source_target_pairs={{0,24},{8,0},{16,8},{24,16},{1,25},{9,1},{17,9},{25,17},{2,26},{10... | collective-permute-start | bytes 147464 | tf_op jit(solution)/shard_map/ppermute | solution.py:20
  8.9 3.8 %collective-permute-start.1 = (bf16[48,256]{1,0:T(8,128)(2,1)S(1)}, bf16[48,256]{1,0:T(8,128)(2,1)S(1)}, u32[]{:S(2)}, u32[]{:S(2)}) collective-permute-start(bf16[48,256]{1,0:T(8,128)(2,1)S(1)} %get-tuple-element.32), channel_id=1, source_target_pairs={{0,4},{4,0},{1,5},{5,1},{2,6},{6,2},{3,7},{7,3},{8,12},{12,8},{9,1... | collective-permute-start | bytes 73736 | tf_op jit(solution)/shard_map/ppermute | solution.py:20
  10.4 2.3 %collective-permute-start.2 = (bf16[48,256]{1,0:T(8,128)(2,1)S(1)}, bf16[48,256]{1,0:T(8,128)(2,1)S(1)}, u32[]{:S(2)}, u32[]{:S(2)}) collective-permute-start(bf16[48,256]{1,0:T(8,128)(2,1)S(1)} %get-tuple-element.33), channel_id=1, source_target_pairs={{0,3},{1,0},{2,1},{3,2},{4,7},{5,4},{6,5},{7,6},{8,11},{9,8},{10,9... | collective-permute-start | bytes 73736 | tf_op jit(solution)/shard_map/ppermute | solution.py:20
  11.8 19.3 %copy-start.3 = (bf16[2,64,512]{2,1,0:T(8,128)(2,1)S(1)}, bf16[2,64,512]{2,1,0:T(8,128)(2,1)}, u32[]{:S(2)}) copy-start(bf16[2,64,512]{2,1,0:T(8,128)(2,1)} %get-tuple-element.44) | copy-start | bytes 393220
  15.0 54.4 %copy-start.1 = (f32[4,4,4]{2,1,0:T(4,128)S(1)}, f32[4,4,4]{2,1,0:T(4,128)}, u32[]{:S(2)}) copy-start(f32[4,4,4]{2,1,0:T(4,128)} %spin_ref.1) | copy-start | bytes 772
  15.0 54.4 %copy-start.2 = (s32[4]{0:T(128)S(1)}, s32[4]{0:T(128)}, u32[]{:S(2)}) copy-start(s32[4]{0:T(128)} %dirs_ref.1) | copy-start | bytes 52
  15.1 2.4 %collective-permute-start.4 = (bf16[2,4,2,48,256]{4,3,1,2,0:T(8,128)(2,1)S(1)}, bf16[2,4,2,48,256]{4,3,1,2,0:T(8,128)(2,1)S(1)}, u32[]{:S(2)}, u32[]{:S(2)}) collective-permute-start(bf16[2,4,2,48,256]{4,3,1,2,0:T(8,128)(2,1)S(1)} %bitcast.43), channel_id=1, source_target_pairs={{0,1},{1,0},{2,3},{3,2},{4,5},{5,4},{6,7},{7,6},{8,9},{9,8},{10,11... | collective-permute-start | bytes 1179656 | tf_op jit(solution)/shard_map/ppermute | solution.py:341
  16.1 8.4 %collective-permute-start.8 = (bf16[2,2,64,512]{3,2,1,0:T(8,128)(2,1)S(1)}, bf16[2,2,64,512]{3,2,1,0:T(8,128)(2,1)S(1)}, u32[]{:S(2)}, u32[]{:S(2)}) collective-permute-start(bf16[2,2,64,512]{3,2,1,0:T(8,128)(2,1)S(1)} %pad_maximum_fusion.3), channel_id=1, source_target_pairs={{0,8},{8,0},{16,24},{24,16},{1,9},{9,1},{17,25},{25,17},{2,10},{10... | collective-permute-start | bytes 786440 | tf_op jit(solution)/shard_map/ppermute | solution.py:363
  17.6 6.9 %collective-permute-start.5 = (bf16[4,48,256]{2,1,0:T(8,128)(2,1)S(1)}, bf16[4,48,256]{2,1,0:T(8,128)(2,1)S(1)}, u32[]{:S(2)}, u32[]{:S(2)}) collective-permute-start(bf16[4,48,256]{2,1,0:T(8,128)(2,1)S(1)} %get-tuple-element.57), channel_id=1, source_target_pairs={{0,4},{1,5},{2,6},{3,7},{4,0},{5,1},{6,2},{7,3},{8,12},{9,13},{10,... | collective-permute-start | bytes 294920 | tf_op jit(solution)/shard_map/ppermute | solution.py:354
  19.0 6.5 %collective-permute-start.7 = (bf16[4,48,256]{2,1,0:T(8,128)(2,1)S(1)}, bf16[4,48,256]{2,1,0:T(8,128)(2,1)S(1)}, u32[]{:S(2)}, u32[]{:S(2)}) collective-permute-start(bf16[4,48,256]{2,1,0:T(8,128)(2,1)S(1)} %get-tuple-element.58), channel_id=1, source_target_pairs={{0,6},{1,7},{2,4},{3,5},{4,2},{5,3},{6,0},{7,1},{8,14},{9,15},{10,... | collective-permute-start | bytes 294920 | tf_op jit(solution)/shard_map/ppermute | solution.py:354
  20.5 6.2 %collective-permute-start.6 = (bf16[4,48,256]{2,1,0:T(8,128)(2,1)S(1)}, bf16[4,48,256]{2,1,0:T(8,128)(2,1)S(1)}, u32[]{:S(2)}, u32[]{:S(2)}) collective-permute-start(bf16[4,48,256]{2,1,0:T(8,128)(2,1)S(1)} %get-tuple-element.59), channel_id=1, source_target_pairs={{0,2},{1,3},{2,0},{3,1},{4,6},{5,7},{6,4},{7,5},{8,10},{9,11},{10,... | collective-permute-start | bytes 294920 | tf_op jit(solution)/shard_map/ppermute | solution.py:354
  26.8 5.1 %collective-permute-start.9 = (bf16[2,48,256]{2,1,0:T(8,128)(2,1)S(1)}, bf16[2,48,256]{2,1,0:T(8,128)(2,1)S(1)}, u32[]{:S(2)}, u32[]{:S(2)}) collective-permute-start(bf16[2,48,256]{2,1,0:T(8,128)(2,1)S(1)} %dynamic-slice_bitcast_fusion.3), channel_id=1, source_target_pairs={{0,16},{8,24},{16,0},{24,8},{1,17},{9,25},{17,1},{25,9},{2,18},{10... | collective-permute-start | bytes 147464 | tf_op jit(solution)/shard_map/ppermute | solution.py:466
  29.1 19.0 %collective-permute-start.16 = (bf16[4,2,64,512]{3,2,1,0:T(8,128)(2,1)S(1)}, bf16[4,2,64,512]{3,2,1,0:T(8,128)(2,1)S(1)}, u32[]{:S(2)}, u32[]{:S(2)}) collective-permute-start(bf16[4,2,64,512]{3,2,1,0:T(8,128)(2,1)S(1)} %pad_maximum_fusion.refs_2_), channel_id=1, source_target_pairs={{0,1},{1,0},{2,3},{3,2},{4,5},{5,4},{6,7},{7,6},{8,9},{9,8},{10,11... | collective-permute-start | bytes 1572872 | tf_op jit(solution)/shard_map/ppermute | solution.py:341
  29.1 19.1 %collective-permute-start.15 = (bf16[4,2,64,512]{3,2,1,0:T(8,128)(2,1)S(1)}, bf16[4,2,64,512]{3,2,1,0:T(8,128)(2,1)S(1)}, u32[]{:S(2)}, u32[]{:S(2)}) collective-permute-start(bf16[4,2,64,512]{3,2,1,0:T(8,128)(2,1)S(1)} %pad_maximum_fusion.refs_2_), channel_id=1, source_target_pairs={{0,2},{1,3},{2,0},{3,1},{4,6},{5,7},{6,4},{7,5},{8,10},{9,11},{10,... | collective-permute-start | bytes 1572872 | tf_op jit(solution)/shard_map/ppermute | solution.py:354
  29.7 18.4 %collective-permute-start.14 = (bf16[4,2,64,512]{3,2,1,0:T(8,128)(2,1)S(1)}, bf16[4,2,64,512]{3,2,1,0:T(8,128)(2,1)S(1)}, u32[]{:S(2)}, u32[]{:S(2)}) collective-permute-start(bf16[4,2,64,512]{3,2,1,0:T(8,128)(2,1)S(1)} %pad_maximum_fusion.refs_2_), channel_id=1, source_target_pairs={{0,4},{1,5},{2,6},{3,7},{4,0},{5,1},{6,2},{7,3},{8,12},{9,13},{10,... | collective-permute-start | bytes 1572872 | tf_op jit(solution)/shard_map/ppermute | solution.py:354
  31.1 9.1 %collective-permute-start.12 = (bf16[1,2,64,512]{3,2,1,0:T(8,128)(2,1)S(1)}, bf16[1,2,64,512]{3,2,1,0:T(8,128)(2,1)S(1)}, u32[]{:S(2)}, u32[]{:S(2)}) collective-permute-start(bf16[1,2,64,512]{3,2,1,0:T(8,128)(2,1)S(1)} %bitcast.40), channel_id=1, source_target_pairs={{0,16},{8,24},{16,0},{24,8},{1,17},{9,25},{17,1},{25,9},{2,18},{10... | collective-permute-start | bytes 393224 | tf_op jit(solution)/shard_map/ppermute | solution.py:363
  31.9 8.3 %collective-permute-start.10 = (bf16[1,48,256]{2,1,0:T(8,128)(2,1)S(1)}, bf16[1,48,256]{2,1,0:T(8,128)(2,1)S(1)}, u32[]{:S(2)}, u32[]{:S(2)}) collective-permute-start(bf16[1,48,256]{2,1,0:T(8,128)(2,1)S(1)} %constant_dynamic-slice_fusion), channel_id=1, source_target_pairs={{0,8},{8,0},{16,24},{24,16},{1,9},{9,1},{17,25},{25,17},{2,10},{10... | collective-permute-start | bytes 73736 | tf_op jit(solution)/shard_map/ppermute | solution.py:466
  40.2 7.9 %collective-permute-start.13 = (bf16[2,2,64,512]{3,2,1,0:T(8,128)(2,1)S(1)}, bf16[2,2,64,512]{3,2,1,0:T(8,128)(2,1)S(1)}, u32[]{:S(2)}, u32[]{:S(2)}) collective-permute-start(bf16[2,2,64,512]{3,2,1,0:T(8,128)(2,1)S(1)} %pad_maximum_fusion.4), channel_id=1, source_target_pairs={{0,8},{8,0},{16,24},{24,16},{1,9},{9,1},{17,25},{25,17},{2,10},{10... | collective-permute-start | bytes 786440 | tf_op jit(solution)/shard_map/ppermute | solution.py:363
  40.3 5.6 %collective-permute-start.11 = (bf16[1,48,256]{2,1,0:T(8,128)(2,1)S(1)}, bf16[1,48,256]{2,1,0:T(8,128)(2,1)S(1)}, u32[]{:S(2)}, u32[]{:S(2)}) collective-permute-start(bf16[1,48,256]{2,1,0:T(8,128)(2,1)S(1)} %add_convert_fusion), channel_id=1, source_target_pairs={{0,16},{8,24},{16,0},{24,8},{1,17},{9,25},{17,1},{25,9},{2,18},{10... | collective-permute-start | bytes 73736 | tf_op jit(solution)/shard_map/ppermute | solution.py:363
  48.1 17.8 %collective-permute-start.22 = (bf16[4,2,64,512]{3,2,1,0:T(8,128)(2,1)S(1)}, bf16[4,2,64,512]{3,2,1,0:T(8,128)(2,1)S(1)}, u32[]{:S(2)}, u32[]{:S(2)}) collective-permute-start(bf16[4,2,64,512]{3,2,1,0:T(8,128)(2,1)S(1)} %pad_maximum_fusion.1.refs_0_), channel_id=1, source_target_pairs={{0,2},{1,3},{2,0},{3,1},{4,6},{5,7},{6,4},{7,5},{8,10},{9,11},{10,... | collective-permute-start | bytes 1572872 | tf_op jit(solution)/shard_map/ppermute | solution.py:341
  49.7 16.3 %collective-permute-start.21 = (bf16[4,2,64,512]{3,2,1,0:T(8,128)(2,1)S(1)}, bf16[4,2,64,512]{3,2,1,0:T(8,128)(2,1)}, u32[]{:S(2)}, u32[]{:S(2)}) collective-permute-start(bf16[4,2,64,512]{3,2,1,0:T(8,128)(2,1)S(1)} %collective-permute-done.15.refs_4_), channel_id=1, source_target_pairs={{0,4},{1,5},{2,6},{3,7},{4,0},{5,1},{6,2},{7,3},{8,12},{9,13},{10,... | collective-permute-start | bytes 1572872 | tf_op jit(solution)/shard_map/ppermute | solution.py:354
  50.3 4.1 %collective-permute-start.17 = (bf16[2,48,256]{2,1,0:T(8,128)(2,1)S(1)}, bf16[2,48,256]{2,1,0:T(8,128)(2,1)S(1)}, u32[]{:S(2)}, u32[]{:S(2)}) collective-permute-start(bf16[2,48,256]{2,1,0:T(8,128)(2,1)S(1)} %pad_maximum_fusion.5), channel_id=1, source_target_pairs={{0,8},{8,0},{16,24},{24,16},{1,9},{9,1},{17,25},{25,17},{2,10},{10... | collective-permute-start | bytes 147464 | tf_op jit(solution)/shard_map/ppermute | solution.py:363
  54.4 10.5 %collective-permute-start.20 = (bf16[4,48,256]{2,1,0:T(8,128)(2,1)S(1)}, bf16[4,48,256]{2,1,0:T(8,128)(2,1)S(1)}, u32[]{:S(2)}, u32[]{:S(2)}) collective-permute-start(bf16[4,48,256]{2,1,0:T(8,128)(2,1)S(1)} %constant_dynamic-update-slice_fusion), channel_id=1, source_target_pairs={{0,6},{1,7},{2,4},{3,5},{4,2},{5,3},{6,0},{7,1},{8,14},{9,15},{10,... | collective-permute-start | bytes 294920 | tf_op jit(solution)/shard_map/ppermute | solution.py:354
  55.8 9.0 %collective-permute-start.19 = (bf16[4,48,256]{2,1,0:T(8,128)(2,1)S(1)}, bf16[4,48,256]{2,1,0:T(8,128)(2,1)S(1)}, u32[]{:S(2)}, u32[]{:S(2)}) collective-permute-start(bf16[4,48,256]{2,1,0:T(8,128)(2,1)S(1)} %constant_dynamic-update-slice_fusion), channel_id=1, source_target_pairs={{0,2},{1,3},{2,0},{3,1},{4,6},{5,7},{6,4},{7,5},{8,10},{9,11},{10,... | collective-permute-start | bytes 294920 | tf_op jit(solution)/shard_map/ppermute | solution.py:354
  57.3 8.6 %collective-permute-start.18 = (bf16[4,48,256]{2,1,0:T(8,128)(2,1)S(1)}, bf16[4,48,256]{2,1,0:T(8,128)(2,1)S(1)}, u32[]{:S(2)}, u32[]{:S(2)}) collective-permute-start(bf16[4,48,256]{2,1,0:T(8,128)(2,1)S(1)} %constant_dynamic-update-slice_fusion), channel_id=1, source_target_pairs={{0,4},{1,5},{2,6},{3,7},{4,0},{5,1},{6,2},{7,3},{8,12},{9,13},{10,... | collective-permute-start | bytes 294920 | tf_op jit(solution)/shard_map/ppermute | solution.py:354
  64.8 3.1 %collective-permute-start.25 = (bf16[4,2,64,512]{3,2,1,0:T(8,128)(2,1)S(1)}, bf16[4,2,64,512]{3,2,1,0:T(8,128)(2,1)}, u32[]{:S(2)}, u32[]{:S(2)}) collective-permute-start(bf16[4,2,64,512]{3,2,1,0:T(8,128)(2,1)S(1)} %collective-permute-done.15.refs_4_), channel_id=1, source_target_pairs={{0,1},{1,0},{2,3},{3,2},{4,5},{5,4},{6,7},{7,6},{8,9},{9,8},{10,11... | collective-permute-start | bytes 1572872 | tf_op jit(solution)/shard_map/ppermute | solution.py:341
  64.8 2.8 %collective-permute-start.24 = (bf16[4,2,64,512]{3,2,1,0:T(8,128)(2,1)S(1)}, bf16[4,2,64,512]{3,2,1,0:T(8,128)(2,1)}, u32[]{:S(2)}, u32[]{:S(2)}) collective-permute-start(bf16[4,2,64,512]{3,2,1,0:T(8,128)(2,1)S(1)} %collective-permute-done.14.refs_3_), channel_id=1, source_target_pairs={{0,1},{1,0},{2,3},{3,2},{4,5},{5,4},{6,7},{7,6},{8,9},{9,8},{10,11... | collective-permute-start | bytes 1572872 | tf_op jit(solution)/shard_map/ppermute | solution.py:341
  66.0 3.3 %collective-permute-start.26 = (bf16[4,2,64,512]{3,2,1,0:T(8,128)(2,1)}, bf16[4,2,64,512]{3,2,1,0:T(8,128)(2,1)}, u32[]{:S(2)}, u32[]{:S(2)}) collective-permute-start(bf16[4,2,64,512]{3,2,1,0:T(8,128)(2,1)} %collective-permute-done.21.refs_6_), channel_id=1, source_target_pairs={{0,1},{1,0},{2,3},{3,2},{4,5},{5,4},{6,7},{7,6},{8,9},{9,8},{10,11... | collective-permute-start | bytes 1572872 | tf_op jit(solution)/shard_map/ppermute | solution.py:341
  66.1 2.6 %collective-permute-start.23 = (bf16[4,4,48,256]{3,2,1,0:T(8,128)(2,1)S(1)}, bf16[4,4,48,256]{3,2,1,0:T(8,128)(2,1)}, u32[]{:S(2)}, u32[]{:S(2)}) collective-permute-start(bf16[4,4,48,256]{3,2,1,0:T(8,128)(2,1)S(1)} %pad_maximum_fusion.2.refs_0_), channel_id=1, source_target_pairs={{0,1},{1,0},{2,3},{3,2},{4,5},{5,4},{6,7},{7,6},{8,9},{9,8},{10,11... | collective-permute-start | bytes 1179656 | tf_op jit(solution)/shard_map/ppermute | solution.py:341
  67.4 12.0 %collective-permute-start.27 = (bf16[4,2,64,512]{3,2,1,0:T(8,128)(2,1)S(1)}, bf16[4,2,64,512]{3,2,1,0:T(8,128)(2,1)S(1)}, u32[]{:S(2)}, u32[]{:S(2)}) collective-permute-start(bf16[4,2,64,512]{3,2,1,0:T(8,128)(2,1)S(1)} %pad_maximum_fusion.1.refs_0_), channel_id=1, source_target_pairs={{0,1},{1,0},{2,3},{3,2},{4,5},{5,4},{6,7},{7,6},{8,9},{9,8},{10,11... | collective-permute-start | bytes 1572872 | tf_op jit(solution)/shard_map/ppermute | solution.py:341
  67.6 11.8 %collective-permute-start.28 = (bf16[4,2,64,512]{3,2,1,0:T(8,128)(2,1)S(1)}, bf16[4,2,64,512]{3,2,1,0:T(8,128)(2,1)S(1)}, u32[]{:S(2)}, u32[]{:S(2)}) collective-permute-start(bf16[4,2,64,512]{3,2,1,0:T(8,128)(2,1)S(1)} %collective-permute-done.22.refs_1_), channel_id=1, source_target_pairs={{0,1},{1,0},{2,3},{3,2},{4,5},{5,4},{6,7},{7,6},{8,9},{9,8},{10,11... | collective-permute-start | bytes 1572872 | tf_op jit(solution)/shard_map/ppermute | solution.py:341
  (1 other events, 0.9 us)

commit v8 on v7

--- a/solution.py
+++ b/solution.py
@@ -217,7 +217,7 @@
 
 
 def left_kernel(inverse, plan, me_ref, dirs_ref, spin_ref, chain_ref, *refs):
-    line, elem_keys, fwd_keys = plan
+    line, fwd_keys = plan
     elem_in, refs = refs[:2], refs[2:]
     fwd_in, refs = refs[: len(fwd_keys)], refs[len(fwd_keys) :]
     out_ref, elem_all, elem_ref, x_ref, p_ref = refs
@@ -239,10 +239,9 @@
         return back(lax.div(gz, 2), dy, gz_n // 2) * 2 + back(lax.rem(gz, 2), dc, 2)
 
     for dc, ref in enumerate(elem_in):
-        for n, (dx, dy) in enumerate(elem_keys):
-            for place, offset in enumerate(line):
-                to = lax.bitwise_xor(gx, offset), gz_from(dy, dc), back(gy, dx, gy_n) if split > 1 else 0
-                elem_all[to] = ref[n, place]
+        for dy in range(gz_n // 2):
+            for n in range(gx_n * split):
+                elem_all[n // split, gz_from(dy, dc), n % split] = ref[dy, n]
     column = lax.broadcasted_iota(jnp.int32, (1, num_vecs), 1)
     source = jnp.zeros_like(column)
     half_rows = vec_rows // halves
@@ -413,7 +412,7 @@
         name="pieces",
     )(me[2:], forward_peram, backward_peram)
     fwd_piece, links = lax.optimization_barrier((fwd_piece, links))
-    fwd_line, line = line_exchange(fwd_piece, "gx", gx_n // 2, 1)
+    fwd_half = lax.ppermute(fwd_piece, "gx", [(n, n ^ (gx_n // 2)) for n in range(gx_n)])
 
     link_mats = pl.pallas_call(
         functools.partial(links_kernel, extent),
@@ -440,42 +439,34 @@
         name="correlate",
     )(vec, *faces, *link_mats)
 
-    partial, fwd_line = lax.optimization_barrier((partial, fwd_line))
+    rounds = gx_n.bit_length() - 1
+    partial, fwd_half = lax.optimization_barrier((partial, fwd_half))
     by_core = partial.reshape((chips, 2) + partial.shape[1:])
     summed = added(part_at(by_core, core, 1), passed_in_gz(part_at(by_core, 1 - core, 1), 0, 1))
-    rounds = gx_n.bit_length() - 1
-    fwd_line, line = line_exchange(fwd_line, "gx", gx_n // 4, rounds - 1, line)
-    plane = [(dx, dy) for dy in range(chips) for dx in range(gy_n)]
-
-    def plane_part(dx, dy):
-        part = part_at(summed, lax.rem(chip + dy, chips))
-        return part_at(part, lax.rem(gy + dx, gy_n) if split > 1 else 0, 1)
-
-    summed = added(*[passed_in_plane(plane_part(dx, dy), dx, dy) for dx, dy in plane])
+    fwd_line = jnp.stack([fwd_piece, fwd_half])
+    fwd_line, line = line_exchange(fwd_line, "gx", gx_n // 4, rounds - 1, (0, gx_n // 2))
+    summed = added(*[passed_in_gz(part_at(summed, lax.rem(chip + dy, chips)), dy, 0) if dy else part_at(summed, chip) for dy in range(chips)])
     summed, fwd_line, bwd_piece = lax.optimization_barrier((summed, fwd_line, bwd_piece))
     bwd_line, _ = line_exchange(bwd_piece, "gx", gx_n // 2, rounds)
 
+    plane = [(dx, dy) for dy in range(chips) for dx in range(gy_n)]
     four = gy_n == 2 and chips == 2
     fwd_parts = {(dx, dy, 0): passed_in_plane(fwd_line, dx, dy) for dx, dy in plane if not (four and dx and dy)}
-
-    distance = gx_n // 2
-    while distance:
-        halves = summed.reshape((2, distance) + summed.shape[1:])
-        bit = lax.rem(lax.div(gx, distance), 2)
-        pairs = [(n, n ^ distance) for n in range(gx_n)]
-        summed = added(part_at(halves, bit), lax.ppermute(part_at(halves, 1 - bit), "gx", pairs))
-        distance //= 2
-    elem_line, offsets = line_exchange(summed[0], "gx", gx_n // 2, rounds - 1)
     fwd_parts[0, 0, 1] = passed_in_gz(fwd_line, 0, 1)
+
+    area = ("gx", "gy") if split > 1 else "gx"
+    if split == 1:
+        summed = added(summed, *[passed_along(summed, "gy", dx) for dx in range(1, gy_n)])
+    summed = lax.all_to_all(summed.reshape(gx_n * split, depth, num_vecs), area, 0, 0, tiled=True)
+    summed = jnp.sum(summed.astype(F32), axis=0).astype(BF16)
+    elem_line = lax.all_to_all(jnp.broadcast_to(summed, (gx_n * split, depth, num_vecs)), area, 0, 0, tiled=True)
     if four:
         keys = [(1, 0, 0), (0, 1, 0), (0, 0, 1)]
         elem_line, bwd_line, *parts = lax.optimization_barrier((elem_line, bwd_line, *[fwd_parts[key] for key in keys]))
         fwd_parts.update(zip(keys, parts))
         fwd_parts[1, 1, 0] = passed_in_plane(fwd_parts[0, 1, 0], 1, 0)
     bwd_parts = {(dy, 0): passed_in_gz(bwd_line, dy, 0) if dy else bwd_line for dy in range(chips)}
-    elem_line, _ = line_exchange(elem_line, "gx", 1, 1, offsets)
-    elem_keys = plane if split > 1 else [(0, dy) for dy in range(chips)]
-    elem_own = jnp.stack([passed_in_plane(elem_line, dx, dy) for dx, dy in elem_keys])
+    elem_own = jnp.stack([passed_in_gz(elem_line, dy, 0) if dy else elem_line for dy in range(chips)])
     late = [(1, 1, 0)] if four else []
     elem_own, *parts = lax.optimization_barrier((elem_own, *[fwd_parts[key] for key in late], *bwd_parts.values()))
     fwd_parts.update(zip(late, parts))
@@ -487,7 +478,7 @@
         bwd_parts[dy, 1] = passed_in_gz(bwd_parts[dy, 0], 0, 1)
 
     op_count = chain_order.shape[0]
-    plan = (line, tuple(elem_keys), tuple(fwd_parts))
+    plan = (line, tuple(fwd_parts))
     left_shape = (op_count, rows, 8 * num_vecs)
     left = pl.pallas_call(
         functools.partial(left_kernel, 1.0 / math.sqrt(4 * num_vecs), plan),

time: 85.5 us -> 92.2 us (1.078)
  waiting for transfers between devices: 29.8 us -> 32.7 us
  other arithmetic: 1.38 us -> 3.93 us
    ppermute x9 -> x11, waiting for transfers between devices: 1.72 us -> 13.1 us  [passed_in_gz(): return lax.ppermute(value, 'gz', pairs)]
    ppermute x9 -> x3, waiting for transfers between devices: 9.73 us -> 0.01 us  [passed_in_plane(): return lax.ppermute(value, ('gy', 'gz'), pairs)]
    all_to_all x0 -> x2, starting transfers between devices: none -> 9.48 us  [the longest x1 5.3 us: on_device(): lax.all_to_all(summed.reshape(gx_n * split, depth, num_vecs), area, 0, 0,...]
    ppermute x6 -> x3, starting transfers between devices: 9.78 us -> 4.07 us  [line_exchange(): gathered = jnp.concatenate([gathered, lax.ppermute(gathered, axis, pairs)])]
    ppermute x9 -> x3, starting transfers between devices: 9.59 us -> 3.9 us  [passed_in_plane(): return lax.ppermute(value, ('gy', 'gz'), pairs)]
    all_to_all x0 -> x2, waiting for transfers between devices: none -> 4.43 us  [the longest x1 4.42 us: on_device(): lax.all_to_all(jnp.broadcast_to(summed, (gx_n * split, depth, num_vecs)),...]
    ppermute x6 -> x3, waiting for transfers between devices: 17.9 us -> 14.8 us  [line_exchange(): gathered = jnp.concatenate([gathered, lax.ppermute(gathered, axis, pairs)])]
    ppermute x9 -> x11, starting transfers between devices: 4.12 us -> 6.29 us  [passed_in_gz(): return lax.ppermute(value, 'gz', pairs)]
  transfers between devices with their start and end apart: 29 -> 23, of which waited for: 15 -> 7; matrix products, arithmetic and copies ran while one was open for 3% -> 6% of each run, Pallas kernels for 14% -> 13%
where the time goes in v8:
time: 92.2 us; the launch traced here: 91.7 us
  waiting for transfers between devices  32.7 us (35%)
  starting transfers between devices  30.9 us (34%)
  Pallas kernels  20.3 us (22%)
  other arithmetic  3.93 us (4%)
  local copies, waits for them, and re-layouts  3.68 us (4%)
    ppermute x3, waiting for transfers between devices, line_exchange(): gathered = jnp.concatenate([gathered, lax.ppermute(gathered, axis, pairs)])  14.8 us
    ppermute x11, waiting for transfers between devices, passed_in_gz(): return lax.ppermute(value, 'gz', pairs)  13.1 us
    pallas_call x1, Pallas kernels, on_device(): pl.pallas_call(functools.partial(left_kernel, 1.0 / math.sqrt(4 * num_vec...  10.1 us
    ppermute x11, starting transfers between devices, passed_in_gz(): return lax.ppermute(value, 'gz', pairs)  6.29 us
    pallas_call x1, Pallas kernels, on_device(): pl.pallas_call(functools.partial(right_kernel, gz_n, tuple(bwd_parts)), o...  5.81 us
    all_to_all x1, starting transfers between devices, on_device(): lax.all_to_all(summed.reshape(gx_n * split, depth, num_vecs), area, 0, 0,...  5.3 us
    all_to_all x1, waiting for transfers between devices, on_device(): lax.all_to_all(jnp.broadcast_to(summed, (gx_n * split, depth, num_vecs)),...  4.42 us
    all_to_all x1, starting transfers between devices, on_device(): lax.all_to_all(jnp.broadcast_to(summed, (gx_n * split, depth, num_vecs)),...  4.18 us
  transfers between devices with their start and end apart: 23, of which 7 were waited for; matrix products, arithmetic and copies ran while one was open for 6% of the time, Pallas kernels for 13%

profile of v8, /device:TPU:0, one launch (start us, length us, event | category | flops | bytes accessed | tf_op | source)
XLA Modules:
  0.0 91.7 jit_solution(9719321045147071597)
XLA Ops:
  0.0 2.5 %pieces.1 = (bf16[2,64,512]{2,1,0:T(8,128)(2,1)}, bf16[2,64,512]{2,1,0:T(8,128)(2,1)}) custom-call(s32[1]{0:T(128)} %bitcast.2.z_ref, bf16[2,256,512]{2,1,0:T(8,128)(2,1)} %fwd_in.1, bf16[2,256,512]{2,1,0:T(8,128)(2,1)} %bwd_in.1), custom_call_target="tpu_custom_call" | custom-call | flops 100000000 | bytes 10000000 | tf_op jit(solution)/shard_map/pieces/pallas_call | solution.py:400
  2.5 4.1 %collective-permute-start.3 = (bf16[2,64,512]{2,1,0:T(8,128)(2,1)}, bf16[2,64,512]{2,1,0:T(8,128)(2,1)S(1)}, u32[]{:S(2)}, u32[]{:S(2)}) collective-permute-start(bf16[2,64,512]{2,1,0:T(8,128)(2,1)} %get-tuple-element.39), channel_id=1, source_target_pairs={{0,16},{8,24},{16,0},{24,8},{1,17},{9,25},{17,1},{25,9},{2,18},{10... | collective-permute-start | bytes 393224 | tf_op jit(solution)/shard_map/ppermute | solution.py:415
  6.6 0.9 copy-done
  7.5 1.4 %collective-permute-start = (bf16[96,256]{1,0:T(8,128)(2,1)S(1)}, bf16[96,256]{1,0:T(8,128)(2,1)S(1)}, u32[]{:S(2)}, u32[]{:S(2)}) collective-permute-start(bf16[96,256]{1,0:T(8,128)(2,1)S(1)} %get-tuple-element.31), channel_id=1, source_target_pairs={{0,24},{8,0},{16,8},{24,16},{1,25},{9,1},{17,9},{25,17},{2,26},{10... | collective-permute-start | bytes 147464 | tf_op jit(solution)/shard_map/ppermute | solution.py:20
  8.9 1.5 %collective-permute-start.1 = (bf16[48,256]{1,0:T(8,128)(2,1)S(1)}, bf16[48,256]{1,0:T(8,128)(2,1)S(1)}, u32[]{:S(2)}, u32[]{:S(2)}) collective-permute-start(bf16[48,256]{1,0:T(8,128)(2,1)S(1)} %get-tuple-element.32), channel_id=1, source_target_pairs={{0,4},{4,0},{1,5},{5,1},{2,6},{6,2},{3,7},{7,3},{8,12},{12,8},{9,1... | collective-permute-start | bytes 73736 | tf_op jit(solution)/shard_map/ppermute | solution.py:20
  10.5 1.0 %copy.10 = f32[2,4,4,3,2,3,3]{2,1,0,6,5,4,3:T(4,128)S(1)} copy(f32[2,4,4,3,2,3,3]{2,4,6,5,3,1,0:T(2,128)} %param.8) | data formatting | bytes 13824 | tf_op jit(solution)/shard_map/optimization_barrier | solution.py:414
  11.8 0.6 link_matrices.1
  12.7 1.3 %correlate.1 = bf16[4,4,2,48,256]{4,3,2,1,0:T(8,128)(2,1)S(1)} custom-call(bf16[192,256]{1,0:T(8,128)(2,1)S(1)} %get-tuple-element.30.vec_ref, bf16[96,256]{1,0:T(8,128)(2,1)S(1)} %collective-permute-done.face0, bf16[48,256]{1,0:T(8,128)(2,1)S(1)} %collective-permute-done.1.face1, bf16[48,256]{1,0:T(8,128)(2,1)S(1)} %collective-permute-done.2.face2, ...), custom_call_target="tpu_custom_call" | custom-call | tf_op jit(solution)/shard_map/correlate/pallas_call | solution.py:433
  14.1 1.0 %collective-permute-start.4 = (bf16[2,4,2,48,256]{4,3,2,1,0:T(8,128)(2,1)S(1)}, bf16[2,4,2,48,256]{4,3,2,1,0:T(8,128)(2,1)S(1)}, u32[]{:S(2)}, u32[]{:S(2)}) collective-permute-start(bf16[2,4,2,48,256]{4,3,2,1,0:T(8,128)(2,1)S(1)} %dynamic-slice_bitcast_fusion), channel_id=1, source_target_pairs={{0,1},{1,0},{2,3},{3,2},{4,5},{5,4},{6,7},{7,6},{8,9},{9,8},{10,11... | collective-permute-start | bytes 1179656 | tf_op jit(solution)/shard_map/ppermute | solution.py:340
  15.1 0.9 %pad_maximum_fusion.3 = bf16[2,2,64,512]{3,2,1,0:T(8,128)(2,1)S(1)} fusion(bf16[1,2,64,512]{3,2,1,0:T(8,128)(2,1)S(1)} %bitcast.34, bf16[1,2,64,512]{3,2,1,0:T(8,128)(2,1)} %bitcast.32), kind=kLoop, calls=%fused_computation.8 | loop fusion | flops 131072 | bytes 524288 | tf_op jit(solution)/shard_map/stack | solution.py:446
  16.1 1.1 %collective-permute-start.6 = (bf16[2,2,64,512]{3,2,1,0:T(8,128)(2,1)S(1)}, bf16[2,2,64,512]{3,2,1,0:T(8,128)(2,1)S(1)}, u32[]{:S(2)}, u32[]{:S(2)}) collective-permute-start(bf16[2,2,64,512]{3,2,1,0:T(8,128)(2,1)S(1)} %pad_maximum_fusion.3), channel_id=1, source_target_pairs={{0,8},{8,0},{16,24},{24,16},{1,9},{9,1},{17,25},{25,17},{2,10},{10... | collective-permute-start | bytes 786440 | tf_op jit(solution)/shard_map/ppermute | solution.py:362
  17.3 1.6 %collective-permute-start.5 = (bf16[4,2,48,256]{3,2,1,0:T(8,128)(2,1)S(1)}, bf16[4,2,48,256]{3,2,1,0:T(8,128)(2,1)S(1)}, u32[]{:S(2)}, u32[]{:S(2)}) collective-permute-start(bf16[4,2,48,256]{3,2,1,0:T(8,128)(2,1)S(1)} %dynamic-slice_bitcast_fusion.1), channel_id=1, source_target_pairs={{0,2},{1,3},{2,0},{3,1},{4,6},{5,7},{6,4},{7,5},{8,10},{9,11},{10,... | collective-permute-start | bytes 589832 | tf_op jit(solution)/shard_map/ppermute | solution.py:340
  18.9 5.5 %collective-permute-done.6 = bf16[2,2,64,512]{3,2,1,0:T(8,128)(2,1)S(1)} collective-permute-done((bf16[2,2,64,512]{3,2,1,0:T(8,128)(2,1)S(1)}, bf16[2,2,64,512]{3,2,1,0:T(8,128)(2,1)S(1)}, u32[]{:S(2)}, u32[]{:S(2)}) %collective-permute-start.6) | collective-permute-done | bytes 262176 | tf_op jit(solution)/shard_map/ppermute | solution.py:362
  24.5 0.7 fusion.1
  25.2 5.3 %all-to-all-start = ((bf16[8,48,256]{2,1,0:T(8,128)(2,1)}), bf16[8,48,256]{2,1,0:T(8,128)(2,1)S(1)}, u32[]{:S(2)}, u32[]{:S(2)}) async-start(bf16[8,48,256]{2,1,0:T(8,128)(2,1)} %bitcast.12), calls=%async_computation | async-start | bytes 393216 | tf_op jit(solution)/shard_map/all_to_all | solution.py:460
  30.5 2.9 %collective-permute-start.7 = (bf16[1,2,64,512]{3,2,1,0:T(8,128)(2,1)S(1)}, bf16[1,2,64,512]{3,2,1,0:T(8,128)(2,1)S(1)}, u32[]{:S(2)}, u32[]{:S(2)}) collective-permute-start(bf16[1,2,64,512]{3,2,1,0:T(8,128)(2,1)S(1)} %bitcast.29), channel_id=1, source_target_pairs={{0,16},{8,24},{16,0},{24,8},{1,17},{9,25},{17,1},{25,9},{2,18},{10... | collective-permute-start | bytes 393224 | tf_op jit(solution)/shard_map/ppermute | solution.py:362
  33.4 1.5 %collective-permute-start.10 = (bf16[4,2,64,512]{3,2,1,0:T(8,128)(2,1)S(1)}, bf16[4,2,64,512]{3,2,1,0:T(8,128)(2,1)S(1)}, u32[]{:S(2)}, u32[]{:S(2)}) collective-permute-start(bf16[4,2,64,512]{3,2,1,0:T(8,128)(2,1)S(1)} %pad_maximum_fusion.refs_2_), channel_id=1, source_target_pairs={{0,2},{1,3},{2,0},{3,1},{4,6},{5,7},{6,4},{7,5},{8,10},{9,11},{10,... | collective-permute-start | bytes 1572872 | tf_op jit(solution)/shard_map/ppermute | solution.py:353
  34.9 1.5 %collective-permute-start.9 = (bf16[4,2,64,512]{3,2,1,0:T(8,128)(2,1)S(1)}, bf16[4,2,64,512]{3,2,1,0:T(8,128)(2,1)S(1)}, u32[]{:S(2)}, u32[]{:S(2)}) collective-permute-start(bf16[4,2,64,512]{3,2,1,0:T(8,128)(2,1)S(1)} %pad_maximum_fusion.refs_2_), channel_id=1, source_target_pairs={{0,4},{1,5},{2,6},{3,7},{4,0},{5,1},{6,2},{7,3},{8,12},{9,13},{10,... | collective-permute-start | bytes 1572872 | tf_op jit(solution)/shard_map/ppermute | solution.py:353
  36.4 7.0 %collective-permute-done.7 = bf16[1,2,64,512]{3,2,1,0:T(8,128)(2,1)S(1)} collective-permute-done((bf16[1,2,64,512]{3,2,1,0:T(8,128)(2,1)S(1)}, bf16[1,2,64,512]{3,2,1,0:T(8,128)(2,1)S(1)}, u32[]{:S(2)}, u32[]{:S(2)}) %collective-permute-start.7) | collective-permute-done | bytes 131104 | tf_op jit(solution)/shard_map/ppermute | solution.py:362
  43.6 0.7 broadcast_in_dim.6
  44.3 4.2 %all-to-all-start.1 = ((bf16[8,48,256]{2,1,0:T(8,128)(2,1)}), bf16[8,48,256]{2,1,0:T(8,128)(2,1)S(1)}, u32[]{:S(2)}, u32[]{:S(2)}) async-start(bf16[8,48,256]{2,1,0:T(8,128)(2,1)} %broadcast_in_dim.6), calls=%async_computation.1 | async-start | bytes 393216 | tf_op jit(solution)/shard_map/all_to_all | solution.py:462
  48.5 2.3 %collective-permute-done.8 = bf16[2,2,64,512]{3,2,1,0:T(8,128)(2,1)} collective-permute-done((bf16[2,2,64,512]{3,2,1,0:T(8,128)(2,1)S(1)}, bf16[2,2,64,512]{3,2,1,0:T(8,128)(2,1)}, u32[]{:S(2)}, u32[]{:S(2)}) %collective-permute-start.8) | collective-permute-done | bytes 262176 | tf_op jit(solution)/shard_map/ppermute | solution.py:362
  50.8 1.0 %pad_maximum_fusion.1.refs_0_ = bf16[4,2,64,512]{3,2,1,0:T(8,128)(2,1)S(1)} fusion(bf16[2,2,64,512]{3,2,1,0:T(8,128)(2,1)} %collective-permute-done.8, bf16[1,2,64,512]{3,2,1,0:T(8,128)(2,1)S(1)} %collective-permute-done.7, bf16[1,2,64,512]{3,2,1,0:T(8,128)(2,1)S(1)} %bitcast.31), kind=kLoop, calls=%fused_computation.3 | loop fusion | flops 524288 | bytes 1048576 | tf_op jit(solution)/shard_map/concatenate | solution.py:362
  51.8 4.4 %all-to-all-done.1 = bf16[8,48,256]{2,1,0:T(8,128)(2,1)S(1)} async-done(((bf16[8,48,256]{2,1,0:T(8,128)(2,1)}), bf16[8,48,256]{2,1,0:T(8,128)(2,1)S(1)}, u32[]{:S(2)}, u32[]{:S(2)}) %all-to-all-start.1) | async-done | bytes 196640 | tf_op jit(solution)/shard_map/all_to_all | solution.py:462
  56.2 1.5 %collective-permute-start.14 = (bf16[4,2,64,512]{3,2,1,0:T(8,128)(2,1)S(1)}, bf16[4,2,64,512]{3,2,1,0:T(8,128)(2,1)S(1)}, u32[]{:S(2)}, u32[]{:S(2)}) collective-permute-start(bf16[4,2,64,512]{3,2,1,0:T(8,128)(2,1)S(1)} %pad_maximum_fusion.1.refs_0_), channel_id=1, source_target_pairs={{0,2},{1,3},{2,0},{3,1},{4,6},{5,7},{6,4},{7,5},{8,10},{9,11},{10,... | collective-permute-start | bytes 1572872 | tf_op jit(solution)/shard_map/ppermute | solution.py:340
  57.8 0.9 %collective-permute-start.13 = (bf16[4,2,64,512]{3,2,1,0:T(8,128)(2,1)S(1)}, bf16[4,2,64,512]{3,2,1,0:T(8,128)(2,1)}, u32[]{:S(2)}, u32[]{:S(2)}) collective-permute-start(bf16[4,2,64,512]{3,2,1,0:T(8,128)(2,1)S(1)} %collective-permute-done.10.refs_4_), channel_id=1, source_target_pairs={{0,4},{1,5},{2,6},{3,7},{4,0},{5,1},{6,2},{7,3},{8,12},{9,13},{10,... | collective-permute-start | bytes 1572872 | tf_op jit(solution)/shard_map/ppermute | solution.py:353
  59.7 12.4 %collective-permute-done.12 = bf16[8,48,256]{2,1,0:T(8,128)(2,1)S(1)} collective-permute-done((bf16[8,48,256]{2,1,0:T(8,128)(2,1)S(1)}, bf16[8,48,256]{2,1,0:T(8,128)(2,1)S(1)}, u32[]{:S(2)}, u32[]{:S(2)}) %collective-permute-start.12) | collective-permute-done | bytes 196640 | tf_op jit(solution)/shard_map/ppermute | solution.py:340
  72.1 1.0 %pad_maximum_fusion.2.refs_0_ = bf16[2,8,48,256]{3,2,1,0:T(8,128)(2,1)S(1)} fusion(bf16[1,8,48,256]{3,2,1,0:T(8,128)(2,1)S(1)} %bitcast.36, bf16[1,8,48,256]{3,2,1,0:T(8,128)(2,1)} %bitcast.28), kind=kLoop, calls=%fused_computation.4 | loop fusion | flops 196608 | bytes 786432 | tf_op jit(solution)/shard_map/stack | solution.py:469
  73.7 0.8 copy.12.chain_ref
  75.0 0.7 collective-permute-done.15.refs_1_
  75.8 10.1 %left.1.left_ref = bf16[4,256,2048]{2,1,0:T(8,128)(2,1)S(1)} custom-call(s32[3]{0:T(128)S(1)} %pad_add_fusion.me_ref, s32[4]{0:T(128)S(1)} %copy-done.2, f32[4,4,4]{2,1,0:T(4,128)S(1)} %copy-done.1, s32[4,2]{1,0:T(4,128)S(1)} %copy.12.chain_ref, bf16[2,8,48,256]{3,2,1,0:T(8,128)(2,1)S(1)} %pad_maximum_fusion.2.refs_0_, ...), custom_call_target="tpu_custom_call" | custom-call | flops 8000000000 | bytes 10000000 | tf_op jit(solution)/shard_map/left/pallas_call | solution.py:483
  85.9 5.8 %right.1 = bf16[4,2,256,512]{3,2,1,0:T(8,128)(2,1)} custom-call(bf16[4,256,2048]{2,1,0:T(8,128)(2,1)S(1)} %left.1.left_ref, bf16[4,2,64,512]{3,2,1,0:T(8,128)(2,1)S(1)} %pad_maximum_fusion.1.refs_0_, bf16[4,2,64,512]{3,2,1,0:T(8,128)(2,1)S(1)} %collective-permute-done.14.refs_1_, bf16[4,2,64,512]{3,2,1,0:T(8,128)(2,1)S(1)} %collective-permute-done.19.refs_2_, ...), custom_call_target="tpu_custom_call" | custom-call | tf_op jit(solution)/shard_map/right/pallas_call | solution.py:498
  (48 shorter events, 3.4 us)
Async XLA Ops:
  2.5 11.6 %collective-permute-start.3 = (bf16[2,64,512]{2,1,0:T(8,128)(2,1)}, bf16[2,64,512]{2,1,0:T(8,128)(2,1)S(1)}, u32[]{:S(2)}, u32[]{:S(2)}) collective-permute-start(bf16[2,64,512]{2,1,0:T(8,128)(2,1)} %get-tuple-element.39), channel_id=1, source_target_pairs={{0,16},{8,24},{16,0},{24,8},{1,17},{9,25},{17,1},{25,9},{2,18},{10... | collective-permute-start | bytes 393224 | tf_op jit(solution)/shard_map/ppermute | solution.py:415
  6.6 0.9 copy-start
  7.5 16.9 %copy-start.5 = (bf16[2,64,512]{2,1,0:T(8,128)(2,1)S(1)}, bf16[2,64,512]{2,1,0:T(8,128)(2,1)}, u32[]{:S(2)}) copy-start(bf16[2,64,512]{2,1,0:T(8,128)(2,1)} %get-tuple-element.39) | copy-start | bytes 393220
  7.5 23.0 %copy-start.4 = (bf16[2,64,512]{2,1,0:T(8,128)(2,1)S(1)}, bf16[2,64,512]{2,1,0:T(8,128)(2,1)}, u32[]{:S(2)}) copy-start(bf16[2,64,512]{2,1,0:T(8,128)(2,1)} %get-tuple-element.44) | copy-start | bytes 393220
  7.5 5.2 %collective-permute-start = (bf16[96,256]{1,0:T(8,128)(2,1)S(1)}, bf16[96,256]{1,0:T(8,128)(2,1)S(1)}, u32[]{:S(2)}, u32[]{:S(2)}) collective-permute-start(bf16[96,256]{1,0:T(8,128)(2,1)S(1)} %get-tuple-element.31), channel_id=1, source_target_pairs={{0,24},{8,0},{16,8},{24,16},{1,25},{9,1},{17,9},{25,17},{2,26},{10... | collective-permute-start | bytes 147464 | tf_op jit(solution)/shard_map/ppermute | solution.py:20
  8.9 3.8 %collective-permute-start.1 = (bf16[48,256]{1,0:T(8,128)(2,1)S(1)}, bf16[48,256]{1,0:T(8,128)(2,1)S(1)}, u32[]{:S(2)}, u32[]{:S(2)}) collective-permute-start(bf16[48,256]{1,0:T(8,128)(2,1)S(1)} %get-tuple-element.32), channel_id=1, source_target_pairs={{0,4},{4,0},{1,5},{5,1},{2,6},{6,2},{3,7},{7,3},{8,12},{12,8},{9,1... | collective-permute-start | bytes 73736 | tf_op jit(solution)/shard_map/ppermute | solution.py:20
  10.4 2.3 %collective-permute-start.2 = (bf16[48,256]{1,0:T(8,128)(2,1)S(1)}, bf16[48,256]{1,0:T(8,128)(2,1)S(1)}, u32[]{:S(2)}, u32[]{:S(2)}) collective-permute-start(bf16[48,256]{1,0:T(8,128)(2,1)S(1)} %get-tuple-element.33), channel_id=1, source_target_pairs={{0,3},{1,0},{2,1},{3,2},{4,7},{5,4},{6,5},{7,6},{8,11},{9,8},{10,9... | collective-permute-start | bytes 73736 | tf_op jit(solution)/shard_map/ppermute | solution.py:20
  14.0 61.7 %copy-start.1 = (f32[4,4,4]{2,1,0:T(4,128)S(1)}, f32[4,4,4]{2,1,0:T(4,128)}, u32[]{:S(2)}) copy-start(f32[4,4,4]{2,1,0:T(4,128)} %spin_ref.1) | copy-start | bytes 772
  14.0 61.7 %copy-start.2 = (s32[4]{0:T(128)S(1)}, s32[4]{0:T(128)}, u32[]{:S(2)}) copy-start(s32[4]{0:T(128)} %dirs_ref.1) | copy-start | bytes 52
  14.1 3.1 %collective-permute-start.4 = (bf16[2,4,2,48,256]{4,3,2,1,0:T(8,128)(2,1)S(1)}, bf16[2,4,2,48,256]{4,3,2,1,0:T(8,128)(2,1)S(1)}, u32[]{:S(2)}, u32[]{:S(2)}) collective-permute-start(bf16[2,4,2,48,256]{4,3,2,1,0:T(8,128)(2,1)S(1)} %dynamic-slice_bitcast_fusion), channel_id=1, source_target_pairs={{0,1},{1,0},{2,3},{3,2},{4,5},{5,4},{6,7},{7,6},{8,9},{9,8},{10,11... | collective-permute-start | bytes 1179656 | tf_op jit(solution)/shard_map/ppermute | solution.py:340
  16.1 8.3 %collective-permute-start.6 = (bf16[2,2,64,512]{3,2,1,0:T(8,128)(2,1)S(1)}, bf16[2,2,64,512]{3,2,1,0:T(8,128)(2,1)S(1)}, u32[]{:S(2)}, u32[]{:S(2)}) collective-permute-start(bf16[2,2,64,512]{3,2,1,0:T(8,128)(2,1)S(1)} %pad_maximum_fusion.3), channel_id=1, source_target_pairs={{0,8},{8,0},{16,24},{24,16},{1,9},{9,1},{17,25},{25,17},{2,10},{10... | collective-permute-start | bytes 786440 | tf_op jit(solution)/shard_map/ppermute | solution.py:362
  17.3 7.1 %collective-permute-start.5 = (bf16[4,2,48,256]{3,2,1,0:T(8,128)(2,1)S(1)}, bf16[4,2,48,256]{3,2,1,0:T(8,128)(2,1)S(1)}, u32[]{:S(2)}, u32[]{:S(2)}) collective-permute-start(bf16[4,2,48,256]{3,2,1,0:T(8,128)(2,1)S(1)} %dynamic-slice_bitcast_fusion.1), channel_id=1, source_target_pairs={{0,2},{1,3},{2,0},{3,1},{4,6},{5,7},{6,4},{7,5},{8,10},{9,11},{10,... | collective-permute-start | bytes 589832 | tf_op jit(solution)/shard_map/ppermute | solution.py:340
  25.2 18.3 %all-to-all-start = ((bf16[8,48,256]{2,1,0:T(8,128)(2,1)}), bf16[8,48,256]{2,1,0:T(8,128)(2,1)S(1)}, u32[]{:S(2)}, u32[]{:S(2)}) async-start(bf16[8,48,256]{2,1,0:T(8,128)(2,1)} %bitcast.12), calls=%async_computation | async-start | bytes 393216 | tf_op jit(solution)/shard_map/all_to_all | solution.py:460
  30.5 12.9 %collective-permute-start.7 = (bf16[1,2,64,512]{3,2,1,0:T(8,128)(2,1)S(1)}, bf16[1,2,64,512]{3,2,1,0:T(8,128)(2,1)S(1)}, u32[]{:S(2)}, u32[]{:S(2)}) collective-permute-start(bf16[1,2,64,512]{3,2,1,0:T(8,128)(2,1)S(1)} %bitcast.29), channel_id=1, source_target_pairs={{0,16},{8,24},{16,0},{24,8},{1,17},{9,25},{17,1},{25,9},{2,18},{10... | collective-permute-start | bytes 393224 | tf_op jit(solution)/shard_map/ppermute | solution.py:362
  33.4 18.4 %collective-permute-start.11 = (bf16[4,2,64,512]{3,2,1,0:T(8,128)(2,1)S(1)}, bf16[4,2,64,512]{3,2,1,0:T(8,128)(2,1)S(1)}, u32[]{:S(2)}, u32[]{:S(2)}) collective-permute-start(bf16[4,2,64,512]{3,2,1,0:T(8,128)(2,1)S(1)} %pad_maximum_fusion.refs_2_), channel_id=1, source_target_pairs={{0,1},{1,0},{2,3},{3,2},{4,5},{5,4},{6,7},{7,6},{8,9},{9,8},{10,11... | collective-permute-start | bytes 1572872 | tf_op jit(solution)/shard_map/ppermute | solution.py:340
  33.4 18.4 %collective-permute-start.10 = (bf16[4,2,64,512]{3,2,1,0:T(8,128)(2,1)S(1)}, bf16[4,2,64,512]{3,2,1,0:T(8,128)(2,1)S(1)}, u32[]{:S(2)}, u32[]{:S(2)}) collective-permute-start(bf16[4,2,64,512]{3,2,1,0:T(8,128)(2,1)S(1)} %pad_maximum_fusion.refs_2_), channel_id=1, source_target_pairs={{0,2},{1,3},{2,0},{3,1},{4,6},{5,7},{6,4},{7,5},{8,10},{9,11},{10,... | collective-permute-start | bytes 1572872 | tf_op jit(solution)/shard_map/ppermute | solution.py:353
  34.9 16.9 %collective-permute-start.9 = (bf16[4,2,64,512]{3,2,1,0:T(8,128)(2,1)S(1)}, bf16[4,2,64,512]{3,2,1,0:T(8,128)(2,1)S(1)}, u32[]{:S(2)}, u32[]{:S(2)}) collective-permute-start(bf16[4,2,64,512]{3,2,1,0:T(8,128)(2,1)S(1)} %pad_maximum_fusion.refs_2_), channel_id=1, source_target_pairs={{0,4},{1,5},{2,6},{3,7},{4,0},{5,1},{6,2},{7,3},{8,12},{9,13},{10,... | collective-permute-start | bytes 1572872 | tf_op jit(solution)/shard_map/ppermute | solution.py:353
  43.5 7.3 %collective-permute-start.8 = (bf16[2,2,64,512]{3,2,1,0:T(8,128)(2,1)S(1)}, bf16[2,2,64,512]{3,2,1,0:T(8,128)(2,1)}, u32[]{:S(2)}, u32[]{:S(2)}) collective-permute-start(bf16[2,2,64,512]{3,2,1,0:T(8,128)(2,1)S(1)} %pad_maximum_fusion.4), channel_id=1, source_target_pairs={{0,8},{8,0},{16,24},{24,16},{1,9},{9,1},{17,25},{25,17},{2,10},{10... | collective-permute-start | bytes 786440 | tf_op jit(solution)/shard_map/ppermute | solution.py:362
  44.3 12.0 %all-to-all-start.1 = ((bf16[8,48,256]{2,1,0:T(8,128)(2,1)}), bf16[8,48,256]{2,1,0:T(8,128)(2,1)S(1)}, u32[]{:S(2)}, u32[]{:S(2)}) async-start(bf16[8,48,256]{2,1,0:T(8,128)(2,1)} %broadcast_in_dim.6), calls=%async_computation.1 | async-start | bytes 393216 | tf_op jit(solution)/shard_map/all_to_all | solution.py:462
  56.2 15.9 %copy-start.3 = (bf16[8,48,256]{2,1,0:T(8,128)(2,1)}, bf16[8,48,256]{2,1,0:T(8,128)(2,1)S(1)}, u32[]{:S(2)}) copy-start(bf16[8,48,256]{2,1,0:T(8,128)(2,1)S(1)} %all-to-all-done.1) | copy-start | bytes 589828
  56.2 16.8 %collective-permute-start.14 = (bf16[4,2,64,512]{3,2,1,0:T(8,128)(2,1)S(1)}, bf16[4,2,64,512]{3,2,1,0:T(8,128)(2,1)S(1)}, u32[]{:S(2)}, u32[]{:S(2)}) collective-permute-start(bf16[4,2,64,512]{3,2,1,0:T(8,128)(2,1)S(1)} %pad_maximum_fusion.1.refs_0_), channel_id=1, source_target_pairs={{0,2},{1,3},{2,0},{3,1},{4,6},{5,7},{6,4},{7,5},{8,10},{9,11},{10,... | collective-permute-start | bytes 1572872 | tf_op jit(solution)/shard_map/ppermute | solution.py:340
  57.8 15.3 %collective-permute-start.13 = (bf16[4,2,64,512]{3,2,1,0:T(8,128)(2,1)S(1)}, bf16[4,2,64,512]{3,2,1,0:T(8,128)(2,1)}, u32[]{:S(2)}, u32[]{:S(2)}) collective-permute-start(bf16[4,2,64,512]{3,2,1,0:T(8,128)(2,1)S(1)} %collective-permute-done.10.refs_4_), channel_id=1, source_target_pairs={{0,4},{1,5},{2,6},{3,7},{4,0},{5,1},{6,2},{7,3},{8,12},{9,13},{10,... | collective-permute-start | bytes 1572872 | tf_op jit(solution)/shard_map/ppermute | solution.py:353
  58.7 13.4 %collective-permute-start.12 = (bf16[8,48,256]{2,1,0:T(8,128)(2,1)S(1)}, bf16[8,48,256]{2,1,0:T(8,128)(2,1)S(1)}, u32[]{:S(2)}, u32[]{:S(2)}) collective-permute-start(bf16[8,48,256]{2,1,0:T(8,128)(2,1)S(1)} %all-to-all-done.1), channel_id=1, source_target_pairs={{0,2},{1,3},{2,0},{3,1},{4,6},{5,7},{6,4},{7,5},{8,10},{9,11},{10,... | collective-permute-start | bytes 589832 | tf_op jit(solution)/shard_map/ppermute | solution.py:340
  59.2 15.8 %collective-permute-start.17 = (bf16[4,2,64,512]{3,2,1,0:T(8,128)(2,1)S(1)}, bf16[4,2,64,512]{3,2,1,0:T(8,128)(2,1)}, u32[]{:S(2)}, u32[]{:S(2)}) collective-permute-start(bf16[4,2,64,512]{3,2,1,0:T(8,128)(2,1)S(1)} %collective-permute-done.10.refs_4_), channel_id=1, source_target_pairs={{0,1},{1,0},{2,3},{3,2},{4,5},{5,4},{6,7},{7,6},{8,9},{9,8},{10,11... | collective-permute-start | bytes 1572872 | tf_op jit(solution)/shard_map/ppermute | solution.py:340
  59.2 15.4 %collective-permute-start.16 = (bf16[4,2,64,512]{3,2,1,0:T(8,128)(2,1)S(1)}, bf16[4,2,64,512]{3,2,1,0:T(8,128)(2,1)}, u32[]{:S(2)}, u32[]{:S(2)}) collective-permute-start(bf16[4,2,64,512]{3,2,1,0:T(8,128)(2,1)S(1)} %collective-permute-done.9.refs_3_), channel_id=1, source_target_pairs={{0,1},{1,0},{2,3},{3,2},{4,5},{5,4},{6,7},{7,6},{8,9},{9,8},{10,11... | collective-permute-start | bytes 1572872 | tf_op jit(solution)/shard_map/ppermute | solution.py:340
  73.1 2.7 %collective-permute-start.18 = (bf16[4,2,64,512]{3,2,1,0:T(8,128)(2,1)}, bf16[4,2,64,512]{3,2,1,0:T(8,128)(2,1)}, u32[]{:S(2)}, u32[]{:S(2)}) collective-permute-start(bf16[4,2,64,512]{3,2,1,0:T(8,128)(2,1)} %collective-permute-done.13.refs_6_), channel_id=1, source_target_pairs={{0,1},{1,0},{2,3},{3,2},{4,5},{5,4},{6,7},{7,6},{8,9},{9,8},{10,11... | collective-permute-start | bytes 1572872 | tf_op jit(solution)/shard_map/ppermute | solution.py:340
  73.2 2.6 %collective-permute-start.15 = (bf16[2,8,48,256]{3,2,1,0:T(8,128)(2,1)S(1)}, bf16[2,8,48,256]{3,2,1,0:T(8,128)(2,1)}, u32[]{:S(2)}, u32[]{:S(2)}) collective-permute-start(bf16[2,8,48,256]{3,2,1,0:T(8,128)(2,1)S(1)} %pad_maximum_fusion.2.refs_0_), channel_id=1, source_target_pairs={{0,1},{1,0},{2,3},{3,2},{4,5},{5,4},{6,7},{7,6},{8,9},{9,8},{10,11... | collective-permute-start | bytes 1179656 | tf_op jit(solution)/shard_map/ppermute | solution.py:340
  74.5 11.4 %collective-permute-start.19 = (bf16[4,2,64,512]{3,2,1,0:T(8,128)(2,1)S(1)}, bf16[4,2,64,512]{3,2,1,0:T(8,128)(2,1)S(1)}, u32[]{:S(2)}, u32[]{:S(2)}) collective-permute-start(bf16[4,2,64,512]{3,2,1,0:T(8,128)(2,1)S(1)} %pad_maximum_fusion.1.refs_0_), channel_id=1, source_target_pairs={{0,1},{1,0},{2,3},{3,2},{4,5},{5,4},{6,7},{7,6},{8,9},{9,8},{10,11... | collective-permute-start | bytes 1572872 | tf_op jit(solution)/shard_map/ppermute | solution.py:340
  74.6 11.3 %collective-permute-start.20 = (bf16[4,2,64,512]{3,2,1,0:T(8,128)(2,1)S(1)}, bf16[4,2,64,512]{3,2,1,0:T(8,128)(2,1)S(1)}, u32[]{:S(2)}, u32[]{:S(2)}) collective-permute-start(bf16[4,2,64,512]{3,2,1,0:T(8,128)(2,1)S(1)} %collective-permute-done.14.refs_1_), channel_id=1, source_target_pairs={{0,1},{1,0},{2,3},{3,2},{4,5},{5,4},{6,7},{7,6},{8,9},{9,8},{10,11... | collective-permute-start | bytes 1572872 | tf_op jit(solution)/shard_map/ppermute | solution.py:340

commit v9 on v8

--- a/solution.py
+++ b/solution.py
@@ -63,9 +63,12 @@
     return total, part, where, colour
 
 
-def rows_kernel(extent, eig_ref, vec_out, *face_outs):
-    vec = eig_ref[...].astype(F32).reshape(vec_out.shape)
-    vec_out[...] = vec.astype(BF16)
+def eig_rows(eig_ref):
+    return eig_ref[...].astype(F32).reshape(2 * eig_ref.shape[0], eig_ref.shape[2])
+
+
+def faces_kernel(extent, eig_ref, *face_outs):
+    vec = eig_rows(eig_ref)
     strides = (6 * extent[1] * extent[2], 6 * extent[2], 6)
     for e, out in enumerate(face_outs):
         begins = [0]
@@ -148,11 +151,11 @@
             out[at, :] = (placed[at] * mask).astype(BF16)
 
 
-def correlate_kernel(scale, vec_ref, face0, face1, face2, mat0, mat1, mat2, out_ref):
+def correlate_kernel(scale, eig_ref, face0, face1, face2, mat0, mat1, mat2, out_ref):
     gz_n, gx_n, split, depth, width = out_ref.shape
     each = 6 // split
     own_rows = depth // each
-    vec = vec_ref[...]
+    vec = eig_rows(eig_ref).astype(BF16)
     rows = vec.shape[0]
     row = lax.broadcasted_iota(jnp.int32, (rows, rows), 0)
     column = lax.broadcasted_iota(jnp.int32, (rows, rows), 1)
@@ -288,8 +291,8 @@
     blocks = [pl.multiple_of(back(gy, dx, gy_n) * lane, lane) for dx in range(gy_n)]
 
     def one_operator(op):
-        a = chain_ref[op, 0]
-        b = chain_ref[op, 1]
+        a = chain_ref[2 * op]
+        b = chain_ref[2 * op + 1]
         dir_a = dirs_ref[a]
         dir_b = dirs_ref[b]
         mix = None
@@ -353,13 +356,15 @@
     return lax.ppermute(value, ("gy", "gz"), pairs)
 
 
+def xor_passed(value, axis, offset):
+    return lax.ppermute(value, axis, [(n, n ^ offset) for n in range(lax.axis_size(axis))])
+
+
 def line_exchange(value, axis, distance, steps, offsets=(0,)):
-    count = lax.axis_size(axis)
     gathered = value if len(offsets) > 1 else value[None]
     offsets = list(offsets)
     for _ in range(steps):
-        pairs = [(n, n ^ distance) for n in range(count)]
-        gathered = jnp.concatenate([gathered, lax.ppermute(gathered, axis, pairs)])
+        gathered = jnp.concatenate([gathered, xor_passed(gathered, axis, distance)])
         offsets += [offset ^ distance for offset in offsets]
         distance //= 2
     return gathered, tuple(offsets)
@@ -386,14 +391,15 @@
     piece = rows // gz_n
     site_rows = 6 * math.prod(extent)
     face_rows = [site_rows // n for n in extent]
-    vec, *faces = pl.pallas_call(
-        functools.partial(rows_kernel, extent),
-        out_shape=[jax.ShapeDtypeStruct((n, num_vecs), BF16) for n in [site_rows] + face_rows],
+    eig = eigvecs.transpose(0, 1, 2, 4, 3, 5).reshape(-1, 2, num_vecs)
+    faces = pl.pallas_call(
+        functools.partial(faces_kernel, extent),
+        out_shape=[jax.ShapeDtypeStruct((n, num_vecs), BF16) for n in face_rows],
         in_specs=[VMEM],
-        out_specs=[VMEM] * 4,
+        out_specs=[VMEM] * 3,
         compiler_params=pltpu.CompilerParams(vmem_limit_bytes=24 * 2**20),
-        name="rows",
-    )(eigvecs.transpose(0, 1, 2, 4, 3, 5).reshape(-1, 2, num_vecs))
+        name="faces",
+    )(eig)
     faces = [passed_along(face, axis, -1) for face, axis in zip(faces, ("gx", "gy", "gz"))]
 
     piece_shape = jax.ShapeDtypeStruct((2, piece, cols), BF16)
@@ -411,8 +417,9 @@
         cost_estimate=pl.CostEstimate(flops=10**8, bytes_accessed=10**7, transcendentals=0),
         name="pieces",
     )(me[2:], forward_peram, backward_peram)
-    fwd_piece, links = lax.optimization_barrier((fwd_piece, links))
-    fwd_half = lax.ppermute(fwd_piece, "gx", [(n, n ^ (gx_n // 2)) for n in range(gx_n)])
+    pairs = chain_order.reshape(-1)
+    fwd_piece, links, pairs = lax.optimization_barrier((fwd_piece, links, pairs))
+    fwd_half = xor_passed(fwd_piece, "gx", gx_n // 2)
 
     link_mats = pl.pallas_call(
         functools.partial(links_kernel, extent),
@@ -437,7 +444,7 @@
         out_specs=VMEM,
         compiler_params=pltpu.CompilerParams(vmem_limit_bytes=24 * 2**20),
         name="correlate",
-    )(vec, *faces, *link_mats)
+    )(eig, *faces, *link_mats)
 
     rounds = gx_n.bit_length() - 1
     partial, fwd_half = lax.optimization_barrier((partial, fwd_half))
@@ -445,9 +452,9 @@
     summed = added(part_at(by_core, core, 1), passed_in_gz(part_at(by_core, 1 - core, 1), 0, 1))
     fwd_line = jnp.stack([fwd_piece, fwd_half])
     fwd_line, line = line_exchange(fwd_line, "gx", gx_n // 4, rounds - 1, (0, gx_n // 2))
+    summed, bwd_piece = lax.optimization_barrier((summed, bwd_piece))
+    bwd_line = jnp.stack([bwd_piece] + [xor_passed(bwd_piece, "gx", offset) for offset in line[1:]])
     summed = added(*[passed_in_gz(part_at(summed, lax.rem(chip + dy, chips)), dy, 0) if dy else part_at(summed, chip) for dy in range(chips)])
-    summed, fwd_line, bwd_piece = lax.optimization_barrier((summed, fwd_line, bwd_piece))
-    bwd_line, _ = line_exchange(bwd_piece, "gx", gx_n // 2, rounds)
 
     plane = [(dx, dy) for dy in range(chips) for dx in range(gy_n)]
     four = gy_n == 2 and chips == 2
@@ -459,18 +466,19 @@
         summed = added(summed, *[passed_along(summed, "gy", dx) for dx in range(1, gy_n)])
     summed = lax.all_to_all(summed.reshape(gx_n * split, depth, num_vecs), area, 0, 0, tiled=True)
     summed = jnp.sum(summed.astype(F32), axis=0).astype(BF16)
+    over_x = [key for key in fwd_parts if key[0] and not key[1] and not key[2]]
+    summed, bwd_line, *parts = lax.optimization_barrier((summed, bwd_line, *[fwd_parts[key] for key in over_x]))
+    fwd_parts.update(zip(over_x, parts))
+    bwd_parts = {(dy, 0): passed_in_gz(bwd_line, dy, 0) if dy else bwd_line for dy in range(chips)}
     elem_line = lax.all_to_all(jnp.broadcast_to(summed, (gx_n * split, depth, num_vecs)), area, 0, 0, tiled=True)
     if four:
-        keys = [(1, 0, 0), (0, 1, 0), (0, 0, 1)]
-        elem_line, bwd_line, *parts = lax.optimization_barrier((elem_line, bwd_line, *[fwd_parts[key] for key in keys]))
-        fwd_parts.update(zip(keys, parts))
         fwd_parts[1, 1, 0] = passed_in_plane(fwd_parts[0, 1, 0], 1, 0)
-    bwd_parts = {(dy, 0): passed_in_gz(bwd_line, dy, 0) if dy else bwd_line for dy in range(chips)}
+    keys = [(0, 0, 1)]
+    tied = lax.optimization_barrier((elem_line, *[fwd_parts[key] for key in keys], *bwd_parts.values()))
+    elem_line = tied[0]
+    fwd_parts.update(zip(keys, tied[1:]))
+    bwd_parts.update(zip(list(bwd_parts), tied[2:]))
     elem_own = jnp.stack([passed_in_gz(elem_line, dy, 0) if dy else elem_line for dy in range(chips)])
-    late = [(1, 1, 0)] if four else []
-    elem_own, *parts = lax.optimization_barrier((elem_own, *[fwd_parts[key] for key in late], *bwd_parts.values()))
-    fwd_parts.update(zip(late, parts))
-    bwd_parts.update(zip(list(bwd_parts), parts[len(late) :]))
     elem_parts = [elem_own, passed_in_gz(elem_own, 0, 1)]
     for dx, dy in plane[1:]:
         fwd_parts[dx, dy, 1] = passed_in_gz(fwd_parts[dx, dy, 0], 0, 1)
@@ -494,7 +502,7 @@
         compiler_params=pltpu.CompilerParams(vmem_limit_bytes=24 * 2**20),
         cost_estimate=pl.CostEstimate(flops=8 * 10**9, bytes_accessed=10**7, transcendentals=0),
         name="left",
-    )(me, directions, spin_mats, chain_order, *elem_parts, *fwd_parts.values())
+    )(me, directions, spin_mats, pairs, *elem_parts, *fwd_parts.values())
     return pl.pallas_call(
         functools.partial(right_kernel, gz_n, tuple(bwd_parts)),
         out_shape=jax.ShapeDtypeStruct((op_count, 2, rows, cols), BF16),

time: 92.2 us -> 90.9 us (0.986)
  waiting for transfers between devices: 32.7 us -> 29.2 us
  starting transfers between devices: 30.9 us -> 32.8 us
  other arithmetic: 3.93 us -> 2.96 us
  local copies, waits for them, and re-layouts: 3.68 us -> 4.65 us
    ppermute x11, waiting for transfers between devices: 13.1 us -> 0.91 us  [passed_in_gz(): return lax.ppermute(value, 'gz', pairs)]
    ppermute x3, waiting for transfers between devices: 0.01 us -> 5.62 us  [passed_in_plane(): return lax.ppermute(value, ('gy', 'gz'), pairs)]
    ppermute x4 -> x5, waiting for transfers between devices: 14.8 us -> 16.4 us  [xor_passed(): lax.ppermute(value, axis, [(n, n ^ offset) for n in range(lax.axis_size(a...]
    all_to_all x1, starting transfers between devices: 5.3 us -> 3.72 us  [on_device(): lax.all_to_all(summed.reshape(gx_n * split, depth, num_vecs), area, 0, 0,...]
    all_to_all x1, waiting for transfers between devices: 4.42 us -> 5.9 us  [on_device(): lax.all_to_all(jnp.broadcast_to(summed, (gx_n * split, depth, num_vecs)),...]
    ppermute x4 -> x5, starting transfers between devices: 8.17 us -> 9.57 us  [xor_passed(): lax.ppermute(value, axis, [(n, n ^ offset) for n in range(lax.axis_size(a...]
    ppermute x11, starting transfers between devices: 6.29 us -> 7.51 us  [passed_in_gz(): return lax.ppermute(value, 'gz', pairs)]
    concatenate x3 -> x1, other arithmetic: 1.08 us -> 0.05 us  [line_exchange(): gathered = jnp.concatenate([gathered, xor_passed(gathered, axis, distance)])]
  transfers between devices with their start and end apart: 23 -> 24, of which waited for: 7 -> 7; matrix products, arithmetic and copies ran while one was open for 6% -> 5% of each run, Pallas kernels for 13% -> 14%
where the time goes in v9:
time: 90.9 us; the launch traced here: 90.4 us
  starting transfers between devices  32.8 us (36%)
  waiting for transfers between devices  29.2 us (32%)
  Pallas kernels  20.6 us (23%)
  local copies, waits for them, and re-layouts  4.65 us (5%)
  other arithmetic  2.96 us (3%)
    ppermute x5, waiting for transfers between devices, xor_passed(): lax.ppermute(value, axis, [(n, n ^ offset) for n in range(lax.axis_size(a...  16.4 us
    pallas_call x1, Pallas kernels, on_device(): pl.pallas_call(functools.partial(left_kernel, 1.0 / math.sqrt(4 * num_vec...  10.4 us
    ppermute x5, starting transfers between devices, xor_passed(): lax.ppermute(value, axis, [(n, n ^ offset) for n in range(lax.axis_size(a...  9.57 us
    ppermute x11, starting transfers between devices, passed_in_gz(): return lax.ppermute(value, 'gz', pairs)  7.51 us
    all_to_all x1, waiting for transfers between devices, on_device(): lax.all_to_all(jnp.broadcast_to(summed, (gx_n * split, depth, num_vecs)),...  5.9 us
    pallas_call x1, Pallas kernels, on_device(): pl.pallas_call(functools.partial(right_kernel, gz_n, tuple(bwd_parts)), o...  5.82 us
    ppermute x3, waiting for transfers between devices, passed_in_plane(): return lax.ppermute(value, ('gy', 'gz'), pairs)  5.62 us
    ppermute x3, starting transfers between devices, passed_in_plane(): return lax.ppermute(value, ('gy', 'gz'), pairs)  4.84 us
  transfers between devices with their start and end apart: 24, of which 7 were waited for; matrix products, arithmetic and copies ran while one was open for 5% of the time, Pallas kernels for 14%

profile of v9, /device:TPU:0, one launch (start us, length us, event | category | flops | bytes accessed | tf_op | source)
XLA Modules:
  0.0 90.4 jit_solution(14748591663800870420)
XLA Ops:
  0.0 0.8 copy.10
  0.9 2.5 %pieces.1 = (bf16[2,64,512]{2,1,0:T(8,128)(2,1)}, bf16[2,64,512]{2,1,0:T(8,128)(2,1)}) custom-call(s32[1]{0:T(128)} %bitcast.2.z_ref, bf16[2,256,512]{2,1,0:T(8,128)(2,1)} %fwd_in.1, bf16[2,256,512]{2,1,0:T(8,128)(2,1)} %bwd_in.1), custom_call_target="tpu_custom_call" | custom-call | flops 100000000 | bytes 10000000 | tf_op jit(solution)/shard_map/pieces/pallas_call | solution.py:406
  3.3 4.1 %collective-permute-start.3 = (bf16[2,64,512]{2,1,0:T(8,128)(2,1)}, bf16[2,64,512]{2,1,0:T(8,128)(2,1)S(1)}, u32[]{:S(2)}, u32[]{:S(2)}) collective-permute-start(bf16[2,64,512]{2,1,0:T(8,128)(2,1)} %get-tuple-element.36), channel_id=1, source_target_pairs={{0,16},{8,24},{16,0},{24,8},{1,17},{9,25},{17,1},{25,9},{2,18},{10... | collective-permute-start | bytes 393224 | tf_op jit(solution)/shard_map/ppermute | solution.py:360
  7.4 0.9 copy-done
  8.3 1.4 %collective-permute-start = (bf16[96,256]{1,0:T(8,128)(2,1)S(1)}, bf16[96,256]{1,0:T(8,128)(2,1)S(1)}, u32[]{:S(2)}, u32[]{:S(2)}) collective-permute-start(bf16[96,256]{1,0:T(8,128)(2,1)S(1)} %get-tuple-element.29), channel_id=1, source_target_pairs={{0,24},{8,0},{16,8},{24,16},{1,25},{9,1},{17,9},{25,17},{2,26},{10... | collective-permute-start | bytes 147464 | tf_op jit(solution)/shard_map/ppermute | solution.py:20
  9.8 1.5 %collective-permute-start.1 = (bf16[48,256]{1,0:T(8,128)(2,1)S(1)}, bf16[48,256]{1,0:T(8,128)(2,1)S(1)}, u32[]{:S(2)}, u32[]{:S(2)}) collective-permute-start(bf16[48,256]{1,0:T(8,128)(2,1)S(1)} %get-tuple-element.30), channel_id=1, source_target_pairs={{0,4},{4,0},{1,5},{5,1},{2,6},{6,2},{3,7},{7,3},{8,12},{12,8},{9,1... | collective-permute-start | bytes 73736 | tf_op jit(solution)/shard_map/ppermute | solution.py:20
  11.4 1.0 %copy.11 = f32[2,4,4,3,2,3,3]{2,1,0,6,5,4,3:T(4,128)S(1)} copy(f32[2,4,4,3,2,3,3]{2,4,6,5,3,1,0:T(2,128)} %param.8) | data formatting | bytes 13824 | tf_op jit(solution)/shard_map/optimization_barrier | solution.py:421
  13.6 0.9 copy-done.1
  14.5 1.3 %correlate.1 = bf16[4,4,2,48,256]{4,3,2,1,0:T(8,128)(2,1)S(1)} custom-call(bf16[96,2,256]{2,1,0:T(2,128)(2,1)S(1)} %bitcast.31, bf16[96,256]{1,0:T(8,128)(2,1)S(1)} %collective-permute-done.face0, bf16[48,256]{1,0:T(8,128)(2,1)S(1)} %collective-permute-done.1.face1, bf16[48,256]{1,0:T(8,128)(2,1)S(1)} %collective-permute-done.2.face2, ...), custom_call_target="tpu_custom_call" | custom-call | tf_op jit(solution)/shard_map/correlate/pallas_call | solution.py:440
  15.8 1.1 %collective-permute-start.4 = (bf16[2,4,2,48,256]{4,3,2,1,0:T(8,128)(2,1)S(1)}, bf16[2,4,2,48,256]{4,3,2,1,0:T(8,128)(2,1)S(1)}, u32[]{:S(2)}, u32[]{:S(2)}) collective-permute-start(bf16[2,4,2,48,256]{4,3,2,1,0:T(8,128)(2,1)S(1)} %dynamic-slice_bitcast_fusion), channel_id=1, source_target_pairs={{0,1},{1,0},{2,3},{3,2},{4,5},{5,4},{6,7},{7,6},{8,9},{9,8},{10,11... | collective-permute-start | bytes 1179656 | tf_op jit(solution)/shard_map/ppermute | solution.py:343
  16.9 0.9 %pad_maximum_fusion.3 = bf16[2,2,64,512]{3,2,1,0:T(8,128)(2,1)S(1)} fusion(bf16[1,2,64,512]{3,2,1,0:T(8,128)(2,1)S(1)} %bitcast.35, bf16[1,2,64,512]{3,2,1,0:T(8,128)(2,1)} %bitcast.33), kind=kLoop, calls=%fused_computation.8 | loop fusion | flops 131072 | bytes 524288 | tf_op jit(solution)/shard_map/stack | solution.py:453
  17.8 1.1 %collective-permute-start.9 = (bf16[2,2,64,512]{3,2,1,0:T(8,128)(2,1)S(1)}, bf16[2,2,64,512]{3,2,1,0:T(8,128)(2,1)S(1)}, u32[]{:S(2)}, u32[]{:S(2)}) collective-permute-start(bf16[2,2,64,512]{3,2,1,0:T(8,128)(2,1)S(1)} %pad_maximum_fusion.3), channel_id=1, source_target_pairs={{0,8},{8,0},{16,24},{24,16},{1,9},{9,1},{17,25},{25,17},{2,10},{10... | collective-permute-start | bytes 786440 | tf_op jit(solution)/shard_map/ppermute | solution.py:360
  19.0 1.6 %collective-permute-start.5 = (bf16[4,2,48,256]{3,2,1,0:T(8,128)(2,1)S(1)}, bf16[4,2,48,256]{3,2,1,0:T(8,128)(2,1)S(1)}, u32[]{:S(2)}, u32[]{:S(2)}) collective-permute-start(bf16[4,2,48,256]{3,2,1,0:T(8,128)(2,1)S(1)} %dynamic-slice_bitcast_fusion.1), channel_id=1, source_target_pairs={{0,2},{1,3},{2,0},{3,1},{4,6},{5,7},{6,4},{7,5},{8,10},{9,11},{10,... | collective-permute-start | bytes 589832 | tf_op jit(solution)/shard_map/ppermute | solution.py:343
  20.7 5.5 %collective-permute-done.9 = bf16[2,2,64,512]{3,2,1,0:T(8,128)(2,1)S(1)} collective-permute-done((bf16[2,2,64,512]{3,2,1,0:T(8,128)(2,1)S(1)}, bf16[2,2,64,512]{3,2,1,0:T(8,128)(2,1)S(1)}, u32[]{:S(2)}, u32[]{:S(2)}) %collective-permute-start.9) | collective-permute-done | bytes 262176 | tf_op jit(solution)/shard_map/ppermute | solution.py:360
  26.2 1.3 %collective-permute-start.10 = (bf16[4,2,64,512]{3,2,1,0:T(8,128)(2,1)S(1)}, bf16[4,2,64,512]{3,2,1,0:T(8,128)(2,1)S(1)}, u32[]{:S(2)}, u32[]{:S(2)}) collective-permute-start(bf16[4,2,64,512]{3,2,1,0:T(8,128)(2,1)S(1)} %pad_maximum_fusion.1.refs_2_), channel_id=1, source_target_pairs={{0,4},{1,5},{2,6},{3,7},{4,0},{5,1},{6,2},{7,3},{8,12},{9,13},{10,... | collective-permute-start | bytes 1572872 | tf_op jit(solution)/shard_map/ppermute | solution.py:356
  27.5 0.7 fusion.1
  28.2 3.7 %all-to-all-start = ((bf16[8,48,256]{2,1,0:T(8,128)(2,1)}), bf16[8,48,256]{2,1,0:T(8,128)(2,1)S(1)}, u32[]{:S(2)}, u32[]{:S(2)}) async-start(bf16[8,48,256]{2,1,0:T(8,128)(2,1)} %bitcast.11), calls=%async_computation | async-start | bytes 393216 | tf_op jit(solution)/shard_map/all_to_all | solution.py:467
  32.0 1.5 %collective-permute-start.15 = (bf16[4,2,64,512]{3,2,1,0:T(8,128)(2,1)S(1)}, bf16[4,2,64,512]{3,2,1,0:T(8,128)(2,1)S(1)}, u32[]{:S(2)}, u32[]{:S(2)}) collective-permute-start(bf16[4,2,64,512]{3,2,1,0:T(8,128)(2,1)S(1)} %pad_maximum_fusion.1.refs_2_), channel_id=1, source_target_pairs={{0,2},{1,3},{2,0},{3,1},{4,6},{5,7},{6,4},{7,5},{8,10},{9,11},{10,... | collective-permute-start | bytes 1572872 | tf_op jit(solution)/shard_map/ppermute | solution.py:356
  33.5 2.9 %collective-permute-start.6 = (bf16[2,64,512]{2,1,0:T(8,128)(2,1)S(1)}, bf16[2,64,512]{2,1,0:T(8,128)(2,1)S(1)}, u32[]{:S(2)}, u32[]{:S(2)}) collective-permute-start(bf16[2,64,512]{2,1,0:T(8,128)(2,1)S(1)} %copy-done.6), channel_id=1, source_target_pairs={{0,16},{8,24},{16,0},{24,8},{1,17},{9,25},{17,1},{25,9},{2,18},{10... | collective-permute-start | bytes 393224 | tf_op jit(solution)/shard_map/ppermute | solution.py:360
  36.4 1.5 %collective-permute-start.7 = (bf16[2,64,512]{2,1,0:T(8,128)(2,1)S(1)}, bf16[2,64,512]{2,1,0:T(8,128)(2,1)S(1)}, u32[]{:S(2)}, u32[]{:S(2)}) collective-permute-start(bf16[2,64,512]{2,1,0:T(8,128)(2,1)S(1)} %copy-done.6), channel_id=1, source_target_pairs={{0,8},{8,0},{16,24},{24,16},{1,9},{9,1},{17,25},{25,17},{2,10},{10... | collective-permute-start | bytes 393224 | tf_op jit(solution)/shard_map/ppermute | solution.py:360
  37.9 11.0 %collective-permute-done.6 = bf16[2,64,512]{2,1,0:T(8,128)(2,1)S(1)} collective-permute-done((bf16[2,64,512]{2,1,0:T(8,128)(2,1)S(1)}, bf16[2,64,512]{2,1,0:T(8,128)(2,1)S(1)}, u32[]{:S(2)}, u32[]{:S(2)}) %collective-permute-start.6) | collective-permute-done | bytes 131104 | tf_op jit(solution)/shard_map/ppermute | solution.py:360
  49.0 1.7 %collective-permute-start.12 = (bf16[4,2,64,512]{3,2,1,0:T(8,128)(2,1)S(1)}, bf16[4,2,64,512]{3,2,1,0:T(8,128)(2,1)S(1)}, u32[]{:S(2)}, u32[]{:S(2)}) collective-permute-start(bf16[4,2,64,512]{3,2,1,0:T(8,128)(2,1)S(1)} %pad_maximum_fusion.refs_0_), channel_id=1, source_target_pairs={{0,2},{1,3},{2,0},{3,1},{4,6},{5,7},{6,4},{7,5},{8,10},{9,11},{10,... | collective-permute-start | bytes 1572872 | tf_op jit(solution)/shard_map/ppermute | solution.py:343
  50.6 0.7 broadcast_in_dim.3
  51.3 4.1 %all-to-all-start.1 = ((bf16[8,48,256]{2,1,0:T(8,128)(2,1)}), bf16[8,48,256]{2,1,0:T(8,128)(2,1)S(1)}, u32[]{:S(2)}, u32[]{:S(2)}) async-start(bf16[8,48,256]{2,1,0:T(8,128)(2,1)} %broadcast_in_dim.3), calls=%async_computation.1 | async-start | bytes 393216 | tf_op jit(solution)/shard_map/all_to_all | solution.py:473
  55.5 2.0 %collective-permute-start.16 = (bf16[4,2,64,512]{3,2,1,0:T(8,128)(2,1)S(1)}, bf16[4,2,64,512]{3,2,1,0:T(8,128)(2,1)}, u32[]{:S(2)}, u32[]{:S(2)}) collective-permute-start(bf16[4,2,64,512]{3,2,1,0:T(8,128)(2,1)S(1)} %collective-permute-done.15.refs_4_), channel_id=1, source_target_pairs={{0,4},{1,5},{2,6},{3,7},{4,0},{5,1},{6,2},{7,3},{8,12},{9,13},{10,... | collective-permute-start | bytes 1572872 | tf_op jit(solution)/shard_map/ppermute | solution.py:356
  57.5 5.9 %all-to-all-done.1 = bf16[8,48,256]{2,1,0:T(8,128)(2,1)S(1)} async-done(((bf16[8,48,256]{2,1,0:T(8,128)(2,1)}), bf16[8,48,256]{2,1,0:T(8,128)(2,1)S(1)}, u32[]{:S(2)}, u32[]{:S(2)}) %all-to-all-start.1) | async-done | bytes 196640 | tf_op jit(solution)/shard_map/all_to_all | solution.py:473
  63.4 1.6 %collective-permute-start.13 = (bf16[8,48,256]{2,1,0:T(8,128)(2,1)S(1)}, bf16[8,48,256]{2,1,0:T(8,128)(2,1)S(1)}, u32[]{:S(2)}, u32[]{:S(2)}) collective-permute-start(bf16[8,48,256]{2,1,0:T(8,128)(2,1)S(1)} %all-to-all-done.1), channel_id=1, source_target_pairs={{0,2},{1,3},{2,0},{3,1},{4,6},{5,7},{6,4},{7,5},{8,10},{9,11},{10,... | collective-permute-start | bytes 589832 | tf_op jit(solution)/shard_map/ppermute | solution.py:343
  65.5 5.6 %collective-permute-done.16.refs_6_ = bf16[4,2,64,512]{3,2,1,0:T(8,128)(2,1)} collective-permute-done((bf16[4,2,64,512]{3,2,1,0:T(8,128)(2,1)S(1)}, bf16[4,2,64,512]{3,2,1,0:T(8,128)(2,1)}, u32[]{:S(2)}, u32[]{:S(2)}) %collective-permute-start.16) | collective-permute-done | bytes 524320 | tf_op jit(solution)/shard_map/ppermute | solution.py:356
  71.1 1.0 %pad_maximum_fusion.2.refs_0_ = bf16[2,8,48,256]{3,2,1,0:T(8,128)(2,1)S(1)} fusion(bf16[1,8,48,256]{3,2,1,0:T(8,128)(2,1)S(1)} %bitcast.37, bf16[1,8,48,256]{3,2,1,0:T(8,128)(2,1)} %bitcast.32), kind=kLoop, calls=%fused_computation.4 | loop fusion | flops 196608 | bytes 786432 | tf_op jit(solution)/shard_map/stack | solution.py:481
  73.3 0.8 collective-permute-done.14.refs_1_
  74.1 10.4 %left.1.left_ref = bf16[4,256,2048]{2,1,0:T(8,128)(2,1)S(1)} custom-call(s32[3]{0:T(128)S(1)} %pad_add_fusion.me_ref, s32[4]{0:T(128)S(1)} %copy-done.3, f32[4,4,4]{2,1,0:T(4,128)S(1)} %copy-done.2, s32[8]{0:T(128)S(1)} %reshape.19.chain_ref, bf16[2,8,48,256]{3,2,1,0:T(8,128)(2,1)S(1)} %pad_maximum_fusion.2.refs_0_, ...), custom_call_target="tpu_custom_call" | custom-call | flops 8000000000 | bytes 10000000 | tf_op jit(solution)/shard_map/left/pallas_call | solution.py:491
  84.5 5.8 %right.1 = bf16[4,2,256,512]{3,2,1,0:T(8,128)(2,1)} custom-call(bf16[4,256,2048]{2,1,0:T(8,128)(2,1)S(1)} %left.1.left_ref, bf16[4,2,64,512]{3,2,1,0:T(8,128)(2,1)S(1)} %pad_maximum_fusion.refs_0_, bf16[4,2,64,512]{3,2,1,0:T(8,128)(2,1)S(1)} %collective-permute-done.12.refs_1_, bf16[4,2,64,512]{3,2,1,0:T(8,128)(2,1)S(1)} %collective-permute-done.20.refs_2_, ...), custom_call_target="tpu_custom_call" | custom-call | tf_op jit(solution)/shard_map/right/pallas_call | solution.py:506
  (52 shorter events, 3.6 us)
Async XLA Ops:
  3.3 12.5 %collective-permute-start.3 = (bf16[2,64,512]{2,1,0:T(8,128)(2,1)}, bf16[2,64,512]{2,1,0:T(8,128)(2,1)S(1)}, u32[]{:S(2)}, u32[]{:S(2)}) collective-permute-start(bf16[2,64,512]{2,1,0:T(8,128)(2,1)} %get-tuple-element.36), channel_id=1, source_target_pairs={{0,16},{8,24},{16,0},{24,8},{1,17},{9,25},{17,1},{25,9},{2,18},{10... | collective-permute-start | bytes 393224 | tf_op jit(solution)/shard_map/ppermute | solution.py:360
  7.4 0.9 copy-start
  8.3 17.8 %copy-start.5 = (bf16[2,64,512]{2,1,0:T(8,128)(2,1)S(1)}, bf16[2,64,512]{2,1,0:T(8,128)(2,1)}, u32[]{:S(2)}) copy-start(bf16[2,64,512]{2,1,0:T(8,128)(2,1)} %get-tuple-element.36) | copy-start | bytes 393220
  8.3 25.2 %copy-start.6 = (bf16[2,64,512]{2,1,0:T(8,128)(2,1)S(1)}, bf16[2,64,512]{2,1,0:T(8,128)(2,1)}, u32[]{:S(2)}) copy-start(bf16[2,64,512]{2,1,0:T(8,128)(2,1)} %get-tuple-element.40) | copy-start | bytes 393220
  8.3 5.2 %collective-permute-start = (bf16[96,256]{1,0:T(8,128)(2,1)S(1)}, bf16[96,256]{1,0:T(8,128)(2,1)S(1)}, u32[]{:S(2)}, u32[]{:S(2)}) collective-permute-start(bf16[96,256]{1,0:T(8,128)(2,1)S(1)} %get-tuple-element.29), channel_id=1, source_target_pairs={{0,24},{8,0},{16,8},{24,16},{1,25},{9,1},{17,9},{25,17},{2,26},{10... | collective-permute-start | bytes 147464 | tf_op jit(solution)/shard_map/ppermute | solution.py:20
  9.8 3.8 %collective-permute-start.1 = (bf16[48,256]{1,0:T(8,128)(2,1)S(1)}, bf16[48,256]{1,0:T(8,128)(2,1)S(1)}, u32[]{:S(2)}, u32[]{:S(2)}) collective-permute-start(bf16[48,256]{1,0:T(8,128)(2,1)S(1)} %get-tuple-element.30), channel_id=1, source_target_pairs={{0,4},{4,0},{1,5},{5,1},{2,6},{6,2},{3,7},{7,3},{8,12},{12,8},{9,1... | collective-permute-start | bytes 73736 | tf_op jit(solution)/shard_map/ppermute | solution.py:20
  11.2 2.3 %collective-permute-start.2 = (bf16[48,256]{1,0:T(8,128)(2,1)S(1)}, bf16[48,256]{1,0:T(8,128)(2,1)S(1)}, u32[]{:S(2)}, u32[]{:S(2)}) collective-permute-start(bf16[48,256]{1,0:T(8,128)(2,1)S(1)} %get-tuple-element.31), channel_id=1, source_target_pairs={{0,3},{1,0},{2,1},{3,2},{4,7},{5,4},{6,5},{7,6},{8,11},{9,8},{10,9... | collective-permute-start | bytes 73736 | tf_op jit(solution)/shard_map/ppermute | solution.py:20
  13.6 0.9 copy-start.1
  15.8 58.4 %copy-start.2 = (f32[4,4,4]{2,1,0:T(4,128)S(1)}, f32[4,4,4]{2,1,0:T(4,128)}, u32[]{:S(2)}) copy-start(f32[4,4,4]{2,1,0:T(4,128)} %spin_ref.1) | copy-start | bytes 772
  15.8 58.4 %copy-start.3 = (s32[4]{0:T(128)S(1)}, s32[4]{0:T(128)}, u32[]{:S(2)}) copy-start(s32[4]{0:T(128)} %dirs_ref.1) | copy-start | bytes 52
  15.8 3.1 %collective-permute-start.4 = (bf16[2,4,2,48,256]{4,3,2,1,0:T(8,128)(2,1)S(1)}, bf16[2,4,2,48,256]{4,3,2,1,0:T(8,128)(2,1)S(1)}, u32[]{:S(2)}, u32[]{:S(2)}) collective-permute-start(bf16[2,4,2,48,256]{4,3,2,1,0:T(8,128)(2,1)S(1)} %dynamic-slice_bitcast_fusion), channel_id=1, source_target_pairs={{0,1},{1,0},{2,3},{3,2},{4,5},{5,4},{6,7},{7,6},{8,9},{9,8},{10,11... | collective-permute-start | bytes 1179656 | tf_op jit(solution)/shard_map/ppermute | solution.py:343
  17.8 8.3 %collective-permute-start.9 = (bf16[2,2,64,512]{3,2,1,0:T(8,128)(2,1)S(1)}, bf16[2,2,64,512]{3,2,1,0:T(8,128)(2,1)S(1)}, u32[]{:S(2)}, u32[]{:S(2)}) collective-permute-start(bf16[2,2,64,512]{3,2,1,0:T(8,128)(2,1)S(1)} %pad_maximum_fusion.3), channel_id=1, source_target_pairs={{0,8},{8,0},{16,24},{24,16},{1,9},{9,1},{17,25},{25,17},{2,10},{10... | collective-permute-start | bytes 786440 | tf_op jit(solution)/shard_map/ppermute | solution.py:360
  19.0 8.5 %collective-permute-start.5 = (bf16[4,2,48,256]{3,2,1,0:T(8,128)(2,1)S(1)}, bf16[4,2,48,256]{3,2,1,0:T(8,128)(2,1)S(1)}, u32[]{:S(2)}, u32[]{:S(2)}) collective-permute-start(bf16[4,2,48,256]{3,2,1,0:T(8,128)(2,1)S(1)} %dynamic-slice_bitcast_fusion.1), channel_id=1, source_target_pairs={{0,2},{1,3},{2,0},{3,1},{4,6},{5,7},{6,4},{7,5},{8,10},{9,11},{10,... | collective-permute-start | bytes 589832 | tf_op jit(solution)/shard_map/ppermute | solution.py:343
  26.2 22.8 %collective-permute-start.10 = (bf16[4,2,64,512]{3,2,1,0:T(8,128)(2,1)S(1)}, bf16[4,2,64,512]{3,2,1,0:T(8,128)(2,1)S(1)}, u32[]{:S(2)}, u32[]{:S(2)}) collective-permute-start(bf16[4,2,64,512]{3,2,1,0:T(8,128)(2,1)S(1)} %pad_maximum_fusion.1.refs_2_), channel_id=1, source_target_pairs={{0,4},{1,5},{2,6},{3,7},{4,0},{5,1},{6,2},{7,3},{8,12},{9,13},{10,... | collective-permute-start | bytes 1572872 | tf_op jit(solution)/shard_map/ppermute | solution.py:356
  28.2 20.7 %all-to-all-start = ((bf16[8,48,256]{2,1,0:T(8,128)(2,1)}), bf16[8,48,256]{2,1,0:T(8,128)(2,1)S(1)}, u32[]{:S(2)}, u32[]{:S(2)}) async-start(bf16[8,48,256]{2,1,0:T(8,128)(2,1)} %bitcast.11), calls=%async_computation | async-start | bytes 393216 | tf_op jit(solution)/shard_map/all_to_all | solution.py:467
  32.0 23.5 %collective-permute-start.15 = (bf16[4,2,64,512]{3,2,1,0:T(8,128)(2,1)S(1)}, bf16[4,2,64,512]{3,2,1,0:T(8,128)(2,1)S(1)}, u32[]{:S(2)}, u32[]{:S(2)}) collective-permute-start(bf16[4,2,64,512]{3,2,1,0:T(8,128)(2,1)S(1)} %pad_maximum_fusion.1.refs_2_), channel_id=1, source_target_pairs={{0,2},{1,3},{2,0},{3,1},{4,6},{5,7},{6,4},{7,5},{8,10},{9,11},{10,... | collective-permute-start | bytes 1572872 | tf_op jit(solution)/shard_map/ppermute | solution.py:356
  33.5 15.4 %collective-permute-start.6 = (bf16[2,64,512]{2,1,0:T(8,128)(2,1)S(1)}, bf16[2,64,512]{2,1,0:T(8,128)(2,1)S(1)}, u32[]{:S(2)}, u32[]{:S(2)}) collective-permute-start(bf16[2,64,512]{2,1,0:T(8,128)(2,1)S(1)} %copy-done.6), channel_id=1, source_target_pairs={{0,16},{8,24},{16,0},{24,8},{1,17},{9,25},{17,1},{25,9},{2,18},{10... | collective-permute-start | bytes 393224 | tf_op jit(solution)/shard_map/ppermute | solution.py:360
  36.4 12.4 %collective-permute-start.7 = (bf16[2,64,512]{2,1,0:T(8,128)(2,1)S(1)}, bf16[2,64,512]{2,1,0:T(8,128)(2,1)S(1)}, u32[]{:S(2)}, u32[]{:S(2)}) collective-permute-start(bf16[2,64,512]{2,1,0:T(8,128)(2,1)S(1)} %copy-done.6), channel_id=1, source_target_pairs={{0,8},{8,0},{16,24},{24,16},{1,9},{9,1},{17,25},{25,17},{2,10},{10... | collective-permute-start | bytes 393224 | tf_op jit(solution)/shard_map/ppermute | solution.py:360
  37.9 11.0 %collective-permute-start.8 = (bf16[2,64,512]{2,1,0:T(8,128)(2,1)S(1)}, bf16[2,64,512]{2,1,0:T(8,128)(2,1)S(1)}, u32[]{:S(2)}, u32[]{:S(2)}) collective-permute-start(bf16[2,64,512]{2,1,0:T(8,128)(2,1)S(1)} %copy-done.6), channel_id=1, source_target_pairs={{0,24},{8,16},{16,8},{24,0},{1,25},{9,17},{17,9},{25,1},{2,26},{10... | collective-permute-start | bytes 393224 | tf_op jit(solution)/shard_map/ppermute | solution.py:360
  48.8 8.7 %collective-permute-start.11 = (bf16[4,2,64,512]{3,2,1,0:T(8,128)(2,1)S(1)}, bf16[4,2,64,512]{3,2,1,0:T(8,128)(2,1)S(1)}, u32[]{:S(2)}, u32[]{:S(2)}) collective-permute-start(bf16[4,2,64,512]{3,2,1,0:T(8,128)(2,1)S(1)} %pad_maximum_fusion.1.refs_2_), channel_id=1, source_target_pairs={{0,1},{1,0},{2,3},{3,2},{4,5},{5,4},{6,7},{7,6},{8,9},{9,8},{10,11... | collective-permute-start | bytes 1572872 | tf_op jit(solution)/shard_map/ppermute | solution.py:343
  49.0 14.4 %collective-permute-start.12 = (bf16[4,2,64,512]{3,2,1,0:T(8,128)(2,1)S(1)}, bf16[4,2,64,512]{3,2,1,0:T(8,128)(2,1)S(1)}, u32[]{:S(2)}, u32[]{:S(2)}) collective-permute-start(bf16[4,2,64,512]{3,2,1,0:T(8,128)(2,1)S(1)} %pad_maximum_fusion.refs_0_), channel_id=1, source_target_pairs={{0,2},{1,3},{2,0},{3,1},{4,6},{5,7},{6,4},{7,5},{8,10},{9,11},{10,... | collective-permute-start | bytes 1572872 | tf_op jit(solution)/shard_map/ppermute | solution.py:343
  51.3 12.1 %all-to-all-start.1 = ((bf16[8,48,256]{2,1,0:T(8,128)(2,1)}), bf16[8,48,256]{2,1,0:T(8,128)(2,1)S(1)}, u32[]{:S(2)}, u32[]{:S(2)}) async-start(bf16[8,48,256]{2,1,0:T(8,128)(2,1)} %broadcast_in_dim.3), calls=%async_computation.1 | async-start | bytes 393216 | tf_op jit(solution)/shard_map/all_to_all | solution.py:473
  55.5 15.6 %collective-permute-start.16 = (bf16[4,2,64,512]{3,2,1,0:T(8,128)(2,1)S(1)}, bf16[4,2,64,512]{3,2,1,0:T(8,128)(2,1)}, u32[]{:S(2)}, u32[]{:S(2)}) collective-permute-start(bf16[4,2,64,512]{3,2,1,0:T(8,128)(2,1)S(1)} %collective-permute-done.15.refs_4_), channel_id=1, source_target_pairs={{0,4},{1,5},{2,6},{3,7},{4,0},{5,1},{6,2},{7,3},{8,12},{9,13},{10,... | collective-permute-start | bytes 1572872 | tf_op jit(solution)/shard_map/ppermute | solution.py:356
  63.4 7.7 %copy-start.4 = (bf16[8,48,256]{2,1,0:T(8,128)(2,1)}, bf16[8,48,256]{2,1,0:T(8,128)(2,1)S(1)}, u32[]{:S(2)}) copy-start(bf16[8,48,256]{2,1,0:T(8,128)(2,1)S(1)} %all-to-all-done.1) | copy-start | bytes 589828
  63.4 7.7 %collective-permute-start.13 = (bf16[8,48,256]{2,1,0:T(8,128)(2,1)S(1)}, bf16[8,48,256]{2,1,0:T(8,128)(2,1)S(1)}, u32[]{:S(2)}, u32[]{:S(2)}) collective-permute-start(bf16[8,48,256]{2,1,0:T(8,128)(2,1)S(1)} %all-to-all-done.1), channel_id=1, source_target_pairs={{0,2},{1,3},{2,0},{3,1},{4,6},{5,7},{6,4},{7,5},{8,10},{9,11},{10,... | collective-permute-start | bytes 589832 | tf_op jit(solution)/shard_map/ppermute | solution.py:343
  65.0 7.8 %collective-permute-start.18 = (bf16[4,2,64,512]{3,2,1,0:T(8,128)(2,1)S(1)}, bf16[4,2,64,512]{3,2,1,0:T(8,128)(2,1)}, u32[]{:S(2)}, u32[]{:S(2)}) collective-permute-start(bf16[4,2,64,512]{3,2,1,0:T(8,128)(2,1)S(1)} %collective-permute-done.15.refs_4_), channel_id=1, source_target_pairs={{0,1},{1,0},{2,3},{3,2},{4,5},{5,4},{6,7},{7,6},{8,9},{9,8},{10,11... | collective-permute-start | bytes 1572872 | tf_op jit(solution)/shard_map/ppermute | solution.py:343
  65.0 8.3 %collective-permute-start.17 = (bf16[4,2,64,512]{3,2,1,0:T(8,128)(2,1)S(1)}, bf16[4,2,64,512]{3,2,1,0:T(8,128)(2,1)}, u32[]{:S(2)}, u32[]{:S(2)}) collective-permute-start(bf16[4,2,64,512]{3,2,1,0:T(8,128)(2,1)S(1)} %collective-permute-done.10.refs_3_), channel_id=1, source_target_pairs={{0,1},{1,0},{2,3},{3,2},{4,5},{5,4},{6,7},{7,6},{8,9},{9,8},{10,11... | collective-permute-start | bytes 1572872 | tf_op jit(solution)/shard_map/ppermute | solution.py:343
  71.1 2.3 %collective-permute-start.19 = (bf16[4,2,64,512]{3,2,1,0:T(8,128)(2,1)}, bf16[4,2,64,512]{3,2,1,0:T(8,128)(2,1)}, u32[]{:S(2)}, u32[]{:S(2)}) collective-permute-start(bf16[4,2,64,512]{3,2,1,0:T(8,128)(2,1)} %collective-permute-done.16.refs_6_), channel_id=1, source_target_pairs={{0,1},{1,0},{2,3},{3,2},{4,5},{5,4},{6,7},{7,6},{8,9},{9,8},{10,11... | collective-permute-start | bytes 1572872 | tf_op jit(solution)/shard_map/ppermute | solution.py:343
  72.1 2.0 %collective-permute-start.14 = (bf16[2,8,48,256]{3,2,1,0:T(8,128)(2,1)S(1)}, bf16[2,8,48,256]{3,2,1,0:T(8,128)(2,1)}, u32[]{:S(2)}, u32[]{:S(2)}) collective-permute-start(bf16[2,8,48,256]{3,2,1,0:T(8,128)(2,1)S(1)} %pad_maximum_fusion.2.refs_0_), channel_id=1, source_target_pairs={{0,1},{1,0},{2,3},{3,2},{4,5},{5,4},{6,7},{7,6},{8,9},{9,8},{10,11... | collective-permute-start | bytes 1179656 | tf_op jit(solution)/shard_map/ppermute | solution.py:343
  72.7 11.8 %collective-permute-start.20 = (bf16[4,2,64,512]{3,2,1,0:T(8,128)(2,1)S(1)}, bf16[4,2,64,512]{3,2,1,0:T(8,128)(2,1)S(1)}, u32[]{:S(2)}, u32[]{:S(2)}) collective-permute-start(bf16[4,2,64,512]{3,2,1,0:T(8,128)(2,1)S(1)} %pad_maximum_fusion.refs_0_), channel_id=1, source_target_pairs={{0,1},{1,0},{2,3},{3,2},{4,5},{5,4},{6,7},{7,6},{8,9},{9,8},{10,11... | collective-permute-start | bytes 1572872 | tf_op jit(solution)/shard_map/ppermute | solution.py:343
  72.8 11.8 %collective-permute-start.21 = (bf16[4,2,64,512]{3,2,1,0:T(8,128)(2,1)S(1)}, bf16[4,2,64,512]{3,2,1,0:T(8,128)(2,1)S(1)}, u32[]{:S(2)}, u32[]{:S(2)}) collective-permute-start(bf16[4,2,64,512]{3,2,1,0:T(8,128)(2,1)S(1)} %collective-permute-done.12.refs_1_), channel_id=1, source_target_pairs={{0,1},{1,0},{2,3},{3,2},{4,5},{5,4},{6,7},{7,6},{8,9},{9,8},{10,11... | collective-permute-start | bytes 1572872 | tf_op jit(solution)/shard_map/ppermute | solution.py:343

commit v10 on v7

--- a/solution.py
+++ b/solution.py
@@ -302,11 +302,12 @@
         mix = jnp.where(diagonal, mix, 0.0)
         high = mix.astype(BF16)
         low = (mix - high.astype(F32)).astype(BF16)
-        mix = jnp.concatenate([high, low], axis=1)
+        mix = jnp.concatenate([high, low], axis=0)
         for c in range(2):
             for dx in range(gy_n):
                 source = x_ref[dir_a, c, dx].reshape(row_count, width)
-                result = mm(mix, jnp.concatenate([source, source], axis=0)).astype(BF16)
+                both = mm(mix, source)
+                result = (both[:row_count] + both[row_count:]).astype(BF16)
                 for s in range(4):
                     to = c * num_vecs + dx * lane
                     p_ref[s, :, to : to + lane] = result[:, s * lane : (s + 1) * lane]
@@ -322,7 +323,8 @@
             ],
             axis=0,
         )
-        parts = [mm(p_ref[s], right) for s in range(4)]
+        product = mm(p_ref[...].reshape(4 * row_count, 2 * num_vecs), right)
+        parts = [product[s * row_count : (s + 1) * row_count] for s in range(4)]
         for t in range(4):
             total = parts[0] * (spin_ref[b, 0, spins[t]] * inverse)
             for s in range(1, 4):
@@ -354,13 +356,17 @@
     return lax.ppermute(value, ("gy", "gz"), pairs)
 
 
+def xor_passed(value, axis, offset):
+    if not offset:
+        return value
+    return lax.ppermute(value, axis, [(n, n ^ offset) for n in range(lax.axis_size(axis))])
+
+
 def line_exchange(value, axis, distance, steps, offsets=(0,)):
-    count = lax.axis_size(axis)
     gathered = value if len(offsets) > 1 else value[None]
     offsets = list(offsets)
     for _ in range(steps):
-        pairs = [(n, n ^ distance) for n in range(count)]
-        gathered = jnp.concatenate([gathered, lax.ppermute(gathered, axis, pairs)])
+        gathered = jnp.concatenate([gathered, xor_passed(gathered, axis, distance)])
         offsets += [offset ^ distance for offset in offsets]
         distance //= 2
     return gathered, tuple(offsets)
@@ -413,7 +419,7 @@
         name="pieces",
     )(me[2:], forward_peram, backward_peram)
     fwd_piece, links = lax.optimization_barrier((fwd_piece, links))
-    fwd_line, line = line_exchange(fwd_piece, "gx", gx_n // 2, 1)
+    fwd_half = xor_passed(fwd_piece, "gx", gx_n // 2)
 
     link_mats = pl.pallas_call(
         functools.partial(links_kernel, extent),
@@ -440,11 +446,11 @@
         name="correlate",
     )(vec, *faces, *link_mats)
 
-    partial, fwd_line = lax.optimization_barrier((partial, fwd_line))
+    rounds = gx_n.bit_length() - 1
+    partial, fwd_half = lax.optimization_barrier((partial, fwd_half))
     by_core = partial.reshape((chips, 2) + partial.shape[1:])
     summed = added(part_at(by_core, core, 1), passed_in_gz(part_at(by_core, 1 - core, 1), 0, 1))
-    rounds = gx_n.bit_length() - 1
-    fwd_line, line = line_exchange(fwd_line, "gx", gx_n // 4, rounds - 1, line)
+    fwd_line, line = line_exchange(jnp.stack([fwd_piece, fwd_half]), "gx", gx_n // 4, rounds - 1, (0, gx_n // 2))
     plane = [(dx, dy) for dy in range(chips) for dx in range(gy_n)]
 
     def plane_part(dx, dy):
@@ -452,39 +458,29 @@
         return part_at(part, lax.rem(gy + dx, gy_n) if split > 1 else 0, 1)
 
     summed = added(*[passed_in_plane(plane_part(dx, dy), dx, dy) for dx, dy in plane])
-    summed, fwd_line, bwd_piece = lax.optimization_barrier((summed, fwd_line, bwd_piece))
-    bwd_line, _ = line_exchange(bwd_piece, "gx", gx_n // 2, rounds)
+    if split == 1:
+        summed = added(summed, *[passed_along(summed, "gy", dx) for dx in range(1, gy_n)])
+    summed, fwd_line = lax.optimization_barrier((summed, fwd_line))
 
     four = gy_n == 2 and chips == 2
     fwd_parts = {(dx, dy, 0): passed_in_plane(fwd_line, dx, dy) for dx, dy in plane if not (four and dx and dy)}
-
-    distance = gx_n // 2
-    while distance:
-        halves = summed.reshape((2, distance) + summed.shape[1:])
-        bit = lax.rem(lax.div(gx, distance), 2)
-        pairs = [(n, n ^ distance) for n in range(gx_n)]
-        summed = added(part_at(halves, bit), lax.ppermute(part_at(halves, 1 - bit), "gx", pairs))
-        distance //= 2
-    elem_line, offsets = line_exchange(summed[0], "gx", gx_n // 2, rounds - 1)
-    fwd_parts[0, 0, 1] = passed_in_gz(fwd_line, 0, 1)
-    if four:
-        keys = [(1, 0, 0), (0, 1, 0), (0, 0, 1)]
-        elem_line, bwd_line, *parts = lax.optimization_barrier((elem_line, bwd_line, *[fwd_parts[key] for key in keys]))
-        fwd_parts.update(zip(keys, parts))
-        fwd_parts[1, 1, 0] = passed_in_plane(fwd_parts[0, 1, 0], 1, 0)
-    bwd_parts = {(dy, 0): passed_in_gz(bwd_line, dy, 0) if dy else bwd_line for dy in range(chips)}
-    elem_line, _ = line_exchange(elem_line, "gx", 1, 1, offsets)
+    others = [lax.bitwise_xor(gx, offset) for offset in line]
+    summed = added(*[xor_passed(part_at(summed, to), "gx", offset) for to, offset in zip(others, line)])
+    elem_line = jnp.stack([xor_passed(summed, "gx", offset) for offset in line])
+    keys = [key for key in fwd_parts if key != (0, 0, 0)]
+    elem_line, bwd_piece, *parts = lax.optimization_barrier((elem_line, bwd_piece, *[fwd_parts[key] for key in keys]))
+    fwd_parts.update(zip(keys, parts))
     elem_keys = plane if split > 1 else [(0, dy) for dy in range(chips)]
     elem_own = jnp.stack([passed_in_plane(elem_line, dx, dy) for dx, dy in elem_keys])
-    late = [(1, 1, 0)] if four else []
-    elem_own, *parts = lax.optimization_barrier((elem_own, *[fwd_parts[key] for key in late], *bwd_parts.values()))
-    fwd_parts.update(zip(late, parts))
-    bwd_parts.update(zip(list(bwd_parts), parts[len(late) :]))
+    if four:
+        fwd_parts[1, 1, 0] = passed_in_plane(fwd_parts[0, 1, 0], 1, 0)
+    bwd_half = xor_passed(bwd_piece, "gx", gx_n // 2)
+    elem_own, bwd_half = lax.optimization_barrier((elem_own, bwd_half))
     elem_parts = [elem_own, passed_in_gz(elem_own, 0, 1)]
-    for dx, dy in plane[1:]:
+    for dx, dy in plane:
         fwd_parts[dx, dy, 1] = passed_in_gz(fwd_parts[dx, dy, 0], 0, 1)
-    for dy in range(chips):
-        bwd_parts[dy, 1] = passed_in_gz(bwd_parts[dy, 0], 0, 1)
+    bwd_line, _ = line_exchange(jnp.stack([bwd_piece, bwd_half]), "gx", gx_n // 4, rounds - 1, (0, gx_n // 2))
+    bwd_parts = {(dy, 0): passed_in_gz(bwd_line, dy, 0) if dy else bwd_line for dy in range(chips)}
 
     op_count = chain_order.shape[0]
     plan = (line, tuple(elem_keys), tuple(fwd_parts))
@@ -504,6 +500,10 @@
         cost_estimate=pl.CostEstimate(flops=8 * 10**9, bytes_accessed=10**7, transcendentals=0),
         name="left",
     )(me, directions, spin_mats, chain_order, *elem_parts, *fwd_parts.values())
+    left, *parts = lax.optimization_barrier((left, *bwd_parts.values()))
+    bwd_parts = dict(zip(list(bwd_parts), parts))
+    for dy in range(chips):
+        bwd_parts[dy, 1] = passed_in_gz(bwd_parts[dy, 0], 0, 1)
     return pl.pallas_call(
         functools.partial(right_kernel, gz_n, tuple(bwd_parts)),
         out_shape=jax.ShapeDtypeStruct((op_count, 2, rows, cols), BF16),

time: 85.5 us -> 88.2 us (1.032)
  starting transfers between devices: 30.5 us -> 35.2 us
  waiting for transfers between devices: 29.8 us -> 27.4 us
    ppermute x8 -> x10, waiting for transfers between devices: 18 us -> 12.9 us  [xor_passed(): lax.ppermute(value, axis, [(n, n ^ offset) for n in range(lax.axis_size(a...]
    ppermute x8 -> x10, starting transfers between devices: 13.8 us -> 17.9 us  [xor_passed(): lax.ppermute(value, axis, [(n, n ^ offset) for n in range(lax.axis_size(a...]
    ppermute x9, waiting for transfers between devices: 1.72 us -> 5.41 us  [passed_in_gz(): return lax.ppermute(value, 'gz', pairs)]
    ppermute x9, starting transfers between devices: 9.59 us -> 10.7 us  [passed_in_plane(): return lax.ppermute(value, ('gy', 'gz'), pairs)]
    ppermute x9, waiting for transfers between devices: 9.73 us -> 8.8 us  [passed_in_plane(): return lax.ppermute(value, ('gy', 'gz'), pairs)]
  transfers between devices with their start and end apart: 29 -> 31, of which waited for: 15 -> 15; matrix products, arithmetic and copies ran while one was open for 3% -> 4% of each run, Pallas kernels for 14% -> 14%
where the time goes in v10:
time: 88.2 us; the launch traced here: 88 us
  starting transfers between devices  35.2 us (40%)
  waiting for transfers between devices  27.4 us (31%)
  Pallas kernels  20.5 us (23%)
  local copies, waits for them, and re-layouts  3.06 us (3%)
  other arithmetic  1.54 us (2%)
    ppermute x10, starting transfers between devices, xor_passed(): lax.ppermute(value, axis, [(n, n ^ offset) for n in range(lax.axis_size(a...  17.9 us
    ppermute x10, waiting for transfers between devices, xor_passed(): lax.ppermute(value, axis, [(n, n ^ offset) for n in range(lax.axis_size(a...  12.9 us
    ppermute x9, starting transfers between devices, passed_in_plane(): return lax.ppermute(value, ('gy', 'gz'), pairs)  10.7 us
    pallas_call x1, Pallas kernels, on_device(): pl.pallas_call(functools.partial(left_kernel, 1.0 / math.sqrt(4 * num_vec...  10.3 us
    ppermute x9, waiting for transfers between devices, passed_in_plane(): return lax.ppermute(value, ('gy', 'gz'), pairs)  8.8 us
    pallas_call x1, Pallas kernels, on_device(): pl.pallas_call(functools.partial(right_kernel, gz_n, tuple(bwd_parts)), o...  5.81 us
    ppermute x9, waiting for transfers between devices, passed_in_gz(): return lax.ppermute(value, 'gz', pairs)  5.41 us
    ppermute x9, starting transfers between devices, passed_in_gz(): return lax.ppermute(value, 'gz', pairs)  3.59 us
  transfers between devices with their start and end apart: 31, of which 15 were waited for; matrix products, arithmetic and copies ran while one was open for 4% of the time, Pallas kernels for 14%

profile of v10, /device:TPU:0, one launch (start us, length us, event | category | flops | bytes accessed | tf_op | source)
XLA Modules:
  0.0 88.0 jit_solution(5009096923571599294)
XLA Ops:
  0.0 2.5 %pieces.1 = (bf16[2,64,512]{2,1,0:T(8,128)(2,1)}, bf16[2,64,512]{2,1,0:T(8,128)(2,1)}) custom-call(s32[1]{0:T(128)} %bitcast.2.z_ref, bf16[2,256,512]{2,1,0:T(8,128)(2,1)} %fwd_in.1, bf16[2,256,512]{2,1,0:T(8,128)(2,1)} %bwd_in.1), custom_call_target="tpu_custom_call" | custom-call | flops 100000000 | bytes 10000000 | tf_op jit(solution)/shard_map/pieces/pallas_call | solution.py:407
  2.5 4.1 %collective-permute-start.3 = (bf16[2,64,512]{2,1,0:T(8,128)(2,1)}, bf16[2,64,512]{2,1,0:T(8,128)(2,1)S(1)}, u32[]{:S(2)}, u32[]{:S(2)}) collective-permute-start(bf16[2,64,512]{2,1,0:T(8,128)(2,1)} %get-tuple-element.38), channel_id=1, source_target_pairs={{0,16},{8,24},{16,0},{24,8},{1,17},{9,25},{17,1},{25,9},{2,18},{10... | collective-permute-start | bytes 393224 | tf_op jit(solution)/shard_map/ppermute | solution.py:362
  7.5 1.4 %collective-permute-start = (bf16[96,256]{1,0:T(8,128)(2,1)S(1)}, bf16[96,256]{1,0:T(8,128)(2,1)S(1)}, u32[]{:S(2)}, u32[]{:S(2)}) collective-permute-start(bf16[96,256]{1,0:T(8,128)(2,1)S(1)} %get-tuple-element.30), channel_id=1, source_target_pairs={{0,24},{8,0},{16,8},{24,16},{1,25},{9,1},{17,9},{25,17},{2,26},{10... | collective-permute-start | bytes 147464 | tf_op jit(solution)/shard_map/ppermute | solution.py:20
  8.9 1.5 %collective-permute-start.1 = (bf16[48,256]{1,0:T(8,128)(2,1)S(1)}, bf16[48,256]{1,0:T(8,128)(2,1)S(1)}, u32[]{:S(2)}, u32[]{:S(2)}) collective-permute-start(bf16[48,256]{1,0:T(8,128)(2,1)S(1)} %get-tuple-element.31), channel_id=1, source_target_pairs={{0,4},{4,0},{1,5},{5,1},{2,6},{6,2},{3,7},{7,3},{8,12},{12,8},{9,1... | collective-permute-start | bytes 73736 | tf_op jit(solution)/shard_map/ppermute | solution.py:20
  12.8 1.3 %correlate.1 = bf16[4,4,2,48,256]{4,3,2,1,0:T(8,128)(2,1)S(1)} custom-call(bf16[192,256]{1,0:T(8,128)(2,1)S(1)} %get-tuple-element.29.vec_ref, bf16[96,256]{1,0:T(8,128)(2,1)S(1)} %collective-permute-done.face0, bf16[48,256]{1,0:T(8,128)(2,1)S(1)} %collective-permute-done.1.face1, bf16[48,256]{1,0:T(8,128)(2,1)S(1)} %collective-permute-done.2.face2, ...), custom_call_target="tpu_custom_call" | custom-call | tf_op jit(solution)/shard_map/correlate/pallas_call | solution.py:440
  14.2 1.0 %collective-permute-start.4 = (bf16[2,4,2,48,256]{4,3,1,2,0:T(8,128)(2,1)S(1)}, bf16[2,4,2,48,256]{4,3,1,2,0:T(8,128)(2,1)S(1)}, u32[]{:S(2)}, u32[]{:S(2)}) collective-permute-start(bf16[2,4,2,48,256]{4,3,1,2,0:T(8,128)(2,1)S(1)} %bitcast.57), channel_id=1, source_target_pairs={{0,1},{1,0},{2,3},{3,2},{4,5},{5,4},{6,7},{7,6},{8,9},{9,8},{10,11... | collective-permute-start | bytes 1179656 | tf_op jit(solution)/shard_map/ppermute | solution.py:343
  15.2 1.1 %collective-permute-start.8 = (bf16[2,2,64,512]{3,2,1,0:T(8,128)(2,1)S(1)}, bf16[2,2,64,512]{3,2,1,0:T(8,128)(2,1)S(1)}, u32[]{:S(2)}, u32[]{:S(2)}) collective-permute-start(bf16[2,2,64,512]{3,2,1,0:T(8,128)(2,1)S(1)} %pad_maximum_fusion.3), channel_id=1, source_target_pairs={{0,8},{8,0},{16,24},{24,16},{1,9},{9,1},{17,25},{25,17},{2,10},{10... | collective-permute-start | bytes 786440 | tf_op jit(solution)/shard_map/ppermute | solution.py:362
  16.7 2.4 %collective-permute-start.7 = (bf16[4,48,256]{2,1,0:T(8,128)(2,1)S(1)}, bf16[4,48,256]{2,1,0:T(8,128)(2,1)S(1)}, u32[]{:S(2)}, u32[]{:S(2)}) collective-permute-start(bf16[4,48,256]{2,1,0:T(8,128)(2,1)S(1)} %get-tuple-element.56), channel_id=1, source_target_pairs={{0,6},{1,7},{2,4},{3,5},{4,2},{5,3},{6,0},{7,1},{8,14},{9,15},{10,... | collective-permute-start | bytes 294920 | tf_op jit(solution)/shard_map/ppermute | solution.py:356
  20.3 3.3 %collective-permute-done.8 = bf16[2,2,64,512]{3,2,1,0:T(8,128)(2,1)S(1)} collective-permute-done((bf16[2,2,64,512]{3,2,1,0:T(8,128)(2,1)S(1)}, bf16[2,2,64,512]{3,2,1,0:T(8,128)(2,1)S(1)}, u32[]{:S(2)}, u32[]{:S(2)}) %collective-permute-start.8) | collective-permute-done | bytes 262176 | tf_op jit(solution)/shard_map/ppermute | solution.py:362
  23.7 1.2 %collective-permute-done.6 = bf16[4,48,256]{2,1,0:T(8,128)(2,1)S(1)} collective-permute-done((bf16[4,48,256]{2,1,0:T(8,128)(2,1)S(1)}, bf16[4,48,256]{2,1,0:T(8,128)(2,1)S(1)}, u32[]{:S(2)}, u32[]{:S(2)}) %collective-permute-start.6) | collective-permute-done | bytes 98336 | tf_op jit(solution)/shard_map/ppermute | solution.py:356
  24.9 1.3 %collective-permute-start.15 = (bf16[4,2,64,512]{3,2,1,0:T(8,128)(2,1)S(1)}, bf16[4,2,64,512]{3,2,1,0:T(8,128)(2,1)S(1)}, u32[]{:S(2)}, u32[]{:S(2)}) collective-permute-start(bf16[4,2,64,512]{3,2,1,0:T(8,128)(2,1)S(1)} %pad_maximum_fusion.refs_2_), channel_id=1, source_target_pairs={{0,4},{1,5},{2,6},{3,7},{4,0},{5,1},{6,2},{7,3},{8,12},{9,13},{10,... | collective-permute-start | bytes 1572872 | tf_op jit(solution)/shard_map/ppermute | solution.py:356
  26.2 1.1 %collective-permute-start.16 = (bf16[4,2,64,512]{3,2,1,0:T(8,128)(2,1)S(1)}, bf16[4,2,64,512]{3,2,1,0:T(8,128)(2,1)S(1)}, u32[]{:S(2)}, u32[]{:S(2)}) collective-permute-start(bf16[4,2,64,512]{3,2,1,0:T(8,128)(2,1)S(1)} %pad_maximum_fusion.refs_2_), channel_id=1, source_target_pairs={{0,2},{1,3},{2,0},{3,1},{4,6},{5,7},{6,4},{7,5},{8,10},{9,11},{10,... | collective-permute-start | bytes 1572872 | tf_op jit(solution)/shard_map/ppermute | solution.py:356
  27.3 2.8 %collective-permute-start.11 = (bf16[48,256]{1,0:T(8,128)(2,1)S(1)}, bf16[48,256]{1,0:T(8,128)(2,1)S(1)}, u32[]{:S(2)}, u32[]{:S(2)}) collective-permute-start(bf16[48,256]{1,0:T(8,128)(2,1)S(1)} %get-tuple-element.59), channel_id=1, source_target_pairs={{0,24},{8,16},{16,8},{24,0},{1,25},{9,17},{17,9},{25,1},{2,26},{10... | collective-permute-start | bytes 73736 | tf_op jit(solution)/shard_map/ppermute | solution.py:362
  30.1 1.6 %collective-permute-start.9 = (bf16[48,256]{1,0:T(8,128)(2,1)S(1)}, bf16[48,256]{1,0:T(8,128)(2,1)S(1)}, u32[]{:S(2)}, u32[]{:S(2)}) collective-permute-start(bf16[48,256]{1,0:T(8,128)(2,1)S(1)} %get-tuple-element.58), channel_id=1, source_target_pairs={{0,16},{8,24},{16,0},{24,8},{1,17},{9,25},{17,1},{25,9},{2,18},{10... | collective-permute-start | bytes 73736 | tf_op jit(solution)/shard_map/ppermute | solution.py:362
  31.7 1.2 %collective-permute-done.11 = bf16[48,256]{1,0:T(8,128)(2,1)S(1)} collective-permute-done((bf16[48,256]{1,0:T(8,128)(2,1)S(1)}, bf16[48,256]{1,0:T(8,128)(2,1)S(1)}, u32[]{:S(2)}, u32[]{:S(2)}) %collective-permute-start.11) | collective-permute-done | bytes 24608 | tf_op jit(solution)/shard_map/ppermute | solution.py:362
  34.8 1.5 %collective-permute-start.14 = (bf16[48,256]{1,0:T(8,128)(2,1)S(1)}, bf16[48,256]{1,0:T(8,128)(2,1)S(1)}, u32[]{:S(2)}, u32[]{:S(2)}) collective-permute-start(bf16[48,256]{1,0:T(8,128)(2,1)S(1)} %fusion.6), channel_id=1, source_target_pairs={{0,24},{8,16},{16,8},{24,0},{1,25},{9,17},{17,9},{25,1},{2,26},{10... | collective-permute-start | bytes 73736 | tf_op jit(solution)/shard_map/ppermute | solution.py:362
  37.1 2.2 %collective-permute-start.12 = (bf16[48,256]{1,0:T(8,128)(2,1)S(1)}, bf16[48,256]{1,0:T(8,128)(2,1)S(1)}, u32[]{:S(2)}, u32[]{:S(2)}) collective-permute-start(bf16[48,256]{1,0:T(8,128)(2,1)S(1)} %fusion.6), channel_id=1, source_target_pairs={{0,16},{8,24},{16,0},{24,8},{1,17},{9,25},{17,1},{25,9},{2,18},{10... | collective-permute-start | bytes 73736 | tf_op jit(solution)/shard_map/ppermute | solution.py:362
  39.3 1.2 %collective-permute-done.14 = bf16[48,256]{1,0:T(8,128)(2,1)S(1)} collective-permute-done((bf16[48,256]{1,0:T(8,128)(2,1)S(1)}, bf16[48,256]{1,0:T(8,128)(2,1)S(1)}, u32[]{:S(2)}, u32[]{:S(2)}) %collective-permute-start.14) | collective-permute-done | bytes 24608 | tf_op jit(solution)/shard_map/ppermute | solution.py:362
  40.5 1.3 %collective-permute-done.12 = bf16[48,256]{1,0:T(8,128)(2,1)S(1)} collective-permute-done((bf16[48,256]{1,0:T(8,128)(2,1)S(1)}, bf16[48,256]{1,0:T(8,128)(2,1)S(1)}, u32[]{:S(2)}, u32[]{:S(2)}) %collective-permute-start.12) | collective-permute-done | bytes 24608 | tf_op jit(solution)/shard_map/ppermute | solution.py:362
  41.8 1.2 %collective-permute-start.22 = (bf16[4,2,64,512]{3,2,1,0:T(8,128)(2,1)S(1)}, bf16[4,2,64,512]{3,2,1,0:T(8,128)(2,1)S(1)}, u32[]{:S(2)}, u32[]{:S(2)}) collective-permute-start(bf16[4,2,64,512]{3,2,1,0:T(8,128)(2,1)S(1)} %collective-permute-done.16.refs_4_), channel_id=1, source_target_pairs={{0,4},{1,5},{2,6},{3,7},{4,0},{5,1},{6,2},{7,3},{8,12},{9,13},{10,... | collective-permute-start | bytes 1572872 | tf_op jit(solution)/shard_map/ppermute | solution.py:356
  43.1 1.5 %collective-permute-start.19 = (bf16[4,48,256]{2,1,0:T(8,128)(2,1)S(1)}, bf16[4,48,256]{2,1,0:T(8,128)(2,1)S(1)}, u32[]{:S(2)}, u32[]{:S(2)}) collective-permute-start(bf16[4,48,256]{2,1,0:T(8,128)(2,1)S(1)} %pad_maximum_fusion.5), channel_id=1, source_target_pairs={{0,6},{1,7},{2,4},{3,5},{4,2},{5,3},{6,0},{7,1},{8,14},{9,15},{10,... | collective-permute-start | bytes 294920 | tf_op jit(solution)/shard_map/ppermute | solution.py:356
  45.4 1.2 %collective-permute-start.17 = (bf16[4,48,256]{2,1,0:T(8,128)(2,1)S(1)}, bf16[4,48,256]{2,1,0:T(8,128)(2,1)S(1)}, u32[]{:S(2)}, u32[]{:S(2)}) collective-permute-start(bf16[4,48,256]{2,1,0:T(8,128)(2,1)S(1)} %pad_maximum_fusion.5), channel_id=1, source_target_pairs={{0,4},{1,5},{2,6},{3,7},{4,0},{5,1},{6,2},{7,3},{8,12},{9,13},{10,... | collective-permute-start | bytes 294920 | tf_op jit(solution)/shard_map/ppermute | solution.py:356
  46.6 2.3 %collective-permute-start.20 = (bf16[2,64,512]{2,1,0:T(8,128)(2,1)S(1)}, bf16[2,64,512]{2,1,0:T(8,128)(2,1)S(1)}, u32[]{:S(2)}, u32[]{:S(2)}) collective-permute-start(bf16[2,64,512]{2,1,0:T(8,128)(2,1)S(1)} %copy-done.3), channel_id=1, source_target_pairs={{0,16},{8,24},{16,0},{24,8},{1,17},{9,25},{17,1},{25,9},{2,18},{10... | collective-permute-start | bytes 393224 | tf_op jit(solution)/shard_map/ppermute | solution.py:362
  48.9 6.9 %collective-permute-done.19 = bf16[4,48,256]{2,1,0:T(8,128)(2,1)S(1)} collective-permute-done((bf16[4,48,256]{2,1,0:T(8,128)(2,1)S(1)}, bf16[4,48,256]{2,1,0:T(8,128)(2,1)S(1)}, u32[]{:S(2)}, u32[]{:S(2)}) %collective-permute-start.19) | collective-permute-done | bytes 98336 | tf_op jit(solution)/shard_map/ppermute | solution.py:356
  56.6 1.6 %collective-permute-start.27 = (bf16[2,2,64,512]{3,2,1,0:T(8,128)(2,1)S(1)}, bf16[2,2,64,512]{3,2,1,0:T(8,128)(2,1)}, u32[]{:S(2)}, u32[]{:S(2)}) collective-permute-start(bf16[2,2,64,512]{3,2,1,0:T(8,128)(2,1)S(1)} %pad_maximum_fusion.4), channel_id=1, source_target_pairs={{0,8},{8,0},{16,24},{24,16},{1,9},{9,1},{17,25},{25,17},{2,10},{10... | collective-permute-start | bytes 786440 | tf_op jit(solution)/shard_map/ppermute | solution.py:362
  59.2 3.9 %collective-permute-done.27 = bf16[2,2,64,512]{3,2,1,0:T(8,128)(2,1)} collective-permute-done((bf16[2,2,64,512]{3,2,1,0:T(8,128)(2,1)S(1)}, bf16[2,2,64,512]{3,2,1,0:T(8,128)(2,1)}, u32[]{:S(2)}, u32[]{:S(2)}) %collective-permute-start.27) | collective-permute-done | bytes 262176 | tf_op jit(solution)/shard_map/ppermute | solution.py:362
  64.0 1.1 %pad_maximum_fusion.1.refs_0_ = bf16[4,2,64,512]{3,2,1,0:T(8,128)(2,1)S(1)} fusion(bf16[2,2,64,512]{3,2,1,0:T(8,128)(2,1)} %collective-permute-done.27, bf16[1,2,64,512]{3,2,1,0:T(8,128)(2,1)} %bitcast.56, bf16[1,2,64,512]{3,2,1,0:T(8,128)(2,1)} %bitcast.49), kind=kLoop, calls=%fused_computation.3 | loop fusion | flops 524288 | bytes 1048576 | tf_op jit(solution)/shard_map/concatenate | solution.py:369
  65.1 1.0 %collective-permute-start.28 = (bf16[4,2,64,512]{3,2,1,0:T(8,128)(2,1)S(1)}, bf16[4,2,64,512]{3,2,1,0:T(8,128)(2,1)S(1)}, u32[]{:S(2)}, u32[]{:S(2)}) collective-permute-start(bf16[4,2,64,512]{3,2,1,0:T(8,128)(2,1)S(1)} %pad_maximum_fusion.1.refs_0_), channel_id=1, source_target_pairs={{0,2},{1,3},{2,0},{3,1},{4,6},{5,7},{6,4},{7,5},{8,10},{9,11},{10,... | collective-permute-start | bytes 1572872 | tf_op jit(solution)/shard_map/ppermute | solution.py:343
  66.1 10.3 %left.1.left_ref = bf16[4,256,2048]{2,1,0:T(8,128)(2,1)S(1)} custom-call(s32[3]{0:T(128)S(1)} %pad_add_fusion.me_ref, s32[4]{0:T(128)S(1)} %copy-done.2, f32[4,4,4]{2,1,0:T(4,128)S(1)} %copy-done.1, s32[4,2]{1,0:T(4,128)S(1)} %copy.14.chain_ref, bf16[4,4,48,256]{3,2,1,0:T(8,128)(2,1)S(1)} %pad_maximum_fusion.2.refs_0_, ...), custom_call_target="tpu_custom_call" | custom-call | flops 8000000000 | bytes 10000000 | tf_op jit(solution)/shard_map/left/pallas_call | solution.py:488
  76.4 3.0 %collective-permute-done.28.refs_1_ = bf16[4,2,64,512]{3,2,1,0:T(8,128)(2,1)S(1)} collective-permute-done((bf16[4,2,64,512]{3,2,1,0:T(8,128)(2,1)S(1)}, bf16[4,2,64,512]{3,2,1,0:T(8,128)(2,1)S(1)}, u32[]{:S(2)}, u32[]{:S(2)}) %collective-permute-start.28) | collective-permute-done | bytes 524320 | tf_op jit(solution)/shard_map/ppermute | solution.py:343
  80.0 1.4 %collective-permute-done.29.refs_2_ = bf16[4,2,64,512]{3,2,1,0:T(8,128)(2,1)S(1)} collective-permute-done((bf16[4,2,64,512]{3,2,1,0:T(8,128)(2,1)S(1)}, bf16[4,2,64,512]{3,2,1,0:T(8,128)(2,1)S(1)}, u32[]{:S(2)}, u32[]{:S(2)}) %collective-permute-start.29) | collective-permute-done | bytes 524320 | tf_op jit(solution)/shard_map/ppermute | solution.py:343
  82.1 5.8 %right.1 = bf16[4,2,256,512]{3,2,1,0:T(8,128)(2,1)} custom-call(bf16[4,256,2048]{2,1,0:T(8,128)(2,1)S(1)} %left.1.left_ref, bf16[4,2,64,512]{3,2,1,0:T(8,128)(2,1)S(1)} %pad_maximum_fusion.1.refs_0_, bf16[4,2,64,512]{3,2,1,0:T(8,128)(2,1)S(1)} %collective-permute-done.28.refs_1_, bf16[4,2,64,512]{3,2,1,0:T(8,128)(2,1)S(1)} %collective-permute-done.29.refs_2_, ...), custom_call_target="tpu_custom_call" | custom-call | tf_op jit(solution)/shard_map/right/pallas_call | solution.py:507
  (66 shorter events, 12.4 us)
Async XLA Ops:
  2.5 11.6 %collective-permute-start.3 = (bf16[2,64,512]{2,1,0:T(8,128)(2,1)}, bf16[2,64,512]{2,1,0:T(8,128)(2,1)S(1)}, u32[]{:S(2)}, u32[]{:S(2)}) collective-permute-start(bf16[2,64,512]{2,1,0:T(8,128)(2,1)} %get-tuple-element.38), channel_id=1, source_target_pairs={{0,16},{8,24},{16,0},{24,8},{1,17},{9,25},{17,1},{25,9},{2,18},{10... | collective-permute-start | bytes 393224 | tf_op jit(solution)/shard_map/ppermute | solution.py:362
  7.5 5.2 %collective-permute-start = (bf16[96,256]{1,0:T(8,128)(2,1)S(1)}, bf16[96,256]{1,0:T(8,128)(2,1)S(1)}, u32[]{:S(2)}, u32[]{:S(2)}) collective-permute-start(bf16[96,256]{1,0:T(8,128)(2,1)S(1)} %get-tuple-element.30), channel_id=1, source_target_pairs={{0,24},{8,0},{16,8},{24,16},{1,25},{9,1},{17,9},{25,17},{2,26},{10... | collective-permute-start | bytes 147464 | tf_op jit(solution)/shard_map/ppermute | solution.py:20
  8.9 3.8 %collective-permute-start.1 = (bf16[48,256]{1,0:T(8,128)(2,1)S(1)}, bf16[48,256]{1,0:T(8,128)(2,1)S(1)}, u32[]{:S(2)}, u32[]{:S(2)}) collective-permute-start(bf16[48,256]{1,0:T(8,128)(2,1)S(1)} %get-tuple-element.31), channel_id=1, source_target_pairs={{0,4},{4,0},{1,5},{5,1},{2,6},{6,2},{3,7},{7,3},{8,12},{12,8},{9,1... | collective-permute-start | bytes 73736 | tf_op jit(solution)/shard_map/ppermute | solution.py:20
  10.4 2.3 %collective-permute-start.2 = (bf16[48,256]{1,0:T(8,128)(2,1)S(1)}, bf16[48,256]{1,0:T(8,128)(2,1)S(1)}, u32[]{:S(2)}, u32[]{:S(2)}) collective-permute-start(bf16[48,256]{1,0:T(8,128)(2,1)S(1)} %get-tuple-element.32), channel_id=1, source_target_pairs={{0,3},{1,0},{2,1},{3,2},{4,7},{5,4},{6,5},{7,6},{8,11},{9,8},{10,9... | collective-permute-start | bytes 73736 | tf_op jit(solution)/shard_map/ppermute | solution.py:20
  14.1 52.0 %copy-start.1 = (f32[4,4,4]{2,1,0:T(4,128)S(1)}, f32[4,4,4]{2,1,0:T(4,128)}, u32[]{:S(2)}) copy-start(f32[4,4,4]{2,1,0:T(4,128)} %spin_ref.1) | copy-start | bytes 772
  14.2 2.4 %collective-permute-start.4 = (bf16[2,4,2,48,256]{4,3,1,2,0:T(8,128)(2,1)S(1)}, bf16[2,4,2,48,256]{4,3,1,2,0:T(8,128)(2,1)S(1)}, u32[]{:S(2)}, u32[]{:S(2)}) collective-permute-start(bf16[2,4,2,48,256]{4,3,1,2,0:T(8,128)(2,1)S(1)} %bitcast.57), channel_id=1, source_target_pairs={{0,1},{1,0},{2,3},{3,2},{4,5},{5,4},{6,7},{7,6},{8,9},{9,8},{10,11... | collective-permute-start | bytes 1179656 | tf_op jit(solution)/shard_map/ppermute | solution.py:343
  15.2 8.4 %collective-permute-start.8 = (bf16[2,2,64,512]{3,2,1,0:T(8,128)(2,1)S(1)}, bf16[2,2,64,512]{3,2,1,0:T(8,128)(2,1)S(1)}, u32[]{:S(2)}, u32[]{:S(2)}) collective-permute-start(bf16[2,2,64,512]{3,2,1,0:T(8,128)(2,1)S(1)} %pad_maximum_fusion.3), channel_id=1, source_target_pairs={{0,8},{8,0},{16,24},{24,16},{1,9},{9,1},{17,25},{25,17},{2,10},{10... | collective-permute-start | bytes 786440 | tf_op jit(solution)/shard_map/ppermute | solution.py:362
  16.7 6.9 %collective-permute-start.7 = (bf16[4,48,256]{2,1,0:T(8,128)(2,1)S(1)}, bf16[4,48,256]{2,1,0:T(8,128)(2,1)S(1)}, u32[]{:S(2)}, u32[]{:S(2)}) collective-permute-start(bf16[4,48,256]{2,1,0:T(8,128)(2,1)S(1)} %get-tuple-element.56), channel_id=1, source_target_pairs={{0,6},{1,7},{2,4},{3,5},{4,2},{5,3},{6,0},{7,1},{8,14},{9,15},{10,... | collective-permute-start | bytes 294920 | tf_op jit(solution)/shard_map/ppermute | solution.py:356
  19.1 5.8 %collective-permute-start.6 = (bf16[4,48,256]{2,1,0:T(8,128)(2,1)S(1)}, bf16[4,48,256]{2,1,0:T(8,128)(2,1)S(1)}, u32[]{:S(2)}, u32[]{:S(2)}) collective-permute-start(bf16[4,48,256]{2,1,0:T(8,128)(2,1)S(1)} %get-tuple-element.57), channel_id=1, source_target_pairs={{0,2},{1,3},{2,0},{3,1},{4,6},{5,7},{6,4},{7,5},{8,10},{9,11},{10,... | collective-permute-start | bytes 294920 | tf_op jit(solution)/shard_map/ppermute | solution.py:356
  19.6 5.3 %collective-permute-start.5 = (bf16[4,48,256]{2,1,0:T(8,128)(2,1)S(1)}, bf16[4,48,256]{2,1,0:T(8,128)(2,1)S(1)}, u32[]{:S(2)}, u32[]{:S(2)}) collective-permute-start(bf16[4,48,256]{2,1,0:T(8,128)(2,1)S(1)} %get-tuple-element.55), channel_id=1, source_target_pairs={{0,4},{1,5},{2,6},{3,7},{4,0},{5,1},{6,2},{7,3},{8,12},{9,13},{10,... | collective-permute-start | bytes 294920 | tf_op jit(solution)/shard_map/ppermute | solution.py:356
  24.9 16.9 %collective-permute-start.15 = (bf16[4,2,64,512]{3,2,1,0:T(8,128)(2,1)S(1)}, bf16[4,2,64,512]{3,2,1,0:T(8,128)(2,1)S(1)}, u32[]{:S(2)}, u32[]{:S(2)}) collective-permute-start(bf16[4,2,64,512]{3,2,1,0:T(8,128)(2,1)S(1)} %pad_maximum_fusion.refs_2_), channel_id=1, source_target_pairs={{0,4},{1,5},{2,6},{3,7},{4,0},{5,1},{6,2},{7,3},{8,12},{9,13},{10,... | collective-permute-start | bytes 1572872 | tf_op jit(solution)/shard_map/ppermute | solution.py:356
  26.2 15.6 %collective-permute-start.16 = (bf16[4,2,64,512]{3,2,1,0:T(8,128)(2,1)S(1)}, bf16[4,2,64,512]{3,2,1,0:T(8,128)(2,1)S(1)}, u32[]{:S(2)}, u32[]{:S(2)}) collective-permute-start(bf16[4,2,64,512]{3,2,1,0:T(8,128)(2,1)S(1)} %pad_maximum_fusion.refs_2_), channel_id=1, source_target_pairs={{0,2},{1,3},{2,0},{3,1},{4,6},{5,7},{6,4},{7,5},{8,10},{9,11},{10,... | collective-permute-start | bytes 1572872 | tf_op jit(solution)/shard_map/ppermute | solution.py:356
  27.3 5.6 %collective-permute-start.11 = (bf16[48,256]{1,0:T(8,128)(2,1)S(1)}, bf16[48,256]{1,0:T(8,128)(2,1)S(1)}, u32[]{:S(2)}, u32[]{:S(2)}) collective-permute-start(bf16[48,256]{1,0:T(8,128)(2,1)S(1)} %get-tuple-element.59), channel_id=1, source_target_pairs={{0,24},{8,16},{16,8},{24,0},{1,25},{9,17},{17,9},{25,1},{2,26},{10... | collective-permute-start | bytes 73736 | tf_op jit(solution)/shard_map/ppermute | solution.py:362
  30.1 3.8 %collective-permute-start.10 = (bf16[48,256]{1,0:T(8,128)(2,1)S(1)}, bf16[48,256]{1,0:T(8,128)(2,1)S(1)}, u32[]{:S(2)}, u32[]{:S(2)}) collective-permute-start(bf16[48,256]{1,0:T(8,128)(2,1)S(1)} %get-tuple-element.60), channel_id=1, source_target_pairs={{0,8},{8,0},{16,24},{24,16},{1,9},{9,1},{17,25},{25,17},{2,10},{10... | collective-permute-start | bytes 73736 | tf_op jit(solution)/shard_map/ppermute | solution.py:362
  30.1 4.7 %collective-permute-start.9 = (bf16[48,256]{1,0:T(8,128)(2,1)S(1)}, bf16[48,256]{1,0:T(8,128)(2,1)S(1)}, u32[]{:S(2)}, u32[]{:S(2)}) collective-permute-start(bf16[48,256]{1,0:T(8,128)(2,1)S(1)} %get-tuple-element.58), channel_id=1, source_target_pairs={{0,16},{8,24},{16,0},{24,8},{1,17},{9,25},{17,1},{25,9},{2,18},{10... | collective-permute-start | bytes 73736 | tf_op jit(solution)/shard_map/ppermute | solution.py:362
  34.8 5.7 %collective-permute-start.14 = (bf16[48,256]{1,0:T(8,128)(2,1)S(1)}, bf16[48,256]{1,0:T(8,128)(2,1)S(1)}, u32[]{:S(2)}, u32[]{:S(2)}) collective-permute-start(bf16[48,256]{1,0:T(8,128)(2,1)S(1)} %fusion.6), channel_id=1, source_target_pairs={{0,24},{8,16},{16,8},{24,0},{1,25},{9,17},{17,9},{25,1},{2,26},{10... | collective-permute-start | bytes 73736 | tf_op jit(solution)/shard_map/ppermute | solution.py:362
  36.4 4.2 %collective-permute-start.13 = (bf16[48,256]{1,0:T(8,128)(2,1)S(1)}, bf16[48,256]{1,0:T(8,128)(2,1)S(1)}, u32[]{:S(2)}, u32[]{:S(2)}) collective-permute-start(bf16[48,256]{1,0:T(8,128)(2,1)S(1)} %fusion.6), channel_id=1, source_target_pairs={{0,8},{8,0},{16,24},{24,16},{1,9},{9,1},{17,25},{25,17},{2,10},{10... | collective-permute-start | bytes 73736 | tf_op jit(solution)/shard_map/ppermute | solution.py:362
  37.1 4.7 %collective-permute-start.12 = (bf16[48,256]{1,0:T(8,128)(2,1)S(1)}, bf16[48,256]{1,0:T(8,128)(2,1)S(1)}, u32[]{:S(2)}, u32[]{:S(2)}) collective-permute-start(bf16[48,256]{1,0:T(8,128)(2,1)S(1)} %fusion.6), channel_id=1, source_target_pairs={{0,16},{8,24},{16,0},{24,8},{1,17},{9,25},{17,1},{25,9},{2,18},{10... | collective-permute-start | bytes 73736 | tf_op jit(solution)/shard_map/ppermute | solution.py:362
  41.8 16.8 %collective-permute-start.22 = (bf16[4,2,64,512]{3,2,1,0:T(8,128)(2,1)S(1)}, bf16[4,2,64,512]{3,2,1,0:T(8,128)(2,1)S(1)}, u32[]{:S(2)}, u32[]{:S(2)}) collective-permute-start(bf16[4,2,64,512]{3,2,1,0:T(8,128)(2,1)S(1)} %collective-permute-done.16.refs_4_), channel_id=1, source_target_pairs={{0,4},{1,5},{2,6},{3,7},{4,0},{5,1},{6,2},{7,3},{8,12},{9,13},{10,... | collective-permute-start | bytes 1572872 | tf_op jit(solution)/shard_map/ppermute | solution.py:356
  43.1 12.7 %collective-permute-start.19 = (bf16[4,48,256]{2,1,0:T(8,128)(2,1)S(1)}, bf16[4,48,256]{2,1,0:T(8,128)(2,1)S(1)}, u32[]{:S(2)}, u32[]{:S(2)}) collective-permute-start(bf16[4,48,256]{2,1,0:T(8,128)(2,1)S(1)} %pad_maximum_fusion.5), channel_id=1, source_target_pairs={{0,6},{1,7},{2,4},{3,5},{4,2},{5,3},{6,0},{7,1},{8,14},{9,15},{10,... | collective-permute-start | bytes 294920 | tf_op jit(solution)/shard_map/ppermute | solution.py:356
  44.6 11.2 %collective-permute-start.18 = (bf16[4,48,256]{2,1,0:T(8,128)(2,1)S(1)}, bf16[4,48,256]{2,1,0:T(8,128)(2,1)S(1)}, u32[]{:S(2)}, u32[]{:S(2)}) collective-permute-start(bf16[4,48,256]{2,1,0:T(8,128)(2,1)S(1)} %pad_maximum_fusion.5), channel_id=1, source_target_pairs={{0,2},{1,3},{2,0},{3,1},{4,6},{5,7},{6,4},{7,5},{8,10},{9,11},{10,... | collective-permute-start | bytes 294920 | tf_op jit(solution)/shard_map/ppermute | solution.py:356
  45.4 11.1 %collective-permute-start.17 = (bf16[4,48,256]{2,1,0:T(8,128)(2,1)S(1)}, bf16[4,48,256]{2,1,0:T(8,128)(2,1)S(1)}, u32[]{:S(2)}, u32[]{:S(2)}) collective-permute-start(bf16[4,48,256]{2,1,0:T(8,128)(2,1)S(1)} %pad_maximum_fusion.5), channel_id=1, source_target_pairs={{0,4},{1,5},{2,6},{3,7},{4,0},{5,1},{6,2},{7,3},{8,12},{9,13},{10,... | collective-permute-start | bytes 294920 | tf_op jit(solution)/shard_map/ppermute | solution.py:356
  46.6 9.9 %collective-permute-start.20 = (bf16[2,64,512]{2,1,0:T(8,128)(2,1)S(1)}, bf16[2,64,512]{2,1,0:T(8,128)(2,1)S(1)}, u32[]{:S(2)}, u32[]{:S(2)}) collective-permute-start(bf16[2,64,512]{2,1,0:T(8,128)(2,1)S(1)} %copy-done.3), channel_id=1, source_target_pairs={{0,16},{8,24},{16,0},{24,8},{1,17},{9,25},{17,1},{25,9},{2,18},{10... | collective-permute-start | bytes 393224 | tf_op jit(solution)/shard_map/ppermute | solution.py:362
  56.6 6.5 %collective-permute-start.27 = (bf16[2,2,64,512]{3,2,1,0:T(8,128)(2,1)S(1)}, bf16[2,2,64,512]{3,2,1,0:T(8,128)(2,1)}, u32[]{:S(2)}, u32[]{:S(2)}) collective-permute-start(bf16[2,2,64,512]{3,2,1,0:T(8,128)(2,1)S(1)} %pad_maximum_fusion.4), channel_id=1, source_target_pairs={{0,8},{8,0},{16,24},{24,16},{1,9},{9,1},{17,25},{25,17},{2,10},{10... | collective-permute-start | bytes 786440 | tf_op jit(solution)/shard_map/ppermute | solution.py:362
  58.2 6.9 %collective-permute-start.23 = (bf16[4,2,64,512]{3,2,1,0:T(8,128)(2,1)S(1)}, bf16[4,2,64,512]{3,2,1,0:T(8,128)(2,1)S(1)}, u32[]{:S(2)}, u32[]{:S(2)}) collective-permute-start(bf16[4,2,64,512]{3,2,1,0:T(8,128)(2,1)S(1)} %pad_maximum_fusion.refs_2_), channel_id=1, source_target_pairs={{0,1},{1,0},{2,3},{3,2},{4,5},{5,4},{6,7},{7,6},{8,9},{9,8},{10,11... | collective-permute-start | bytes 1572872 | tf_op jit(solution)/shard_map/ppermute | solution.py:343
  58.2 7.9 %collective-permute-start.25 = (bf16[4,2,64,512]{3,2,1,0:T(8,128)(2,1)S(1)}, bf16[4,2,64,512]{3,2,1,0:T(8,128)(2,1)S(1)}, u32[]{:S(2)}, u32[]{:S(2)}) collective-permute-start(bf16[4,2,64,512]{3,2,1,0:T(8,128)(2,1)S(1)} %collective-permute-done.16.refs_4_), channel_id=1, source_target_pairs={{0,1},{1,0},{2,3},{3,2},{4,5},{5,4},{6,7},{7,6},{8,9},{9,8},{10,11... | collective-permute-start | bytes 1572872 | tf_op jit(solution)/shard_map/ppermute | solution.py:343
  58.7 7.4 %collective-permute-start.24 = (bf16[4,2,64,512]{3,2,1,0:T(8,128)(2,1)S(1)}, bf16[4,2,64,512]{3,2,1,0:T(8,128)(2,1)}, u32[]{:S(2)}, u32[]{:S(2)}) collective-permute-start(bf16[4,2,64,512]{3,2,1,0:T(8,128)(2,1)S(1)} %collective-permute-done.15.refs_3_), channel_id=1, source_target_pairs={{0,1},{1,0},{2,3},{3,2},{4,5},{5,4},{6,7},{7,6},{8,9},{9,8},{10,11... | collective-permute-start | bytes 1572872 | tf_op jit(solution)/shard_map/ppermute | solution.py:343
  58.7 7.4 %collective-permute-start.26 = (bf16[4,2,64,512]{3,2,1,0:T(8,128)(2,1)S(1)}, bf16[4,2,64,512]{3,2,1,0:T(8,128)(2,1)}, u32[]{:S(2)}, u32[]{:S(2)}) collective-permute-start(bf16[4,2,64,512]{3,2,1,0:T(8,128)(2,1)S(1)} %collective-permute-done.22.refs_5_), channel_id=1, source_target_pairs={{0,1},{1,0},{2,3},{3,2},{4,5},{5,4},{6,7},{7,6},{8,9},{9,8},{10,11... | collective-permute-start | bytes 1572872 | tf_op jit(solution)/shard_map/ppermute | solution.py:343
  63.1 3.0 %collective-permute-start.21 = (bf16[4,4,48,256]{3,2,1,0:T(8,128)(2,1)S(1)}, bf16[4,4,48,256]{3,2,1,0:T(8,128)(2,1)}, u32[]{:S(2)}, u32[]{:S(2)}) collective-permute-start(bf16[4,4,48,256]{3,2,1,0:T(8,128)(2,1)S(1)} %pad_maximum_fusion.2.refs_0_), channel_id=1, source_target_pairs={{0,1},{1,0},{2,3},{3,2},{4,5},{5,4},{6,7},{7,6},{8,9},{9,8},{10,11... | collective-permute-start | bytes 1179656 | tf_op jit(solution)/shard_map/ppermute | solution.py:343
  65.1 14.4 %collective-permute-start.28 = (bf16[4,2,64,512]{3,2,1,0:T(8,128)(2,1)S(1)}, bf16[4,2,64,512]{3,2,1,0:T(8,128)(2,1)S(1)}, u32[]{:S(2)}, u32[]{:S(2)}) collective-permute-start(bf16[4,2,64,512]{3,2,1,0:T(8,128)(2,1)S(1)} %pad_maximum_fusion.1.refs_0_), channel_id=1, source_target_pairs={{0,2},{1,3},{2,0},{3,1},{4,6},{5,7},{6,4},{7,5},{8,10},{9,11},{10,... | collective-permute-start | bytes 1572872 | tf_op jit(solution)/shard_map/ppermute | solution.py:343
  79.5 1.9 %collective-permute-start.29 = (bf16[4,2,64,512]{3,2,1,0:T(8,128)(2,1)S(1)}, bf16[4,2,64,512]{3,2,1,0:T(8,128)(2,1)S(1)}, u32[]{:S(2)}, u32[]{:S(2)}) collective-permute-start(bf16[4,2,64,512]{3,2,1,0:T(8,128)(2,1)S(1)} %pad_maximum_fusion.1.refs_0_), channel_id=1, source_target_pairs={{0,1},{1,0},{2,3},{3,2},{4,5},{5,4},{6,7},{7,6},{8,9},{9,8},{10,11... | collective-permute-start | bytes 1572872 | tf_op jit(solution)/shard_map/ppermute | solution.py:343
  79.5 2.7 %collective-permute-start.30 = (bf16[4,2,64,512]{3,2,1,0:T(8,128)(2,1)S(1)}, bf16[4,2,64,512]{3,2,1,0:T(8,128)(2,1)S(1)}, u32[]{:S(2)}, u32[]{:S(2)}) collective-permute-start(bf16[4,2,64,512]{3,2,1,0:T(8,128)(2,1)S(1)} %collective-permute-done.28.refs_1_), channel_id=1, source_target_pairs={{0,1},{1,0},{2,3},{3,2},{4,5},{5,4},{6,7},{7,6},{8,9},{9,8},{10,11... | collective-permute-start | bytes 1572872 | tf_op jit(solution)/shard_map/ppermute | solution.py:343
  (5 other events, 101.1 us)

commit v11 on v10

--- a/solution.py
+++ b/solution.py
@@ -289,8 +289,8 @@
     blocks = [pl.multiple_of(back(gy, dx, gy_n) * lane, lane) for dx in range(gy_n)]
 
     def one_operator(op):
-        a = chain_ref[op, 0]
-        b = chain_ref[op, 1]
+        a = chain_ref[2 * op]
+        b = chain_ref[2 * op + 1]
         dir_a = dirs_ref[a]
         dir_b = dirs_ref[b]
         mix = None
@@ -468,14 +468,20 @@
     summed = added(*[xor_passed(part_at(summed, to), "gx", offset) for to, offset in zip(others, line)])
     elem_line = jnp.stack([xor_passed(summed, "gx", offset) for offset in line])
     keys = [key for key in fwd_parts if key != (0, 0, 0)]
-    elem_line, bwd_piece, *parts = lax.optimization_barrier((elem_line, bwd_piece, *[fwd_parts[key] for key in keys]))
+    pairs = chain_order.reshape(-1)
+    elem_line, bwd_piece, pairs, *parts = lax.optimization_barrier(
+        (elem_line, bwd_piece, pairs, *[fwd_parts[key] for key in keys])
+    )
     fwd_parts.update(zip(keys, parts))
     elem_keys = plane if split > 1 else [(0, dy) for dy in range(chips)]
     elem_own = jnp.stack([passed_in_plane(elem_line, dx, dy) for dx, dy in elem_keys])
+    bwd_half = xor_passed(bwd_piece, "gx", gx_n // 2)
     if four:
-        fwd_parts[1, 1, 0] = passed_in_plane(fwd_parts[0, 1, 0], 1, 0)
-    bwd_half = xor_passed(bwd_piece, "gx", gx_n // 2)
-    elem_own, bwd_half = lax.optimization_barrier((elem_own, bwd_half))
+        tied = (elem_own, bwd_half, fwd_parts[1, 0, 0], fwd_parts[0, 1, 0])
+        elem_own, bwd_half, over_x, over_y = lax.optimization_barrier(tied)
+        fwd_parts[1, 0, 0], fwd_parts[0, 1, 0] = over_x, over_y
+        corner = [passed_in_plane(over_y[:, :1], 1, 0), passed_in_plane(over_x[:, 1:], 0, 1)]
+        fwd_parts[1, 1, 0] = jnp.concatenate(corner, axis=1)
     elem_parts = [elem_own, passed_in_gz(elem_own, 0, 1)]
     for dx, dy in plane:
         fwd_parts[dx, dy, 1] = passed_in_gz(fwd_parts[dx, dy, 0], 0, 1)
@@ -499,9 +505,10 @@
         compiler_params=pltpu.CompilerParams(vmem_limit_bytes=24 * 2**20),
         cost_estimate=pl.CostEstimate(flops=8 * 10**9, bytes_accessed=10**7, transcendentals=0),
         name="left",
-    )(me, directions, spin_mats, chain_order, *elem_parts, *fwd_parts.values())
-    left, *parts = lax.optimization_barrier((left, *bwd_parts.values()))
-    bwd_parts = dict(zip(list(bwd_parts), parts))
+    )(me, directions, spin_mats, pairs, *elem_parts, *fwd_parts.values())
+    late = [key for key in bwd_parts if key[0]]
+    left, *parts = lax.optimization_barrier((left, *[bwd_parts[key] for key in late]))
+    bwd_parts.update(zip(late, parts))
     for dy in range(chips):
         bwd_parts[dy, 1] = passed_in_gz(bwd_parts[dy, 0], 0, 1)
     return pl.pallas_call(

time: 88.2 us -> 87.9 us (level)
  waiting for transfers between devices: 27.4 us -> 31 us
  starting transfers between devices: 35.2 us -> 33.8 us
  other arithmetic: 1.54 us -> 0.48 us
    ppermute x10, waiting for transfers between devices: 12.9 us -> 17.3 us  [xor_passed(): lax.ppermute(value, axis, [(n, n ^ offset) for n in range(lax.axis_size(a...]
    ppermute x10, starting transfers between devices: 17.9 us -> 16.3 us  [xor_passed(): lax.ppermute(value, axis, [(n, n ^ offset) for n in range(lax.axis_size(a...]
    concatenate x2, other arithmetic: 1.15 us -> 0.11 us  [line_exchange(): gathered = jnp.concatenate([gathered, xor_passed(gathered, axis, distance)])]
    ppermute x9 -> x10, waiting for transfers between devices: 8.8 us -> 7.92 us  [passed_in_plane(): return lax.ppermute(value, ('gy', 'gz'), pairs)]
    ppermute x9 -> x10, starting transfers between devices: 10.7 us -> 11.4 us  [passed_in_plane(): return lax.ppermute(value, ('gy', 'gz'), pairs)]
  transfers between devices with their start and end apart: 31 -> 32, of which waited for: 15 -> 18; matrix products, arithmetic and copies ran while one was open for 4% -> 2% of each run, Pallas kernels for 14% -> 13%
where the time goes in v11:
time: 87.9 us; the launch traced here: 87.7 us
  starting transfers between devices  33.8 us (38%)
  waiting for transfers between devices  31 us (35%)
  Pallas kernels  19.8 us (23%)
  local copies, waits for them, and re-layouts  2.53 us (3%)
    ppermute x10, waiting for transfers between devices, xor_passed(): lax.ppermute(value, axis, [(n, n ^ offset) for n in range(lax.axis_size(a...  17.3 us
    ppermute x10, starting transfers between devices, xor_passed(): lax.ppermute(value, axis, [(n, n ^ offset) for n in range(lax.axis_size(a...  16.3 us
    ppermute x10, starting transfers between devices, passed_in_plane(): return lax.ppermute(value, ('gy', 'gz'), pairs)  11.4 us
    pallas_call x1, Pallas kernels, on_device(): pl.pallas_call(functools.partial(left_kernel, 1.0 / math.sqrt(4 * num_vec...  9.58 us
    ppermute x10, waiting for transfers between devices, passed_in_plane(): return lax.ppermute(value, ('gy', 'gz'), pairs)  7.92 us
    pallas_call x1, Pallas kernels, on_device(): pl.pallas_call(functools.partial(right_kernel, gz_n, tuple(bwd_parts)), o...  5.8 us
    ppermute x9, waiting for transfers between devices, passed_in_gz(): return lax.ppermute(value, 'gz', pairs)  5.43 us
    ppermute x9, starting transfers between devices, passed_in_gz(): return lax.ppermute(value, 'gz', pairs)  3.07 us
  transfers between devices with their start and end apart: 32, of which 18 were waited for; matrix products, arithmetic and copies ran while one was open for 2% of the time, Pallas kernels for 13%

profile of v11, /device:TPU:0, one launch (start us, length us, event | category | flops | bytes accessed | tf_op | source)
XLA Modules:
  0.0 87.7 jit_solution(17267756089170229084)
XLA Ops:
  0.0 2.4 %pieces.1 = (bf16[2,64,512]{2,1,0:T(8,128)(2,1)}, bf16[2,64,512]{2,1,0:T(8,128)(2,1)}) custom-call(s32[1]{0:T(128)} %bitcast.2.z_ref, bf16[2,256,512]{2,1,0:T(8,128)(2,1)} %fwd_in.1, bf16[2,256,512]{2,1,0:T(8,128)(2,1)} %bwd_in.1), custom_call_target="tpu_custom_call" | custom-call | flops 100000000 | bytes 10000000 | tf_op jit(solution)/shard_map/pieces/pallas_call | solution.py:407
  2.5 4.1 %collective-permute-start.3 = (bf16[2,64,512]{2,1,0:T(8,128)(2,1)}, bf16[2,64,512]{2,1,0:T(8,128)(2,1)S(1)}, u32[]{:S(2)}, u32[]{:S(2)}) collective-permute-start(bf16[2,64,512]{2,1,0:T(8,128)(2,1)} %get-tuple-element.40), channel_id=1, source_target_pairs={{0,16},{8,24},{16,0},{24,8},{1,17},{9,25},{17,1},{25,9},{2,18},{10... | collective-permute-start | bytes 393224 | tf_op jit(solution)/shard_map/ppermute | solution.py:362
  7.5 1.4 %collective-permute-start = (bf16[96,256]{1,0:T(8,128)(2,1)S(1)}, bf16[96,256]{1,0:T(8,128)(2,1)S(1)}, u32[]{:S(2)}, u32[]{:S(2)}) collective-permute-start(bf16[96,256]{1,0:T(8,128)(2,1)S(1)} %get-tuple-element.32), channel_id=1, source_target_pairs={{0,24},{8,0},{16,8},{24,16},{1,25},{9,1},{17,9},{25,17},{2,26},{10... | collective-permute-start | bytes 147464 | tf_op jit(solution)/shard_map/ppermute | solution.py:20
  8.9 1.5 %collective-permute-start.1 = (bf16[48,256]{1,0:T(8,128)(2,1)S(1)}, bf16[48,256]{1,0:T(8,128)(2,1)S(1)}, u32[]{:S(2)}, u32[]{:S(2)}) collective-permute-start(bf16[48,256]{1,0:T(8,128)(2,1)S(1)} %get-tuple-element.33), channel_id=1, source_target_pairs={{0,4},{4,0},{1,5},{5,1},{2,6},{6,2},{3,7},{7,3},{8,12},{12,8},{9,1... | collective-permute-start | bytes 73736 | tf_op jit(solution)/shard_map/ppermute | solution.py:20
  12.8 1.3 %correlate.1 = bf16[4,4,2,48,256]{4,3,2,1,0:T(8,128)(2,1)S(1)} custom-call(bf16[192,256]{1,0:T(8,128)(2,1)S(1)} %get-tuple-element.31.vec_ref, bf16[96,256]{1,0:T(8,128)(2,1)S(1)} %collective-permute-done.face0, bf16[48,256]{1,0:T(8,128)(2,1)S(1)} %collective-permute-done.1.face1, bf16[48,256]{1,0:T(8,128)(2,1)S(1)} %collective-permute-done.2.face2, ...), custom_call_target="tpu_custom_call" | custom-call | tf_op jit(solution)/shard_map/correlate/pallas_call | solution.py:440
  14.1 1.0 %collective-permute-start.4 = (bf16[2,4,2,48,256]{4,3,1,2,0:T(8,128)(2,1)S(1)}, bf16[2,4,2,48,256]{4,3,1,2,0:T(8,128)(2,1)S(1)}, u32[]{:S(2)}, u32[]{:S(2)}) collective-permute-start(bf16[2,4,2,48,256]{4,3,1,2,0:T(8,128)(2,1)S(1)} %bitcast.57), channel_id=1, source_target_pairs={{0,1},{1,0},{2,3},{3,2},{4,5},{5,4},{6,7},{7,6},{8,9},{9,8},{10,11... | collective-permute-start | bytes 1179656 | tf_op jit(solution)/shard_map/ppermute | solution.py:343
  15.2 1.1 %collective-permute-start.8 = (bf16[2,2,64,512]{3,2,1,0:T(8,128)(2,1)S(1)}, bf16[2,2,64,512]{3,2,1,0:T(8,128)(2,1)S(1)}, u32[]{:S(2)}, u32[]{:S(2)}) collective-permute-start(bf16[2,2,64,512]{3,2,1,0:T(8,128)(2,1)S(1)} %pad_maximum_fusion.3), channel_id=1, source_target_pairs={{0,8},{8,0},{16,24},{24,16},{1,9},{9,1},{17,25},{25,17},{2,10},{10... | collective-permute-start | bytes 786440 | tf_op jit(solution)/shard_map/ppermute | solution.py:362
  16.7 2.4 %collective-permute-start.7 = (bf16[4,48,256]{2,1,0:T(8,128)(2,1)S(1)}, bf16[4,48,256]{2,1,0:T(8,128)(2,1)S(1)}, u32[]{:S(2)}, u32[]{:S(2)}) collective-permute-start(bf16[4,48,256]{2,1,0:T(8,128)(2,1)S(1)} %get-tuple-element.60), channel_id=1, source_target_pairs={{0,6},{1,7},{2,4},{3,5},{4,2},{5,3},{6,0},{7,1},{8,14},{9,15},{10,... | collective-permute-start | bytes 294920 | tf_op jit(solution)/shard_map/ppermute | solution.py:356
  20.2 3.4 %collective-permute-done.8 = bf16[2,2,64,512]{3,2,1,0:T(8,128)(2,1)S(1)} collective-permute-done((bf16[2,2,64,512]{3,2,1,0:T(8,128)(2,1)S(1)}, bf16[2,2,64,512]{3,2,1,0:T(8,128)(2,1)S(1)}, u32[]{:S(2)}, u32[]{:S(2)}) %collective-permute-start.8) | collective-permute-done | bytes 262176 | tf_op jit(solution)/shard_map/ppermute | solution.py:362
  23.7 1.2 %collective-permute-done.6 = bf16[4,48,256]{2,1,0:T(8,128)(2,1)S(1)} collective-permute-done((bf16[4,48,256]{2,1,0:T(8,128)(2,1)S(1)}, bf16[4,48,256]{2,1,0:T(8,128)(2,1)S(1)}, u32[]{:S(2)}, u32[]{:S(2)}) %collective-permute-start.6) | collective-permute-done | bytes 98336 | tf_op jit(solution)/shard_map/ppermute | solution.py:356
  24.9 1.3 %collective-permute-start.15 = (bf16[4,2,64,512]{3,2,1,0:T(8,128)(2,1)S(1)}, bf16[4,2,64,512]{3,2,1,0:T(8,128)(2,1)S(1)}, u32[]{:S(2)}, u32[]{:S(2)}) collective-permute-start(bf16[4,2,64,512]{3,2,1,0:T(8,128)(2,1)S(1)} %pad_maximum_fusion.refs_2_), channel_id=1, source_target_pairs={{0,4},{1,5},{2,6},{3,7},{4,0},{5,1},{6,2},{7,3},{8,12},{9,13},{10,... | collective-permute-start | bytes 1572872 | tf_op jit(solution)/shard_map/ppermute | solution.py:356
  26.2 1.1 %collective-permute-start.16 = (bf16[4,2,64,512]{3,2,1,0:T(8,128)(2,1)S(1)}, bf16[4,2,64,512]{3,2,1,0:T(8,128)(2,1)S(1)}, u32[]{:S(2)}, u32[]{:S(2)}) collective-permute-start(bf16[4,2,64,512]{3,2,1,0:T(8,128)(2,1)S(1)} %pad_maximum_fusion.refs_2_), channel_id=1, source_target_pairs={{0,2},{1,3},{2,0},{3,1},{4,6},{5,7},{6,4},{7,5},{8,10},{9,11},{10,... | collective-permute-start | bytes 1572872 | tf_op jit(solution)/shard_map/ppermute | solution.py:356
  27.3 2.8 %collective-permute-start.11 = (bf16[48,256]{1,0:T(8,128)(2,1)S(1)}, bf16[48,256]{1,0:T(8,128)(2,1)S(1)}, u32[]{:S(2)}, u32[]{:S(2)}) collective-permute-start(bf16[48,256]{1,0:T(8,128)(2,1)S(1)} %get-tuple-element.63), channel_id=1, source_target_pairs={{0,24},{8,16},{16,8},{24,0},{1,25},{9,17},{17,9},{25,1},{2,26},{10... | collective-permute-start | bytes 73736 | tf_op jit(solution)/shard_map/ppermute | solution.py:362
  30.1 1.6 %collective-permute-start.9 = (bf16[48,256]{1,0:T(8,128)(2,1)S(1)}, bf16[48,256]{1,0:T(8,128)(2,1)S(1)}, u32[]{:S(2)}, u32[]{:S(2)}) collective-permute-start(bf16[48,256]{1,0:T(8,128)(2,1)S(1)} %get-tuple-element.62), channel_id=1, source_target_pairs={{0,16},{8,24},{16,0},{24,8},{1,17},{9,25},{17,1},{25,9},{2,18},{10... | collective-permute-start | bytes 73736 | tf_op jit(solution)/shard_map/ppermute | solution.py:362
  31.7 1.2 %collective-permute-done.11 = bf16[48,256]{1,0:T(8,128)(2,1)S(1)} collective-permute-done((bf16[48,256]{1,0:T(8,128)(2,1)S(1)}, bf16[48,256]{1,0:T(8,128)(2,1)S(1)}, u32[]{:S(2)}, u32[]{:S(2)}) %collective-permute-start.11) | collective-permute-done | bytes 24608 | tf_op jit(solution)/shard_map/ppermute | solution.py:362
  34.8 1.5 %collective-permute-start.14 = (bf16[48,256]{1,0:T(8,128)(2,1)S(1)}, bf16[48,256]{1,0:T(8,128)(2,1)S(1)}, u32[]{:S(2)}, u32[]{:S(2)}) collective-permute-start(bf16[48,256]{1,0:T(8,128)(2,1)S(1)} %fusion.6), channel_id=1, source_target_pairs={{0,24},{8,16},{16,8},{24,0},{1,25},{9,17},{17,9},{25,1},{2,26},{10... | collective-permute-start | bytes 73736 | tf_op jit(solution)/shard_map/ppermute | solution.py:362
  37.0 2.2 %collective-permute-start.12 = (bf16[48,256]{1,0:T(8,128)(2,1)S(1)}, bf16[48,256]{1,0:T(8,128)(2,1)S(1)}, u32[]{:S(2)}, u32[]{:S(2)}) collective-permute-start(bf16[48,256]{1,0:T(8,128)(2,1)S(1)} %fusion.6), channel_id=1, source_target_pairs={{0,16},{8,24},{16,0},{24,8},{1,17},{9,25},{17,1},{25,9},{2,18},{10... | collective-permute-start | bytes 73736 | tf_op jit(solution)/shard_map/ppermute | solution.py:362
  39.4 1.1 %collective-permute-done.14 = bf16[48,256]{1,0:T(8,128)(2,1)S(1)} collective-permute-done((bf16[48,256]{1,0:T(8,128)(2,1)S(1)}, bf16[48,256]{1,0:T(8,128)(2,1)S(1)}, u32[]{:S(2)}, u32[]{:S(2)}) %collective-permute-start.14) | collective-permute-done | bytes 24608 | tf_op jit(solution)/shard_map/ppermute | solution.py:362
  40.5 1.3 %collective-permute-done.12 = bf16[48,256]{1,0:T(8,128)(2,1)S(1)} collective-permute-done((bf16[48,256]{1,0:T(8,128)(2,1)S(1)}, bf16[48,256]{1,0:T(8,128)(2,1)S(1)}, u32[]{:S(2)}, u32[]{:S(2)}) %collective-permute-start.12) | collective-permute-done | bytes 24608 | tf_op jit(solution)/shard_map/ppermute | solution.py:362
  41.8 1.2 %collective-permute-start.19 = (bf16[4,48,256]{2,1,0:T(8,128)(2,1)S(1)}, bf16[4,48,256]{2,1,0:T(8,128)(2,1)S(1)}, u32[]{:S(2)}, u32[]{:S(2)}) collective-permute-start(bf16[4,48,256]{2,1,0:T(8,128)(2,1)S(1)} %pad_maximum_fusion.5), channel_id=1, source_target_pairs={{0,6},{1,7},{2,4},{3,5},{4,2},{5,3},{6,0},{7,1},{8,14},{9,15},{10,... | collective-permute-start | bytes 294920 | tf_op jit(solution)/shard_map/ppermute | solution.py:356
  43.0 1.5 %collective-permute-start.18 = (bf16[4,48,256]{2,1,0:T(8,128)(2,1)S(1)}, bf16[4,48,256]{2,1,0:T(8,128)(2,1)S(1)}, u32[]{:S(2)}, u32[]{:S(2)}) collective-permute-start(bf16[4,48,256]{2,1,0:T(8,128)(2,1)S(1)} %pad_maximum_fusion.5), channel_id=1, source_target_pairs={{0,2},{1,3},{2,0},{3,1},{4,6},{5,7},{6,4},{7,5},{8,10},{9,11},{10,... | collective-permute-start | bytes 294920 | tf_op jit(solution)/shard_map/ppermute | solution.py:356
  45.4 2.2 %collective-permute-start.20 = (bf16[2,64,512]{2,1,0:T(8,128)(2,1)S(1)}, bf16[2,64,512]{2,1,0:T(8,128)(2,1)S(1)}, u32[]{:S(2)}, u32[]{:S(2)}) collective-permute-start(bf16[2,64,512]{2,1,0:T(8,128)(2,1)S(1)} %copy-done.3), channel_id=1, source_target_pairs={{0,16},{8,24},{16,0},{24,8},{1,17},{9,25},{17,1},{25,9},{2,18},{10... | collective-permute-start | bytes 393224 | tf_op jit(solution)/shard_map/ppermute | solution.py:362
  49.2 3.5 %collective-permute-done.20 = bf16[2,64,512]{2,1,0:T(8,128)(2,1)S(1)} collective-permute-done((bf16[2,64,512]{2,1,0:T(8,128)(2,1)S(1)}, bf16[2,64,512]{2,1,0:T(8,128)(2,1)S(1)}, u32[]{:S(2)}, u32[]{:S(2)}) %collective-permute-start.20) | collective-permute-done | bytes 131104 | tf_op jit(solution)/shard_map/ppermute | solution.py:362
  52.7 1.2 %collective-permute-start.22 = (bf16[4,1,64,512]{3,2,1,0:T(8,128)(2,1)S(1)}, bf16[4,1,64,512]{3,2,1,0:T(8,128)(2,1)S(1)}, u32[]{:S(2)}, u32[]{:S(2)}) collective-permute-start(bf16[4,1,64,512]{3,2,1,0:T(8,128)(2,1)S(1)} %slice.6), channel_id=1, source_target_pairs={{0,4},{1,5},{2,6},{3,7},{4,0},{5,1},{6,2},{7,3},{8,12},{9,13},{10,... | collective-permute-start | bytes 786440 | tf_op jit(solution)/shard_map/ppermute | solution.py:356
  55.1 4.0 %collective-permute-done.22 = bf16[4,1,64,512]{3,2,1,0:T(8,128)(2,1)S(1)} collective-permute-done((bf16[4,1,64,512]{3,2,1,0:T(8,128)(2,1)S(1)}, bf16[4,1,64,512]{3,2,1,0:T(8,128)(2,1)S(1)}, u32[]{:S(2)}, u32[]{:S(2)}) %collective-permute-start.22) | collective-permute-done | bytes 262176 | tf_op jit(solution)/shard_map/ppermute | solution.py:356
  59.1 1.2 %collective-permute-done.23 = bf16[4,1,64,512]{3,2,1,0:T(8,128)(2,1)S(1)} collective-permute-done((bf16[4,1,64,512]{3,2,1,0:T(8,128)(2,1)S(1)}, bf16[4,1,64,512]{3,2,1,0:T(8,128)(2,1)S(1)}, u32[]{:S(2)}, u32[]{:S(2)}) %collective-permute-start.23) | collective-permute-done | bytes 262176 | tf_op jit(solution)/shard_map/ppermute | solution.py:356
  60.5 5.0 %collective-permute-done.28 = bf16[2,2,64,512]{3,2,1,0:T(8,128)(2,1)S(1)} collective-permute-done((bf16[2,2,64,512]{3,2,1,0:T(8,128)(2,1)S(1)}, bf16[2,2,64,512]{3,2,1,0:T(8,128)(2,1)S(1)}, u32[]{:S(2)}, u32[]{:S(2)}) %collective-permute-start.28) | collective-permute-done | bytes 262176 | tf_op jit(solution)/shard_map/ppermute | solution.py:362
  65.6 1.3 %collective-permute-start.29 = (bf16[4,2,64,512]{3,2,1,0:T(8,128)(2,1)S(1)}, bf16[4,2,64,512]{3,2,1,0:T(8,128)(2,1)S(1)}, u32[]{:S(2)}, u32[]{:S(2)}) collective-permute-start(bf16[4,2,64,512]{3,2,1,0:T(8,128)(2,1)S(1)} %pad_maximum_fusion.1.refs_0_), channel_id=1, source_target_pairs={{0,2},{1,3},{2,0},{3,1},{4,6},{5,7},{6,4},{7,5},{8,10},{9,11},{10,... | collective-permute-start | bytes 1572872 | tf_op jit(solution)/shard_map/ppermute | solution.py:343
  67.4 9.6 %left.1.left_ref = bf16[4,256,2048]{2,1,0:T(8,128)(2,1)S(1)} custom-call(s32[3]{0:T(128)S(1)} %pad_add_fusion.me_ref, s32[4]{0:T(128)S(1)} %copy-done.2, f32[4,4,4]{2,1,0:T(4,128)S(1)} %copy-done.1, s32[8]{0:T(128)S(1)} %reshape.29.chain_ref, bf16[4,4,48,256]{3,2,1,0:T(8,128)(2,1)S(1)} %pad_maximum_fusion.2.refs_0_, ...), custom_call_target="tpu_custom_call" | custom-call | flops 8000000000 | bytes 10000000 | tf_op jit(solution)/shard_map/left/pallas_call | solution.py:494
  76.9 3.1 %collective-permute-done.29.refs_1_ = bf16[4,2,64,512]{3,2,1,0:T(8,128)(2,1)S(1)} collective-permute-done((bf16[4,2,64,512]{3,2,1,0:T(8,128)(2,1)S(1)}, bf16[4,2,64,512]{3,2,1,0:T(8,128)(2,1)S(1)}, u32[]{:S(2)}, u32[]{:S(2)}) %collective-permute-start.29) | collective-permute-done | bytes 524320 | tf_op jit(solution)/shard_map/ppermute | solution.py:343
  80.0 1.9 %collective-permute-done.31.refs_3_ = bf16[4,2,64,512]{3,2,1,0:T(8,128)(2,1)S(1)} collective-permute-done((bf16[4,2,64,512]{3,2,1,0:T(8,128)(2,1)S(1)}, bf16[4,2,64,512]{3,2,1,0:T(8,128)(2,1)S(1)}, u32[]{:S(2)}, u32[]{:S(2)}) %collective-permute-start.31) | collective-permute-done | bytes 524320 | tf_op jit(solution)/shard_map/ppermute | solution.py:343
  81.9 5.8 %right.1 = bf16[4,2,256,512]{3,2,1,0:T(8,128)(2,1)} custom-call(bf16[4,256,2048]{2,1,0:T(8,128)(2,1)S(1)} %left.1.left_ref, bf16[4,2,64,512]{3,2,1,0:T(8,128)(2,1)S(1)} %pad_maximum_fusion.1.refs_0_, bf16[4,2,64,512]{3,2,1,0:T(8,128)(2,1)S(1)} %collective-permute-done.29.refs_1_, bf16[4,2,64,512]{3,2,1,0:T(8,128)(2,1)S(1)} %collective-permute-done.30.refs_2_, ...), custom_call_target="tpu_custom_call" | custom-call | tf_op jit(solution)/shard_map/right/pallas_call | solution.py:514
  (73 shorter events, 12.1 us)
Async XLA Ops:
  2.5 11.6 %collective-permute-start.3 = (bf16[2,64,512]{2,1,0:T(8,128)(2,1)}, bf16[2,64,512]{2,1,0:T(8,128)(2,1)S(1)}, u32[]{:S(2)}, u32[]{:S(2)}) collective-permute-start(bf16[2,64,512]{2,1,0:T(8,128)(2,1)} %get-tuple-element.40), channel_id=1, source_target_pairs={{0,16},{8,24},{16,0},{24,8},{1,17},{9,25},{17,1},{25,9},{2,18},{10... | collective-permute-start | bytes 393224 | tf_op jit(solution)/shard_map/ppermute | solution.py:362
  7.5 5.2 %collective-permute-start = (bf16[96,256]{1,0:T(8,128)(2,1)S(1)}, bf16[96,256]{1,0:T(8,128)(2,1)S(1)}, u32[]{:S(2)}, u32[]{:S(2)}) collective-permute-start(bf16[96,256]{1,0:T(8,128)(2,1)S(1)} %get-tuple-element.32), channel_id=1, source_target_pairs={{0,24},{8,0},{16,8},{24,16},{1,25},{9,1},{17,9},{25,17},{2,26},{10... | collective-permute-start | bytes 147464 | tf_op jit(solution)/shard_map/ppermute | solution.py:20
  8.9 3.8 %collective-permute-start.1 = (bf16[48,256]{1,0:T(8,128)(2,1)S(1)}, bf16[48,256]{1,0:T(8,128)(2,1)S(1)}, u32[]{:S(2)}, u32[]{:S(2)}) collective-permute-start(bf16[48,256]{1,0:T(8,128)(2,1)S(1)} %get-tuple-element.33), channel_id=1, source_target_pairs={{0,4},{4,0},{1,5},{5,1},{2,6},{6,2},{3,7},{7,3},{8,12},{12,8},{9,1... | collective-permute-start | bytes 73736 | tf_op jit(solution)/shard_map/ppermute | solution.py:20
  10.4 2.3 %collective-permute-start.2 = (bf16[48,256]{1,0:T(8,128)(2,1)S(1)}, bf16[48,256]{1,0:T(8,128)(2,1)S(1)}, u32[]{:S(2)}, u32[]{:S(2)}) collective-permute-start(bf16[48,256]{1,0:T(8,128)(2,1)S(1)} %get-tuple-element.34), channel_id=1, source_target_pairs={{0,3},{1,0},{2,1},{3,2},{4,7},{5,4},{6,5},{7,6},{8,11},{9,8},{10,9... | collective-permute-start | bytes 73736 | tf_op jit(solution)/shard_map/ppermute | solution.py:20
  14.1 2.4 %collective-permute-start.4 = (bf16[2,4,2,48,256]{4,3,1,2,0:T(8,128)(2,1)S(1)}, bf16[2,4,2,48,256]{4,3,1,2,0:T(8,128)(2,1)S(1)}, u32[]{:S(2)}, u32[]{:S(2)}) collective-permute-start(bf16[2,4,2,48,256]{4,3,1,2,0:T(8,128)(2,1)S(1)} %bitcast.57), channel_id=1, source_target_pairs={{0,1},{1,0},{2,3},{3,2},{4,5},{5,4},{6,7},{7,6},{8,9},{9,8},{10,11... | collective-permute-start | bytes 1179656 | tf_op jit(solution)/shard_map/ppermute | solution.py:343
  15.2 8.4 %collective-permute-start.8 = (bf16[2,2,64,512]{3,2,1,0:T(8,128)(2,1)S(1)}, bf16[2,2,64,512]{3,2,1,0:T(8,128)(2,1)S(1)}, u32[]{:S(2)}, u32[]{:S(2)}) collective-permute-start(bf16[2,2,64,512]{3,2,1,0:T(8,128)(2,1)S(1)} %pad_maximum_fusion.3), channel_id=1, source_target_pairs={{0,8},{8,0},{16,24},{24,16},{1,9},{9,1},{17,25},{25,17},{2,10},{10... | collective-permute-start | bytes 786440 | tf_op jit(solution)/shard_map/ppermute | solution.py:362
  16.7 7.0 %collective-permute-start.7 = (bf16[4,48,256]{2,1,0:T(8,128)(2,1)S(1)}, bf16[4,48,256]{2,1,0:T(8,128)(2,1)S(1)}, u32[]{:S(2)}, u32[]{:S(2)}) collective-permute-start(bf16[4,48,256]{2,1,0:T(8,128)(2,1)S(1)} %get-tuple-element.60), channel_id=1, source_target_pairs={{0,6},{1,7},{2,4},{3,5},{4,2},{5,3},{6,0},{7,1},{8,14},{9,15},{10,... | collective-permute-start | bytes 294920 | tf_op jit(solution)/shard_map/ppermute | solution.py:356
  19.1 5.8 %collective-permute-start.6 = (bf16[4,48,256]{2,1,0:T(8,128)(2,1)S(1)}, bf16[4,48,256]{2,1,0:T(8,128)(2,1)S(1)}, u32[]{:S(2)}, u32[]{:S(2)}) collective-permute-start(bf16[4,48,256]{2,1,0:T(8,128)(2,1)S(1)} %get-tuple-element.61), channel_id=1, source_target_pairs={{0,2},{1,3},{2,0},{3,1},{4,6},{5,7},{6,4},{7,5},{8,10},{9,11},{10,... | collective-permute-start | bytes 294920 | tf_op jit(solution)/shard_map/ppermute | solution.py:356
  19.6 5.3 %collective-permute-start.5 = (bf16[4,48,256]{2,1,0:T(8,128)(2,1)S(1)}, bf16[4,48,256]{2,1,0:T(8,128)(2,1)S(1)}, u32[]{:S(2)}, u32[]{:S(2)}) collective-permute-start(bf16[4,48,256]{2,1,0:T(8,128)(2,1)S(1)} %get-tuple-element.59), channel_id=1, source_target_pairs={{0,4},{1,5},{2,6},{3,7},{4,0},{5,1},{6,2},{7,3},{8,12},{9,13},{10,... | collective-permute-start | bytes 294920 | tf_op jit(solution)/shard_map/ppermute | solution.py:356
  24.9 16.9 %collective-permute-start.15 = (bf16[4,2,64,512]{3,2,1,0:T(8,128)(2,1)S(1)}, bf16[4,2,64,512]{3,2,1,0:T(8,128)(2,1)S(1)}, u32[]{:S(2)}, u32[]{:S(2)}) collective-permute-start(bf16[4,2,64,512]{3,2,1,0:T(8,128)(2,1)S(1)} %pad_maximum_fusion.refs_2_), channel_id=1, source_target_pairs={{0,4},{1,5},{2,6},{3,7},{4,0},{5,1},{6,2},{7,3},{8,12},{9,13},{10,... | collective-permute-start | bytes 1572872 | tf_op jit(solution)/shard_map/ppermute | solution.py:356
  26.2 15.6 %collective-permute-start.16 = (bf16[4,2,64,512]{3,2,1,0:T(8,128)(2,1)S(1)}, bf16[4,2,64,512]{3,2,1,0:T(8,128)(2,1)S(1)}, u32[]{:S(2)}, u32[]{:S(2)}) collective-permute-start(bf16[4,2,64,512]{3,2,1,0:T(8,128)(2,1)S(1)} %pad_maximum_fusion.refs_2_), channel_id=1, source_target_pairs={{0,2},{1,3},{2,0},{3,1},{4,6},{5,7},{6,4},{7,5},{8,10},{9,11},{10,... | collective-permute-start | bytes 1572872 | tf_op jit(solution)/shard_map/ppermute | solution.py:356
  27.3 5.6 %collective-permute-start.11 = (bf16[48,256]{1,0:T(8,128)(2,1)S(1)}, bf16[48,256]{1,0:T(8,128)(2,1)S(1)}, u32[]{:S(2)}, u32[]{:S(2)}) collective-permute-start(bf16[48,256]{1,0:T(8,128)(2,1)S(1)} %get-tuple-element.63), channel_id=1, source_target_pairs={{0,24},{8,16},{16,8},{24,0},{1,25},{9,17},{17,9},{25,1},{2,26},{10... | collective-permute-start | bytes 73736 | tf_op jit(solution)/shard_map/ppermute | solution.py:362
  30.1 3.8 %collective-permute-start.10 = (bf16[48,256]{1,0:T(8,128)(2,1)S(1)}, bf16[48,256]{1,0:T(8,128)(2,1)S(1)}, u32[]{:S(2)}, u32[]{:S(2)}) collective-permute-start(bf16[48,256]{1,0:T(8,128)(2,1)S(1)} %get-tuple-element.64), channel_id=1, source_target_pairs={{0,8},{8,0},{16,24},{24,16},{1,9},{9,1},{17,25},{25,17},{2,10},{10... | collective-permute-start | bytes 73736 | tf_op jit(solution)/shard_map/ppermute | solution.py:362
  30.1 4.7 %collective-permute-start.9 = (bf16[48,256]{1,0:T(8,128)(2,1)S(1)}, bf16[48,256]{1,0:T(8,128)(2,1)S(1)}, u32[]{:S(2)}, u32[]{:S(2)}) collective-permute-start(bf16[48,256]{1,0:T(8,128)(2,1)S(1)} %get-tuple-element.62), channel_id=1, source_target_pairs={{0,16},{8,24},{16,0},{24,8},{1,17},{9,25},{17,1},{25,9},{2,18},{10... | collective-permute-start | bytes 73736 | tf_op jit(solution)/shard_map/ppermute | solution.py:362
  34.8 5.7 %collective-permute-start.14 = (bf16[48,256]{1,0:T(8,128)(2,1)S(1)}, bf16[48,256]{1,0:T(8,128)(2,1)S(1)}, u32[]{:S(2)}, u32[]{:S(2)}) collective-permute-start(bf16[48,256]{1,0:T(8,128)(2,1)S(1)} %fusion.6), channel_id=1, source_target_pairs={{0,24},{8,16},{16,8},{24,0},{1,25},{9,17},{17,9},{25,1},{2,26},{10... | collective-permute-start | bytes 73736 | tf_op jit(solution)/shard_map/ppermute | solution.py:362
  36.3 4.2 %collective-permute-start.13 = (bf16[48,256]{1,0:T(8,128)(2,1)S(1)}, bf16[48,256]{1,0:T(8,128)(2,1)S(1)}, u32[]{:S(2)}, u32[]{:S(2)}) collective-permute-start(bf16[48,256]{1,0:T(8,128)(2,1)S(1)} %fusion.6), channel_id=1, source_target_pairs={{0,8},{8,0},{16,24},{24,16},{1,9},{9,1},{17,25},{25,17},{2,10},{10... | collective-permute-start | bytes 73736 | tf_op jit(solution)/shard_map/ppermute | solution.py:362
  37.0 4.7 %collective-permute-start.12 = (bf16[48,256]{1,0:T(8,128)(2,1)S(1)}, bf16[48,256]{1,0:T(8,128)(2,1)S(1)}, u32[]{:S(2)}, u32[]{:S(2)}) collective-permute-start(bf16[48,256]{1,0:T(8,128)(2,1)S(1)} %fusion.6), channel_id=1, source_target_pairs={{0,16},{8,24},{16,0},{24,8},{1,17},{9,25},{17,1},{25,9},{2,18},{10... | collective-permute-start | bytes 73736 | tf_op jit(solution)/shard_map/ppermute | solution.py:362
  41.8 5.8 %collective-permute-start.19 = (bf16[4,48,256]{2,1,0:T(8,128)(2,1)S(1)}, bf16[4,48,256]{2,1,0:T(8,128)(2,1)S(1)}, u32[]{:S(2)}, u32[]{:S(2)}) collective-permute-start(bf16[4,48,256]{2,1,0:T(8,128)(2,1)S(1)} %pad_maximum_fusion.5), channel_id=1, source_target_pairs={{0,6},{1,7},{2,4},{3,5},{4,2},{5,3},{6,0},{7,1},{8,14},{9,15},{10,... | collective-permute-start | bytes 294920 | tf_op jit(solution)/shard_map/ppermute | solution.py:356
  43.0 5.4 %collective-permute-start.18 = (bf16[4,48,256]{2,1,0:T(8,128)(2,1)S(1)}, bf16[4,48,256]{2,1,0:T(8,128)(2,1)S(1)}, u32[]{:S(2)}, u32[]{:S(2)}) collective-permute-start(bf16[4,48,256]{2,1,0:T(8,128)(2,1)S(1)} %pad_maximum_fusion.5), channel_id=1, source_target_pairs={{0,2},{1,3},{2,0},{3,1},{4,6},{5,7},{6,4},{7,5},{8,10},{9,11},{10,... | collective-permute-start | bytes 294920 | tf_op jit(solution)/shard_map/ppermute | solution.py:356
  44.5 4.6 %collective-permute-start.17 = (bf16[4,48,256]{2,1,0:T(8,128)(2,1)S(1)}, bf16[4,48,256]{2,1,0:T(8,128)(2,1)S(1)}, u32[]{:S(2)}, u32[]{:S(2)}) collective-permute-start(bf16[4,48,256]{2,1,0:T(8,128)(2,1)S(1)} %pad_maximum_fusion.5), channel_id=1, source_target_pairs={{0,4},{1,5},{2,6},{3,7},{4,0},{5,1},{6,2},{7,3},{8,12},{9,13},{10,... | collective-permute-start | bytes 294920 | tf_op jit(solution)/shard_map/ppermute | solution.py:356
  45.4 7.3 %collective-permute-start.20 = (bf16[2,64,512]{2,1,0:T(8,128)(2,1)S(1)}, bf16[2,64,512]{2,1,0:T(8,128)(2,1)S(1)}, u32[]{:S(2)}, u32[]{:S(2)}) collective-permute-start(bf16[2,64,512]{2,1,0:T(8,128)(2,1)S(1)} %copy-done.3), channel_id=1, source_target_pairs={{0,16},{8,24},{16,0},{24,8},{1,17},{9,25},{17,1},{25,9},{2,18},{10... | collective-permute-start | bytes 393224 | tf_op jit(solution)/shard_map/ppermute | solution.py:362
  52.7 6.4 %collective-permute-start.22 = (bf16[4,1,64,512]{3,2,1,0:T(8,128)(2,1)S(1)}, bf16[4,1,64,512]{3,2,1,0:T(8,128)(2,1)S(1)}, u32[]{:S(2)}, u32[]{:S(2)}) collective-permute-start(bf16[4,1,64,512]{3,2,1,0:T(8,128)(2,1)S(1)} %slice.6), channel_id=1, source_target_pairs={{0,4},{1,5},{2,6},{3,7},{4,0},{5,1},{6,2},{7,3},{8,12},{9,13},{10,... | collective-permute-start | bytes 786440 | tf_op jit(solution)/shard_map/ppermute | solution.py:356
  53.9 6.4 %collective-permute-start.23 = (bf16[4,1,64,512]{3,2,1,0:T(8,128)(2,1)S(1)}, bf16[4,1,64,512]{3,2,1,0:T(8,128)(2,1)S(1)}, u32[]{:S(2)}, u32[]{:S(2)}) collective-permute-start(bf16[4,1,64,512]{3,2,1,0:T(8,128)(2,1)S(1)} %slice.7), channel_id=1, source_target_pairs={{0,2},{1,3},{2,0},{3,1},{4,6},{5,7},{6,4},{7,5},{8,10},{9,11},{10,... | collective-permute-start | bytes 786440 | tf_op jit(solution)/shard_map/ppermute | solution.py:356
  54.5 11.1 %collective-permute-start.24 = (bf16[4,2,64,512]{3,2,1,0:T(8,128)(2,1)S(1)}, bf16[4,2,64,512]{3,2,1,0:T(8,128)(2,1)S(1)}, u32[]{:S(2)}, u32[]{:S(2)}) collective-permute-start(bf16[4,2,64,512]{3,2,1,0:T(8,128)(2,1)S(1)} %pad_maximum_fusion.refs_2_), channel_id=1, source_target_pairs={{0,1},{1,0},{2,3},{3,2},{4,5},{5,4},{6,7},{7,6},{8,9},{9,8},{10,11... | collective-permute-start | bytes 1572872 | tf_op jit(solution)/shard_map/ppermute | solution.py:343
  54.5 12.8 %collective-permute-start.25 = (bf16[4,2,64,512]{3,2,1,0:T(8,128)(2,1)S(1)}, bf16[4,2,64,512]{3,2,1,0:T(8,128)(2,1)S(1)}, u32[]{:S(2)}, u32[]{:S(2)}) collective-permute-start(bf16[4,2,64,512]{3,2,1,0:T(8,128)(2,1)S(1)} %collective-permute-done.15.refs_3_), channel_id=1, source_target_pairs={{0,1},{1,0},{2,3},{3,2},{4,5},{5,4},{6,7},{7,6},{8,9},{9,8},{10,11... | collective-permute-start | bytes 1572872 | tf_op jit(solution)/shard_map/ppermute | solution.py:343
  55.1 12.3 %collective-permute-start.26 = (bf16[4,2,64,512]{3,2,1,0:T(8,128)(2,1)S(1)}, bf16[4,2,64,512]{3,2,1,0:T(8,128)(2,1)S(1)}, u32[]{:S(2)}, u32[]{:S(2)}) collective-permute-start(bf16[4,2,64,512]{3,2,1,0:T(8,128)(2,1)S(1)} %collective-permute-done.16.refs_4_), channel_id=1, source_target_pairs={{0,1},{1,0},{2,3},{3,2},{4,5},{5,4},{6,7},{7,6},{8,9},{9,8},{10,11... | collective-permute-start | bytes 1572872 | tf_op jit(solution)/shard_map/ppermute | solution.py:343
  59.1 6.4 %collective-permute-start.28 = (bf16[2,2,64,512]{3,2,1,0:T(8,128)(2,1)S(1)}, bf16[2,2,64,512]{3,2,1,0:T(8,128)(2,1)S(1)}, u32[]{:S(2)}, u32[]{:S(2)}) collective-permute-start(bf16[2,2,64,512]{3,2,1,0:T(8,128)(2,1)S(1)} %pad_maximum_fusion.4), channel_id=1, source_target_pairs={{0,8},{8,0},{16,24},{24,16},{1,9},{9,1},{17,25},{25,17},{2,10},{10... | collective-permute-start | bytes 786440 | tf_op jit(solution)/shard_map/ppermute | solution.py:362
  60.4 7.0 %collective-permute-start.27 = (bf16[4,2,64,512]{3,2,1,0:T(8,128)(2,1)S(1)}, bf16[4,2,64,512]{3,2,1,0:T(8,128)(2,1)S(1)}, u32[]{:S(2)}, u32[]{:S(2)}) collective-permute-start(bf16[4,2,64,512]{3,2,1,0:T(8,128)(2,1)S(1)} %constant_dynamic-update-slice_fusion.refs_5_), channel_id=1, source_target_pairs={{0,1},{1,0},{2,3},{3,2},{4,5},{5,4},{6,7},{7,6},{8,9},{9,8},{10,11... | collective-permute-start | bytes 1572872 | tf_op jit(solution)/shard_map/ppermute | solution.py:343
  65.5 1.7 %collective-permute-start.21 = (bf16[4,4,48,256]{3,2,1,0:T(8,128)(2,1)S(1)}, bf16[4,4,48,256]{3,2,1,0:T(8,128)(2,1)S(1)}, u32[]{:S(2)}, u32[]{:S(2)}) collective-permute-start(bf16[4,4,48,256]{3,2,1,0:T(8,128)(2,1)S(1)} %pad_maximum_fusion.2.refs_0_), channel_id=1, source_target_pairs={{0,1},{1,0},{2,3},{3,2},{4,5},{5,4},{6,7},{7,6},{8,9},{9,8},{10,11... | collective-permute-start | bytes 1179656 | tf_op jit(solution)/shard_map/ppermute | solution.py:343
  65.6 14.4 %collective-permute-start.29 = (bf16[4,2,64,512]{3,2,1,0:T(8,128)(2,1)S(1)}, bf16[4,2,64,512]{3,2,1,0:T(8,128)(2,1)S(1)}, u32[]{:S(2)}, u32[]{:S(2)}) collective-permute-start(bf16[4,2,64,512]{3,2,1,0:T(8,128)(2,1)S(1)} %pad_maximum_fusion.1.refs_0_), channel_id=1, source_target_pairs={{0,2},{1,3},{2,0},{3,1},{4,6},{5,7},{6,4},{7,5},{8,10},{9,11},{10,... | collective-permute-start | bytes 1572872 | tf_op jit(solution)/shard_map/ppermute | solution.py:343
  67.2 12.8 %collective-permute-start.30 = (bf16[4,2,64,512]{3,2,1,0:T(8,128)(2,1)S(1)}, bf16[4,2,64,512]{3,2,1,0:T(8,128)(2,1)S(1)}, u32[]{:S(2)}, u32[]{:S(2)}) collective-permute-start(bf16[4,2,64,512]{3,2,1,0:T(8,128)(2,1)S(1)} %pad_maximum_fusion.1.refs_0_), channel_id=1, source_target_pairs={{0,1},{1,0},{2,3},{3,2},{4,5},{5,4},{6,7},{7,6},{8,9},{9,8},{10,11... | collective-permute-start | bytes 1572872 | tf_op jit(solution)/shard_map/ppermute | solution.py:343
  80.0 1.9 %collective-permute-start.31 = (bf16[4,2,64,512]{3,2,1,0:T(8,128)(2,1)S(1)}, bf16[4,2,64,512]{3,2,1,0:T(8,128)(2,1)S(1)}, u32[]{:S(2)}, u32[]{:S(2)}) collective-permute-start(bf16[4,2,64,512]{3,2,1,0:T(8,128)(2,1)S(1)} %collective-permute-done.29.refs_1_), channel_id=1, source_target_pairs={{0,1},{1,0},{2,3},{3,2},{4,5},{5,4},{6,7},{7,6},{8,9},{9,8},{10,11... | collective-permute-start | bytes 1572872 | tf_op jit(solution)/shard_map/ppermute | solution.py:343
  (6 other events, 172.0 us)

commit v12 on v7

--- a/solution.py
+++ b/solution.py
@@ -289,8 +289,8 @@
     blocks = [pl.multiple_of(back(gy, dx, gy_n) * lane, lane) for dx in range(gy_n)]
 
     def one_operator(op):
-        a = chain_ref[op, 0]
-        b = chain_ref[op, 1]
+        a = chain_ref[2 * op]
+        b = chain_ref[2 * op + 1]
         dir_a = dirs_ref[a]
         dir_b = dirs_ref[b]
         mix = None
@@ -302,11 +302,12 @@
         mix = jnp.where(diagonal, mix, 0.0)
         high = mix.astype(BF16)
         low = (mix - high.astype(F32)).astype(BF16)
-        mix = jnp.concatenate([high, low], axis=1)
+        mix = jnp.concatenate([high, low], axis=0)
         for c in range(2):
             for dx in range(gy_n):
                 source = x_ref[dir_a, c, dx].reshape(row_count, width)
-                result = mm(mix, jnp.concatenate([source, source], axis=0)).astype(BF16)
+                both = mm(mix, source)
+                result = (both[:row_count] + both[row_count:]).astype(BF16)
                 for s in range(4):
                     to = c * num_vecs + dx * lane
                     p_ref[s, :, to : to + lane] = result[:, s * lane : (s + 1) * lane]
@@ -322,7 +323,8 @@
             ],
             axis=0,
         )
-        parts = [mm(p_ref[s], right) for s in range(4)]
+        product = mm(p_ref[...].reshape(4 * row_count, 2 * num_vecs), right)
+        parts = [product[s * row_count : (s + 1) * row_count] for s in range(4)]
         for t in range(4):
             total = parts[0] * (spin_ref[b, 0, spins[t]] * inverse)
             for s in range(1, 4):
@@ -413,7 +415,7 @@
         name="pieces",
     )(me[2:], forward_peram, backward_peram)
     fwd_piece, links = lax.optimization_barrier((fwd_piece, links))
-    fwd_line, line = line_exchange(fwd_piece, "gx", gx_n // 2, 1)
+    fwd_half = lax.ppermute(fwd_piece, "gx", [(n, n ^ (gx_n // 2)) for n in range(gx_n)])
 
     link_mats = pl.pallas_call(
         functools.partial(links_kernel, extent),
@@ -440,11 +442,12 @@
         name="correlate",
     )(vec, *faces, *link_mats)
 
-    partial, fwd_line = lax.optimization_barrier((partial, fwd_line))
+    partial, fwd_half = lax.optimization_barrier((partial, fwd_half))
     by_core = partial.reshape((chips, 2) + partial.shape[1:])
     summed = added(part_at(by_core, core, 1), passed_in_gz(part_at(by_core, 1 - core, 1), 0, 1))
     rounds = gx_n.bit_length() - 1
-    fwd_line, line = line_exchange(fwd_line, "gx", gx_n // 4, rounds - 1, line)
+    fwd_line = jnp.stack([fwd_piece, fwd_half])
+    fwd_line, line = line_exchange(fwd_line, "gx", gx_n // 4, rounds - 1, (0, gx_n // 2))
     plane = [(dx, dy) for dy in range(chips) for dx in range(gy_n)]
 
     def plane_part(dx, dy):
@@ -467,9 +470,11 @@
         distance //= 2
     elem_line, offsets = line_exchange(summed[0], "gx", gx_n // 2, rounds - 1)
     fwd_parts[0, 0, 1] = passed_in_gz(fwd_line, 0, 1)
+    order = chain_order.reshape(-1)
     if four:
         keys = [(1, 0, 0), (0, 1, 0), (0, 0, 1)]
-        elem_line, bwd_line, *parts = lax.optimization_barrier((elem_line, bwd_line, *[fwd_parts[key] for key in keys]))
+        tied = (elem_line, bwd_line, order, *[fwd_parts[key] for key in keys])
+        elem_line, bwd_line, order, *parts = lax.optimization_barrier(tied)
         fwd_parts.update(zip(keys, parts))
         fwd_parts[1, 1, 0] = passed_in_plane(fwd_parts[0, 1, 0], 1, 0)
     bwd_parts = {(dy, 0): passed_in_gz(bwd_line, dy, 0) if dy else bwd_line for dy in range(chips)}
@@ -503,7 +508,7 @@
         compiler_params=pltpu.CompilerParams(vmem_limit_bytes=24 * 2**20),
         cost_estimate=pl.CostEstimate(flops=8 * 10**9, bytes_accessed=10**7, transcendentals=0),
         name="left",
-    )(me, directions, spin_mats, chain_order, *elem_parts, *fwd_parts.values())
+    )(me, directions, spin_mats, order, *elem_parts, *fwd_parts.values())
     return pl.pallas_call(
         functools.partial(right_kernel, gz_n, tuple(bwd_parts)),
         out_shape=jax.ShapeDtypeStruct((op_count, 2, rows, cols), BF16),

time: 85.5 us -> 83.6 us (0.978)
  other arithmetic: 1.38 us -> 0.48 us
    ppermute x0 -> x1, starting transfers between devices: none -> 4.1 us  [on_device(): lax.ppermute(fwd_piece, 'gx', [(n, n ^ gx_n // 2) for n in range(gx_n)])]
    ppermute x6 -> x5, starting transfers between devices: 9.78 us -> 5.69 us  [line_exchange(): gathered = jnp.concatenate([gathered, lax.ppermute(gathered, axis, pairs)])]
    concatenate x5 -> x4, other arithmetic: 1.06 us -> 0.14 us  [line_exchange(): gathered = jnp.concatenate([gathered, lax.ppermute(gathered, axis, pairs)])]
    ppermute x6 -> x5, waiting for transfers between devices: 17.9 us -> 17.9 us  [line_exchange(): gathered = jnp.concatenate([gathered, lax.ppermute(gathered, axis, pairs)])]
  transfers between devices with their start and end apart: 29 -> 29, of which waited for: 15 -> 14; matrix products, arithmetic and copies ran while one was open for 3% -> 2% of each run, Pallas kernels for 14% -> 14%
where the time goes in v12:
time: 83.6 us; the launch traced here: 83.4 us
  waiting for transfers between devices  30.3 us (36%)
  starting transfers between devices  30.1 us (36%)
  Pallas kernels  19.7 us (24%)
  local copies, waits for them, and re-layouts  2.49 us (3%)
    ppermute x5, waiting for transfers between devices, line_exchange(): gathered = jnp.concatenate([gathered, lax.ppermute(gathered, axis, pairs)])  17.9 us
    ppermute x9, waiting for transfers between devices, passed_in_plane(): return lax.ppermute(value, ('gy', 'gz'), pairs)  9.85 us
    ppermute x9, starting transfers between devices, passed_in_plane(): return lax.ppermute(value, ('gy', 'gz'), pairs)  9.59 us
    pallas_call x1, Pallas kernels, on_device(): pl.pallas_call(functools.partial(left_kernel, 1.0 / math.sqrt(4 * num_vec...  9.57 us
    pallas_call x1, Pallas kernels, on_device(): pl.pallas_call(functools.partial(right_kernel, gz_n, tuple(bwd_parts)), o...  5.81 us
    ppermute x5, starting transfers between devices, line_exchange(): gathered = jnp.concatenate([gathered, lax.ppermute(gathered, axis, pairs)])  5.69 us
    ppermute x1, starting transfers between devices, on_device(): lax.ppermute(fwd_piece, 'gx', [(n, n ^ gx_n // 2) for n in range(gx_n)])  4.1 us
    ppermute x9, starting transfers between devices, passed_in_gz(): return lax.ppermute(value, 'gz', pairs)  3.93 us
  transfers between devices with their start and end apart: 29, of which 14 were waited for; matrix products, arithmetic and copies ran while one was open for 2% of the time, Pallas kernels for 14%

profile of v12, /device:TPU:0, one launch (start us, length us, event | category | flops | bytes accessed | tf_op | source)
XLA Modules:
  0.0 83.4 jit_solution(12358681156023101369)
XLA Ops:
  0.0 2.4 %pieces.1 = (bf16[2,64,512]{2,1,0:T(8,128)(2,1)}, bf16[2,64,512]{2,1,0:T(8,128)(2,1)}) custom-call(s32[1]{0:T(128)} %bitcast.2.z_ref, bf16[2,256,512]{2,1,0:T(8,128)(2,1)} %fwd_in.1, bf16[2,256,512]{2,1,0:T(8,128)(2,1)} %bwd_in.1), custom_call_target="tpu_custom_call" | custom-call | flops 100000000 | bytes 10000000 | tf_op jit(solution)/shard_map/pieces/pallas_call | solution.py:403
  2.4 4.1 %collective-permute-start.3 = (bf16[2,64,512]{2,1,0:T(8,128)(2,1)}, bf16[2,64,512]{2,1,0:T(8,128)(2,1)S(1)}, u32[]{:S(2)}, u32[]{:S(2)}) collective-permute-start(bf16[2,64,512]{2,1,0:T(8,128)(2,1)} %get-tuple-element.40), channel_id=1, source_target_pairs={{0,16},{8,24},{16,0},{24,8},{1,17},{9,25},{17,1},{25,9},{2,18},{10... | collective-permute-start | bytes 393224 | tf_op jit(solution)/shard_map/ppermute | solution.py:418
  6.6 0.9 %copy-done = bf16[2,4,4,2,3,256]{5,3,4,2,1,0:T(2,128)(2,1)S(1)} copy-done((bf16[2,4,4,2,3,256]{5,3,4,2,1,0:T(2,128)(2,1)S(1)}, bf16[2,4,4,2,3,256]{5,3,4,2,1,0:T(2,128)(2,1)}, u32[]{:S(2)}) %copy-start) | copy-done | bytes 98328
  7.5 1.4 %collective-permute-start = (bf16[96,256]{1,0:T(8,128)(2,1)S(1)}, bf16[96,256]{1,0:T(8,128)(2,1)S(1)}, u32[]{:S(2)}, u32[]{:S(2)}) collective-permute-start(bf16[96,256]{1,0:T(8,128)(2,1)S(1)} %get-tuple-element.32), channel_id=1, source_target_pairs={{0,24},{8,0},{16,8},{24,16},{1,25},{9,1},{17,9},{25,17},{2,26},{10... | collective-permute-start | bytes 147464 | tf_op jit(solution)/shard_map/ppermute | solution.py:20
  8.9 1.5 %collective-permute-start.1 = (bf16[48,256]{1,0:T(8,128)(2,1)S(1)}, bf16[48,256]{1,0:T(8,128)(2,1)S(1)}, u32[]{:S(2)}, u32[]{:S(2)}) collective-permute-start(bf16[48,256]{1,0:T(8,128)(2,1)S(1)} %get-tuple-element.33), channel_id=1, source_target_pairs={{0,4},{4,0},{1,5},{5,1},{2,6},{6,2},{3,7},{7,3},{8,12},{12,8},{9,1... | collective-permute-start | bytes 73736 | tf_op jit(solution)/shard_map/ppermute | solution.py:20
  10.5 1.0 %copy.12 = f32[2,4,4,3,2,3,3]{2,1,0,6,5,4,3:T(4,128)S(1)} copy(f32[2,4,4,3,2,3,3]{2,4,6,5,3,1,0:T(2,128)} %param.8) | data formatting | bytes 13824 | tf_op jit(solution)/shard_map/optimization_barrier | solution.py:417
  12.7 1.3 %correlate.1 = bf16[4,4,2,48,256]{4,3,2,1,0:T(8,128)(2,1)S(1)} custom-call(bf16[192,256]{1,0:T(8,128)(2,1)S(1)} %get-tuple-element.31.vec_ref, bf16[96,256]{1,0:T(8,128)(2,1)S(1)} %collective-permute-done.face0, bf16[48,256]{1,0:T(8,128)(2,1)S(1)} %collective-permute-done.1.face1, bf16[48,256]{1,0:T(8,128)(2,1)S(1)} %collective-permute-done.2.face2, ...), custom_call_target="tpu_custom_call" | custom-call | tf_op jit(solution)/shard_map/correlate/pallas_call | solution.py:436
  14.1 1.0 %collective-permute-start.4 = (bf16[2,4,2,48,256]{4,3,1,2,0:T(8,128)(2,1)S(1)}, bf16[2,4,2,48,256]{4,3,1,2,0:T(8,128)(2,1)S(1)}, u32[]{:S(2)}, u32[]{:S(2)}) collective-permute-start(bf16[2,4,2,48,256]{4,3,1,2,0:T(8,128)(2,1)S(1)} %bitcast.48), channel_id=1, source_target_pairs={{0,1},{1,0},{2,3},{3,2},{4,5},{5,4},{6,7},{7,6},{8,9},{9,8},{10,11... | collective-permute-start | bytes 1179656 | tf_op jit(solution)/shard_map/ppermute | solution.py:343
  15.2 1.1 %collective-permute-start.8 = (bf16[2,2,64,512]{3,2,1,0:T(8,128)(2,1)S(1)}, bf16[2,2,64,512]{3,2,1,0:T(8,128)(2,1)S(1)}, u32[]{:S(2)}, u32[]{:S(2)}) collective-permute-start(bf16[2,2,64,512]{3,2,1,0:T(8,128)(2,1)S(1)} %pad_maximum_fusion.3), channel_id=1, source_target_pairs={{0,8},{8,0},{16,24},{24,16},{1,9},{9,1},{17,25},{25,17},{2,10},{10... | collective-permute-start | bytes 786440 | tf_op jit(solution)/shard_map/ppermute | solution.py:365
  16.7 1.4 %collective-permute-start.5 = (bf16[4,48,256]{2,1,0:T(8,128)(2,1)S(1)}, bf16[4,48,256]{2,1,0:T(8,128)(2,1)S(1)}, u32[]{:S(2)}, u32[]{:S(2)}) collective-permute-start(bf16[4,48,256]{2,1,0:T(8,128)(2,1)S(1)} %get-tuple-element.59), channel_id=1, source_target_pairs={{0,4},{1,5},{2,6},{3,7},{4,0},{5,1},{6,2},{7,3},{8,12},{9,13},{10,... | collective-permute-start | bytes 294920 | tf_op jit(solution)/shard_map/ppermute | solution.py:356
  18.1 1.5 %collective-permute-start.7 = (bf16[4,48,256]{2,1,0:T(8,128)(2,1)S(1)}, bf16[4,48,256]{2,1,0:T(8,128)(2,1)S(1)}, u32[]{:S(2)}, u32[]{:S(2)}) collective-permute-start(bf16[4,48,256]{2,1,0:T(8,128)(2,1)S(1)} %get-tuple-element.60), channel_id=1, source_target_pairs={{0,6},{1,7},{2,4},{3,5},{4,2},{5,3},{6,0},{7,1},{8,14},{9,15},{10,... | collective-permute-start | bytes 294920 | tf_op jit(solution)/shard_map/ppermute | solution.py:356
  20.2 3.3 %collective-permute-done.8 = bf16[2,2,64,512]{3,2,1,0:T(8,128)(2,1)S(1)} collective-permute-done((bf16[2,2,64,512]{3,2,1,0:T(8,128)(2,1)S(1)}, bf16[2,2,64,512]{3,2,1,0:T(8,128)(2,1)S(1)}, u32[]{:S(2)}, u32[]{:S(2)}) %collective-permute-start.8) | collective-permute-done | bytes 262176 | tf_op jit(solution)/shard_map/ppermute | solution.py:365
  23.7 1.0 %collective-permute-done.7 = bf16[4,48,256]{2,1,0:T(8,128)(2,1)S(1)} collective-permute-done((bf16[4,48,256]{2,1,0:T(8,128)(2,1)S(1)}, bf16[4,48,256]{2,1,0:T(8,128)(2,1)S(1)}, u32[]{:S(2)}, u32[]{:S(2)}) %collective-permute-start.7) | collective-permute-done | bytes 98336 | tf_op jit(solution)/shard_map/ppermute | solution.py:356
  24.6 1.3 %collective-permute-done.6 = bf16[4,48,256]{2,1,0:T(8,128)(2,1)S(1)} collective-permute-done((bf16[4,48,256]{2,1,0:T(8,128)(2,1)S(1)}, bf16[4,48,256]{2,1,0:T(8,128)(2,1)S(1)}, u32[]{:S(2)}, u32[]{:S(2)}) %collective-permute-start.6) | collective-permute-done | bytes 98336 | tf_op jit(solution)/shard_map/ppermute | solution.py:356
  26.0 2.3 %collective-permute-start.9 = (bf16[2,48,256]{2,1,0:T(8,128)(2,1)S(1)}, bf16[2,48,256]{2,1,0:T(8,128)(2,1)S(1)}, u32[]{:S(2)}, u32[]{:S(2)}) collective-permute-start(bf16[2,48,256]{2,1,0:T(8,128)(2,1)S(1)} %dynamic-slice_bitcast_fusion.3), channel_id=1, source_target_pairs={{0,16},{8,24},{16,0},{24,8},{1,17},{9,25},{17,1},{25,9},{2,18},{10... | collective-permute-start | bytes 147464 | tf_op jit(solution)/shard_map/ppermute | solution.py:469
  28.9 1.4 %collective-permute-start.14 = (bf16[4,2,64,512]{3,2,1,0:T(8,128)(2,1)S(1)}, bf16[4,2,64,512]{3,2,1,0:T(8,128)(2,1)S(1)}, u32[]{:S(2)}, u32[]{:S(2)}) collective-permute-start(bf16[4,2,64,512]{3,2,1,0:T(8,128)(2,1)S(1)} %pad_maximum_fusion.refs_2_), channel_id=1, source_target_pairs={{0,4},{1,5},{2,6},{3,7},{4,0},{5,1},{6,2},{7,3},{8,12},{9,13},{10,... | collective-permute-start | bytes 1572872 | tf_op jit(solution)/shard_map/ppermute | solution.py:356
  30.3 0.7 collective-permute-start.12
  31.1 1.6 %collective-permute-start.10 = (bf16[1,48,256]{2,1,0:T(8,128)(2,1)S(1)}, bf16[1,48,256]{2,1,0:T(8,128)(2,1)S(1)}, u32[]{:S(2)}, u32[]{:S(2)}) collective-permute-start(bf16[1,48,256]{2,1,0:T(8,128)(2,1)S(1)} %constant_dynamic-slice_fusion), channel_id=1, source_target_pairs={{0,8},{8,0},{16,24},{24,16},{1,9},{9,1},{17,25},{25,17},{2,10},{10... | collective-permute-start | bytes 73736 | tf_op jit(solution)/shard_map/ppermute | solution.py:469
  32.7 6.7 %collective-permute-done.12 = bf16[1,2,64,512]{3,2,1,0:T(8,128)(2,1)S(1)} collective-permute-done((bf16[1,2,64,512]{3,2,1,0:T(8,128)(2,1)S(1)}, bf16[1,2,64,512]{3,2,1,0:T(8,128)(2,1)S(1)}, u32[]{:S(2)}, u32[]{:S(2)}) %collective-permute-start.12) | collective-permute-done | bytes 131104 | tf_op jit(solution)/shard_map/ppermute | solution.py:365
  39.5 2.3 %collective-permute-start.11 = (bf16[1,48,256]{2,1,0:T(8,128)(2,1)S(1)}, bf16[1,48,256]{2,1,0:T(8,128)(2,1)S(1)}, u32[]{:S(2)}, u32[]{:S(2)}) collective-permute-start(bf16[1,48,256]{2,1,0:T(8,128)(2,1)S(1)} %add_convert_fusion), channel_id=1, source_target_pairs={{0,16},{8,24},{16,0},{24,8},{1,17},{9,25},{17,1},{25,9},{2,18},{10... | collective-permute-start | bytes 73736 | tf_op jit(solution)/shard_map/ppermute | solution.py:365
  42.0 3.1 %collective-permute-done.11 = bf16[1,48,256]{2,1,0:T(8,128)(2,1)S(1)} collective-permute-done((bf16[1,48,256]{2,1,0:T(8,128)(2,1)S(1)}, bf16[1,48,256]{2,1,0:T(8,128)(2,1)S(1)}, u32[]{:S(2)}, u32[]{:S(2)}) %collective-permute-start.11) | collective-permute-done | bytes 24608 | tf_op jit(solution)/shard_map/ppermute | solution.py:365
  45.1 2.2 %collective-permute-done.13 = bf16[2,2,64,512]{3,2,1,0:T(8,128)(2,1)S(1)} collective-permute-done((bf16[2,2,64,512]{3,2,1,0:T(8,128)(2,1)S(1)}, bf16[2,2,64,512]{3,2,1,0:T(8,128)(2,1)S(1)}, u32[]{:S(2)}, u32[]{:S(2)}) %collective-permute-start.13) | collective-permute-done | bytes 262176 | tf_op jit(solution)/shard_map/ppermute | solution.py:365
  47.4 1.6 %collective-permute-start.22 = (bf16[4,2,64,512]{3,2,1,0:T(8,128)(2,1)S(1)}, bf16[4,2,64,512]{3,2,1,0:T(8,128)(2,1)S(1)}, u32[]{:S(2)}, u32[]{:S(2)}) collective-permute-start(bf16[4,2,64,512]{3,2,1,0:T(8,128)(2,1)S(1)} %pad_maximum_fusion.1.refs_0_), channel_id=1, source_target_pairs={{0,2},{1,3},{2,0},{3,1},{4,6},{5,7},{6,4},{7,5},{8,10},{9,11},{10,... | collective-permute-start | bytes 1572872 | tf_op jit(solution)/shard_map/ppermute | solution.py:343
  49.5 1.4 %collective-permute-start.17 = (bf16[2,48,256]{2,1,0:T(8,128)(2,1)S(1)}, bf16[2,48,256]{2,1,0:T(8,128)(2,1)S(1)}, u32[]{:S(2)}, u32[]{:S(2)}) collective-permute-start(bf16[2,48,256]{2,1,0:T(8,128)(2,1)S(1)} %pad_maximum_fusion.5), channel_id=1, source_target_pairs={{0,8},{8,0},{16,24},{24,16},{1,9},{9,1},{17,25},{25,17},{2,10},{10... | collective-permute-start | bytes 147464 | tf_op jit(solution)/shard_map/ppermute | solution.py:365
  50.9 2.7 %collective-permute-done.17 = bf16[2,48,256]{2,1,0:T(8,128)(2,1)S(1)} collective-permute-done((bf16[2,48,256]{2,1,0:T(8,128)(2,1)S(1)}, bf16[2,48,256]{2,1,0:T(8,128)(2,1)S(1)}, u32[]{:S(2)}, u32[]{:S(2)}) %collective-permute-start.17) | collective-permute-done | bytes 49184 | tf_op jit(solution)/shard_map/ppermute | solution.py:365
  53.6 1.4 %collective-permute-start.20 = (bf16[4,48,256]{2,1,0:T(8,128)(2,1)S(1)}, bf16[4,48,256]{2,1,0:T(8,128)(2,1)S(1)}, u32[]{:S(2)}, u32[]{:S(2)}) collective-permute-start(bf16[4,48,256]{2,1,0:T(8,128)(2,1)S(1)} %constant_dynamic-update-slice_fusion), channel_id=1, source_target_pairs={{0,6},{1,7},{2,4},{3,5},{4,2},{5,3},{6,0},{7,1},{8,14},{9,15},{10,... | collective-permute-start | bytes 294920 | tf_op jit(solution)/shard_map/ppermute | solution.py:356
  55.0 1.5 %collective-permute-start.19 = (bf16[4,48,256]{2,1,0:T(8,128)(2,1)S(1)}, bf16[4,48,256]{2,1,0:T(8,128)(2,1)S(1)}, u32[]{:S(2)}, u32[]{:S(2)}) collective-permute-start(bf16[4,48,256]{2,1,0:T(8,128)(2,1)S(1)} %constant_dynamic-update-slice_fusion), channel_id=1, source_target_pairs={{0,2},{1,3},{2,0},{3,1},{4,6},{5,7},{6,4},{7,5},{8,10},{9,11},{10,... | collective-permute-start | bytes 294920 | tf_op jit(solution)/shard_map/ppermute | solution.py:356
  57.1 7.0 %collective-permute-done.20 = bf16[4,48,256]{2,1,0:T(8,128)(2,1)S(1)} collective-permute-done((bf16[4,48,256]{2,1,0:T(8,128)(2,1)S(1)}, bf16[4,48,256]{2,1,0:T(8,128)(2,1)S(1)}, u32[]{:S(2)}, u32[]{:S(2)}) %collective-permute-start.20) | collective-permute-done | bytes 98336 | tf_op jit(solution)/shard_map/ppermute | solution.py:356
  66.0 0.7 collective-permute-done.24.refs_7_
  66.8 1.2 %collective-permute-done.23.refs_1_ = bf16[4,4,48,256]{3,2,1,0:T(8,128)(2,1)S(1)} collective-permute-done((bf16[4,4,48,256]{3,2,1,0:T(8,128)(2,1)S(1)}, bf16[4,4,48,256]{3,2,1,0:T(8,128)(2,1)S(1)}, u32[]{:S(2)}, u32[]{:S(2)}) %collective-permute-start.23) | collective-permute-done | bytes 393248 | tf_op jit(solution)/shard_map/ppermute | solution.py:343
  68.0 9.6 %left.1.left_ref = bf16[4,256,2048]{2,1,0:T(8,128)(2,1)S(1)} custom-call(s32[3]{0:T(128)S(1)} %pad_add_fusion.me_ref, s32[4]{0:T(128)S(1)} %copy-done.2, f32[4,4,4]{2,1,0:T(4,128)S(1)} %copy-done.1, s32[8]{0:T(128)S(1)} %reshape.40.chain_ref, bf16[4,4,48,256]{3,2,1,0:T(8,128)(2,1)S(1)} %pad_maximum_fusion.2.refs_0_, ...), custom_call_target="tpu_custom_call" | custom-call | flops 8000000000 | bytes 10000000 | tf_op jit(solution)/shard_map/left/pallas_call | solution.py:497
  77.6 5.8 %right.1 = bf16[4,2,256,512]{3,2,1,0:T(8,128)(2,1)} custom-call(bf16[4,256,2048]{2,1,0:T(8,128)(2,1)S(1)} %left.1.left_ref, bf16[4,2,64,512]{3,2,1,0:T(8,128)(2,1)S(1)} %pad_maximum_fusion.1.refs_0_, bf16[4,2,64,512]{3,2,1,0:T(8,128)(2,1)S(1)} %collective-permute-done.22.refs_1_, bf16[4,2,64,512]{3,2,1,0:T(8,128)(2,1)S(1)} %collective-permute-done.27.refs_2_, ...), custom_call_target="tpu_custom_call" | custom-call | tf_op jit(solution)/shard_map/right/pallas_call | solution.py:512
  (67 shorter events, 6.8 us)
Async XLA Ops:
  2.4 11.6 %collective-permute-start.3 = (bf16[2,64,512]{2,1,0:T(8,128)(2,1)}, bf16[2,64,512]{2,1,0:T(8,128)(2,1)S(1)}, u32[]{:S(2)}, u32[]{:S(2)}) collective-permute-start(bf16[2,64,512]{2,1,0:T(8,128)(2,1)} %get-tuple-element.40), channel_id=1, source_target_pairs={{0,16},{8,24},{16,0},{24,8},{1,17},{9,25},{17,1},{25,9},{2,18},{10... | collective-permute-start | bytes 393224 | tf_op jit(solution)/shard_map/ppermute | solution.py:418
  7.5 5.2 %collective-permute-start = (bf16[96,256]{1,0:T(8,128)(2,1)S(1)}, bf16[96,256]{1,0:T(8,128)(2,1)S(1)}, u32[]{:S(2)}, u32[]{:S(2)}) collective-permute-start(bf16[96,256]{1,0:T(8,128)(2,1)S(1)} %get-tuple-element.32), channel_id=1, source_target_pairs={{0,24},{8,0},{16,8},{24,16},{1,25},{9,1},{17,9},{25,17},{2,26},{10... | collective-permute-start | bytes 147464 | tf_op jit(solution)/shard_map/ppermute | solution.py:20
  8.9 3.8 %collective-permute-start.1 = (bf16[48,256]{1,0:T(8,128)(2,1)S(1)}, bf16[48,256]{1,0:T(8,128)(2,1)S(1)}, u32[]{:S(2)}, u32[]{:S(2)}) collective-permute-start(bf16[48,256]{1,0:T(8,128)(2,1)S(1)} %get-tuple-element.33), channel_id=1, source_target_pairs={{0,4},{4,0},{1,5},{5,1},{2,6},{6,2},{3,7},{7,3},{8,12},{12,8},{9,1... | collective-permute-start | bytes 73736 | tf_op jit(solution)/shard_map/ppermute | solution.py:20
  10.4 2.3 %collective-permute-start.2 = (bf16[48,256]{1,0:T(8,128)(2,1)S(1)}, bf16[48,256]{1,0:T(8,128)(2,1)S(1)}, u32[]{:S(2)}, u32[]{:S(2)}) collective-permute-start(bf16[48,256]{1,0:T(8,128)(2,1)S(1)} %get-tuple-element.34), channel_id=1, source_target_pairs={{0,3},{1,0},{2,1},{3,2},{4,7},{5,4},{6,5},{7,6},{8,11},{9,8},{10,9... | collective-permute-start | bytes 73736 | tf_op jit(solution)/shard_map/ppermute | solution.py:20
  12.7 29.1 %copy-start.5 = (s32[4,2]{0,1:T(2,128)S(1)}, s32[4,2]{0,1:T(2,128)}, u32[]{:S(2)}) copy-start(s32[4,2]{0,1:T(2,128)} %param.13) | copy-start | bytes 100
  14.1 53.9 %copy-start.1 = (f32[4,4,4]{2,1,0:T(4,128)S(1)}, f32[4,4,4]{2,1,0:T(4,128)}, u32[]{:S(2)}) copy-start(f32[4,4,4]{2,1,0:T(4,128)} %spin_ref.1) | copy-start | bytes 772
  14.1 53.9 %copy-start.2 = (s32[4]{0:T(128)S(1)}, s32[4]{0:T(128)}, u32[]{:S(2)}) copy-start(s32[4]{0:T(128)} %dirs_ref.1) | copy-start | bytes 52
  14.1 2.4 %collective-permute-start.4 = (bf16[2,4,2,48,256]{4,3,1,2,0:T(8,128)(2,1)S(1)}, bf16[2,4,2,48,256]{4,3,1,2,0:T(8,128)(2,1)S(1)}, u32[]{:S(2)}, u32[]{:S(2)}) collective-permute-start(bf16[2,4,2,48,256]{4,3,1,2,0:T(8,128)(2,1)S(1)} %bitcast.48), channel_id=1, source_target_pairs={{0,1},{1,0},{2,3},{3,2},{4,5},{5,4},{6,7},{7,6},{8,9},{9,8},{10,11... | collective-permute-start | bytes 1179656 | tf_op jit(solution)/shard_map/ppermute | solution.py:343
  15.2 8.4 %collective-permute-start.8 = (bf16[2,2,64,512]{3,2,1,0:T(8,128)(2,1)S(1)}, bf16[2,2,64,512]{3,2,1,0:T(8,128)(2,1)S(1)}, u32[]{:S(2)}, u32[]{:S(2)}) collective-permute-start(bf16[2,2,64,512]{3,2,1,0:T(8,128)(2,1)S(1)} %pad_maximum_fusion.3), channel_id=1, source_target_pairs={{0,8},{8,0},{16,24},{24,16},{1,9},{9,1},{17,25},{25,17},{2,10},{10... | collective-permute-start | bytes 786440 | tf_op jit(solution)/shard_map/ppermute | solution.py:365
  16.7 7.0 %collective-permute-start.5 = (bf16[4,48,256]{2,1,0:T(8,128)(2,1)S(1)}, bf16[4,48,256]{2,1,0:T(8,128)(2,1)S(1)}, u32[]{:S(2)}, u32[]{:S(2)}) collective-permute-start(bf16[4,48,256]{2,1,0:T(8,128)(2,1)S(1)} %get-tuple-element.59), channel_id=1, source_target_pairs={{0,4},{1,5},{2,6},{3,7},{4,0},{5,1},{6,2},{7,3},{8,12},{9,13},{10,... | collective-permute-start | bytes 294920 | tf_op jit(solution)/shard_map/ppermute | solution.py:356
  18.1 6.5 %collective-permute-start.7 = (bf16[4,48,256]{2,1,0:T(8,128)(2,1)S(1)}, bf16[4,48,256]{2,1,0:T(8,128)(2,1)S(1)}, u32[]{:S(2)}, u32[]{:S(2)}) collective-permute-start(bf16[4,48,256]{2,1,0:T(8,128)(2,1)S(1)} %get-tuple-element.60), channel_id=1, source_target_pairs={{0,6},{1,7},{2,4},{3,5},{4,2},{5,3},{6,0},{7,1},{8,14},{9,15},{10,... | collective-permute-start | bytes 294920 | tf_op jit(solution)/shard_map/ppermute | solution.py:356
  19.6 6.3 %collective-permute-start.6 = (bf16[4,48,256]{2,1,0:T(8,128)(2,1)S(1)}, bf16[4,48,256]{2,1,0:T(8,128)(2,1)S(1)}, u32[]{:S(2)}, u32[]{:S(2)}) collective-permute-start(bf16[4,48,256]{2,1,0:T(8,128)(2,1)S(1)} %get-tuple-element.61), channel_id=1, source_target_pairs={{0,2},{1,3},{2,0},{3,1},{4,6},{5,7},{6,4},{7,5},{8,10},{9,11},{10,... | collective-permute-start | bytes 294920 | tf_op jit(solution)/shard_map/ppermute | solution.py:356
  26.0 5.1 %collective-permute-start.9 = (bf16[2,48,256]{2,1,0:T(8,128)(2,1)S(1)}, bf16[2,48,256]{2,1,0:T(8,128)(2,1)S(1)}, u32[]{:S(2)}, u32[]{:S(2)}) collective-permute-start(bf16[2,48,256]{2,1,0:T(8,128)(2,1)S(1)} %dynamic-slice_bitcast_fusion.3), channel_id=1, source_target_pairs={{0,16},{8,24},{16,0},{24,8},{1,17},{9,25},{17,1},{25,9},{2,18},{10... | collective-permute-start | bytes 147464 | tf_op jit(solution)/shard_map/ppermute | solution.py:469
  28.3 19.1 %collective-permute-start.16 = (bf16[4,2,64,512]{3,2,1,0:T(8,128)(2,1)S(1)}, bf16[4,2,64,512]{3,2,1,0:T(8,128)(2,1)S(1)}, u32[]{:S(2)}, u32[]{:S(2)}) collective-permute-start(bf16[4,2,64,512]{3,2,1,0:T(8,128)(2,1)S(1)} %pad_maximum_fusion.refs_2_), channel_id=1, source_target_pairs={{0,1},{1,0},{2,3},{3,2},{4,5},{5,4},{6,7},{7,6},{8,9},{9,8},{10,11... | collective-permute-start | bytes 1572872 | tf_op jit(solution)/shard_map/ppermute | solution.py:343
  28.3 19.1 %collective-permute-start.15 = (bf16[4,2,64,512]{3,2,1,0:T(8,128)(2,1)S(1)}, bf16[4,2,64,512]{3,2,1,0:T(8,128)(2,1)S(1)}, u32[]{:S(2)}, u32[]{:S(2)}) collective-permute-start(bf16[4,2,64,512]{3,2,1,0:T(8,128)(2,1)S(1)} %pad_maximum_fusion.refs_2_), channel_id=1, source_target_pairs={{0,2},{1,3},{2,0},{3,1},{4,6},{5,7},{6,4},{7,5},{8,10},{9,11},{10,... | collective-permute-start | bytes 1572872 | tf_op jit(solution)/shard_map/ppermute | solution.py:356
  28.9 18.5 %collective-permute-start.14 = (bf16[4,2,64,512]{3,2,1,0:T(8,128)(2,1)S(1)}, bf16[4,2,64,512]{3,2,1,0:T(8,128)(2,1)S(1)}, u32[]{:S(2)}, u32[]{:S(2)}) collective-permute-start(bf16[4,2,64,512]{3,2,1,0:T(8,128)(2,1)S(1)} %pad_maximum_fusion.refs_2_), channel_id=1, source_target_pairs={{0,4},{1,5},{2,6},{3,7},{4,0},{5,1},{6,2},{7,3},{8,12},{9,13},{10,... | collective-permute-start | bytes 1572872 | tf_op jit(solution)/shard_map/ppermute | solution.py:356
  30.3 9.1 %collective-permute-start.12 = (bf16[1,2,64,512]{3,2,1,0:T(8,128)(2,1)S(1)}, bf16[1,2,64,512]{3,2,1,0:T(8,128)(2,1)S(1)}, u32[]{:S(2)}, u32[]{:S(2)}) collective-permute-start(bf16[1,2,64,512]{3,2,1,0:T(8,128)(2,1)S(1)} %bitcast.41), channel_id=1, source_target_pairs={{0,16},{8,24},{16,0},{24,8},{1,17},{9,25},{17,1},{25,9},{2,18},{10... | collective-permute-start | bytes 393224 | tf_op jit(solution)/shard_map/ppermute | solution.py:365
  31.1 8.3 %collective-permute-start.10 = (bf16[1,48,256]{2,1,0:T(8,128)(2,1)S(1)}, bf16[1,48,256]{2,1,0:T(8,128)(2,1)S(1)}, u32[]{:S(2)}, u32[]{:S(2)}) collective-permute-start(bf16[1,48,256]{2,1,0:T(8,128)(2,1)S(1)} %constant_dynamic-slice_fusion), channel_id=1, source_target_pairs={{0,8},{8,0},{16,24},{24,16},{1,9},{9,1},{17,25},{25,17},{2,10},{10... | collective-permute-start | bytes 73736 | tf_op jit(solution)/shard_map/ppermute | solution.py:469
  39.4 7.9 %collective-permute-start.13 = (bf16[2,2,64,512]{3,2,1,0:T(8,128)(2,1)S(1)}, bf16[2,2,64,512]{3,2,1,0:T(8,128)(2,1)S(1)}, u32[]{:S(2)}, u32[]{:S(2)}) collective-permute-start(bf16[2,2,64,512]{3,2,1,0:T(8,128)(2,1)S(1)} %pad_maximum_fusion.4), channel_id=1, source_target_pairs={{0,8},{8,0},{16,24},{24,16},{1,9},{9,1},{17,25},{25,17},{2,10},{10... | collective-permute-start | bytes 786440 | tf_op jit(solution)/shard_map/ppermute | solution.py:365
  39.5 5.6 %collective-permute-start.11 = (bf16[1,48,256]{2,1,0:T(8,128)(2,1)S(1)}, bf16[1,48,256]{2,1,0:T(8,128)(2,1)S(1)}, u32[]{:S(2)}, u32[]{:S(2)}) collective-permute-start(bf16[1,48,256]{2,1,0:T(8,128)(2,1)S(1)} %add_convert_fusion), channel_id=1, source_target_pairs={{0,16},{8,24},{16,0},{24,8},{1,17},{9,25},{17,1},{25,9},{2,18},{10... | collective-permute-start | bytes 73736 | tf_op jit(solution)/shard_map/ppermute | solution.py:365
  47.4 17.8 %collective-permute-start.22 = (bf16[4,2,64,512]{3,2,1,0:T(8,128)(2,1)S(1)}, bf16[4,2,64,512]{3,2,1,0:T(8,128)(2,1)S(1)}, u32[]{:S(2)}, u32[]{:S(2)}) collective-permute-start(bf16[4,2,64,512]{3,2,1,0:T(8,128)(2,1)S(1)} %pad_maximum_fusion.1.refs_0_), channel_id=1, source_target_pairs={{0,2},{1,3},{2,0},{3,1},{4,6},{5,7},{6,4},{7,5},{8,10},{9,11},{10,... | collective-permute-start | bytes 1572872 | tf_op jit(solution)/shard_map/ppermute | solution.py:343
  48.9 16.3 %collective-permute-start.21 = (bf16[4,2,64,512]{3,2,1,0:T(8,128)(2,1)S(1)}, bf16[4,2,64,512]{3,2,1,0:T(8,128)(2,1)S(1)}, u32[]{:S(2)}, u32[]{:S(2)}) collective-permute-start(bf16[4,2,64,512]{3,2,1,0:T(8,128)(2,1)S(1)} %collective-permute-done.15.refs_4_), channel_id=1, source_target_pairs={{0,4},{1,5},{2,6},{3,7},{4,0},{5,1},{6,2},{7,3},{8,12},{9,13},{10,... | collective-permute-start | bytes 1572872 | tf_op jit(solution)/shard_map/ppermute | solution.py:356
  49.5 4.1 %collective-permute-start.17 = (bf16[2,48,256]{2,1,0:T(8,128)(2,1)S(1)}, bf16[2,48,256]{2,1,0:T(8,128)(2,1)S(1)}, u32[]{:S(2)}, u32[]{:S(2)}) collective-permute-start(bf16[2,48,256]{2,1,0:T(8,128)(2,1)S(1)} %pad_maximum_fusion.5), channel_id=1, source_target_pairs={{0,8},{8,0},{16,24},{24,16},{1,9},{9,1},{17,25},{25,17},{2,10},{10... | collective-permute-start | bytes 147464 | tf_op jit(solution)/shard_map/ppermute | solution.py:365
  53.6 10.5 %collective-permute-start.20 = (bf16[4,48,256]{2,1,0:T(8,128)(2,1)S(1)}, bf16[4,48,256]{2,1,0:T(8,128)(2,1)S(1)}, u32[]{:S(2)}, u32[]{:S(2)}) collective-permute-start(bf16[4,48,256]{2,1,0:T(8,128)(2,1)S(1)} %constant_dynamic-update-slice_fusion), channel_id=1, source_target_pairs={{0,6},{1,7},{2,4},{3,5},{4,2},{5,3},{6,0},{7,1},{8,14},{9,15},{10,... | collective-permute-start | bytes 294920 | tf_op jit(solution)/shard_map/ppermute | solution.py:356
  55.0 9.0 %collective-permute-start.19 = (bf16[4,48,256]{2,1,0:T(8,128)(2,1)S(1)}, bf16[4,48,256]{2,1,0:T(8,128)(2,1)S(1)}, u32[]{:S(2)}, u32[]{:S(2)}) collective-permute-start(bf16[4,48,256]{2,1,0:T(8,128)(2,1)S(1)} %constant_dynamic-update-slice_fusion), channel_id=1, source_target_pairs={{0,2},{1,3},{2,0},{3,1},{4,6},{5,7},{6,4},{7,5},{8,10},{9,11},{10,... | collective-permute-start | bytes 294920 | tf_op jit(solution)/shard_map/ppermute | solution.py:356
  56.5 8.6 %collective-permute-start.18 = (bf16[4,48,256]{2,1,0:T(8,128)(2,1)S(1)}, bf16[4,48,256]{2,1,0:T(8,128)(2,1)S(1)}, u32[]{:S(2)}, u32[]{:S(2)}) collective-permute-start(bf16[4,48,256]{2,1,0:T(8,128)(2,1)S(1)} %constant_dynamic-update-slice_fusion), channel_id=1, source_target_pairs={{0,4},{1,5},{2,6},{3,7},{4,0},{5,1},{6,2},{7,3},{8,12},{9,13},{10,... | collective-permute-start | bytes 294920 | tf_op jit(solution)/shard_map/ppermute | solution.py:356
  64.0 2.8 %collective-permute-start.25 = (bf16[4,2,64,512]{3,2,1,0:T(8,128)(2,1)S(1)}, bf16[4,2,64,512]{3,2,1,0:T(8,128)(2,1)S(1)}, u32[]{:S(2)}, u32[]{:S(2)}) collective-permute-start(bf16[4,2,64,512]{3,2,1,0:T(8,128)(2,1)S(1)} %collective-permute-done.15.refs_4_), channel_id=1, source_target_pairs={{0,1},{1,0},{2,3},{3,2},{4,5},{5,4},{6,7},{7,6},{8,9},{9,8},{10,11... | collective-permute-start | bytes 1572872 | tf_op jit(solution)/shard_map/ppermute | solution.py:343
  64.0 2.7 %collective-permute-start.24 = (bf16[4,2,64,512]{3,2,1,0:T(8,128)(2,1)S(1)}, bf16[4,2,64,512]{3,2,1,0:T(8,128)(2,1)S(1)}, u32[]{:S(2)}, u32[]{:S(2)}) collective-permute-start(bf16[4,2,64,512]{3,2,1,0:T(8,128)(2,1)S(1)} %collective-permute-done.14.refs_3_), channel_id=1, source_target_pairs={{0,1},{1,0},{2,3},{3,2},{4,5},{5,4},{6,7},{7,6},{8,9},{9,8},{10,11... | collective-permute-start | bytes 1572872 | tf_op jit(solution)/shard_map/ppermute | solution.py:343
  65.2 2.8 %collective-permute-start.26 = (bf16[4,2,64,512]{3,2,1,0:T(8,128)(2,1)S(1)}, bf16[4,2,64,512]{3,2,1,0:T(8,128)(2,1)S(1)}, u32[]{:S(2)}, u32[]{:S(2)}) collective-permute-start(bf16[4,2,64,512]{3,2,1,0:T(8,128)(2,1)S(1)} %collective-permute-done.21.refs_6_), channel_id=1, source_target_pairs={{0,1},{1,0},{2,3},{3,2},{4,5},{5,4},{6,7},{7,6},{8,9},{9,8},{10,11... | collective-permute-start | bytes 1572872 | tf_op jit(solution)/shard_map/ppermute | solution.py:343
  65.3 2.7 %collective-permute-start.23 = (bf16[4,4,48,256]{3,2,1,0:T(8,128)(2,1)S(1)}, bf16[4,4,48,256]{3,2,1,0:T(8,128)(2,1)S(1)}, u32[]{:S(2)}, u32[]{:S(2)}) collective-permute-start(bf16[4,4,48,256]{3,2,1,0:T(8,128)(2,1)S(1)} %pad_maximum_fusion.2.refs_0_), channel_id=1, source_target_pairs={{0,1},{1,0},{2,3},{3,2},{4,5},{5,4},{6,7},{7,6},{8,9},{9,8},{10,11... | collective-permute-start | bytes 1179656 | tf_op jit(solution)/shard_map/ppermute | solution.py:343
  65.9 11.7 %collective-permute-start.27 = (bf16[4,2,64,512]{3,2,1,0:T(8,128)(2,1)S(1)}, bf16[4,2,64,512]{3,2,1,0:T(8,128)(2,1)S(1)}, u32[]{:S(2)}, u32[]{:S(2)}) collective-permute-start(bf16[4,2,64,512]{3,2,1,0:T(8,128)(2,1)S(1)} %pad_maximum_fusion.1.refs_0_), channel_id=1, source_target_pairs={{0,1},{1,0},{2,3},{3,2},{4,5},{5,4},{6,7},{7,6},{8,9},{9,8},{10,11... | collective-permute-start | bytes 1572872 | tf_op jit(solution)/shard_map/ppermute | solution.py:343
  66.7 10.9 %collective-permute-start.28 = (bf16[4,2,64,512]{3,2,1,0:T(8,128)(2,1)S(1)}, bf16[4,2,64,512]{3,2,1,0:T(8,128)(2,1)S(1)}, u32[]{:S(2)}, u32[]{:S(2)}) collective-permute-start(bf16[4,2,64,512]{3,2,1,0:T(8,128)(2,1)S(1)} %collective-permute-done.22.refs_1_), channel_id=1, source_target_pairs={{0,1},{1,0},{2,3},{3,2},{4,5},{5,4},{6,7},{7,6},{8,9},{9,8},{10,11... | collective-permute-start | bytes 1572872 | tf_op jit(solution)/shard_map/ppermute | solution.py:343
  (3 other events, 27.2 us)

commit v13 on v12

--- a/solution.py
+++ b/solution.py
@@ -208,7 +208,7 @@
         b_ref[at + num_vecs : at + 2 * num_vecs, :width] = -imag
         b_ref[at + num_vecs : at + 2 * num_vecs, width:] = real
     left = left_ref[...].reshape(op_count * row_count, 8 * num_vecs)
-    block = min(width, 256)
+    block = min(width, 512)
     for c in range(2):
         for begin in range(0, width, block):
             at = c * width + begin

time: 83.6 us -> 83.6 us (level)
  no operation moved by 1% of the time
where the time goes in v13:
time: 83.6 us; the launch traced here: 83.4 us
  waiting for transfers between devices  30.3 us (36%)
  starting transfers between devices  30.1 us (36%)
  Pallas kernels  19.7 us (24%)
  local copies, waits for them, and re-layouts  2.49 us (3%)
    ppermute x5, waiting for transfers between devices, line_exchange(): gathered = jnp.concatenate([gathered, lax.ppermute(gathered, axis, pairs)])  17.9 us
    ppermute x9, waiting for transfers between devices, passed_in_plane(): return lax.ppermute(value, ('gy', 'gz'), pairs)  9.85 us
    ppermute x9, starting transfers between devices, passed_in_plane(): return lax.ppermute(value, ('gy', 'gz'), pairs)  9.59 us
    pallas_call x1, Pallas kernels, on_device(): pl.pallas_call(functools.partial(left_kernel, 1.0 / math.sqrt(4 * num_vec...  9.57 us
    pallas_call x1, Pallas kernels, on_device(): pl.pallas_call(functools.partial(right_kernel, gz_n, tuple(bwd_parts)), o...  5.81 us
    ppermute x5, starting transfers between devices, line_exchange(): gathered = jnp.concatenate([gathered, lax.ppermute(gathered, axis, pairs)])  5.69 us
    ppermute x1, starting transfers between devices, on_device(): lax.ppermute(fwd_piece, 'gx', [(n, n ^ gx_n // 2) for n in range(gx_n)])  4.1 us
    ppermute x9, starting transfers between devices, passed_in_gz(): return lax.ppermute(value, 'gz', pairs)  3.93 us
  transfers between devices with their start and end apart: 29, of which 14 were waited for; matrix products, arithmetic and copies ran while one was open for 2% of the time, Pallas kernels for 14%

profile of v13, /device:TPU:0, one launch (start us, length us, event | category | flops | bytes accessed | tf_op | source)
XLA Modules:
  0.0 83.4 jit_solution(12358681156023101369)
XLA Ops:
  0.0 2.4 %pieces.1 = (bf16[2,64,512]{2,1,0:T(8,128)(2,1)}, bf16[2,64,512]{2,1,0:T(8,128)(2,1)}) custom-call(s32[1]{0:T(128)} %bitcast.2.z_ref, bf16[2,256,512]{2,1,0:T(8,128)(2,1)} %fwd_in.1, bf16[2,256,512]{2,1,0:T(8,128)(2,1)} %bwd_in.1), custom_call_target="tpu_custom_call" | custom-call | flops 100000000 | bytes 10000000 | tf_op jit(solution)/shard_map/pieces/pallas_call | solution.py:403
  2.4 4.1 %collective-permute-start.3 = (bf16[2,64,512]{2,1,0:T(8,128)(2,1)}, bf16[2,64,512]{2,1,0:T(8,128)(2,1)S(1)}, u32[]{:S(2)}, u32[]{:S(2)}) collective-permute-start(bf16[2,64,512]{2,1,0:T(8,128)(2,1)} %get-tuple-element.40), channel_id=1, source_target_pairs={{0,16},{8,24},{16,0},{24,8},{1,17},{9,25},{17,1},{25,9},{2,18},{10... | collective-permute-start | bytes 393224 | tf_op jit(solution)/shard_map/ppermute | solution.py:418
  6.6 0.9 %copy-done = bf16[2,4,4,2,3,256]{5,3,4,2,1,0:T(2,128)(2,1)S(1)} copy-done((bf16[2,4,4,2,3,256]{5,3,4,2,1,0:T(2,128)(2,1)S(1)}, bf16[2,4,4,2,3,256]{5,3,4,2,1,0:T(2,128)(2,1)}, u32[]{:S(2)}) %copy-start) | copy-done | bytes 98328
  7.5 1.4 %collective-permute-start = (bf16[96,256]{1,0:T(8,128)(2,1)S(1)}, bf16[96,256]{1,0:T(8,128)(2,1)S(1)}, u32[]{:S(2)}, u32[]{:S(2)}) collective-permute-start(bf16[96,256]{1,0:T(8,128)(2,1)S(1)} %get-tuple-element.32), channel_id=1, source_target_pairs={{0,24},{8,0},{16,8},{24,16},{1,25},{9,1},{17,9},{25,17},{2,26},{10... | collective-permute-start | bytes 147464 | tf_op jit(solution)/shard_map/ppermute | solution.py:20
  8.9 1.5 %collective-permute-start.1 = (bf16[48,256]{1,0:T(8,128)(2,1)S(1)}, bf16[48,256]{1,0:T(8,128)(2,1)S(1)}, u32[]{:S(2)}, u32[]{:S(2)}) collective-permute-start(bf16[48,256]{1,0:T(8,128)(2,1)S(1)} %get-tuple-element.33), channel_id=1, source_target_pairs={{0,4},{4,0},{1,5},{5,1},{2,6},{6,2},{3,7},{7,3},{8,12},{12,8},{9,1... | collective-permute-start | bytes 73736 | tf_op jit(solution)/shard_map/ppermute | solution.py:20
  10.5 1.0 %copy.12 = f32[2,4,4,3,2,3,3]{2,1,0,6,5,4,3:T(4,128)S(1)} copy(f32[2,4,4,3,2,3,3]{2,4,6,5,3,1,0:T(2,128)} %param.8) | data formatting | bytes 13824 | tf_op jit(solution)/shard_map/optimization_barrier | solution.py:417
  12.7 1.3 %correlate.1 = bf16[4,4,2,48,256]{4,3,2,1,0:T(8,128)(2,1)S(1)} custom-call(bf16[192,256]{1,0:T(8,128)(2,1)S(1)} %get-tuple-element.31.vec_ref, bf16[96,256]{1,0:T(8,128)(2,1)S(1)} %collective-permute-done.face0, bf16[48,256]{1,0:T(8,128)(2,1)S(1)} %collective-permute-done.1.face1, bf16[48,256]{1,0:T(8,128)(2,1)S(1)} %collective-permute-done.2.face2, ...), custom_call_target="tpu_custom_call" | custom-call | tf_op jit(solution)/shard_map/correlate/pallas_call | solution.py:436
  14.1 1.0 %collective-permute-start.4 = (bf16[2,4,2,48,256]{4,3,1,2,0:T(8,128)(2,1)S(1)}, bf16[2,4,2,48,256]{4,3,1,2,0:T(8,128)(2,1)S(1)}, u32[]{:S(2)}, u32[]{:S(2)}) collective-permute-start(bf16[2,4,2,48,256]{4,3,1,2,0:T(8,128)(2,1)S(1)} %bitcast.48), channel_id=1, source_target_pairs={{0,1},{1,0},{2,3},{3,2},{4,5},{5,4},{6,7},{7,6},{8,9},{9,8},{10,11... | collective-permute-start | bytes 1179656 | tf_op jit(solution)/shard_map/ppermute | solution.py:343
  15.2 1.1 %collective-permute-start.8 = (bf16[2,2,64,512]{3,2,1,0:T(8,128)(2,1)S(1)}, bf16[2,2,64,512]{3,2,1,0:T(8,128)(2,1)S(1)}, u32[]{:S(2)}, u32[]{:S(2)}) collective-permute-start(bf16[2,2,64,512]{3,2,1,0:T(8,128)(2,1)S(1)} %pad_maximum_fusion.3), channel_id=1, source_target_pairs={{0,8},{8,0},{16,24},{24,16},{1,9},{9,1},{17,25},{25,17},{2,10},{10... | collective-permute-start | bytes 786440 | tf_op jit(solution)/shard_map/ppermute | solution.py:365
  16.7 1.4 %collective-permute-start.5 = (bf16[4,48,256]{2,1,0:T(8,128)(2,1)S(1)}, bf16[4,48,256]{2,1,0:T(8,128)(2,1)S(1)}, u32[]{:S(2)}, u32[]{:S(2)}) collective-permute-start(bf16[4,48,256]{2,1,0:T(8,128)(2,1)S(1)} %get-tuple-element.59), channel_id=1, source_target_pairs={{0,4},{1,5},{2,6},{3,7},{4,0},{5,1},{6,2},{7,3},{8,12},{9,13},{10,... | collective-permute-start | bytes 294920 | tf_op jit(solution)/shard_map/ppermute | solution.py:356
  18.1 1.5 %collective-permute-start.7 = (bf16[4,48,256]{2,1,0:T(8,128)(2,1)S(1)}, bf16[4,48,256]{2,1,0:T(8,128)(2,1)S(1)}, u32[]{:S(2)}, u32[]{:S(2)}) collective-permute-start(bf16[4,48,256]{2,1,0:T(8,128)(2,1)S(1)} %get-tuple-element.60), channel_id=1, source_target_pairs={{0,6},{1,7},{2,4},{3,5},{4,2},{5,3},{6,0},{7,1},{8,14},{9,15},{10,... | collective-permute-start | bytes 294920 | tf_op jit(solution)/shard_map/ppermute | solution.py:356
  20.2 3.3 %collective-permute-done.8 = bf16[2,2,64,512]{3,2,1,0:T(8,128)(2,1)S(1)} collective-permute-done((bf16[2,2,64,512]{3,2,1,0:T(8,128)(2,1)S(1)}, bf16[2,2,64,512]{3,2,1,0:T(8,128)(2,1)S(1)}, u32[]{:S(2)}, u32[]{:S(2)}) %collective-permute-start.8) | collective-permute-done | bytes 262176 | tf_op jit(solution)/shard_map/ppermute | solution.py:365
  23.7 1.0 %collective-permute-done.7 = bf16[4,48,256]{2,1,0:T(8,128)(2,1)S(1)} collective-permute-done((bf16[4,48,256]{2,1,0:T(8,128)(2,1)S(1)}, bf16[4,48,256]{2,1,0:T(8,128)(2,1)S(1)}, u32[]{:S(2)}, u32[]{:S(2)}) %collective-permute-start.7) | collective-permute-done | bytes 98336 | tf_op jit(solution)/shard_map/ppermute | solution.py:356
  24.6 1.3 %collective-permute-done.6 = bf16[4,48,256]{2,1,0:T(8,128)(2,1)S(1)} collective-permute-done((bf16[4,48,256]{2,1,0:T(8,128)(2,1)S(1)}, bf16[4,48,256]{2,1,0:T(8,128)(2,1)S(1)}, u32[]{:S(2)}, u32[]{:S(2)}) %collective-permute-start.6) | collective-permute-done | bytes 98336 | tf_op jit(solution)/shard_map/ppermute | solution.py:356
  26.0 2.3 %collective-permute-start.9 = (bf16[2,48,256]{2,1,0:T(8,128)(2,1)S(1)}, bf16[2,48,256]{2,1,0:T(8,128)(2,1)S(1)}, u32[]{:S(2)}, u32[]{:S(2)}) collective-permute-start(bf16[2,48,256]{2,1,0:T(8,128)(2,1)S(1)} %dynamic-slice_bitcast_fusion.3), channel_id=1, source_target_pairs={{0,16},{8,24},{16,0},{24,8},{1,17},{9,25},{17,1},{25,9},{2,18},{10... | collective-permute-start | bytes 147464 | tf_op jit(solution)/shard_map/ppermute | solution.py:469
  28.9 1.4 %collective-permute-start.14 = (bf16[4,2,64,512]{3,2,1,0:T(8,128)(2,1)S(1)}, bf16[4,2,64,512]{3,2,1,0:T(8,128)(2,1)S(1)}, u32[]{:S(2)}, u32[]{:S(2)}) collective-permute-start(bf16[4,2,64,512]{3,2,1,0:T(8,128)(2,1)S(1)} %pad_maximum_fusion.refs_2_), channel_id=1, source_target_pairs={{0,4},{1,5},{2,6},{3,7},{4,0},{5,1},{6,2},{7,3},{8,12},{9,13},{10,... | collective-permute-start | bytes 1572872 | tf_op jit(solution)/shard_map/ppermute | solution.py:356
  30.3 0.7 collective-permute-start.12
  31.1 1.6 %collective-permute-start.10 = (bf16[1,48,256]{2,1,0:T(8,128)(2,1)S(1)}, bf16[1,48,256]{2,1,0:T(8,128)(2,1)S(1)}, u32[]{:S(2)}, u32[]{:S(2)}) collective-permute-start(bf16[1,48,256]{2,1,0:T(8,128)(2,1)S(1)} %constant_dynamic-slice_fusion), channel_id=1, source_target_pairs={{0,8},{8,0},{16,24},{24,16},{1,9},{9,1},{17,25},{25,17},{2,10},{10... | collective-permute-start | bytes 73736 | tf_op jit(solution)/shard_map/ppermute | solution.py:469
  32.7 6.7 %collective-permute-done.12 = bf16[1,2,64,512]{3,2,1,0:T(8,128)(2,1)S(1)} collective-permute-done((bf16[1,2,64,512]{3,2,1,0:T(8,128)(2,1)S(1)}, bf16[1,2,64,512]{3,2,1,0:T(8,128)(2,1)S(1)}, u32[]{:S(2)}, u32[]{:S(2)}) %collective-permute-start.12) | collective-permute-done | bytes 131104 | tf_op jit(solution)/shard_map/ppermute | solution.py:365
  39.5 2.3 %collective-permute-start.11 = (bf16[1,48,256]{2,1,0:T(8,128)(2,1)S(1)}, bf16[1,48,256]{2,1,0:T(8,128)(2,1)S(1)}, u32[]{:S(2)}, u32[]{:S(2)}) collective-permute-start(bf16[1,48,256]{2,1,0:T(8,128)(2,1)S(1)} %add_convert_fusion), channel_id=1, source_target_pairs={{0,16},{8,24},{16,0},{24,8},{1,17},{9,25},{17,1},{25,9},{2,18},{10... | collective-permute-start | bytes 73736 | tf_op jit(solution)/shard_map/ppermute | solution.py:365
  42.0 3.1 %collective-permute-done.11 = bf16[1,48,256]{2,1,0:T(8,128)(2,1)S(1)} collective-permute-done((bf16[1,48,256]{2,1,0:T(8,128)(2,1)S(1)}, bf16[1,48,256]{2,1,0:T(8,128)(2,1)S(1)}, u32[]{:S(2)}, u32[]{:S(2)}) %collective-permute-start.11) | collective-permute-done | bytes 24608 | tf_op jit(solution)/shard_map/ppermute | solution.py:365
  45.1 2.2 %collective-permute-done.13 = bf16[2,2,64,512]{3,2,1,0:T(8,128)(2,1)S(1)} collective-permute-done((bf16[2,2,64,512]{3,2,1,0:T(8,128)(2,1)S(1)}, bf16[2,2,64,512]{3,2,1,0:T(8,128)(2,1)S(1)}, u32[]{:S(2)}, u32[]{:S(2)}) %collective-permute-start.13) | collective-permute-done | bytes 262176 | tf_op jit(solution)/shard_map/ppermute | solution.py:365
  47.4 1.6 %collective-permute-start.22 = (bf16[4,2,64,512]{3,2,1,0:T(8,128)(2,1)S(1)}, bf16[4,2,64,512]{3,2,1,0:T(8,128)(2,1)S(1)}, u32[]{:S(2)}, u32[]{:S(2)}) collective-permute-start(bf16[4,2,64,512]{3,2,1,0:T(8,128)(2,1)S(1)} %pad_maximum_fusion.1.refs_0_), channel_id=1, source_target_pairs={{0,2},{1,3},{2,0},{3,1},{4,6},{5,7},{6,4},{7,5},{8,10},{9,11},{10,... | collective-permute-start | bytes 1572872 | tf_op jit(solution)/shard_map/ppermute | solution.py:343
  49.5 1.4 %collective-permute-start.17 = (bf16[2,48,256]{2,1,0:T(8,128)(2,1)S(1)}, bf16[2,48,256]{2,1,0:T(8,128)(2,1)S(1)}, u32[]{:S(2)}, u32[]{:S(2)}) collective-permute-start(bf16[2,48,256]{2,1,0:T(8,128)(2,1)S(1)} %pad_maximum_fusion.5), channel_id=1, source_target_pairs={{0,8},{8,0},{16,24},{24,16},{1,9},{9,1},{17,25},{25,17},{2,10},{10... | collective-permute-start | bytes 147464 | tf_op jit(solution)/shard_map/ppermute | solution.py:365
  50.9 2.7 %collective-permute-done.17 = bf16[2,48,256]{2,1,0:T(8,128)(2,1)S(1)} collective-permute-done((bf16[2,48,256]{2,1,0:T(8,128)(2,1)S(1)}, bf16[2,48,256]{2,1,0:T(8,128)(2,1)S(1)}, u32[]{:S(2)}, u32[]{:S(2)}) %collective-permute-start.17) | collective-permute-done | bytes 49184 | tf_op jit(solution)/shard_map/ppermute | solution.py:365
  53.6 1.4 %collective-permute-start.20 = (bf16[4,48,256]{2,1,0:T(8,128)(2,1)S(1)}, bf16[4,48,256]{2,1,0:T(8,128)(2,1)S(1)}, u32[]{:S(2)}, u32[]{:S(2)}) collective-permute-start(bf16[4,48,256]{2,1,0:T(8,128)(2,1)S(1)} %constant_dynamic-update-slice_fusion), channel_id=1, source_target_pairs={{0,6},{1,7},{2,4},{3,5},{4,2},{5,3},{6,0},{7,1},{8,14},{9,15},{10,... | collective-permute-start | bytes 294920 | tf_op jit(solution)/shard_map/ppermute | solution.py:356
  55.0 1.5 %collective-permute-start.19 = (bf16[4,48,256]{2,1,0:T(8,128)(2,1)S(1)}, bf16[4,48,256]{2,1,0:T(8,128)(2,1)S(1)}, u32[]{:S(2)}, u32[]{:S(2)}) collective-permute-start(bf16[4,48,256]{2,1,0:T(8,128)(2,1)S(1)} %constant_dynamic-update-slice_fusion), channel_id=1, source_target_pairs={{0,2},{1,3},{2,0},{3,1},{4,6},{5,7},{6,4},{7,5},{8,10},{9,11},{10,... | collective-permute-start | bytes 294920 | tf_op jit(solution)/shard_map/ppermute | solution.py:356
  57.1 7.0 %collective-permute-done.20 = bf16[4,48,256]{2,1,0:T(8,128)(2,1)S(1)} collective-permute-done((bf16[4,48,256]{2,1,0:T(8,128)(2,1)S(1)}, bf16[4,48,256]{2,1,0:T(8,128)(2,1)S(1)}, u32[]{:S(2)}, u32[]{:S(2)}) %collective-permute-start.20) | collective-permute-done | bytes 98336 | tf_op jit(solution)/shard_map/ppermute | solution.py:356
  66.0 0.7 collective-permute-done.24.refs_7_
  66.8 1.2 %collective-permute-done.23.refs_1_ = bf16[4,4,48,256]{3,2,1,0:T(8,128)(2,1)S(1)} collective-permute-done((bf16[4,4,48,256]{3,2,1,0:T(8,128)(2,1)S(1)}, bf16[4,4,48,256]{3,2,1,0:T(8,128)(2,1)S(1)}, u32[]{:S(2)}, u32[]{:S(2)}) %collective-permute-start.23) | collective-permute-done | bytes 393248 | tf_op jit(solution)/shard_map/ppermute | solution.py:343
  68.0 9.6 %left.1.left_ref = bf16[4,256,2048]{2,1,0:T(8,128)(2,1)S(1)} custom-call(s32[3]{0:T(128)S(1)} %pad_add_fusion.me_ref, s32[4]{0:T(128)S(1)} %copy-done.2, f32[4,4,4]{2,1,0:T(4,128)S(1)} %copy-done.1, s32[8]{0:T(128)S(1)} %reshape.40.chain_ref, bf16[4,4,48,256]{3,2,1,0:T(8,128)(2,1)S(1)} %pad_maximum_fusion.2.refs_0_, ...), custom_call_target="tpu_custom_call" | custom-call | flops 8000000000 | bytes 10000000 | tf_op jit(solution)/shard_map/left/pallas_call | solution.py:497
  77.6 5.8 %right.1 = bf16[4,2,256,512]{3,2,1,0:T(8,128)(2,1)} custom-call(bf16[4,256,2048]{2,1,0:T(8,128)(2,1)S(1)} %left.1.left_ref, bf16[4,2,64,512]{3,2,1,0:T(8,128)(2,1)S(1)} %pad_maximum_fusion.1.refs_0_, bf16[4,2,64,512]{3,2,1,0:T(8,128)(2,1)S(1)} %collective-permute-done.22.refs_1_, bf16[4,2,64,512]{3,2,1,0:T(8,128)(2,1)S(1)} %collective-permute-done.27.refs_2_, ...), custom_call_target="tpu_custom_call" | custom-call | tf_op jit(solution)/shard_map/right/pallas_call | solution.py:512
  (67 shorter events, 6.8 us)
Async XLA Ops:
  2.4 11.6 %collective-permute-start.3 = (bf16[2,64,512]{2,1,0:T(8,128)(2,1)}, bf16[2,64,512]{2,1,0:T(8,128)(2,1)S(1)}, u32[]{:S(2)}, u32[]{:S(2)}) collective-permute-start(bf16[2,64,512]{2,1,0:T(8,128)(2,1)} %get-tuple-element.40), channel_id=1, source_target_pairs={{0,16},{8,24},{16,0},{24,8},{1,17},{9,25},{17,1},{25,9},{2,18},{10... | collective-permute-start | bytes 393224 | tf_op jit(solution)/shard_map/ppermute | solution.py:418
  7.5 5.2 %collective-permute-start = (bf16[96,256]{1,0:T(8,128)(2,1)S(1)}, bf16[96,256]{1,0:T(8,128)(2,1)S(1)}, u32[]{:S(2)}, u32[]{:S(2)}) collective-permute-start(bf16[96,256]{1,0:T(8,128)(2,1)S(1)} %get-tuple-element.32), channel_id=1, source_target_pairs={{0,24},{8,0},{16,8},{24,16},{1,25},{9,1},{17,9},{25,17},{2,26},{10... | collective-permute-start | bytes 147464 | tf_op jit(solution)/shard_map/ppermute | solution.py:20
  8.9 3.8 %collective-permute-start.1 = (bf16[48,256]{1,0:T(8,128)(2,1)S(1)}, bf16[48,256]{1,0:T(8,128)(2,1)S(1)}, u32[]{:S(2)}, u32[]{:S(2)}) collective-permute-start(bf16[48,256]{1,0:T(8,128)(2,1)S(1)} %get-tuple-element.33), channel_id=1, source_target_pairs={{0,4},{4,0},{1,5},{5,1},{2,6},{6,2},{3,7},{7,3},{8,12},{12,8},{9,1... | collective-permute-start | bytes 73736 | tf_op jit(solution)/shard_map/ppermute | solution.py:20
  10.4 2.3 %collective-permute-start.2 = (bf16[48,256]{1,0:T(8,128)(2,1)S(1)}, bf16[48,256]{1,0:T(8,128)(2,1)S(1)}, u32[]{:S(2)}, u32[]{:S(2)}) collective-permute-start(bf16[48,256]{1,0:T(8,128)(2,1)S(1)} %get-tuple-element.34), channel_id=1, source_target_pairs={{0,3},{1,0},{2,1},{3,2},{4,7},{5,4},{6,5},{7,6},{8,11},{9,8},{10,9... | collective-permute-start | bytes 73736 | tf_op jit(solution)/shard_map/ppermute | solution.py:20
  12.7 29.1 %copy-start.5 = (s32[4,2]{0,1:T(2,128)S(1)}, s32[4,2]{0,1:T(2,128)}, u32[]{:S(2)}) copy-start(s32[4,2]{0,1:T(2,128)} %param.13) | copy-start | bytes 100
  14.1 53.9 %copy-start.1 = (f32[4,4,4]{2,1,0:T(4,128)S(1)}, f32[4,4,4]{2,1,0:T(4,128)}, u32[]{:S(2)}) copy-start(f32[4,4,4]{2,1,0:T(4,128)} %spin_ref.1) | copy-start | bytes 772
  14.1 53.9 %copy-start.2 = (s32[4]{0:T(128)S(1)}, s32[4]{0:T(128)}, u32[]{:S(2)}) copy-start(s32[4]{0:T(128)} %dirs_ref.1) | copy-start | bytes 52
  14.1 2.4 %collective-permute-start.4 = (bf16[2,4,2,48,256]{4,3,1,2,0:T(8,128)(2,1)S(1)}, bf16[2,4,2,48,256]{4,3,1,2,0:T(8,128)(2,1)S(1)}, u32[]{:S(2)}, u32[]{:S(2)}) collective-permute-start(bf16[2,4,2,48,256]{4,3,1,2,0:T(8,128)(2,1)S(1)} %bitcast.48), channel_id=1, source_target_pairs={{0,1},{1,0},{2,3},{3,2},{4,5},{5,4},{6,7},{7,6},{8,9},{9,8},{10,11... | collective-permute-start | bytes 1179656 | tf_op jit(solution)/shard_map/ppermute | solution.py:343
  15.2 8.4 %collective-permute-start.8 = (bf16[2,2,64,512]{3,2,1,0:T(8,128)(2,1)S(1)}, bf16[2,2,64,512]{3,2,1,0:T(8,128)(2,1)S(1)}, u32[]{:S(2)}, u32[]{:S(2)}) collective-permute-start(bf16[2,2,64,512]{3,2,1,0:T(8,128)(2,1)S(1)} %pad_maximum_fusion.3), channel_id=1, source_target_pairs={{0,8},{8,0},{16,24},{24,16},{1,9},{9,1},{17,25},{25,17},{2,10},{10... | collective-permute-start | bytes 786440 | tf_op jit(solution)/shard_map/ppermute | solution.py:365
  16.7 7.0 %collective-permute-start.5 = (bf16[4,48,256]{2,1,0:T(8,128)(2,1)S(1)}, bf16[4,48,256]{2,1,0:T(8,128)(2,1)S(1)}, u32[]{:S(2)}, u32[]{:S(2)}) collective-permute-start(bf16[4,48,256]{2,1,0:T(8,128)(2,1)S(1)} %get-tuple-element.59), channel_id=1, source_target_pairs={{0,4},{1,5},{2,6},{3,7},{4,0},{5,1},{6,2},{7,3},{8,12},{9,13},{10,... | collective-permute-start | bytes 294920 | tf_op jit(solution)/shard_map/ppermute | solution.py:356
  18.1 6.5 %collective-permute-start.7 = (bf16[4,48,256]{2,1,0:T(8,128)(2,1)S(1)}, bf16[4,48,256]{2,1,0:T(8,128)(2,1)S(1)}, u32[]{:S(2)}, u32[]{:S(2)}) collective-permute-start(bf16[4,48,256]{2,1,0:T(8,128)(2,1)S(1)} %get-tuple-element.60), channel_id=1, source_target_pairs={{0,6},{1,7},{2,4},{3,5},{4,2},{5,3},{6,0},{7,1},{8,14},{9,15},{10,... | collective-permute-start | bytes 294920 | tf_op jit(solution)/shard_map/ppermute | solution.py:356
  19.6 6.3 %collective-permute-start.6 = (bf16[4,48,256]{2,1,0:T(8,128)(2,1)S(1)}, bf16[4,48,256]{2,1,0:T(8,128)(2,1)S(1)}, u32[]{:S(2)}, u32[]{:S(2)}) collective-permute-start(bf16[4,48,256]{2,1,0:T(8,128)(2,1)S(1)} %get-tuple-element.61), channel_id=1, source_target_pairs={{0,2},{1,3},{2,0},{3,1},{4,6},{5,7},{6,4},{7,5},{8,10},{9,11},{10,... | collective-permute-start | bytes 294920 | tf_op jit(solution)/shard_map/ppermute | solution.py:356
  26.0 5.1 %collective-permute-start.9 = (bf16[2,48,256]{2,1,0:T(8,128)(2,1)S(1)}, bf16[2,48,256]{2,1,0:T(8,128)(2,1)S(1)}, u32[]{:S(2)}, u32[]{:S(2)}) collective-permute-start(bf16[2,48,256]{2,1,0:T(8,128)(2,1)S(1)} %dynamic-slice_bitcast_fusion.3), channel_id=1, source_target_pairs={{0,16},{8,24},{16,0},{24,8},{1,17},{9,25},{17,1},{25,9},{2,18},{10... | collective-permute-start | bytes 147464 | tf_op jit(solution)/shard_map/ppermute | solution.py:469
  28.3 19.1 %collective-permute-start.16 = (bf16[4,2,64,512]{3,2,1,0:T(8,128)(2,1)S(1)}, bf16[4,2,64,512]{3,2,1,0:T(8,128)(2,1)S(1)}, u32[]{:S(2)}, u32[]{:S(2)}) collective-permute-start(bf16[4,2,64,512]{3,2,1,0:T(8,128)(2,1)S(1)} %pad_maximum_fusion.refs_2_), channel_id=1, source_target_pairs={{0,1},{1,0},{2,3},{3,2},{4,5},{5,4},{6,7},{7,6},{8,9},{9,8},{10,11... | collective-permute-start | bytes 1572872 | tf_op jit(solution)/shard_map/ppermute | solution.py:343
  28.3 19.1 %collective-permute-start.15 = (bf16[4,2,64,512]{3,2,1,0:T(8,128)(2,1)S(1)}, bf16[4,2,64,512]{3,2,1,0:T(8,128)(2,1)S(1)}, u32[]{:S(2)}, u32[]{:S(2)}) collective-permute-start(bf16[4,2,64,512]{3,2,1,0:T(8,128)(2,1)S(1)} %pad_maximum_fusion.refs_2_), channel_id=1, source_target_pairs={{0,2},{1,3},{2,0},{3,1},{4,6},{5,7},{6,4},{7,5},{8,10},{9,11},{10,... | collective-permute-start | bytes 1572872 | tf_op jit(solution)/shard_map/ppermute | solution.py:356
  28.9 18.5 %collective-permute-start.14 = (bf16[4,2,64,512]{3,2,1,0:T(8,128)(2,1)S(1)}, bf16[4,2,64,512]{3,2,1,0:T(8,128)(2,1)S(1)}, u32[]{:S(2)}, u32[]{:S(2)}) collective-permute-start(bf16[4,2,64,512]{3,2,1,0:T(8,128)(2,1)S(1)} %pad_maximum_fusion.refs_2_), channel_id=1, source_target_pairs={{0,4},{1,5},{2,6},{3,7},{4,0},{5,1},{6,2},{7,3},{8,12},{9,13},{10,... | collective-permute-start | bytes 1572872 | tf_op jit(solution)/shard_map/ppermute | solution.py:356
  30.3 9.1 %collective-permute-start.12 = (bf16[1,2,64,512]{3,2,1,0:T(8,128)(2,1)S(1)}, bf16[1,2,64,512]{3,2,1,0:T(8,128)(2,1)S(1)}, u32[]{:S(2)}, u32[]{:S(2)}) collective-permute-start(bf16[1,2,64,512]{3,2,1,0:T(8,128)(2,1)S(1)} %bitcast.41), channel_id=1, source_target_pairs={{0,16},{8,24},{16,0},{24,8},{1,17},{9,25},{17,1},{25,9},{2,18},{10... | collective-permute-start | bytes 393224 | tf_op jit(solution)/shard_map/ppermute | solution.py:365
  31.1 8.3 %collective-permute-start.10 = (bf16[1,48,256]{2,1,0:T(8,128)(2,1)S(1)}, bf16[1,48,256]{2,1,0:T(8,128)(2,1)S(1)}, u32[]{:S(2)}, u32[]{:S(2)}) collective-permute-start(bf16[1,48,256]{2,1,0:T(8,128)(2,1)S(1)} %constant_dynamic-slice_fusion), channel_id=1, source_target_pairs={{0,8},{8,0},{16,24},{24,16},{1,9},{9,1},{17,25},{25,17},{2,10},{10... | collective-permute-start | bytes 73736 | tf_op jit(solution)/shard_map/ppermute | solution.py:469
  39.4 7.9 %collective-permute-start.13 = (bf16[2,2,64,512]{3,2,1,0:T(8,128)(2,1)S(1)}, bf16[2,2,64,512]{3,2,1,0:T(8,128)(2,1)S(1)}, u32[]{:S(2)}, u32[]{:S(2)}) collective-permute-start(bf16[2,2,64,512]{3,2,1,0:T(8,128)(2,1)S(1)} %pad_maximum_fusion.4), channel_id=1, source_target_pairs={{0,8},{8,0},{16,24},{24,16},{1,9},{9,1},{17,25},{25,17},{2,10},{10... | collective-permute-start | bytes 786440 | tf_op jit(solution)/shard_map/ppermute | solution.py:365
  39.5 5.6 %collective-permute-start.11 = (bf16[1,48,256]{2,1,0:T(8,128)(2,1)S(1)}, bf16[1,48,256]{2,1,0:T(8,128)(2,1)S(1)}, u32[]{:S(2)}, u32[]{:S(2)}) collective-permute-start(bf16[1,48,256]{2,1,0:T(8,128)(2,1)S(1)} %add_convert_fusion), channel_id=1, source_target_pairs={{0,16},{8,24},{16,0},{24,8},{1,17},{9,25},{17,1},{25,9},{2,18},{10... | collective-permute-start | bytes 73736 | tf_op jit(solution)/shard_map/ppermute | solution.py:365
  47.4 17.8 %collective-permute-start.22 = (bf16[4,2,64,512]{3,2,1,0:T(8,128)(2,1)S(1)}, bf16[4,2,64,512]{3,2,1,0:T(8,128)(2,1)S(1)}, u32[]{:S(2)}, u32[]{:S(2)}) collective-permute-start(bf16[4,2,64,512]{3,2,1,0:T(8,128)(2,1)S(1)} %pad_maximum_fusion.1.refs_0_), channel_id=1, source_target_pairs={{0,2},{1,3},{2,0},{3,1},{4,6},{5,7},{6,4},{7,5},{8,10},{9,11},{10,... | collective-permute-start | bytes 1572872 | tf_op jit(solution)/shard_map/ppermute | solution.py:343
  48.9 16.3 %collective-permute-start.21 = (bf16[4,2,64,512]{3,2,1,0:T(8,128)(2,1)S(1)}, bf16[4,2,64,512]{3,2,1,0:T(8,128)(2,1)S(1)}, u32[]{:S(2)}, u32[]{:S(2)}) collective-permute-start(bf16[4,2,64,512]{3,2,1,0:T(8,128)(2,1)S(1)} %collective-permute-done.15.refs_4_), channel_id=1, source_target_pairs={{0,4},{1,5},{2,6},{3,7},{4,0},{5,1},{6,2},{7,3},{8,12},{9,13},{10,... | collective-permute-start | bytes 1572872 | tf_op jit(solution)/shard_map/ppermute | solution.py:356
  49.5 4.1 %collective-permute-start.17 = (bf16[2,48,256]{2,1,0:T(8,128)(2,1)S(1)}, bf16[2,48,256]{2,1,0:T(8,128)(2,1)S(1)}, u32[]{:S(2)}, u32[]{:S(2)}) collective-permute-start(bf16[2,48,256]{2,1,0:T(8,128)(2,1)S(1)} %pad_maximum_fusion.5), channel_id=1, source_target_pairs={{0,8},{8,0},{16,24},{24,16},{1,9},{9,1},{17,25},{25,17},{2,10},{10... | collective-permute-start | bytes 147464 | tf_op jit(solution)/shard_map/ppermute | solution.py:365
  53.6 10.5 %collective-permute-start.20 = (bf16[4,48,256]{2,1,0:T(8,128)(2,1)S(1)}, bf16[4,48,256]{2,1,0:T(8,128)(2,1)S(1)}, u32[]{:S(2)}, u32[]{:S(2)}) collective-permute-start(bf16[4,48,256]{2,1,0:T(8,128)(2,1)S(1)} %constant_dynamic-update-slice_fusion), channel_id=1, source_target_pairs={{0,6},{1,7},{2,4},{3,5},{4,2},{5,3},{6,0},{7,1},{8,14},{9,15},{10,... | collective-permute-start | bytes 294920 | tf_op jit(solution)/shard_map/ppermute | solution.py:356
  55.0 9.0 %collective-permute-start.19 = (bf16[4,48,256]{2,1,0:T(8,128)(2,1)S(1)}, bf16[4,48,256]{2,1,0:T(8,128)(2,1)S(1)}, u32[]{:S(2)}, u32[]{:S(2)}) collective-permute-start(bf16[4,48,256]{2,1,0:T(8,128)(2,1)S(1)} %constant_dynamic-update-slice_fusion), channel_id=1, source_target_pairs={{0,2},{1,3},{2,0},{3,1},{4,6},{5,7},{6,4},{7,5},{8,10},{9,11},{10,... | collective-permute-start | bytes 294920 | tf_op jit(solution)/shard_map/ppermute | solution.py:356
  56.5 8.6 %collective-permute-start.18 = (bf16[4,48,256]{2,1,0:T(8,128)(2,1)S(1)}, bf16[4,48,256]{2,1,0:T(8,128)(2,1)S(1)}, u32[]{:S(2)}, u32[]{:S(2)}) collective-permute-start(bf16[4,48,256]{2,1,0:T(8,128)(2,1)S(1)} %constant_dynamic-update-slice_fusion), channel_id=1, source_target_pairs={{0,4},{1,5},{2,6},{3,7},{4,0},{5,1},{6,2},{7,3},{8,12},{9,13},{10,... | collective-permute-start | bytes 294920 | tf_op jit(solution)/shard_map/ppermute | solution.py:356
  64.0 2.8 %collective-permute-start.25 = (bf16[4,2,64,512]{3,2,1,0:T(8,128)(2,1)S(1)}, bf16[4,2,64,512]{3,2,1,0:T(8,128)(2,1)S(1)}, u32[]{:S(2)}, u32[]{:S(2)}) collective-permute-start(bf16[4,2,64,512]{3,2,1,0:T(8,128)(2,1)S(1)} %collective-permute-done.15.refs_4_), channel_id=1, source_target_pairs={{0,1},{1,0},{2,3},{3,2},{4,5},{5,4},{6,7},{7,6},{8,9},{9,8},{10,11... | collective-permute-start | bytes 1572872 | tf_op jit(solution)/shard_map/ppermute | solution.py:343
  64.0 2.7 %collective-permute-start.24 = (bf16[4,2,64,512]{3,2,1,0:T(8,128)(2,1)S(1)}, bf16[4,2,64,512]{3,2,1,0:T(8,128)(2,1)S(1)}, u32[]{:S(2)}, u32[]{:S(2)}) collective-permute-start(bf16[4,2,64,512]{3,2,1,0:T(8,128)(2,1)S(1)} %collective-permute-done.14.refs_3_), channel_id=1, source_target_pairs={{0,1},{1,0},{2,3},{3,2},{4,5},{5,4},{6,7},{7,6},{8,9},{9,8},{10,11... | collective-permute-start | bytes 1572872 | tf_op jit(solution)/shard_map/ppermute | solution.py:343
  65.2 2.8 %collective-permute-start.26 = (bf16[4,2,64,512]{3,2,1,0:T(8,128)(2,1)S(1)}, bf16[4,2,64,512]{3,2,1,0:T(8,128)(2,1)S(1)}, u32[]{:S(2)}, u32[]{:S(2)}) collective-permute-start(bf16[4,2,64,512]{3,2,1,0:T(8,128)(2,1)S(1)} %collective-permute-done.21.refs_6_), channel_id=1, source_target_pairs={{0,1},{1,0},{2,3},{3,2},{4,5},{5,4},{6,7},{7,6},{8,9},{9,8},{10,11... | collective-permute-start | bytes 1572872 | tf_op jit(solution)/shard_map/ppermute | solution.py:343
  65.3 2.7 %collective-permute-start.23 = (bf16[4,4,48,256]{3,2,1,0:T(8,128)(2,1)S(1)}, bf16[4,4,48,256]{3,2,1,0:T(8,128)(2,1)S(1)}, u32[]{:S(2)}, u32[]{:S(2)}) collective-permute-start(bf16[4,4,48,256]{3,2,1,0:T(8,128)(2,1)S(1)} %pad_maximum_fusion.2.refs_0_), channel_id=1, source_target_pairs={{0,1},{1,0},{2,3},{3,2},{4,5},{5,4},{6,7},{7,6},{8,9},{9,8},{10,11... | collective-permute-start | bytes 1179656 | tf_op jit(solution)/shard_map/ppermute | solution.py:343
  65.9 11.7 %collective-permute-start.27 = (bf16[4,2,64,512]{3,2,1,0:T(8,128)(2,1)S(1)}, bf16[4,2,64,512]{3,2,1,0:T(8,128)(2,1)S(1)}, u32[]{:S(2)}, u32[]{:S(2)}) collective-permute-start(bf16[4,2,64,512]{3,2,1,0:T(8,128)(2,1)S(1)} %pad_maximum_fusion.1.refs_0_), channel_id=1, source_target_pairs={{0,1},{1,0},{2,3},{3,2},{4,5},{5,4},{6,7},{7,6},{8,9},{9,8},{10,11... | collective-permute-start | bytes 1572872 | tf_op jit(solution)/shard_map/ppermute | solution.py:343
  66.7 10.9 %collective-permute-start.28 = (bf16[4,2,64,512]{3,2,1,0:T(8,128)(2,1)S(1)}, bf16[4,2,64,512]{3,2,1,0:T(8,128)(2,1)S(1)}, u32[]{:S(2)}, u32[]{:S(2)}) collective-permute-start(bf16[4,2,64,512]{3,2,1,0:T(8,128)(2,1)S(1)} %collective-permute-done.22.refs_1_), channel_id=1, source_target_pairs={{0,1},{1,0},{2,3},{3,2},{4,5},{5,4},{6,7},{7,6},{8,9},{9,8},{10,11... | collective-permute-start | bytes 1572872 | tf_op jit(solution)/shard_map/ppermute | solution.py:343
  (3 other events, 27.2 us)
